TPU v7x, 768 devices: a whole 4x8x12 slice. The times are simulated.
768 devices in a mesh: dp: 48 (over z_hi, y, core), fsdp: 16 (over x, z_lo).
Axes of the slice: x: 4, y: 8, z: 12 (z_hi: 3, z_lo: 4; z = z_hi * 4 + z_lo), core: 2. Of those that a mesh axis runs over, the one named last changes fastest.
Arguments:
- queries: bfloat16 [18432, 4096], P('dp', 'fsdp'), may hold values from -16 to 16
- key_rows: bfloat16 [18432, 4096], P('dp', 'fsdp'), may hold values from -16 to 16
- value_rows: bfloat16 [18432, 4096], P('dp', 'fsdp'), may hold values from -6 to 6
- image_ids: int32 [18432], P('dp'), may hold values from 0 to 18304, as said below
- send_slot: int32 [18432], P('dp'), may hold values from 0 to 511, as said below
- out_weight: bfloat16 [4096, 6144], P('fsdp'), may hold values from -0.09375 to 0.09375
- grad_out: bfloat16 [24576, 6144], P('dp'), may hold values from -0.59765625 to 0.59765625
Outputs:
- grad_query: bfloat16 [18432, 4096], P('dp', 'fsdp')
- grad_key: bfloat16 [18432, 4096], P('dp', 'fsdp')
- grad_value: bfloat16 [18432, 4096], P('dp', 'fsdp')
- grad_weight: float32 [4096, 6144], P('fsdp', 'dp')
Inputs may be any that keep to these rules, and one draw needn't show every extreme that they name: `send_slot`: each rank moves at most one image, of exactly 128 rows, to the next rank along dp (the last rank to the first); its rows take slots 384 to 511 in order; every other row keeps its own position in its rank; some rank moves an image in every draw. `image_ids`: images are runs of consecutive rows of one rank made of 1 to 3 whole aligned blocks of 128 rows; the id is the global index of the image's first row.
All inputs are finite; a program needn't handle non-finite values.
Results may differ from a plain program's by a relative error of at most 0.0074.
Values may be sent and summed in bfloat16 or wider, within the bound.
No kernel may reach another device: no remote copies, remote signals or barrier semaphores. Data moves between devices by JAX's collectives and lax.ppermute only.
A program may use at most 64 MiB of HBM per device.

v0:
```python
import jax
import jax.numpy as jnp
from jax import lax
from jax.sharding import PartitionSpec as P

HD = 128


def shifted(block, axis, distance):
    devices = range(lax.axis_size(axis))
    route = [((i - distance) % len(devices), i) for i in devices]
    return lax.ppermute(block, axis, route)


def local(queries, key_rows, value_rows, image_ids, send_slot, out_weight, grad_out):
    row_count = queries.shape[0]
    feat_width = queries.shape[1]
    head_count = feat_width // HD
    slot_count = grad_out.shape[0]
    score_scale = HD ** (-0.5)
    packed = jnp.concatenate([queries, key_rows, value_rows], axis=1)
    sectioned = jnp.zeros((slot_count, 3 * feat_width), jnp.bfloat16).at[send_slot].set(packed)
    sectioned_labels = jnp.full((slot_count,), -1, jnp.int32).at[send_slot].set(image_ids)
    incoming, incoming_labels = shifted(
        (sectioned[row_count:], sectioned_labels[row_count:]), "dp", 1
    )
    arrived = jnp.concatenate([sectioned[:row_count], incoming], axis=0).reshape(
        slot_count, 3, head_count, HD
    )
    owners = jnp.concatenate([sectioned_labels[:row_count], incoming_labels], axis=0)
    query_slot = arrived[:, 0]
    key_slot = arrived[:, 1]
    value_slot = arrived[:, 2]
    scores = (
        jnp.einsum("qhd,khd->hqk", query_slot, key_slot, preferred_element_type=jnp.float32)
        * score_scale
    )
    same_image = owners[:, None] == owners[None, :]
    scores = jnp.where(same_image[None], scores, -jnp.inf)
    row_top = jnp.max(scores, axis=-1, keepdims=True)
    expo = jnp.exp(scores - row_top)
    weights = expo / jnp.sum(expo, axis=-1, keepdims=True)
    prob_bf = weights.astype(jnp.bfloat16)
    context = jnp.einsum(
        "hqk,khd->qhd", prob_bf, value_slot, preferred_element_type=jnp.float32
    ).astype(jnp.bfloat16)
    flat_ctx = context.reshape(slot_count, feat_width)
    grad_ctx = lax.dot_general(
        grad_out, out_weight, (((1,), (1,)), ((), ())), preferred_element_type=jnp.float32
    ).astype(jnp.bfloat16)
    partial_grad = lax.dot_general(
        flat_ctx, grad_out, (((0,), (0,)), ((), ())), preferred_element_type=jnp.float32
    )
    grad_weight = lax.psum_scatter(partial_grad, "dp", scatter_dimension=1, tiled=True)
    grad_heads = grad_ctx.reshape(slot_count, head_count, HD)
    value_back = jnp.einsum(
        "hqk,qhd->khd", prob_bf, grad_heads, preferred_element_type=jnp.float32
    ).astype(jnp.bfloat16)
    grad_prob = jnp.einsum(
        "qhd,khd->hqk", grad_heads, value_slot, preferred_element_type=jnp.float32
    )
    inner_sum = jnp.sum(weights * grad_prob, axis=-1, keepdims=True)
    grad_score = (weights * (grad_prob - inner_sum)).astype(jnp.bfloat16)
    query_back = (
        jnp.einsum("hqk,khd->qhd", grad_score, key_slot, preferred_element_type=jnp.float32)
        * score_scale
    ).astype(jnp.bfloat16)
    key_back = (
        jnp.einsum("hqk,qhd->khd", grad_score, query_slot, preferred_element_type=jnp.float32)
        * score_scale
    ).astype(jnp.bfloat16)
    leaving = jnp.stack([query_back, key_back, value_back], axis=1).reshape(
        slot_count, 3 * feat_width
    )
    returned = shifted(leaving[row_count:], "dp", -1)
    combined = jnp.concatenate([leaving[:row_count], returned], axis=0)
    own_rows = combined[send_slot]
    grad_query = own_rows[:, :feat_width]
    grad_key = own_rows[:, feat_width : 2 * feat_width]
    grad_value = own_rows[:, 2 * feat_width :]
    return (grad_query, grad_key, grad_value, grad_weight)


def solution(mesh):
    placed = (
        P("dp", "fsdp"),
        P("dp", "fsdp"),
        P("dp", "fsdp"),
        P("dp"),
        P("dp"),
        P("fsdp", None),
        P("dp", None),
    )
    return jax.shard_map(
        local,
        mesh=mesh,
        in_specs=placed,
        out_specs=(P("dp", "fsdp"), P("dp", "fsdp"), P("dp", "fsdp"), P("fsdp", "dp")),
        check_vma=False,
    )
```

profile of v0, /device:TPU:6, one launch (start us, length us, event | category | flops | bytes accessed | tf_op | source)
XLA Modules:
  0.0 290.4 jit_solution(2500409916489629959)
XLA Ops:
  7.2 0.0 copy-start
  7.2 0.0 reduce-scatter.2.cloned.1.call-start
  7.2 0.8 compare_select_fusion
  8.1 3.2 %scatter_custom_fusion.1 = s32[512]{0:T(512)S(1)} fusion(s32[384]{0:T(512)S(1)} %compare_select_fusion, s32[384]{0:T(512)} %param.10, s32[]{:T(128)} %constant.2.clone.1), kind=kCustom, calls=%fused_computation.45 | custom fusion | bytes 2560 | tf_op jit(solution)/shard_map/scatter | solution.py:23
  11.3 1.9 collective-permute-start.1
  13.2 3.7 %scatter_custom_fusion = bf16[512,768]{1,0:T(8,128)(2,1)} fusion(s32[384]{0:T(512)S(1)} %compare_select_fusion, bf16[384,256]{1,0:T(8,128)(2,1)} %param.9, bf16[]{:T(256)} %constant.16, bf16[384,256]{1,0:T(8,128)(2,1)} %param.8, bf16[384,256]{1,0:T(8,128)(2,1)} %param.7, bf16[]{:T(256)} %constant.7.clone.1), kind=kCustom, calls=%fused_computation.26 | custom fusion | flops 1769472 | bytes 1376260 | tf_op jit(solution)/shard_map/scatter | solution.py:22
  16.9 0.0 slice-start
  16.9 1.0 slice.59
  17.9 3.8 %collective-permute-start = (bf16[128,768]{1,0:T(8,128)(2,1)S(1)}, bf16[128,768]{1,0:T(8,128)(2,1)S(1)}, u32[]{:S(2)}, u32[]{:S(2)}) collective-permute-start(bf16[128,768]{1,0:T(8,128)(2,1)S(1)} %slice.59), channel_id=1, source_target_pairs={{752,0},{0,16},{16,32},{32,48},{48,64},{64,80},{80,96},{96,112},{1... | collective-permute-start | bytes 589832 | tf_op jit(solution)/shard_map/ppermute | solution.py:12
  21.6 7.7 %collective-permute-done.1 = s32[128]{0:T(128)S(1)} collective-permute-done((s32[128]{0:T(128)S(1)}, s32[128]{0:T(128)S(1)}, u32[]{:S(2)}, u32[]{:S(2)}) %collective-permute-start.1) | collective-permute-done | bytes 544 | tf_op jit(solution)/shard_map/ppermute | solution.py:12
  29.4 0.2 broadcast_compare_fusion
  29.6 0.0 copy-start.5
  29.6 8.8 %collective-permute-done = bf16[128,768]{1,0:T(8,128)(2,1)S(1)} collective-permute-done((bf16[128,768]{1,0:T(8,128)(2,1)S(1)}, bf16[128,768]{1,0:T(8,128)(2,1)S(1)}, u32[]{:S(2)}, u32[]{:S(2)}) %collective-permute-start) | collective-permute-done | bytes 196640 | tf_op jit(solution)/shard_map/ppermute | solution.py:12
  38.4 0.0 slice-done
  38.4 0.9 pad_maximum_fusion
  39.3 2.3 copy.21
  41.7 3.3 %fusion.26 = (f32[2,512]{1,0:T(2,128)S(1)}, f32[2,512,512]{1,2,0:T(8,128)}) fusion(pred[512,512]{0,1:T(8,128)(4,1)S(1)} %broadcast_compare_fusion, bf16[512,3,2,128]{0,3,2,1:T(8,128)(2,1)} %bitcast.83), kind=kOutput, calls=%fused_computation.50 | convolution fusion | flops 136315392 | bytes 2887680 | tf_op jit(solution)/shard_map/sub | solution.py:41
  45.0 0.0 copy-done.5
  45.0 2.4 convolution_convert_fusion.1
  47.5 7.3 %fusion.27 = f32[256,6144]{1,0:T(8,128)} fusion(bf16[512,256]{0,1:T(8,128)(2,1)S(1)} %bitcast.90, bf16[512,6144]{1,0:T(8,128)(2,1)} %param.13), kind=kOutput, calls=%fused_computation.51 | convolution fusion | flops 1610612736 | bytes 12845056 | tf_op jit(solution)/shard_map/dot_general | solution.py:51
  54.7 0.0 reduce-scatter.2.cloned.1.call-update
  54.7 0.0 copy-done
  54.7 4.6 %convolution_convert_fusion = bf16[512,256]{0,1:T(8,128)(2,1)S(1)} fusion(bf16[512,6144]{1,0:T(8,128)(2,1)} %param.13, bf16[256,6144]{1,0:T(8,128)(2,1)S(1)} %copy-done), kind=kOutput, calls=%fused_computation.11 | convolution fusion | flops 1610743808 | bytes 9699328 | tf_op jit(solution)/shard_map/dot_general | solution.py:48
  59.4 3.1 %fusion.4 = bf16[512,1,2,128]{0,3,2,1:T(8,128)(2,1)} fusion(bf16[512,2,128]{0,2,1:T(8,128)(2,1)S(1)} %bitcast.92, f32[2,512]{1,0:T(2,128)S(1)} %get-tuple-element.7, pred[512,512]{0,1:T(8,128)(4,1)} %copy-done.5, bf16[512,3,2,128]{0,3,2,1:T(8,128)(2,1)} %bitcast.85), kind=kOutput, calls=%fused_computation.16 | convolution fusion | flops 271189504 | bytes 1314816 | tf_op jit(solution)/shard_map/hqk,qhd->khd/dot_general | solution.py:56
  62.5 0.0 copy-start.3
  62.5 2.3 multiply_reduce_fusion
  64.8 0.0 copy-done.3
  64.8 0.0 copy-start.2
  64.8 0.6 multiply_convert_fusion
  65.4 0.6 copy-done.2
  65.9 0.0 copy-start.4
  65.9 0.5 fusion.5
  66.4 0.3 fusion.6
  66.7 0.0 copy-start.1
  66.7 0.7 copy-done.1
  67.4 0.0 copy-done.4
  67.4 0.7 pad_maximum_fusion.3
  68.2 1.7 copy.31
  69.9 1.9 collective-permute-start.2
  71.8 1.1 pad_maximum_fusion.1
  73.0 0.9 slice.63
  73.8 2.1 copy.32
  76.0 0.0 collective-permute-done.2
  76.0 2.1 pad_maximum_fusion.2
  78.1 4.3 %gather_fusion = bf16[384,768]{1,0:T(8,128)(2,1)} fusion(bf16[512,768]{1,0:T(8,128)(2,1)} %pad_maximum_fusion.2, s32[1024]{0:T(1024)S(1)} %pad_clamp_fusion), kind=kCustom, calls=%fused_computation | custom fusion | bytes 1181184 | tf_op jit(solution)/shard_map/gather | solution.py:77
  82.4 2.0 fusion.25
  84.4 199.2 %reduce-scatter.2.cloned.1.call-done = f32[256,128]{1,0:T(8,128)} async-done(((f32[256,6144]{1,0:T(8,128)}), f32[256,128]{1,0:T(8,128)}) %reduce-scatter.2.cloned.1.call-update) | async-done | bytes 131088 | tf_op jit(solution)/shard_map/reduce_scatter | solution.py:54
  (3 shorter events, 0.0 us)
Async XLA Ops:
  7.2 47.6 %copy-start = (bf16[256,6144]{1,0:T(8,128)(2,1)S(1)}, bf16[256,6144]{1,0:T(8,128)(2,1)}, u32[]{:S(2)}) copy-start(bf16[256,6144]{1,0:T(8,128)(2,1)} %param.12) | copy-start | bytes 9437188
  7.2 276.4 %reduce-scatter.2.cloned.1.call-start = ((), (), s32[]{:S(2)}) async-start(), calls=%async_computation.1 | async-start | bytes 6422528 | tf_op jit(solution)/shard_map/reduce_scatter | solution.py:54
  11.3 18.1 %collective-permute-start.1 = (s32[128]{0:T(128)S(1)}, s32[128]{0:T(128)S(1)}, u32[]{:S(2)}, u32[]{:S(2)}) collective-permute-start(s32[128]{0:T(128)S(1)} %slice.46), channel_id=1, source_target_pairs={{752,0},{0,16},{16,32},{32,48},{48,64},{64,80},{80,96},{96,112},{1... | collective-permute-start | bytes 1544 | tf_op jit(solution)/shard_map/ppermute | solution.py:12
  16.9 21.6 %slice-start = ((bf16[512,768]{1,0:T(8,128)(2,1)}), bf16[384,768]{1,0:T(8,128)(2,1)S(1)}, s32[]{:S(2)}) async-start(bf16[512,768]{1,0:T(8,128)(2,1)} %scatter_custom_fusion), calls=%async_computation.2 | async-start | bytes 1179648 | tf_op jit(solution)/shard_map/slice | solution.py:27
  17.9 20.5 %collective-permute-start = (bf16[128,768]{1,0:T(8,128)(2,1)S(1)}, bf16[128,768]{1,0:T(8,128)(2,1)S(1)}, u32[]{:S(2)}, u32[]{:S(2)}) collective-permute-start(bf16[128,768]{1,0:T(8,128)(2,1)S(1)} %slice.59), channel_id=1, source_target_pairs={{752,0},{0,16},{16,32},{32,48},{48,64},{64,80},{80,96},{96,112},{1... | collective-permute-start | bytes 589832 | tf_op jit(solution)/shard_map/ppermute | solution.py:12
  29.6 15.4 %copy-start.5 = (pred[512,512]{0,1:T(8,128)(4,1)}, pred[512,512]{0,1:T(8,128)(4,1)S(1)}, u32[]{:S(2)}) copy-start(pred[512,512]{0,1:T(8,128)(4,1)S(1)} %broadcast_compare_fusion) | copy-start | bytes 786436
  62.5 2.3 copy-start.3
  64.8 1.1 copy-start.2
  65.9 1.5 copy-start.4
  66.7 0.7 copy-start.1
  69.9 6.1 %collective-permute-start.2 = (bf16[128,768]{1,0:T(8,128)(2,1)}, bf16[128,768]{1,0:T(8,128)(2,1)}, u32[]{:S(2)}, u32[]{:S(2)}) collective-permute-start(bf16[128,768]{1,0:T(8,128)(2,1)} %copy.31), channel_id=1, source_target_pairs={{16,0},{32,16},{48,32},{64,48},{80,64},{96,80},{112,96},{128,112},... | collective-permute-start | bytes 589832 | tf_op jit(solution)/shard_map/ppermute | solution.py:12
Sparse Core Ops, SparseCore 0:
  54.9 228.6 reduce-scatter.1
where the time goes:
time: 292 us; the launch traced here: 290 us
  waiting for transfers between devices  216 us (74%)
  matrix products  23.8 us (8%)
  local copies, waits for them, and re-layouts  18.8 us (6%)
  between operations  14.2 us (5%)
  other arithmetic  10.2 us (3%)
  starting transfers between devices  7.64 us (3%)
    reduce_scatter x1, waiting for transfers between devices, local(): lax.psum_scatter(partial_grad, 'dp', scatter_dimension=1, tiled=True)  199 us
    ppermute x3, waiting for transfers between devices, shifted(): return lax.ppermute(block, axis, route)  16.5 us
    ppermute x3, starting transfers between devices, shifted(): return lax.ppermute(block, axis, route)  7.6 us
    dot_general x1, matrix products, local(): lax.dot_general(flat_ctx, grad_out, (((0,), (0,)), ((), ())), preferred_e...  7.25 us
  transfers between devices with their start and end apart: 4, of which 3 were waited for; matrix products, arithmetic and copies ran while one was open for 11% of the time, Pallas kernels for 0%

commit v1 on v0

v1 whole, which is shorter than its diff:
```python
import functools

import jax
import jax.numpy as jnp
from jax import lax
from jax.experimental import pallas as pl
from jax.experimental.pallas import tpu as pltpu
from jax.sharding import PartitionSpec as P

HD = 128
UNIT = 128
NZ, NY, NC = 3, 8, 2
FIRST = (4, 3, 5)
SECOND = (2, 6, 1, 7, 0)
SMEM = pl.BlockSpec(memory_space=pltpu.SMEM)
VMEM = pl.BlockSpec(memory_space=pltpu.VMEM)
PARAMS = pltpu.CompilerParams(vmem_limit_bytes=48 * 1024 * 1024)


def dot(a, b, dims):
    return lax.dot_general(a, b, (dims, ((), ())), preferred_element_type=jnp.float32)


def block_masks(ids_ref, units):
    lane_unit = lax.broadcasted_iota(jnp.int32, (1, units * UNIT), 1) // UNIT
    lane_ids = jnp.full((1, units * UNIT), ids_ref[0], jnp.int32)
    for u in range(1, units):
        lane_ids = jnp.where(lane_unit == u, ids_ref[u * UNIT], lane_ids)
    return [lane_ids == ids_ref[u * UNIT] for u in range(units)]


def softmax(scores):
    expo = jnp.exp(scores - jnp.max(scores, axis=-1, keepdims=True))
    return expo / jnp.sum(expo, axis=-1, keepdims=True)


def unit_weights(q, k, mask):
    return softmax(jnp.where(mask, dot(q, k, ((1,), (1,))) * HD**-0.5, -jnp.inf))


def moved_unit(slot_ref, units):
    unit = jnp.int32(0)
    for u in range(1, units):
        unit = jnp.where(slot_ref[u * UNIT] >= units * UNIT, u, unit)
    return unit


def moved_kernel(units, slot_ref, q_ref, k_ref, v_ref, out_ref):
    moves = slot_ref[moved_unit(slot_ref, units) * UNIT] >= units * UNIT
    for h in range(q_ref.shape[1] // HD):
        cols = pl.ds(h * HD, HD)
        w = softmax(dot(q_ref[:, cols], k_ref[:, cols], ((1,), (1,))) * HD**-0.5)
        ctx = dot(v_ref[:, cols].T, w.astype(jnp.bfloat16), ((1,), (1,)))
        out_ref[cols, :] = jnp.where(moves, ctx, 0.0).astype(jnp.bfloat16)


def moved_context(send_slot, q, k, v):
    units, width = q.shape[0] // UNIT, q.shape[1]
    block = pl.BlockSpec((UNIT, width), lambda i, slot: (moved_unit(slot, units), 0))
    return pl.pallas_call(
        functools.partial(moved_kernel, units),
        grid_spec=pltpu.PrefetchScalarGridSpec(
            num_scalar_prefetch=1,
            grid=(1,),
            in_specs=[block] * 3,
            out_specs=pl.BlockSpec((width, UNIT), lambda i, slot: (0, 0)),
        ),
        out_shape=jax.ShapeDtypeStruct((width, UNIT), jnp.bfloat16),
    )(send_slot, q, k, v)


def context_kernel(ids_ref, slot_ref, q_ref, k_ref, v_ref, out_ref):
    units = q_ref.shape[0] // UNIT
    masks = block_masks(ids_ref, units)
    for h in range(q_ref.shape[1] // HD):
        cols = pl.ds(h * HD, HD)
        v_t = v_ref[:, cols].T
        for u in range(units):
            rows = pl.ds(u * UNIT, UNIT)
            w = unit_weights(q_ref[rows, cols], k_ref[:, cols], masks[u])
            ctx = dot(v_t, w.astype(jnp.bfloat16), ((1,), (1,)))
            stays = slot_ref[u * UNIT] < units * UNIT
            out_ref[cols, rows] = jnp.where(stays, ctx, 0.0).astype(jnp.bfloat16)


def staying_context(image_ids, send_slot, q, k, v):
    return pl.pallas_call(
        context_kernel,
        in_specs=[SMEM, SMEM, VMEM, VMEM, VMEM],
        out_specs=VMEM,
        out_shape=jax.ShapeDtypeStruct(q.shape[::-1], jnp.bfloat16),
        compiler_params=PARAMS,
    )(image_ids, send_slot, q, k, v)


def partial_kernel(picks, stay_ref, came_ref, g_ref, *out_refs):
    me = lax.axis_index("dp")
    z, y, c = me // (NY * NC), (me // NC) % NY, me % NC
    ctx_t = jnp.concatenate([stay_ref[...], came_ref[...]], axis=1)
    width = ctx_t.shape[0]
    for out_ref, (distances, other) in zip(out_refs, picks, strict=True):
        core = 1 - c if other else c
        for n, distance in enumerate(distances):
            dest = [((z + i) % NZ * NY + (y + distance) % NY) * NC + core for i in range(NZ)]
            g = jnp.concatenate([g_ref[:, pl.ds(pl.multiple_of(d * UNIT, UNIT), UNIT)] for d in dest], axis=1)
            part = dot(ctx_t, g, ((1,), (0,))).astype(jnp.bfloat16)
            for i in range(NZ):
                out_ref[pl.ds((n * NZ + i) * width, width), :] = part[:, i * UNIT : (i + 1) * UNIT]


def partial_grad(picks, stay, came, grad_out):
    rows = [len(distances) * NZ * stay.shape[0] for distances, _ in picks]
    return pl.pallas_call(
        functools.partial(partial_kernel, picks),
        in_specs=[VMEM] * 3,
        out_specs=[VMEM] * len(rows),
        out_shape=[jax.ShapeDtypeStruct((r, UNIT), jnp.bfloat16) for r in rows],
        compiler_params=PARAMS,
    )(stay, came, grad_out)


def grad_context_kernel(g_ref, w_ref, out_ref, acc_ref):
    @pl.when(pl.program_id(0) == 0)
    def _():
        acc_ref[...] = jnp.zeros_like(acc_ref)

    acc_ref[...] += dot(g_ref[...], w_ref[...], ((1,), (1,)))

    @pl.when(pl.program_id(0) == pl.num_programs(0) - 1)
    def _():
        out_ref[...] = acc_ref[...].astype(jnp.bfloat16)


def grad_context(grad_out, out_weight):
    rows, depth = grad_out.shape
    width = out_weight.shape[0]
    step = 1024
    return pl.pallas_call(
        grad_context_kernel,
        grid=(depth // step,),
        in_specs=[
            pl.BlockSpec((rows, step), lambda i: (0, i)),
            pl.BlockSpec((width, step), lambda i: (0, i)),
        ],
        out_specs=pl.BlockSpec((rows, width), lambda i: (0, 0)),
        out_shape=jax.ShapeDtypeStruct((rows, width), jnp.bfloat16),
        scratch_shapes=[pltpu.VMEM((rows, width), jnp.float32)],
        compiler_params=PARAMS,
    )(grad_out, out_weight)


def backward_kernel(ids_ref, slot_ref, q_ref, k_ref, v_ref, g_ref, back_ref, dq_ref, dk_ref, dv_ref):
    units = q_ref.shape[0] // UNIT
    masks = block_masks(ids_ref, units)
    for h in range(q_ref.shape[1] // HD):
        cols = pl.ds(h * HD, HD)
        k, v = k_ref[:, cols], v_ref[:, cols]
        dk = jnp.zeros(k.shape, jnp.float32)
        dv = jnp.zeros(v.shape, jnp.float32)
        for u in range(units):
            rows = pl.ds(u * UNIT, UNIT)
            q = q_ref[rows, cols]
            w = unit_weights(q, k, masks[u])
            stays = slot_ref[u * UNIT] < units * UNIT
            g = jnp.where(stays, g_ref[rows, cols].astype(jnp.float32), back_ref[:, cols].astype(jnp.float32))
            g = g.astype(jnp.bfloat16)
            dv += dot(w.astype(jnp.bfloat16), g, ((0,), (0,)))
            dw = dot(g, v, ((1,), (1,)))
            ds = (w * (dw - jnp.sum(w * dw, axis=-1, keepdims=True))).astype(jnp.bfloat16)
            dq_ref[rows, cols] = (dot(ds, k, ((1,), (0,))) * HD**-0.5).astype(jnp.bfloat16)
            dk += dot(ds, q, ((0,), (0,)))
        dk_ref[:, cols] = (dk * HD**-0.5).astype(jnp.bfloat16)
        dv_ref[:, cols] = dv.astype(jnp.bfloat16)


def backward(image_ids, send_slot, q, k, v, g, back):
    return pl.pallas_call(
        backward_kernel,
        in_specs=[SMEM, SMEM] + [VMEM] * 5,
        out_specs=[VMEM] * 3,
        out_shape=[jax.ShapeDtypeStruct(q.shape, jnp.bfloat16)] * 3,
        compiler_params=PARAMS,
    )(image_ids, send_slot, q, k, v, g, back)


PLACES = [(z, y, c) for z in range(NZ) for y in range(NY) for c in range(NC)]


def index(z, y, c):
    return (z % NZ * NY + y % NY) * NC + c


def send(block, to):
    return lax.ppermute(block, "dp", [(index(*p), index(*to(*p))) for p in PLACES])


def along_y(step):
    return lambda z, y, c: (z, y + step, c)


def apart_y(z, y, c):
    return (z, y + 1 - 2 * c, c)


def along_z(step):
    return lambda z, y, c: (z + step, y, c)


def sibling(z, y, c):
    return (z, y, 1 - c)


def total(*terms):
    return sum(t.astype(jnp.float32) for t in terms)


def rounded_total(*terms):
    return total(*terms).astype(jnp.bfloat16)


def local(queries, key_rows, value_rows, image_ids, send_slot, out_weight, grad_out):
    row_count, width = queries.shape
    ranks = lax.axis_size("dp")
    core = lax.axis_index("dp") % NC

    leaving = moved_context(send_slot, queries, key_rows, value_rows)
    came = lax.ppermute(leaving, "dp", [(i, (i + 1) % ranks) for i in range(ranks)])
    stay = staying_context(image_ids, send_slot, queries, key_rows, value_rows)

    (given1,) = partial_grad([(FIRST, True)], stay, came, grad_out)
    got1 = send(given1, sibling)
    given2, = partial_grad([(SECOND, True)], stay, came, grad_out)
    got2 = send(given2, sibling)
    (own,) = partial_grad([(FIRST + SECOND, False)], stay, came, grad_out)

    size = NZ * width
    mine = {d: own[i * size : (i + 1) * size] for i, d in enumerate(FIRST + SECOND)}
    theirs = {d: got1[i * size : (i + 1) * size] for i, d in enumerate(FIRST)}
    theirs |= {d: got2[i * size : (i + 1) * size] for i, d in enumerate(SECOND)}

    half = send(rounded_total(mine[4], theirs[4]), apart_y)
    none = jnp.zeros_like(half)
    up = rounded_total(mine[3], theirs[3], jnp.where(core == 0, half, none))
    down = rounded_total(mine[5], theirs[5], jnp.where(core == 1, half, none))
    up, down = send(up, along_y(1)), send(down, along_y(-1))
    up, down = rounded_total(mine[2], theirs[2], up), rounded_total(mine[6], theirs[6], down)
    up, down = send(up, along_y(1)), send(down, along_y(-1))
    up, down = rounded_total(mine[1], theirs[1], up), rounded_total(mine[7], theirs[7], down)
    up, down = send(up, along_y(1)), send(down, along_y(-1))
    ring = total(mine[0], theirs[0], up, down)
    above = send(ring[width : 2 * width].astype(jnp.bfloat16), along_z(1))
    below = send(ring[2 * width :].astype(jnp.bfloat16), along_z(-1))
    grad_weight = total(ring[:width], above, below)

    grad_ctx = grad_context(grad_out, out_weight)
    back = lax.ppermute(grad_ctx[row_count:], "dp", [((i + 1) % ranks, i) for i in range(ranks)])
    grads = backward(image_ids, send_slot, queries, key_rows, value_rows, grad_ctx, back)
    return (*grads, grad_weight)


def solution(mesh):
    placed = (
        P("dp", "fsdp"),
        P("dp", "fsdp"),
        P("dp", "fsdp"),
        P("dp"),
        P("dp"),
        P("fsdp", None),
        P("dp", None),
    )
    return jax.shard_map(
        local,
        mesh=mesh,
        in_specs=placed,
        out_specs=(P("dp", "fsdp"), P("dp", "fsdp"), P("dp", "fsdp"), P("fsdp", "dp")),
        check_vma=False,
    )
```

time: 292 us -> 109 us (0.37)
  waiting for transfers between devices: 216 us -> 32.8 us
  starting transfers between devices: 7.64 us -> 39.3 us
  Pallas kernels: 0 us -> 27.3 us
  matrix products: 23.8 us -> 0 us
  local copies, waits for them, and re-layouts: 18.8 us -> 5.01 us
  between operations: 14.2 us -> 0.98 us
  other arithmetic: 10.2 us -> 3.12 us
    reduce_scatter x1 -> x0, waiting for transfers between devices: 199 us -> none  [local(): lax.psum_scatter(partial_grad, 'dp', scatter_dimension=1, tiled=True)]
    ppermute x3 -> x13, starting transfers between devices: 7.6 us -> 39.3 us  [the longest x11 34.9 us: send(): lax.ppermute(block, 'dp', [(index(*p), index(*to(*p))) for p in PLACES])]
    pallas_call x0 -> x7, Pallas kernels: none -> 27.3 us  [the longest x3 11.3 us: partial_grad(): pl.pallas_call(functools.partial(partial_kernel, picks), in_specs=[VMEM]...]
    dot_general x7 -> x0, matrix products: 20.5 us -> none  [the longest x1 7.25 us: local(): lax.dot_general(flat_ctx, grad_out, (((0,), (0,)), ((), ())), preferred_e...]
    ppermute x3 -> x13, waiting for transfers between devices: 16.5 us -> 32.8 us  [the longest x11 22.6 us: send(): lax.ppermute(block, 'dp', [(index(*p), index(*to(*p))) for p in PLACES])]
    slice x8 -> x2, local copies, waits for them, and re-layouts: 7.74 us -> 0.02 us  [the longest x1 0.01 us: local(): above = send(ring[width:2 * width].astype(jnp.bfloat16), along_z(1))]
    gather x1 -> x0, local copies, waits for them, and re-layouts: 4.27 us -> none  [local(): own_rows = combined[send_slot]]
    unnamed x12 -> x24, local copies, waits for them, and re-layouts: 1.29 us -> 4.99 us
  transfers between devices with their start and end apart: 4 -> 13, of which waited for: 3 -> 6; matrix products, arithmetic and copies ran while one was open for 11% -> 2% of each run, Pallas kernels for 0% -> 19%
where the time goes in v1:
time: 109 us
  starting transfers between devices  39.3 us (36%)
  waiting for transfers between devices  32.8 us (30%)
  Pallas kernels  27.3 us (25%)
  local copies, waits for them, and re-layouts  5.01 us (5%)
  other arithmetic  3.12 us (3%)
    ppermute x11, starting transfers between devices, send(): lax.ppermute(block, 'dp', [(index(*p), index(*to(*p))) for p in PLACES])  34.9 us
    ppermute x11, waiting for transfers between devices, send(): lax.ppermute(block, 'dp', [(index(*p), index(*to(*p))) for p in PLACES])  22.6 us
    pallas_call x3, Pallas kernels, partial_grad(): pl.pallas_call(functools.partial(partial_kernel, picks), in_specs=[VMEM]...  11.3 us
    ppermute x1, waiting for transfers between devices, local(): lax.ppermute(leaving, 'dp', [(i, (i + 1) % ranks) for i in range(ranks)])  10.2 us
    pallas_call x1, Pallas kernels, grad_context(): pl.pallas_call(grad_context_kernel, grid=(depth // step,), in_specs=[pl.B...  5.88 us
    unnamed x24, local copies, waits for them, and re-layouts  4.99 us
    pallas_call x1, Pallas kernels, backward(): pl.pallas_call(backward_kernel, in_specs=[SMEM, SMEM] + [VMEM] * 5, out_s...  4.33 us
    pallas_call x1, Pallas kernels, staying_context(): pl.pallas_call(context_kernel, in_specs=[SMEM, SMEM, VMEM, VMEM, VMEM], o...  3.03 us
  transfers between devices with their start and end apart: 13, of which 6 were waited for; matrix products, arithmetic and copies ran while one was open for 2% of the time, Pallas kernels for 19%

profile of v1, /device:TPU:6, one launch (start us, length us, event | category | flops | bytes accessed | tf_op | source)
XLA Modules:
  0.0 108.5 jit_solution(17935071214228839190)
XLA Ops:
  0.6 2.8 %shard_map.105 = bf16[256,128]{1,0:T(8,128)(2,1)} custom-call(s32[384]{0:T(512)} %slot_ref.5, bf16[384,256]{1,0:T(8,128)(2,1)} %q_ref.5, bf16[384,256]{1,0:T(8,128)(2,1)} %k_ref.5, bf16[384,256]{1,0:T(8,128)(2,1)} %v_ref.5), custom_call_target="tpu_custom_call" | custom-call | tf_op jit(solution)/shard_map/pallas_call | solution.py:60
  3.4 1.9 %collective-permute-start.1 = (bf16[256,128]{1,0:T(8,128)(2,1)}, bf16[256,128]{1,0:T(8,128)(2,1)S(1)}, u32[]{:S(2)}, u32[]{:S(2)}) collective-permute-start(bf16[256,128]{1,0:T(8,128)(2,1)} %shard_map.105), channel_id=1, source_target_pairs={{0,16},{16,32},{32,48},{48,64},{64,80},{80,96},{96,112},{112,128},... | collective-permute-start | bytes 196616 | tf_op jit(solution)/shard_map/ppermute | solution.py:227
  5.3 0.0 copy-start.1
  5.4 0.9 copy-done.1
  6.3 0.9 copy-done.3
  7.2 0.9 copy-done.5
  8.1 0.7 copy-done.7
  8.8 0.7 copy-done.9
  9.5 3.0 %shard_map.104.stay_ref = bf16[256,384]{1,0:T(8,128)(2,1)S(1)} custom-call(s32[384]{0:T(512)S(1)} %copy-done.9, s32[384]{0:T(512)S(1)} %copy-done.7, bf16[384,256]{1,0:T(8,128)(2,1)S(1)} %copy-done.1, bf16[384,256]{1,0:T(8,128)(2,1)S(1)} %copy-done.3, bf16[384,256]{1,0:T(8,128)(2,1)S(1)} %copy-done.5), custom_call_target="tpu_custom_call" | custom-call | tf_op jit(solution)/shard_map/pallas_call | solution.py:87
  12.5 10.2 %collective-permute-done.1.came_ref = bf16[256,128]{1,0:T(8,128)(2,1)S(1)} collective-permute-done((bf16[256,128]{1,0:T(8,128)(2,1)}, bf16[256,128]{1,0:T(8,128)(2,1)S(1)}, u32[]{:S(2)}, u32[]{:S(2)}) %collective-permute-start.1) | collective-permute-done | bytes 65568 | tf_op jit(solution)/shard_map/ppermute | solution.py:227
  22.7 3.4 %shard_map.108 = bf16[2304,128]{1,0:T(8,128)(2,1)S(1)} custom-call(bf16[256,384]{1,0:T(8,128)(2,1)S(1)} %shard_map.104.stay_ref, bf16[256,128]{1,0:T(8,128)(2,1)S(1)} %collective-permute-done.1.came_ref, bf16[512,6144]{1,0:T(8,128)(2,1)} %g_ref.7), custom_call_target="tpu_custom_call" | custom-call | tf_op jit(solution)/shard_map/pallas_call | solution.py:113
  26.1 1.9 %collective-permute-start.3 = (bf16[2304,128]{1,0:T(8,128)(2,1)S(1)}, bf16[2304,128]{1,0:T(8,128)(2,1)S(1)}, u32[]{:S(2)}, u32[]{:S(2)}) collective-permute-start(bf16[2304,128]{1,0:T(8,128)(2,1)S(1)} %shard_map.108), channel_id=1, source_target_pairs={{0,16},{16,0},{32,48},{48,32},{64,80},{80,64},{96,112},{112,96},{1... | collective-permute-start | bytes 1769480 | tf_op jit(solution)/shard_map/ppermute | solution.py:194
  28.1 3.7 %shard_map.107 = bf16[3840,128]{1,0:T(8,128)(2,1)S(1)} custom-call(bf16[256,384]{1,0:T(8,128)(2,1)S(1)} %shard_map.104.stay_ref, bf16[256,128]{1,0:T(8,128)(2,1)S(1)} %collective-permute-done.1.came_ref, bf16[512,6144]{1,0:T(8,128)(2,1)} %g_ref.7), custom_call_target="tpu_custom_call" | custom-call | tf_op jit(solution)/shard_map/pallas_call | solution.py:113
  31.8 2.4 %collective-permute-start.2 = (bf16[3840,128]{1,0:T(8,128)(2,1)S(1)}, bf16[3840,128]{1,0:T(8,128)(2,1)S(1)}, u32[]{:S(2)}, u32[]{:S(2)}) collective-permute-start(bf16[3840,128]{1,0:T(8,128)(2,1)S(1)} %shard_map.107), channel_id=1, source_target_pairs={{0,16},{16,0},{32,48},{48,32},{64,80},{80,64},{96,112},{112,96},{1... | collective-permute-start | bytes 2949128 | tf_op jit(solution)/shard_map/ppermute | solution.py:194
  34.2 4.2 %shard_map.106 = bf16[6144,128]{1,0:T(8,128)(2,1)S(1)} custom-call(bf16[256,384]{1,0:T(8,128)(2,1)S(1)} %shard_map.104.stay_ref, bf16[256,128]{1,0:T(8,128)(2,1)S(1)} %collective-permute-done.1.came_ref, bf16[512,6144]{1,0:T(8,128)(2,1)} %g_ref.7), custom_call_target="tpu_custom_call" | custom-call | tf_op jit(solution)/shard_map/pallas_call | solution.py:113
  38.4 0.0 collective-permute-done.3
  38.4 0.8 copy-done.11
  39.2 0.7 add_convert_fusion.6
  39.9 1.9 %collective-permute-start.4 = (bf16[768,128]{1,0:T(8,128)(2,1)}, bf16[768,128]{1,0:T(8,128)(2,1)}, u32[]{:S(2)}, u32[]{:S(2)}) collective-permute-start(bf16[768,128]{1,0:T(8,128)(2,1)} %add_convert_fusion.6), channel_id=1, source_target_pairs={{0,32},{16,240},{32,64},{48,16},{64,96},{80,48},{96,128},{112,80},... | collective-permute-start | bytes 589832 | tf_op jit(solution)/shard_map/ppermute | solution.py:194
  41.9 7.1 %collective-permute-done.4 = bf16[768,128]{1,0:T(8,128)(2,1)} collective-permute-done((bf16[768,128]{1,0:T(8,128)(2,1)}, bf16[768,128]{1,0:T(8,128)(2,1)}, u32[]{:S(2)}, u32[]{:S(2)}) %collective-permute-start.4) | collective-permute-done | bytes 196640 | tf_op jit(solution)/shard_map/ppermute | solution.py:194
  49.0 1.3 %add_convert_fusion.5 = (bf16[768,128]{1,0:T(8,128)(2,1)S(1)}, bf16[768,128]{1,0:T(8,128)(2,1)S(1)}) fusion(bf16[2304,128]{1,0:T(8,128)(2,1)} %copy-done.11, bf16[6144,128]{1,0:T(8,128)(2,1)S(1)} %shard_map.106, bf16[768,128]{1,0:T(8,128)(2,1)} %collective-permute-done.4, pred[]{:T(512)S(6)} %eq.8, pred[]{:T(512)S(6)} %eq.9), kind=kLoop, calls=%fused_computation.6 | loop fusion | flops 1376256 | bytes 1376258 | tf_op jit(solution)/shard_map/convert_element_type | solution.py:218
  50.3 1.9 %collective-permute-start.5 = (bf16[768,128]{1,0:T(8,128)(2,1)S(1)}, bf16[768,128]{1,0:T(8,128)(2,1)S(1)}, u32[]{:S(2)}, u32[]{:S(2)}) collective-permute-start(bf16[768,128]{1,0:T(8,128)(2,1)S(1)} %get-tuple-element.14), channel_id=1, source_target_pairs={{0,32},{16,48},{32,64},{48,80},{64,96},{80,112},{96,128},{112,144}... | collective-permute-start | bytes 589832 | tf_op jit(solution)/shard_map/ppermute | solution.py:194
  52.2 0.0 copy-start
  52.2 5.4 %collective-permute-start.8 = (bf16[768,128]{1,0:T(8,128)(2,1)S(1)}, bf16[768,128]{1,0:T(8,128)(2,1)S(1)}, u32[]{:S(2)}, u32[]{:S(2)}) collective-permute-start(bf16[768,128]{1,0:T(8,128)(2,1)S(1)} %get-tuple-element.15), channel_id=1, source_target_pairs={{0,224},{16,240},{32,0},{48,16},{64,32},{80,48},{96,64},{112,80},{... | collective-permute-start | bytes 589832 | tf_op jit(solution)/shard_map/ppermute | solution.py:194
  57.6 1.4 %collective-permute-done.5 = bf16[768,128]{1,0:T(8,128)(2,1)S(1)} collective-permute-done((bf16[768,128]{1,0:T(8,128)(2,1)S(1)}, bf16[768,128]{1,0:T(8,128)(2,1)S(1)}, u32[]{:S(2)}, u32[]{:S(2)}) %collective-permute-start.5) | collective-permute-done | bytes 196640 | tf_op jit(solution)/shard_map/ppermute | solution.py:194
  59.1 0.0 collective-permute-done.2
  59.1 0.1 add_convert_fusion.4
  59.1 1.9 %collective-permute-start.6 = (bf16[768,128]{1,0:T(8,128)(2,1)S(1)}, bf16[768,128]{1,0:T(8,128)(2,1)S(1)}, u32[]{:S(2)}, u32[]{:S(2)}) collective-permute-start(bf16[768,128]{1,0:T(8,128)(2,1)S(1)} %add_convert_fusion.4), channel_id=1, source_target_pairs={{0,32},{16,48},{32,64},{48,80},{64,96},{80,112},{96,128},{112,144}... | collective-permute-start | bytes 589832 | tf_op jit(solution)/shard_map/ppermute | solution.py:194
  61.1 6.8 %collective-permute-done.6 = bf16[768,128]{1,0:T(8,128)(2,1)S(1)} collective-permute-done((bf16[768,128]{1,0:T(8,128)(2,1)S(1)}, bf16[768,128]{1,0:T(8,128)(2,1)S(1)}, u32[]{:S(2)}, u32[]{:S(2)}) %collective-permute-start.6) | collective-permute-done | bytes 196640 | tf_op jit(solution)/shard_map/ppermute | solution.py:194
  67.9 0.2 add_convert_fusion.3
  68.1 2.0 %collective-permute-start.9 = (bf16[768,128]{1,0:T(8,128)(2,1)S(1)}, bf16[768,128]{1,0:T(8,128)(2,1)S(1)}, u32[]{:S(2)}, u32[]{:S(2)}) collective-permute-start(bf16[768,128]{1,0:T(8,128)(2,1)S(1)} %get-tuple-element.13), channel_id=1, source_target_pairs={{0,224},{16,240},{32,0},{48,16},{64,32},{80,48},{96,64},{112,80},{... | collective-permute-start | bytes 589832 | tf_op jit(solution)/shard_map/ppermute | solution.py:194
  70.1 3.8 %collective-permute-start.7 = (bf16[768,128]{1,0:T(8,128)(2,1)S(1)}, bf16[768,128]{1,0:T(8,128)(2,1)S(1)}, u32[]{:S(2)}, u32[]{:S(2)}) collective-permute-start(bf16[768,128]{1,0:T(8,128)(2,1)S(1)} %get-tuple-element.12), channel_id=1, source_target_pairs={{0,32},{16,48},{32,64},{48,80},{64,96},{80,112},{96,128},{112,144}... | collective-permute-start | bytes 589832 | tf_op jit(solution)/shard_map/ppermute | solution.py:194
  73.9 1.7 %collective-permute-done.9 = bf16[768,128]{1,0:T(8,128)(2,1)S(1)} collective-permute-done((bf16[768,128]{1,0:T(8,128)(2,1)S(1)}, bf16[768,128]{1,0:T(8,128)(2,1)S(1)}, u32[]{:S(2)}, u32[]{:S(2)}) %collective-permute-start.9) | collective-permute-done | bytes 196640 | tf_op jit(solution)/shard_map/ppermute | solution.py:194
  75.6 0.1 add_convert_fusion
  75.7 3.3 %collective-permute-start.10 = (bf16[768,128]{1,0:T(8,128)(2,1)S(1)}, bf16[768,128]{1,0:T(8,128)(2,1)S(1)}, u32[]{:S(2)}, u32[]{:S(2)}) collective-permute-start(bf16[768,128]{1,0:T(8,128)(2,1)S(1)} %add_convert_fusion), channel_id=1, source_target_pairs={{0,224},{16,240},{32,0},{48,16},{64,32},{80,48},{96,64},{112,80},{... | collective-permute-start | bytes 589832 | tf_op jit(solution)/shard_map/ppermute | solution.py:194
  79.0 5.9 %shard_map.102.g_ref = bf16[512,256]{1,0:T(8,128)(2,1)S(1)} custom-call(bf16[512,6144]{1,0:T(8,128)(2,1)} %g_ref.7, bf16[256,6144]{1,0:T(8,128)(2,1)S(1)} %copy-done), custom_call_target="tpu_custom_call" | custom-call | tf_op jit(solution)/shard_map/pallas_call | solution.py:138
  84.9 0.0 copy-start.2
  84.9 0.0 copy-start.4
  84.9 0.0 copy-start.6
  84.9 0.0 copy-start.8
  84.9 0.0 copy-start.10
  85.0 2.6 %collective-permute-start = (bf16[128,256]{1,0:T(8,128)(2,1)S(1)}, bf16[128,256]{1,0:T(8,128)(2,1)S(1)}, u32[]{:S(2)}, u32[]{:S(2)}) collective-permute-start(bf16[128,256]{1,0:T(8,128)(2,1)S(1)} %slice.82), channel_id=1, source_target_pairs={{16,0},{32,16},{48,32},{64,48},{80,64},{96,80},{112,96},{128,112},... | collective-permute-start | bytes 196616 | tf_op jit(solution)/shard_map/ppermute | solution.py:256
  87.6 0.1 fusion.1
  87.7 8.0 %collective-permute-start.11 = (bf16[256,128]{1,0:T(8,128)(2,1)S(1)}, bf16[256,128]{1,0:T(8,128)(2,1)S(1)}, u32[]{:S(2)}, u32[]{:S(2)}) collective-permute-start(bf16[256,128]{1,0:T(8,128)(2,1)S(1)} %get-tuple-element.16), channel_id=1, source_target_pairs={{0,256},{16,272},{32,288},{48,304},{64,320},{80,336},{96,352},{112... | collective-permute-start | bytes 196616 | tf_op jit(solution)/shard_map/ppermute | solution.py:194
  95.7 2.3 %collective-permute-start.12 = (bf16[256,128]{1,0:T(8,128)(2,1)S(1)}, bf16[256,128]{1,0:T(8,128)(2,1)S(1)}, u32[]{:S(2)}, u32[]{:S(2)}) collective-permute-start(bf16[256,128]{1,0:T(8,128)(2,1)S(1)} %get-tuple-element.17), channel_id=1, source_target_pairs={{0,512},{16,528},{32,544},{48,560},{64,576},{80,592},{96,608},{112... | collective-permute-start | bytes 196616 | tf_op jit(solution)/shard_map/ppermute | solution.py:194
  98.1 4.3 %shard_map.103 = (bf16[384,256]{1,0:T(8,128)(2,1)}, bf16[384,256]{1,0:T(8,128)(2,1)}, bf16[384,256]{1,0:T(8,128)(2,1)}) custom-call(s32[384]{0:T(512)S(1)} %copy-done.10, s32[384]{0:T(512)S(1)} %copy-done.8, bf16[384,256]{1,0:T(8,128)(2,1)S(1)} %copy-done.2, bf16[384,256]{1,0:T(8,128)(2,1)S(1)} %copy-done.4, bf16[384,256]{1,0:T(8,128)(2,1)S(1)} %copy-done.6, ...), custom_call_target="tpu_custom_call" | custom-call | tf_op jit(solution)/shard_map/pallas_call | solution.py:177
  102.4 5.5 %collective-permute-done.12 = bf16[256,128]{1,0:T(8,128)(2,1)S(1)} collective-permute-done((bf16[256,128]{1,0:T(8,128)(2,1)S(1)}, bf16[256,128]{1,0:T(8,128)(2,1)S(1)}, u32[]{:S(2)}, u32[]{:S(2)}) %collective-permute-start.12) | collective-permute-done | bytes 65568 | tf_op jit(solution)/shard_map/ppermute | solution.py:194
  107.9 0.7 fusion
  (18 shorter events, 0.1 us)
Async XLA Ops:
  3.4 19.3 %collective-permute-start.1 = (bf16[256,128]{1,0:T(8,128)(2,1)}, bf16[256,128]{1,0:T(8,128)(2,1)S(1)}, u32[]{:S(2)}, u32[]{:S(2)}) collective-permute-start(bf16[256,128]{1,0:T(8,128)(2,1)} %shard_map.105), channel_id=1, source_target_pairs={{0,16},{16,32},{32,48},{48,64},{64,80},{80,96},{96,112},{112,128},... | collective-permute-start | bytes 196616 | tf_op jit(solution)/shard_map/ppermute | solution.py:227
  5.3 0.9 copy-start.1
  6.3 0.9 copy-start.3
  7.2 0.9 copy-start.5
  8.1 0.7 copy-start.7
  8.8 0.7 copy-start.9
  26.1 12.2 %collective-permute-start.3 = (bf16[2304,128]{1,0:T(8,128)(2,1)S(1)}, bf16[2304,128]{1,0:T(8,128)(2,1)S(1)}, u32[]{:S(2)}, u32[]{:S(2)}) collective-permute-start(bf16[2304,128]{1,0:T(8,128)(2,1)S(1)} %shard_map.108), channel_id=1, source_target_pairs={{0,16},{16,0},{32,48},{48,32},{64,80},{80,64},{96,112},{112,96},{1... | collective-permute-start | bytes 1769480 | tf_op jit(solution)/shard_map/ppermute | solution.py:194
  31.8 27.3 %collective-permute-start.2 = (bf16[3840,128]{1,0:T(8,128)(2,1)S(1)}, bf16[3840,128]{1,0:T(8,128)(2,1)S(1)}, u32[]{:S(2)}, u32[]{:S(2)}) collective-permute-start(bf16[3840,128]{1,0:T(8,128)(2,1)S(1)} %shard_map.107), channel_id=1, source_target_pairs={{0,16},{16,0},{32,48},{48,32},{64,80},{80,64},{96,112},{112,96},{1... | collective-permute-start | bytes 2949128 | tf_op jit(solution)/shard_map/ppermute | solution.py:194
  38.4 0.8 copy-start.11
  39.9 9.1 %collective-permute-start.4 = (bf16[768,128]{1,0:T(8,128)(2,1)}, bf16[768,128]{1,0:T(8,128)(2,1)}, u32[]{:S(2)}, u32[]{:S(2)}) collective-permute-start(bf16[768,128]{1,0:T(8,128)(2,1)} %add_convert_fusion.6), channel_id=1, source_target_pairs={{0,32},{16,240},{32,64},{48,16},{64,96},{80,48},{96,128},{112,80},... | collective-permute-start | bytes 589832 | tf_op jit(solution)/shard_map/ppermute | solution.py:194
  50.3 8.8 %collective-permute-start.5 = (bf16[768,128]{1,0:T(8,128)(2,1)S(1)}, bf16[768,128]{1,0:T(8,128)(2,1)S(1)}, u32[]{:S(2)}, u32[]{:S(2)}) collective-permute-start(bf16[768,128]{1,0:T(8,128)(2,1)S(1)} %get-tuple-element.14), channel_id=1, source_target_pairs={{0,32},{16,48},{32,64},{48,80},{64,96},{80,112},{96,128},{112,144}... | collective-permute-start | bytes 589832 | tf_op jit(solution)/shard_map/ppermute | solution.py:194
  52.2 26.8 %copy-start = (bf16[256,6144]{1,0:T(8,128)(2,1)S(1)}, bf16[256,6144]{1,0:T(8,128)(2,1)}, u32[]{:S(2)}) copy-start(bf16[256,6144]{1,0:T(8,128)(2,1)} %w_ref.1) | copy-start | bytes 9437188
  52.2 8.9 %collective-permute-start.8 = (bf16[768,128]{1,0:T(8,128)(2,1)S(1)}, bf16[768,128]{1,0:T(8,128)(2,1)S(1)}, u32[]{:S(2)}, u32[]{:S(2)}) collective-permute-start(bf16[768,128]{1,0:T(8,128)(2,1)S(1)} %get-tuple-element.15), channel_id=1, source_target_pairs={{0,224},{16,240},{32,0},{48,16},{64,32},{80,48},{96,64},{112,80},{... | collective-permute-start | bytes 589832 | tf_op jit(solution)/shard_map/ppermute | solution.py:194
  59.1 8.8 %collective-permute-start.6 = (bf16[768,128]{1,0:T(8,128)(2,1)S(1)}, bf16[768,128]{1,0:T(8,128)(2,1)S(1)}, u32[]{:S(2)}, u32[]{:S(2)}) collective-permute-start(bf16[768,128]{1,0:T(8,128)(2,1)S(1)} %add_convert_fusion.4), channel_id=1, source_target_pairs={{0,32},{16,48},{32,64},{48,80},{64,96},{80,112},{96,128},{112,144}... | collective-permute-start | bytes 589832 | tf_op jit(solution)/shard_map/ppermute | solution.py:194
  68.1 7.6 %collective-permute-start.9 = (bf16[768,128]{1,0:T(8,128)(2,1)S(1)}, bf16[768,128]{1,0:T(8,128)(2,1)S(1)}, u32[]{:S(2)}, u32[]{:S(2)}) collective-permute-start(bf16[768,128]{1,0:T(8,128)(2,1)S(1)} %get-tuple-element.13), channel_id=1, source_target_pairs={{0,224},{16,240},{32,0},{48,16},{64,32},{80,48},{96,64},{112,80},{... | collective-permute-start | bytes 589832 | tf_op jit(solution)/shard_map/ppermute | solution.py:194
  70.1 17.4 %collective-permute-start.7 = (bf16[768,128]{1,0:T(8,128)(2,1)S(1)}, bf16[768,128]{1,0:T(8,128)(2,1)S(1)}, u32[]{:S(2)}, u32[]{:S(2)}) collective-permute-start(bf16[768,128]{1,0:T(8,128)(2,1)S(1)} %get-tuple-element.12), channel_id=1, source_target_pairs={{0,32},{16,48},{32,64},{48,80},{64,96},{80,112},{96,128},{112,144}... | collective-permute-start | bytes 589832 | tf_op jit(solution)/shard_map/ppermute | solution.py:194
  75.7 11.8 %collective-permute-start.10 = (bf16[768,128]{1,0:T(8,128)(2,1)S(1)}, bf16[768,128]{1,0:T(8,128)(2,1)S(1)}, u32[]{:S(2)}, u32[]{:S(2)}) collective-permute-start(bf16[768,128]{1,0:T(8,128)(2,1)S(1)} %add_convert_fusion), channel_id=1, source_target_pairs={{0,224},{16,240},{32,0},{48,16},{64,32},{80,48},{96,64},{112,80},{... | collective-permute-start | bytes 589832 | tf_op jit(solution)/shard_map/ppermute | solution.py:194
  84.9 13.1 %copy-start.2 = (bf16[384,256]{1,0:T(8,128)(2,1)S(1)}, bf16[384,256]{1,0:T(8,128)(2,1)}, u32[]{:S(2)}) copy-start(bf16[384,256]{1,0:T(8,128)(2,1)} %q_ref.5) | copy-start | bytes 589828
  84.9 13.1 %copy-start.4 = (bf16[384,256]{1,0:T(8,128)(2,1)S(1)}, bf16[384,256]{1,0:T(8,128)(2,1)}, u32[]{:S(2)}) copy-start(bf16[384,256]{1,0:T(8,128)(2,1)} %k_ref.5) | copy-start | bytes 589828
  84.9 13.1 %copy-start.6 = (bf16[384,256]{1,0:T(8,128)(2,1)S(1)}, bf16[384,256]{1,0:T(8,128)(2,1)}, u32[]{:S(2)}) copy-start(bf16[384,256]{1,0:T(8,128)(2,1)} %v_ref.5) | copy-start | bytes 589828
  84.9 13.1 %copy-start.8 = (s32[384]{0:T(512)S(1)}, s32[384]{0:T(512)}, u32[]{:S(2)}) copy-start(s32[384]{0:T(512)} %slot_ref.5) | copy-start | bytes 4612
  84.9 13.1 %copy-start.10 = (s32[384]{0:T(512)S(1)}, s32[384]{0:T(512)}, u32[]{:S(2)}) copy-start(s32[384]{0:T(512)} %ids_ref.3) | copy-start | bytes 4612
  85.0 13.0 %collective-permute-start = (bf16[128,256]{1,0:T(8,128)(2,1)S(1)}, bf16[128,256]{1,0:T(8,128)(2,1)S(1)}, u32[]{:S(2)}, u32[]{:S(2)}) collective-permute-start(bf16[128,256]{1,0:T(8,128)(2,1)S(1)} %slice.82), channel_id=1, source_target_pairs={{16,0},{32,16},{48,32},{64,48},{80,64},{96,80},{112,96},{128,112},... | collective-permute-start | bytes 196616 | tf_op jit(solution)/shard_map/ppermute | solution.py:256
  87.7 14.7 %collective-permute-start.11 = (bf16[256,128]{1,0:T(8,128)(2,1)S(1)}, bf16[256,128]{1,0:T(8,128)(2,1)S(1)}, u32[]{:S(2)}, u32[]{:S(2)}) collective-permute-start(bf16[256,128]{1,0:T(8,128)(2,1)S(1)} %get-tuple-element.16), channel_id=1, source_target_pairs={{0,256},{16,272},{32,288},{48,304},{64,320},{80,336},{96,352},{112... | collective-permute-start | bytes 196616 | tf_op jit(solution)/shard_map/ppermute | solution.py:194
  95.7 12.2 %collective-permute-start.12 = (bf16[256,128]{1,0:T(8,128)(2,1)S(1)}, bf16[256,128]{1,0:T(8,128)(2,1)S(1)}, u32[]{:S(2)}, u32[]{:S(2)}) collective-permute-start(bf16[256,128]{1,0:T(8,128)(2,1)S(1)} %get-tuple-element.17), channel_id=1, source_target_pairs={{0,512},{16,528},{32,544},{48,560},{64,576},{80,592},{96,608},{112... | collective-permute-start | bytes 196616 | tf_op jit(solution)/shard_map/ppermute | solution.py:194

commit v2 on v1

v2 whole, which is shorter than its diff:
```python
import functools

import jax
import jax.numpy as jnp
from jax import lax
from jax.experimental import pallas as pl
from jax.experimental.pallas import tpu as pltpu
from jax.sharding import PartitionSpec as P

HD = 128
UNIT = 128
NZ, NY, NC = 3, 8, 2
ORDER = (4, 3, 5, 2, 6, 1, 7, 0)
SMEM = pl.BlockSpec(memory_space=pltpu.SMEM)
VMEM = pl.BlockSpec(memory_space=pltpu.VMEM)
PARAMS = pltpu.CompilerParams(vmem_limit_bytes=16 * 1024 * 1024)


def dot(a, b, dims):
    return lax.dot_general(a, b, (dims, ((), ())), preferred_element_type=jnp.float32)


def block_masks(ids_ref, units):
    lane_unit = lax.broadcasted_iota(jnp.int32, (1, units * UNIT), 1) // UNIT
    lane_ids = jnp.full((1, units * UNIT), ids_ref[0], jnp.int32)
    for u in range(1, units):
        lane_ids = jnp.where(lane_unit == u, ids_ref[u * UNIT], lane_ids)
    return [lane_ids == ids_ref[u * UNIT] for u in range(units)]


def softmax(scores):
    expo = jnp.exp(scores - jnp.max(scores, axis=-1, keepdims=True))
    return expo / jnp.sum(expo, axis=-1, keepdims=True)


def unit_weights(q, k, mask):
    return softmax(jnp.where(mask, dot(q, k, ((1,), (1,))) * HD**-0.5, -jnp.inf))


def context_kernel(ids_hbm, slot_hbm, q_hbm, k_hbm, v_hbm, g_hbm, w_hbm, stay_ref, leave_ref, g_ref, w_ref,
                   ids_ref, slot_ref, q_ref, k_ref, v_ref, sems):
    pairs = [(ids_hbm, ids_ref), (slot_hbm, slot_ref), (q_hbm, q_ref), (k_hbm, k_ref), (v_hbm, v_ref),
             (g_hbm, g_ref), (w_hbm, w_ref)]
    copies = [pltpu.make_async_copy(src, dst, sems.at[i]) for i, (src, dst) in enumerate(pairs)]
    for copy in copies:
        copy.start()
    for copy in copies[:5]:
        copy.wait()
    units = q_ref.shape[0] // UNIT
    masks = block_masks(ids_ref, units)
    for h in range(q_ref.shape[1] // HD):
        cols = pl.ds(h * HD, HD)
        v_t = v_ref[:, cols].T
        leave = jnp.zeros((HD, UNIT), jnp.float32)
        for u in range(units):
            rows = pl.ds(u * UNIT, UNIT)
            w = unit_weights(q_ref[rows, cols], k_ref[:, cols], masks[u])
            ctx = dot(v_t, w.astype(jnp.bfloat16), ((1,), (1,)))
            stays = slot_ref[u * UNIT] < units * UNIT
            stay_ref[cols, rows] = jnp.where(stays, ctx, 0.0).astype(jnp.bfloat16)
            leave = jnp.where(stays, leave, ctx)
        leave_ref[cols, :] = leave.astype(jnp.bfloat16)
    for copy in copies[5:]:
        copy.wait()


def whole(shape):
    return pl.BlockSpec(shape, lambda i: (0,) * len(shape))


def contexts(image_ids, send_slot, q, k, v, grad_out, out_weight):
    rows, width = q.shape
    shapes = [(width, rows), (width, UNIT), grad_out.shape, out_weight.shape]
    return pl.pallas_call(
        context_kernel,
        in_specs=[pl.BlockSpec(memory_space=pltpu.HBM)] * 7,
        out_specs=[VMEM] * 4,
        out_shape=[jax.ShapeDtypeStruct(shape, jnp.bfloat16) for shape in shapes],
        scratch_shapes=[pltpu.SMEM(image_ids.shape, jnp.int32), pltpu.SMEM(send_slot.shape, jnp.int32)]
        + [pltpu.VMEM(q.shape, jnp.bfloat16)] * 3
        + [pltpu.SemaphoreType.DMA((7,))],
        compiler_params=PARAMS,
    )(*[pltpu.with_memory_space_constraint(x, pltpu.HBM) for x in (image_ids, send_slot, q, k, v, grad_out, out_weight)])


def partial_kernel(other, stay_ref, came_ref, g_ref, out_ref):
    me = lax.axis_index("dp")
    z, y, c = me // (NY * NC), (me // NC) % NY, me % NC
    core = 1 - c if other else c
    ctx_t = jnp.concatenate([stay_ref[...], came_ref[...]], axis=1)
    width = ctx_t.shape[0]
    for n, distance in enumerate(ORDER):
        dest = [((z + i) % NZ * NY + (y + distance) % NY) * NC + core for i in range(NZ)]
        g = jnp.concatenate([g_ref[:, pl.ds(pl.multiple_of(d * UNIT, UNIT), UNIT)] for d in dest], axis=1)
        part = dot(ctx_t, g, ((1,), (0,))).astype(jnp.bfloat16)
        for i in range(NZ):
            out_ref[pl.ds((n * NZ + i) * width, width), :] = part[:, i * UNIT : (i + 1) * UNIT]


def partial_grad(other, stay, came, grad_out):
    shape = (NY * NZ * stay.shape[0], UNIT)
    return pl.pallas_call(
        functools.partial(partial_kernel, other),
        in_specs=[VMEM, VMEM, VMEM],
        out_specs=VMEM,
        out_shape=jax.ShapeDtypeStruct(shape, jnp.bfloat16),
        compiler_params=PARAMS,
    )(stay, came, grad_out)


def grad_context_kernel(g_ref, w_ref, out_ref):
    step = 1024
    acc = jnp.zeros(out_ref.shape, jnp.float32)
    for i in range(0, g_ref.shape[1], step):
        acc += dot(g_ref[:, i : i + step], w_ref[:, i : i + step], ((1,), (1,)))
    out_ref[...] = acc.astype(jnp.bfloat16)


def grad_context(grad_out, out_weight):
    shape = (grad_out.shape[0], out_weight.shape[0])
    return pl.pallas_call(
        grad_context_kernel,
        in_specs=[VMEM] * 2,
        out_specs=VMEM,
        out_shape=jax.ShapeDtypeStruct(shape, jnp.bfloat16),
        compiler_params=PARAMS,
    )(grad_out, out_weight)


def backward_kernel(ids_ref, slot_ref, q_ref, k_ref, v_ref, g_ref, back_ref, dq_ref, dk_ref, dv_ref):
    units = q_ref.shape[0] // UNIT
    masks = block_masks(ids_ref, units)
    for h in range(q_ref.shape[1] // HD):
        cols = pl.ds(h * HD, HD)
        k, v = k_ref[:, cols], v_ref[:, cols]
        dk = jnp.zeros(k.shape, jnp.float32)
        dv = jnp.zeros(v.shape, jnp.float32)
        for u in range(units):
            rows = pl.ds(u * UNIT, UNIT)
            q = q_ref[rows, cols]
            w = unit_weights(q, k, masks[u])
            stays = slot_ref[u * UNIT] < units * UNIT
            g = jnp.where(stays, g_ref[rows, cols].astype(jnp.float32), back_ref[:, cols].astype(jnp.float32))
            g = g.astype(jnp.bfloat16)
            dv += dot(w.astype(jnp.bfloat16), g, ((0,), (0,)))
            dw = dot(g, v, ((1,), (1,)))
            ds = (w * (dw - jnp.sum(w * dw, axis=-1, keepdims=True))).astype(jnp.bfloat16)
            dq_ref[rows, cols] = (dot(ds, k, ((1,), (0,))) * HD**-0.5).astype(jnp.bfloat16)
            dk += dot(ds, q, ((0,), (0,)))
        dk_ref[:, cols] = (dk * HD**-0.5).astype(jnp.bfloat16)
        dv_ref[:, cols] = dv.astype(jnp.bfloat16)


def backward(image_ids, send_slot, q, k, v, g, back):
    return pl.pallas_call(
        backward_kernel,
        grid=(1,),
        in_specs=[SMEM, SMEM] + [whole(q.shape)] * 3 + [whole(g.shape), whole(back.shape)],
        out_specs=[whole(q.shape)] * 3,
        out_shape=[jax.ShapeDtypeStruct(q.shape, jnp.bfloat16)] * 3,
    )(image_ids, send_slot, q, k, v, g, back)


PLACES = [(z, y, c) for z in range(NZ) for y in range(NY) for c in range(NC)]


def index(z, y, c):
    return (z % NZ * NY + y % NY) * NC + c


def send(block, to):
    return lax.ppermute(block, "dp", [(index(*p), index(*to(*p))) for p in PLACES])


def along_y(step):
    return lambda z, y, c: (z, y + step, c)


def apart_y(step):
    return lambda z, y, c: (z, y + step * (1 - 2 * c), c)


def along_z(step):
    return lambda z, y, c: (z + step, y, c)


def sibling(z, y, c):
    return (z, y, 1 - c)


def total(*terms):
    return sum(t.astype(jnp.float32) for t in terms)


def rounded_total(*terms):
    return total(*terms).astype(jnp.bfloat16)


def local(queries, key_rows, value_rows, image_ids, send_slot, out_weight, grad_out):
    row_count, width = queries.shape
    ranks = lax.axis_size("dp")
    core = lax.axis_index("dp") % NC

    stay, leave, g_near, w_near = contexts(
        image_ids, send_slot, queries, key_rows, value_rows, grad_out, out_weight
    )
    came = lax.ppermute(leave, "dp", [(i, (i + 1) % ranks) for i in range(ranks)])
    grad_ctx = grad_context(g_near, w_near)
    stay, grad_ctx = lax.optimization_barrier((stay, grad_ctx))

    given = partial_grad(True, stay, came, g_near)
    got = send(given, sibling)
    own = partial_grad(False, stay, came, g_near)

    size = NZ * width
    mine = {d: own[i * size : (i + 1) * size] for i, d in enumerate(ORDER)}
    theirs = {d: got[i * size : (i + 1) * size] for i, d in enumerate(ORDER)}
    part = {d: rounded_total(mine[d], theirs[d]) for d in (4, 3, 5, 1, 7)}

    far = send(part[4], apart_y(2))
    up, down = send(part[3], along_y(1)), send(part[5], along_y(-1))
    near_up, near_down = send(part[1], along_y(1)), send(part[7], along_y(-1))
    none = jnp.zeros_like(far)
    up = rounded_total(mine[2], theirs[2], up, jnp.where(core == 0, far, none))
    down = rounded_total(mine[6], theirs[6], down, jnp.where(core == 1, far, none))
    up, down = send(up, along_y(2)), send(down, along_y(-2))
    ring = total(mine[0], theirs[0], near_up, near_down, up, down)
    above = send(ring[width : 2 * width].astype(jnp.bfloat16), along_z(1))
    below = send(ring[2 * width :].astype(jnp.bfloat16), along_z(-1))
    grad_weight = total(ring[:width], above, below)

    back = lax.ppermute(grad_ctx[row_count:], "dp", [((i + 1) % ranks, i) for i in range(ranks)])
    grads = backward(image_ids, send_slot, queries, key_rows, value_rows, grad_ctx, back)
    return (*grads, grad_weight)


def solution(mesh):
    placed = (
        P("dp", "fsdp"),
        P("dp", "fsdp"),
        P("dp", "fsdp"),
        P("dp"),
        P("dp"),
        P("fsdp", None),
        P("dp", None),
    )
    return jax.shard_map(
        local,
        mesh=mesh,
        in_specs=placed,
        out_specs=(P("dp", "fsdp"), P("dp", "fsdp"), P("dp", "fsdp"), P("fsdp", "dp")),
        check_vma=False,
    )
```

time: 109 us -> 90.2 us (0.83)
  Pallas kernels: 27.3 us -> 13.6 us
  waiting for transfers between devices: 32.8 us -> 20.6 us
  starting transfers between devices: 39.3 us -> 48.4 us
  local copies, waits for them, and re-layouts: 5.01 us -> 0.64 us
  other arithmetic: 3.12 us -> 4.88 us
    ppermute x11 -> x10, waiting for transfers between devices: 22.6 us -> 5.31 us  [send(): lax.ppermute(block, 'dp', [(index(*p), index(*to(*p))) for p in PLACES])]
    pallas_call x7 -> x5, Pallas kernels: 27.3 us -> 13.6 us  [the longest x1 4.97 us: backward(): pl.pallas_call(backward_kernel, grid=(1,), in_specs=[SMEM, SMEM] + [whole...]
    ppermute x1, starting transfers between devices: 2.56 us -> 8.35 us  [local(): lax.ppermute(grad_ctx[row_count:], 'dp', [((i + 1) % ranks, i) for i in r...]
    ppermute x1, waiting for transfers between devices: 10.2 us -> 15.3 us  [local(): lax.ppermute(leave, 'dp', [(i, (i + 1) % ranks) for i in range(ranks)])]
    unnamed x24 -> x4, local copies, waits for them, and re-layouts: 4.99 us -> 0.63 us
    ppermute x11 -> x10, starting transfers between devices: 34.9 us -> 38.1 us  [send(): lax.ppermute(block, 'dp', [(index(*p), index(*to(*p))) for p in PLACES])]
    convert_element_type x5 -> x2, other arithmetic: 2.33 us -> 2.4 us  [rounded_total(): return total(*terms).astype(jnp.bfloat16)]
  transfers between devices with their start and end apart: 13 -> 12, of which waited for: 6 -> 3; matrix products, arithmetic and copies ran while one was open for 2% -> 3% of each run, Pallas kernels for 19% -> 9%
where the time goes in v2:
time: 90.2 us; the launch traced here: 89 us
  starting transfers between devices  48.4 us (54%)
  waiting for transfers between devices  20.6 us (23%)
  Pallas kernels  13.6 us (15%)
  other arithmetic  4.88 us (5%)
    ppermute x10, starting transfers between devices, send(): lax.ppermute(block, 'dp', [(index(*p), index(*to(*p))) for p in PLACES])  38.1 us
    ppermute x1, waiting for transfers between devices, local(): lax.ppermute(leave, 'dp', [(i, (i + 1) % ranks) for i in range(ranks)])  15.3 us
    ppermute x1, starting transfers between devices, local(): lax.ppermute(grad_ctx[row_count:], 'dp', [((i + 1) % ranks, i) for i in r...  8.35 us
    ppermute x10, waiting for transfers between devices, send(): lax.ppermute(block, 'dp', [(index(*p), index(*to(*p))) for p in PLACES])  5.31 us
    pallas_call x1, Pallas kernels, backward(): pl.pallas_call(backward_kernel, grid=(1,), in_specs=[SMEM, SMEM] + [whole...  4.97 us
    pallas_call x1, Pallas kernels, contexts(): pl.pallas_call(context_kernel, in_specs=[pl.BlockSpec(memory_space=pltpu....  4.07 us
    pallas_call x2, Pallas kernels, partial_grad(): pl.pallas_call(functools.partial(partial_kernel, other), in_specs=[VMEM,...  2.73 us
    convert_element_type x2, other arithmetic, rounded_total(): return total(*terms).astype(jnp.bfloat16)  2.4 us
  transfers between devices with their start and end apart: 12, of which 3 were waited for; matrix products, arithmetic and copies ran while one was open for 3% of the time, Pallas kernels for 9%

profile of v2, /device:TPU:6, one launch (start us, length us, event | category | flops | bytes accessed | tf_op | source)
XLA Modules:
  0.0 89.0 jit_solution(12603378514612524673)
XLA Ops:
  0.6 4.1 %shard_map.102 = (bf16[256,384]{1,0:T(8,128)(2,1)S(1)}, bf16[256,128]{1,0:T(8,128)(2,1)S(1)}, bf16[512,6144]{1,0:T(8,128)(2,1)S(1)}, bf16[256,6144]{1,0:T(8,128)(2,1)S(1)}) custom-call(s32[384]{0:T(512)} %ids_ref.1, s32[384]{0:T(512)} %slot_ref.1, bf16[384,256]{1,0:T(8,128)(2,1)} %q_ref.1, bf16[384,256]{1,0:T(8,128)(2,1)} %k_ref.1, bf16[384,256]{1,0:T(8,128)(2,1)} %v_ref.1, ...), custom_call_target="tpu_custom_call" | custom-call | tf_op jit(solution)/shard_map/pallas_call | solution.py:74
  4.7 1.9 %collective-permute-start.1 = (bf16[256,128]{1,0:T(8,128)(2,1)S(1)}, bf16[256,128]{1,0:T(8,128)(2,1)S(1)}, u32[]{:S(2)}, u32[]{:S(2)}) collective-permute-start(bf16[256,128]{1,0:T(8,128)(2,1)S(1)} %get-tuple-element.21), channel_id=1, source_target_pairs={{0,16},{16,32},{32,48},{48,64},{64,80},{80,96},{96,112},{112,128},... | collective-permute-start | bytes 196616 | tf_op jit(solution)/shard_map/ppermute | solution.py:207
  6.6 1.8 %shard_map.103.g_ref = bf16[512,256]{1,0:T(8,128)(2,1)S(1)} custom-call(bf16[512,6144]{1,0:T(8,128)(2,1)S(1)} %get-tuple-element.14.g_ref, bf16[256,6144]{1,0:T(8,128)(2,1)S(1)} %get-tuple-element.15.w_ref), custom_call_target="tpu_custom_call" | custom-call | tf_op jit(solution)/shard_map/pallas_call | solution.py:121
  8.5 0.0 copy-start
  8.5 15.3 %collective-permute-done.1.came_ref = bf16[256,128]{1,0:T(8,128)(2,1)S(1)} collective-permute-done((bf16[256,128]{1,0:T(8,128)(2,1)S(1)}, bf16[256,128]{1,0:T(8,128)(2,1)S(1)}, u32[]{:S(2)}, u32[]{:S(2)}) %collective-permute-start.1) | collective-permute-done | bytes 65568 | tf_op jit(solution)/shard_map/ppermute | solution.py:207
  23.8 1.3 %shard_map.106 = bf16[6144,128]{1,0:T(8,128)(2,1)S(1)} custom-call(bf16[256,384]{1,0:T(8,128)(2,1)S(1)} %get-tuple-element.20.stay_ref, bf16[256,128]{1,0:T(8,128)(2,1)S(1)} %collective-permute-done.1.came_ref, bf16[512,6144]{1,0:T(8,128)(2,1)S(1)} %get-tuple-element.14.g_ref), custom_call_target="tpu_custom_call" | custom-call | tf_op jit(solution)/shard_map/pallas_call | solution.py:102
  25.1 1.9 %collective-permute-start.2 = (bf16[6144,128]{1,0:T(8,128)(2,1)S(1)}, bf16[6144,128]{1,0:T(8,128)(2,1)S(1)}, u32[]{:S(2)}, u32[]{:S(2)}) collective-permute-start(bf16[6144,128]{1,0:T(8,128)(2,1)S(1)} %shard_map.106), channel_id=1, source_target_pairs={{0,16},{16,0},{32,48},{48,32},{64,80},{80,64},{96,112},{112,96},{1... | collective-permute-start | bytes 4718600 | tf_op jit(solution)/shard_map/ppermute | solution.py:172
  27.1 1.4 %shard_map.105 = bf16[6144,128]{1,0:T(8,128)(2,1)S(1)} custom-call(bf16[256,384]{1,0:T(8,128)(2,1)S(1)} %get-tuple-element.20.stay_ref, bf16[256,128]{1,0:T(8,128)(2,1)S(1)} %collective-permute-done.1.came_ref, bf16[512,6144]{1,0:T(8,128)(2,1)S(1)} %get-tuple-element.14.g_ref), custom_call_target="tpu_custom_call" | custom-call | tf_op jit(solution)/shard_map/pallas_call | solution.py:102
  28.5 2.0 %collective-permute-done.2 = bf16[6144,128]{1,0:T(8,128)(2,1)S(1)} collective-permute-done((bf16[6144,128]{1,0:T(8,128)(2,1)S(1)}, bf16[6144,128]{1,0:T(8,128)(2,1)S(1)}, u32[]{:S(2)}, u32[]{:S(2)}) %collective-permute-start.2) | collective-permute-done | bytes 1572896 | tf_op jit(solution)/shard_map/ppermute | solution.py:172
  30.4 1.1 %add_convert_fusion.6 = (bf16[768,128]{1,0:T(8,128)(2,1)}, bf16[768,128]{1,0:T(8,128)(2,1)}, bf16[768,128]{1,0:T(8,128)(2,1)}, bf16[768,128]{1,0:T(8,128)(2,1)}, bf16[768,128]{1,0:T(8,128)(2,1)}) fusion(bf16[6144,128]{1,0:T(8,128)(2,1)S(1)} %collective-permute-done.2, bf16[6144,128]{1,0:T(8,128)(2,1)S(1)} %shard_map.105), kind=kLoop, calls=%fused_computation.7 | loop fusion | flops 1966080 | bytes 2949120 | tf_op jit(solution)/shard_map/convert_element_type | solution.py:196
  31.5 1.9 %collective-permute-start.5 = (bf16[768,128]{1,0:T(8,128)(2,1)}, bf16[768,128]{1,0:T(8,128)(2,1)}, u32[]{:S(2)}, u32[]{:S(2)}) collective-permute-start(bf16[768,128]{1,0:T(8,128)(2,1)} %get-tuple-element.29), channel_id=1, source_target_pairs={{0,32},{16,48},{32,64},{48,80},{64,96},{80,112},{96,128},{112,144}... | collective-permute-start | bytes 589832 | tf_op jit(solution)/shard_map/ppermute | solution.py:172
  33.4 1.9 %collective-permute-start.6 = (bf16[768,128]{1,0:T(8,128)(2,1)}, bf16[768,128]{1,0:T(8,128)(2,1)}, u32[]{:S(2)}, u32[]{:S(2)}) collective-permute-start(bf16[768,128]{1,0:T(8,128)(2,1)} %get-tuple-element.28), channel_id=1, source_target_pairs={{0,64},{16,208},{32,96},{48,240},{64,128},{80,16},{96,160},{112,48... | collective-permute-start | bytes 589832 | tf_op jit(solution)/shard_map/ppermute | solution.py:172
  35.3 5.1 %collective-permute-start.8 = (bf16[768,128]{1,0:T(8,128)(2,1)}, bf16[768,128]{1,0:T(8,128)(2,1)}, u32[]{:S(2)}, u32[]{:S(2)}) collective-permute-start(bf16[768,128]{1,0:T(8,128)(2,1)} %get-tuple-element.27), channel_id=1, source_target_pairs={{0,224},{16,240},{32,0},{48,16},{64,32},{80,48},{96,64},{112,80},{... | collective-permute-start | bytes 589832 | tf_op jit(solution)/shard_map/ppermute | solution.py:172
  40.5 1.9 %collective-permute-start.3 = (bf16[768,128]{1,0:T(8,128)(2,1)}, bf16[768,128]{1,0:T(8,128)(2,1)S(1)}, u32[]{:S(2)}, u32[]{:S(2)}) collective-permute-start(bf16[768,128]{1,0:T(8,128)(2,1)} %get-tuple-element.26), channel_id=1, source_target_pairs={{0,32},{16,48},{32,64},{48,80},{64,96},{80,112},{96,128},{112,144}... | collective-permute-start | bytes 589832 | tf_op jit(solution)/shard_map/ppermute | solution.py:172
  42.4 5.1 %collective-permute-start.4 = (bf16[768,128]{1,0:T(8,128)(2,1)}, bf16[768,128]{1,0:T(8,128)(2,1)S(1)}, u32[]{:S(2)}, u32[]{:S(2)}) collective-permute-start(bf16[768,128]{1,0:T(8,128)(2,1)} %get-tuple-element.30), channel_id=1, source_target_pairs={{0,224},{16,240},{32,0},{48,16},{64,32},{80,48},{96,64},{112,80},{... | collective-permute-start | bytes 589832 | tf_op jit(solution)/shard_map/ppermute | solution.py:172
  47.6 0.0 collective-permute-done.5
  47.6 0.0 collective-permute-done.6
  47.6 0.0 collective-permute-done.8
  47.6 1.3 %add_convert_fusion.2 = (bf16[768,128]{1,0:T(8,128)(2,1)S(1)}, bf16[768,128]{1,0:T(8,128)(2,1)S(1)}) fusion(bf16[768,128]{1,0:T(8,128)(2,1)} %collective-permute-done.5, bf16[6144,128]{1,0:T(8,128)(2,1)S(1)} %collective-permute-done.2, bf16[6144,128]{1,0:T(8,128)(2,1)S(1)} %shard_map.105, bf16[768,128]{1,0:T(8,128)(2,1)} %collective-permute-done.6, ...), kind=kLoop, calls=%fused_computation.3 | loop fusion | flops 1769472 | bytes 1769474 | tf_op jit(solution)/shard_map/convert_element_type | solution.py:196
  49.0 1.9 %collective-permute-start.7 = (bf16[768,128]{1,0:T(8,128)(2,1)S(1)}, bf16[768,128]{1,0:T(8,128)(2,1)S(1)}, u32[]{:S(2)}, u32[]{:S(2)}) collective-permute-start(bf16[768,128]{1,0:T(8,128)(2,1)S(1)} %get-tuple-element.24), channel_id=1, source_target_pairs={{0,64},{16,80},{32,96},{48,112},{64,128},{80,144},{96,160},{112,17... | collective-permute-start | bytes 589832 | tf_op jit(solution)/shard_map/ppermute | solution.py:172
  50.9 6.0 %collective-permute-start.9 = (bf16[768,128]{1,0:T(8,128)(2,1)S(1)}, bf16[768,128]{1,0:T(8,128)(2,1)S(1)}, u32[]{:S(2)}, u32[]{:S(2)}) collective-permute-start(bf16[768,128]{1,0:T(8,128)(2,1)S(1)} %get-tuple-element.25), channel_id=1, source_target_pairs={{0,192},{16,208},{32,224},{48,240},{64,0},{80,16},{96,32},{112,48}... | collective-permute-start | bytes 589832 | tf_op jit(solution)/shard_map/ppermute | solution.py:172
  56.9 0.0 copy-done
  56.9 8.3 %collective-permute-start = (bf16[128,256]{1,0:T(8,128)(2,1)S(1)}, bf16[128,256]{1,0:T(8,128)(2,1)S(1)}, u32[]{:S(2)}, u32[]{:S(2)}) collective-permute-start(bf16[128,256]{1,0:T(8,128)(2,1)S(1)} %slice.62), channel_id=1, source_target_pairs={{16,0},{32,16},{48,32},{64,48},{80,64},{96,80},{112,96},{128,112},... | collective-permute-start | bytes 196616 | tf_op jit(solution)/shard_map/ppermute | solution.py:232
  65.3 0.0 collective-permute-done.3
  65.3 0.0 collective-permute-done.4
  65.3 0.0 collective-permute-done.7
  65.3 0.0 collective-permute-done.9
  65.3 0.9 %fusion.1 = (bf16[768,128]{1,0:T(8,128)(2,1)S(1)}, f32[768,128]{1,0:T(8,128)}) fusion(bf16[768,128]{1,0:T(8,128)(2,1)S(1)} %collective-permute-done.9, bf16[768,128]{1,0:T(8,128)(2,1)S(1)} %collective-permute-done.7, bf16[768,128]{1,0:T(8,128)(2,1)S(1)} %collective-permute-done.4, bf16[768,128]{1,0:T(8,128)(2,1)S(1)} %collective-permute-done.3, ...), kind=kLoop, calls=%fused_computation.10 | loop fusion | flops 1179648 | bytes 1769472 | tf_op jit(solution)/shard_map/convert.1
  66.3 3.0 %collective-permute-start.10 = (bf16[256,128]{1,0:T(8,128)(2,1)S(1)}, bf16[256,128]{1,0:T(8,128)(2,1)S(1)}, u32[]{:S(2)}, u32[]{:S(2)}) collective-permute-start(bf16[256,128]{1,0:T(8,128)(2,1)S(1)} %get-tuple-element.31), channel_id=1, source_target_pairs={{0,256},{16,272},{32,288},{48,304},{64,320},{80,336},{96,352},{112... | collective-permute-start | bytes 196616 | tf_op jit(solution)/shard_map/ppermute | solution.py:172
  69.2 9.3 %collective-permute-start.11 = (bf16[256,128]{1,0:T(8,128)(2,1)S(1)}, bf16[256,128]{1,0:T(8,128)(2,1)S(1)}, u32[]{:S(2)}, u32[]{:S(2)}) collective-permute-start(bf16[256,128]{1,0:T(8,128)(2,1)S(1)} %get-tuple-element.32), channel_id=1, source_target_pairs={{0,512},{16,528},{32,544},{48,560},{64,576},{80,592},{96,608},{112... | collective-permute-start | bytes 196616 | tf_op jit(solution)/shard_map/ppermute | solution.py:172
  78.5 0.0 collective-permute-done.back_ref
  78.5 0.0 copy-start.1
  78.5 0.6 copy-done.1
  79.2 5.0 %shard_map.104 = (bf16[384,256]{1,0:T(8,128)(2,1)}, bf16[384,256]{1,0:T(8,128)(2,1)}, bf16[384,256]{1,0:T(8,128)(2,1)}) custom-call(s32[384]{0:T(512)} %ids_ref.1, s32[384]{0:T(512)} %slot_ref.1, bf16[384,256]{1,0:T(8,128)(2,1)} %q_ref.1, bf16[384,256]{1,0:T(8,128)(2,1)} %k_ref.1, bf16[384,256]{1,0:T(8,128)(2,1)} %v_ref.1, bf16[512,256]{1,0:T(8,128)(2,1)} %copy-done, ...), custom_call_target="tpu_custom_call" | custom-call | tf_op jit(solution)/shard_map/pallas_call | solution.py:155
  84.1 0.0 collective-permute-done.10
  84.1 3.3 %collective-permute-done.11 = bf16[256,128]{1,0:T(8,128)(2,1)S(1)} collective-permute-done((bf16[256,128]{1,0:T(8,128)(2,1)S(1)}, bf16[256,128]{1,0:T(8,128)(2,1)S(1)}, u32[]{:S(2)}, u32[]{:S(2)}) %collective-permute-start.11) | collective-permute-done | bytes 65568 | tf_op jit(solution)/shard_map/ppermute | solution.py:172
  87.4 1.6 %fusion = f32[256,128]{1,0:T(8,128)} fusion(f32[768,128]{1,0:T(8,128)} %get-tuple-element.23, bf16[256,128]{1,0:T(8,128)(2,1)S(1)} %collective-permute-done.11, bf16[256,128]{1,0:T(8,128)(2,1)S(1)} %collective-permute-done.10), kind=kLoop, calls=%fused_computation.9 | loop fusion | flops 131072 | bytes 393216 | tf_op jit(solution)/shard_map/add | solution.py:192
  (2 shorter events, 0.0 us)
Async XLA Ops:
  4.7 19.1 %collective-permute-start.1 = (bf16[256,128]{1,0:T(8,128)(2,1)S(1)}, bf16[256,128]{1,0:T(8,128)(2,1)S(1)}, u32[]{:S(2)}, u32[]{:S(2)}) collective-permute-start(bf16[256,128]{1,0:T(8,128)(2,1)S(1)} %get-tuple-element.21), channel_id=1, source_target_pairs={{0,16},{16,32},{32,48},{48,64},{64,80},{80,96},{96,112},{112,128},... | collective-permute-start | bytes 196616 | tf_op jit(solution)/shard_map/ppermute | solution.py:207
  8.5 48.5 %copy-start = (bf16[512,256]{1,0:T(8,128)(2,1)}, bf16[512,256]{1,0:T(8,128)(2,1)S(1)}, u32[]{:S(2)}) copy-start(bf16[512,256]{1,0:T(8,128)(2,1)S(1)} %shard_map.103.g_ref) | copy-start | bytes 786436
  25.1 5.3 %collective-permute-start.2 = (bf16[6144,128]{1,0:T(8,128)(2,1)S(1)}, bf16[6144,128]{1,0:T(8,128)(2,1)S(1)}, u32[]{:S(2)}, u32[]{:S(2)}) collective-permute-start(bf16[6144,128]{1,0:T(8,128)(2,1)S(1)} %shard_map.106), channel_id=1, source_target_pairs={{0,16},{16,0},{32,48},{48,32},{64,80},{80,64},{96,112},{112,96},{1... | collective-permute-start | bytes 4718600 | tf_op jit(solution)/shard_map/ppermute | solution.py:172
  31.5 16.1 %collective-permute-start.5 = (bf16[768,128]{1,0:T(8,128)(2,1)}, bf16[768,128]{1,0:T(8,128)(2,1)}, u32[]{:S(2)}, u32[]{:S(2)}) collective-permute-start(bf16[768,128]{1,0:T(8,128)(2,1)} %get-tuple-element.29), channel_id=1, source_target_pairs={{0,32},{16,48},{32,64},{48,80},{64,96},{80,112},{96,128},{112,144}... | collective-permute-start | bytes 589832 | tf_op jit(solution)/shard_map/ppermute | solution.py:172
  33.4 14.2 %collective-permute-start.6 = (bf16[768,128]{1,0:T(8,128)(2,1)}, bf16[768,128]{1,0:T(8,128)(2,1)}, u32[]{:S(2)}, u32[]{:S(2)}) collective-permute-start(bf16[768,128]{1,0:T(8,128)(2,1)} %get-tuple-element.28), channel_id=1, source_target_pairs={{0,64},{16,208},{32,96},{48,240},{64,128},{80,16},{96,160},{112,48... | collective-permute-start | bytes 589832 | tf_op jit(solution)/shard_map/ppermute | solution.py:172
  35.3 12.3 %collective-permute-start.8 = (bf16[768,128]{1,0:T(8,128)(2,1)}, bf16[768,128]{1,0:T(8,128)(2,1)}, u32[]{:S(2)}, u32[]{:S(2)}) collective-permute-start(bf16[768,128]{1,0:T(8,128)(2,1)} %get-tuple-element.27), channel_id=1, source_target_pairs={{0,224},{16,240},{32,0},{48,16},{64,32},{80,48},{96,64},{112,80},{... | collective-permute-start | bytes 589832 | tf_op jit(solution)/shard_map/ppermute | solution.py:172
  40.5 24.8 %collective-permute-start.3 = (bf16[768,128]{1,0:T(8,128)(2,1)}, bf16[768,128]{1,0:T(8,128)(2,1)S(1)}, u32[]{:S(2)}, u32[]{:S(2)}) collective-permute-start(bf16[768,128]{1,0:T(8,128)(2,1)} %get-tuple-element.26), channel_id=1, source_target_pairs={{0,32},{16,48},{32,64},{48,80},{64,96},{80,112},{96,128},{112,144}... | collective-permute-start | bytes 589832 | tf_op jit(solution)/shard_map/ppermute | solution.py:172
  42.4 22.9 %collective-permute-start.4 = (bf16[768,128]{1,0:T(8,128)(2,1)}, bf16[768,128]{1,0:T(8,128)(2,1)S(1)}, u32[]{:S(2)}, u32[]{:S(2)}) collective-permute-start(bf16[768,128]{1,0:T(8,128)(2,1)} %get-tuple-element.30), channel_id=1, source_target_pairs={{0,224},{16,240},{32,0},{48,16},{64,32},{80,48},{96,64},{112,80},{... | collective-permute-start | bytes 589832 | tf_op jit(solution)/shard_map/ppermute | solution.py:172
  49.0 16.4 %collective-permute-start.7 = (bf16[768,128]{1,0:T(8,128)(2,1)S(1)}, bf16[768,128]{1,0:T(8,128)(2,1)S(1)}, u32[]{:S(2)}, u32[]{:S(2)}) collective-permute-start(bf16[768,128]{1,0:T(8,128)(2,1)S(1)} %get-tuple-element.24), channel_id=1, source_target_pairs={{0,64},{16,80},{32,96},{48,112},{64,128},{80,144},{96,160},{112,17... | collective-permute-start | bytes 589832 | tf_op jit(solution)/shard_map/ppermute | solution.py:172
  50.9 14.5 %collective-permute-start.9 = (bf16[768,128]{1,0:T(8,128)(2,1)S(1)}, bf16[768,128]{1,0:T(8,128)(2,1)S(1)}, u32[]{:S(2)}, u32[]{:S(2)}) collective-permute-start(bf16[768,128]{1,0:T(8,128)(2,1)S(1)} %get-tuple-element.25), channel_id=1, source_target_pairs={{0,192},{16,208},{32,224},{48,240},{64,0},{80,16},{96,32},{112,48}... | collective-permute-start | bytes 589832 | tf_op jit(solution)/shard_map/ppermute | solution.py:172
  56.9 21.6 %collective-permute-start = (bf16[128,256]{1,0:T(8,128)(2,1)S(1)}, bf16[128,256]{1,0:T(8,128)(2,1)S(1)}, u32[]{:S(2)}, u32[]{:S(2)}) collective-permute-start(bf16[128,256]{1,0:T(8,128)(2,1)S(1)} %slice.62), channel_id=1, source_target_pairs={{16,0},{32,16},{48,32},{64,48},{80,64},{96,80},{112,96},{128,112},... | collective-permute-start | bytes 196616 | tf_op jit(solution)/shard_map/ppermute | solution.py:232
  66.3 17.9 %collective-permute-start.10 = (bf16[256,128]{1,0:T(8,128)(2,1)S(1)}, bf16[256,128]{1,0:T(8,128)(2,1)S(1)}, u32[]{:S(2)}, u32[]{:S(2)}) collective-permute-start(bf16[256,128]{1,0:T(8,128)(2,1)S(1)} %get-tuple-element.31), channel_id=1, source_target_pairs={{0,256},{16,272},{32,288},{48,304},{64,320},{80,336},{96,352},{112... | collective-permute-start | bytes 196616 | tf_op jit(solution)/shard_map/ppermute | solution.py:172
  69.2 18.2 %collective-permute-start.11 = (bf16[256,128]{1,0:T(8,128)(2,1)S(1)}, bf16[256,128]{1,0:T(8,128)(2,1)S(1)}, u32[]{:S(2)}, u32[]{:S(2)}) collective-permute-start(bf16[256,128]{1,0:T(8,128)(2,1)S(1)} %get-tuple-element.32), channel_id=1, source_target_pairs={{0,512},{16,528},{32,544},{48,560},{64,576},{80,592},{96,608},{112... | collective-permute-start | bytes 196616 | tf_op jit(solution)/shard_map/ppermute | solution.py:172
  78.5 0.6 copy-start.1

commit v3 on v2

--- a/solution.py
+++ b/solution.py
@@ -10,7 +10,7 @@
 HD = 128
 UNIT = 128
 NZ, NY, NC = 3, 8, 2
-ORDER = (4, 3, 5, 2, 6, 1, 7, 0)
+ORDER = (4, 3, 1, 5, 7, 2, 6, 0)
 SMEM = pl.BlockSpec(memory_space=pltpu.SMEM)
 VMEM = pl.BlockSpec(memory_space=pltpu.VMEM)
 PARAMS = pltpu.CompilerParams(vmem_limit_bytes=16 * 1024 * 1024)
@@ -37,10 +37,10 @@
     return softmax(jnp.where(mask, dot(q, k, ((1,), (1,))) * HD**-0.5, -jnp.inf))
 
 
-def context_kernel(ids_hbm, slot_hbm, q_hbm, k_hbm, v_hbm, g_hbm, w_hbm, stay_ref, leave_ref, g_ref, w_ref,
+def context_kernel(ids_hbm, slot_hbm, q_hbm, k_hbm, v_hbm, g_hbm, stay_ref, leave_ref, g_ref,
                    ids_ref, slot_ref, q_ref, k_ref, v_ref, sems):
     pairs = [(ids_hbm, ids_ref), (slot_hbm, slot_ref), (q_hbm, q_ref), (k_hbm, k_ref), (v_hbm, v_ref),
-             (g_hbm, g_ref), (w_hbm, w_ref)]
+             (g_hbm, g_ref)]
     copies = [pltpu.make_async_copy(src, dst, sems.at[i]) for i, (src, dst) in enumerate(pairs)]
     for copy in copies:
         copy.start()
@@ -60,27 +60,30 @@
             stay_ref[cols, rows] = jnp.where(stays, ctx, 0.0).astype(jnp.bfloat16)
             leave = jnp.where(stays, leave, ctx)
         leave_ref[cols, :] = leave.astype(jnp.bfloat16)
-    for copy in copies[5:]:
-        copy.wait()
+    copies[5].wait()
+
+
+def in_hbm(x):
+    return pltpu.with_memory_space_constraint(x, pltpu.HBM)
 
 
 def whole(shape):
     return pl.BlockSpec(shape, lambda i: (0,) * len(shape))
 
 
-def contexts(image_ids, send_slot, q, k, v, grad_out, out_weight):
+def contexts(image_ids, send_slot, q, k, v, grad_out):
     rows, width = q.shape
-    shapes = [(width, rows), (width, UNIT), grad_out.shape, out_weight.shape]
+    shapes = [(width, rows), (width, UNIT), grad_out.shape]
     return pl.pallas_call(
         context_kernel,
-        in_specs=[pl.BlockSpec(memory_space=pltpu.HBM)] * 7,
-        out_specs=[VMEM] * 4,
+        in_specs=[pl.BlockSpec(memory_space=pltpu.HBM)] * 6,
+        out_specs=[VMEM] * 3,
         out_shape=[jax.ShapeDtypeStruct(shape, jnp.bfloat16) for shape in shapes],
         scratch_shapes=[pltpu.SMEM(image_ids.shape, jnp.int32), pltpu.SMEM(send_slot.shape, jnp.int32)]
         + [pltpu.VMEM(q.shape, jnp.bfloat16)] * 3
-        + [pltpu.SemaphoreType.DMA((7,))],
+        + [pltpu.SemaphoreType.DMA((6,))],
         compiler_params=PARAMS,
-    )(*[pltpu.with_memory_space_constraint(x, pltpu.HBM) for x in (image_ids, send_slot, q, k, v, grad_out, out_weight)])
+    )(*[in_hbm(x) for x in (image_ids, send_slot, q, k, v, grad_out)])
 
 
 def partial_kernel(other, stay_ref, came_ref, g_ref, out_ref):
@@ -108,23 +111,36 @@
     )(stay, came, grad_out)
 
 
-def grad_context_kernel(g_ref, w_ref, out_ref):
-    step = 1024
-    acc = jnp.zeros(out_ref.shape, jnp.float32)
-    for i in range(0, g_ref.shape[1], step):
-        acc += dot(g_ref[:, i : i + step], w_ref[:, i : i + step], ((1,), (1,)))
-    out_ref[...] = acc.astype(jnp.bfloat16)
+def grad_context_kernel(g_ref, w_ref, out_ref, acc_ref):
+    i = pl.program_id(0)
+    step = w_ref.shape[1]
+    part = dot(g_ref[:, pl.ds(pl.multiple_of(i * step, step), step)], w_ref[...], ((1,), (1,)))
+
+    @pl.when(i == 0)
+    def _():
+        acc_ref[...] = part
+
+    @pl.when(i > 0)
+    def _():
+        acc_ref[...] += part
+
+    @pl.when(i == pl.num_programs(0) - 1)
+    def _():
+        out_ref[...] = acc_ref[...].astype(jnp.bfloat16)
 
 
 def grad_context(grad_out, out_weight):
     shape = (grad_out.shape[0], out_weight.shape[0])
+    step = 1536
     return pl.pallas_call(
         grad_context_kernel,
-        in_specs=[VMEM] * 2,
+        grid=(grad_out.shape[1] // step,),
+        in_specs=[VMEM, pl.BlockSpec((shape[1], step), lambda i: (0, i))],
         out_specs=VMEM,
         out_shape=jax.ShapeDtypeStruct(shape, jnp.bfloat16),
+        scratch_shapes=[pltpu.VMEM(shape, jnp.float32)],
         compiler_params=PARAMS,
-    )(grad_out, out_weight)
+    )(grad_out, in_hbm(out_weight))
 
 
 def backward_kernel(ids_ref, slot_ref, q_ref, k_ref, v_ref, g_ref, back_ref, dq_ref, dk_ref, dv_ref):
@@ -201,36 +217,36 @@
     ranks = lax.axis_size("dp")
     core = lax.axis_index("dp") % NC
 
-    stay, leave, g_near, w_near = contexts(
-        image_ids, send_slot, queries, key_rows, value_rows, grad_out, out_weight
-    )
+    stay, leave, g_near = contexts(image_ids, send_slot, queries, key_rows, value_rows, grad_out)
     came = lax.ppermute(leave, "dp", [(i, (i + 1) % ranks) for i in range(ranks)])
-    grad_ctx = grad_context(g_near, w_near)
+    grad_ctx = grad_context(g_near, out_weight)
     stay, grad_ctx = lax.optimization_barrier((stay, grad_ctx))
 
     given = partial_grad(True, stay, came, g_near)
+    given, tail = lax.optimization_barrier((given, grad_ctx[row_count:]))
     got = send(given, sibling)
     own = partial_grad(False, stay, came, g_near)
+    back = lax.ppermute(tail, "dp", [((i + 1) % ranks, i) for i in range(ranks)])
+    got, back = lax.optimization_barrier((got, back))
+
+    def blocks(first, last):
+        rows = slice(ORDER.index(first) * NZ * width, (ORDER.index(last) + 1) * NZ * width)
+        return own[rows], got[rows]
 
     size = NZ * width
-    mine = {d: own[i * size : (i + 1) * size] for i, d in enumerate(ORDER)}
-    theirs = {d: got[i * size : (i + 1) * size] for i, d in enumerate(ORDER)}
-    part = {d: rounded_total(mine[d], theirs[d]) for d in (4, 3, 5, 1, 7)}
-
-    far = send(part[4], apart_y(2))
-    up, down = send(part[3], along_y(1)), send(part[5], along_y(-1))
-    near_up, near_down = send(part[1], along_y(1)), send(part[7], along_y(-1))
+    far = send(rounded_total(*blocks(4, 4)), apart_y(2))
+    up = send(rounded_total(*blocks(3, 1)), along_y(1))
+    down = send(rounded_total(*blocks(5, 7)), along_y(-1))
+    grads = backward(image_ids, send_slot, queries, key_rows, value_rows, grad_ctx, back)
     none = jnp.zeros_like(far)
-    up = rounded_total(mine[2], theirs[2], up, jnp.where(core == 0, far, none))
-    down = rounded_total(mine[6], theirs[6], down, jnp.where(core == 1, far, none))
-    up, down = send(up, along_y(2)), send(down, along_y(-2))
-    ring = total(mine[0], theirs[0], near_up, near_down, up, down)
+    up2 = rounded_total(*blocks(2, 2), up[:size], jnp.where(core == 0, far, none))
+    down2 = rounded_total(*blocks(6, 6), down[:size], jnp.where(core == 1, far, none))
+    up2, down2, *grads = lax.optimization_barrier((up2, down2, *grads))
+    up2, down2 = send(up2, along_y(2)), send(down2, along_y(-2))
+    ring = total(*blocks(0, 0), up[size:], down[size:], up2, down2)
     above = send(ring[width : 2 * width].astype(jnp.bfloat16), along_z(1))
     below = send(ring[2 * width :].astype(jnp.bfloat16), along_z(-1))
     grad_weight = total(ring[:width], above, below)
-
-    back = lax.ppermute(grad_ctx[row_count:], "dp", [((i + 1) % ranks, i) for i in range(ranks)])
-    grads = backward(image_ids, send_slot, queries, key_rows, value_rows, grad_ctx, back)
     return (*grads, grad_weight)
 
 

time: 90.2 us -> 95.6 us (1.060)
  the two profiles are of different devices: /device:TPU:6 before, /device:TPU:8 now
where the time goes in v3:
time: 95.6 us; the launch traced here: 95.1 us
  starting transfers between devices  46.4 us (49%)
  waiting for transfers between devices  27.2 us (28%)
  Pallas kernels  15.7 us (16%)
  other arithmetic  4.95 us (5%)
    ppermute x8, starting transfers between devices, send(): lax.ppermute(block, 'dp', [(index(*p), index(*to(*p))) for p in PLACES])  29.5 us
    ppermute x8, waiting for transfers between devices, send(): lax.ppermute(block, 'dp', [(index(*p), index(*to(*p))) for p in PLACES])  26.7 us
    ppermute x1, starting transfers between devices, local(): lax.ppermute(tail, 'dp', [((i + 1) % ranks, i) for i in range(ranks)])  15 us
    pallas_call x1, Pallas kernels, backward(): pl.pallas_call(backward_kernel, grid=(1,), in_specs=[SMEM, SMEM] + [whole...  4.98 us
    pallas_call x1, Pallas kernels, grad_context(): pl.pallas_call(grad_context_kernel, grid=(grad_out.shape[1] // step,), in...  4.35 us
    pallas_call x1, Pallas kernels, contexts(): pl.pallas_call(context_kernel, in_specs=[pl.BlockSpec(memory_space=pltpu....  3.62 us
    convert_element_type x3, other arithmetic, rounded_total(): return total(*terms).astype(jnp.bfloat16)  3.1 us
    pallas_call x2, Pallas kernels, partial_grad(): pl.pallas_call(functools.partial(partial_kernel, other), in_specs=[VMEM,...  2.77 us
  transfers between devices with their start and end apart: 10, of which 6 were waited for; matrix products, arithmetic and copies ran while one was open for 1% of the time, Pallas kernels for 11%

profile of v3, /device:TPU:8, one launch (start us, length us, event | category | flops | bytes accessed | tf_op | source)
XLA Modules:
  0.0 95.1 jit_solution(14165024939765712070)
XLA Ops:
  0.6 3.6 %shard_map.102 = (bf16[256,384]{1,0:T(8,128)(2,1)S(1)}, bf16[256,128]{1,0:T(8,128)(2,1)S(1)}, bf16[512,6144]{1,0:T(8,128)(2,1)S(1)}) custom-call(s32[384]{0:T(512)} %ids_ref.1, s32[384]{0:T(512)} %slot_ref.1, bf16[384,256]{1,0:T(8,128)(2,1)} %q_ref.1, bf16[384,256]{1,0:T(8,128)(2,1)} %k_ref.1, bf16[384,256]{1,0:T(8,128)(2,1)} %v_ref.1, bf16[512,6144]{1,0:T(8,128)(2,1)} %g_hbm.1), custom_call_target="tpu_custom_call" | custom-call | tf_op jit(solution)/shard_map/pallas_call | solution.py:77
  4.3 1.9 %collective-permute-start = (bf16[256,128]{1,0:T(8,128)(2,1)S(1)}, bf16[256,128]{1,0:T(8,128)(2,1)S(1)}, u32[]{:S(2)}, u32[]{:S(2)}) collective-permute-start(bf16[256,128]{1,0:T(8,128)(2,1)S(1)} %get-tuple-element.24), channel_id=1, source_target_pairs={{0,16},{16,32},{32,48},{48,64},{64,80},{80,96},{96,112},{112,128},... | collective-permute-start | bytes 196616 | tf_op jit(solution)/shard_map/ppermute | solution.py:221
  6.2 4.3 %shard_map.103.g_ref = bf16[512,256]{1,0:T(8,128)(2,1)S(1)} custom-call(bf16[512,6144]{1,0:T(8,128)(2,1)S(1)} %get-tuple-element.22.g_ref, bf16[256,6144]{1,0:T(8,128)(2,1)} %w_ref.1), custom_call_target="tpu_custom_call" | custom-call | tf_op jit(solution)/shard_map/pallas_call | solution.py:135
  10.5 0.0 copy-start
  10.6 0.0 collective-permute-done.came_ref
  10.6 1.4 %shard_map.105 = bf16[6144,128]{1,0:T(8,128)(2,1)S(1)} custom-call(bf16[256,384]{1,0:T(8,128)(2,1)S(1)} %get-tuple-element.23.stay_ref, bf16[256,128]{1,0:T(8,128)(2,1)S(1)} %collective-permute-done.came_ref, bf16[512,6144]{1,0:T(8,128)(2,1)S(1)} %get-tuple-element.22.g_ref), custom_call_target="tpu_custom_call" | custom-call | tf_op jit(solution)/shard_map/pallas_call | solution.py:105
  12.0 0.0 copy-done
  12.0 3.6 %collective-permute-start.1 = (bf16[6144,128]{1,0:T(8,128)(2,1)S(1)}, bf16[6144,128]{1,0:T(8,128)(2,1)S(1)}, u32[]{:S(2)}, u32[]{:S(2)}) collective-permute-start(bf16[6144,128]{1,0:T(8,128)(2,1)S(1)} %shard_map.105), channel_id=1, source_target_pairs={{0,16},{16,0},{32,48},{48,32},{64,80},{80,64},{96,112},{112,96},{1... | collective-permute-start | bytes 4718600 | tf_op jit(solution)/shard_map/ppermute | solution.py:188
  15.6 15.0 %collective-permute-start.2 = (bf16[128,256]{1,0:T(8,128)(2,1)S(1)}, bf16[128,256]{1,0:T(8,128)(2,1)S(1)}, u32[]{:S(2)}, u32[]{:S(2)}) collective-permute-start(bf16[128,256]{1,0:T(8,128)(2,1)S(1)} %slice.63), channel_id=1, source_target_pairs={{16,0},{32,16},{48,32},{64,48},{80,64},{96,80},{112,96},{128,112},... | collective-permute-start | bytes 196616 | tf_op jit(solution)/shard_map/ppermute | solution.py:229
  30.6 1.4 %shard_map.104 = bf16[6144,128]{1,0:T(8,128)(2,1)S(1)} custom-call(bf16[256,384]{1,0:T(8,128)(2,1)S(1)} %get-tuple-element.23.stay_ref, bf16[256,128]{1,0:T(8,128)(2,1)S(1)} %collective-permute-done.came_ref, bf16[512,6144]{1,0:T(8,128)(2,1)S(1)} %get-tuple-element.22.g_ref), custom_call_target="tpu_custom_call" | custom-call | tf_op jit(solution)/shard_map/pallas_call | solution.py:105
  32.0 0.5 collective-permute-done.2.back_ref
  32.5 0.0 copy-start.1
  32.5 0.0 collective-permute-done.1
  32.5 1.1 %add_convert_fusion = (bf16[1536,128]{1,0:T(8,128)(2,1)}, bf16[1536,128]{1,0:T(8,128)(2,1)}) fusion(bf16[6144,128]{1,0:T(8,128)(2,1)S(1)} %shard_map.104, bf16[6144,128]{1,0:T(8,128)(2,1)S(1)} %collective-permute-done.1), kind=kLoop, calls=%fused_computation | loop fusion | flops 1572864 | bytes 2359296 | tf_op jit(solution)/shard_map/convert_element_type | solution.py:212
  33.6 5.5 %collective-permute-start.5 = (bf16[1536,128]{1,0:T(8,128)(2,1)}, bf16[1536,128]{1,0:T(8,128)(2,1)}, u32[]{:S(2)}, u32[]{:S(2)}) collective-permute-start(bf16[1536,128]{1,0:T(8,128)(2,1)} %get-tuple-element.42), channel_id=1, source_target_pairs={{0,224},{16,240},{32,0},{48,16},{64,32},{80,48},{96,64},{112,80},{... | collective-permute-start | bytes 1179656 | tf_op jit(solution)/shard_map/ppermute | solution.py:188
  39.2 1.9 %collective-permute-start.3 = (bf16[1536,128]{1,0:T(8,128)(2,1)}, bf16[1536,128]{1,0:T(8,128)(2,1)}, u32[]{:S(2)}, u32[]{:S(2)}) collective-permute-start(bf16[1536,128]{1,0:T(8,128)(2,1)} %get-tuple-element.43), channel_id=1, source_target_pairs={{0,32},{16,48},{32,64},{48,80},{64,96},{80,112},{96,128},{112,144}... | collective-permute-start | bytes 1179656 | tf_op jit(solution)/shard_map/ppermute | solution.py:188
  41.1 0.8 add_convert_fusion.4
  41.8 1.9 %collective-permute-start.4 = (bf16[768,128]{1,0:T(8,128)(2,1)}, bf16[768,128]{1,0:T(8,128)(2,1)S(1)}, u32[]{:S(2)}, u32[]{:S(2)}) collective-permute-start(bf16[768,128]{1,0:T(8,128)(2,1)} %add_convert_fusion.4), channel_id=1, source_target_pairs={{0,64},{16,208},{32,96},{48,240},{64,128},{80,16},{96,160},{112,48... | collective-permute-start | bytes 589832 | tf_op jit(solution)/shard_map/ppermute | solution.py:188
  43.8 0.0 copy-done.1
  43.8 5.0 %shard_map.106 = (bf16[384,256]{1,0:T(8,128)(2,1)}, bf16[384,256]{1,0:T(8,128)(2,1)}, bf16[384,256]{1,0:T(8,128)(2,1)}) custom-call(s32[384]{0:T(512)} %ids_ref.1, s32[384]{0:T(512)} %slot_ref.1, bf16[384,256]{1,0:T(8,128)(2,1)} %q_ref.1, bf16[384,256]{1,0:T(8,128)(2,1)} %k_ref.1, bf16[384,256]{1,0:T(8,128)(2,1)} %v_ref.1, bf16[512,256]{1,0:T(8,128)(2,1)} %copy-done, ...), custom_call_target="tpu_custom_call" | custom-call | tf_op jit(solution)/shard_map/pallas_call | solution.py:171
  48.8 9.4 %collective-permute-done.4 = bf16[768,128]{1,0:T(8,128)(2,1)S(1)} collective-permute-done((bf16[768,128]{1,0:T(8,128)(2,1)}, bf16[768,128]{1,0:T(8,128)(2,1)S(1)}, u32[]{:S(2)}, u32[]{:S(2)}) %collective-permute-start.4) | collective-permute-done | bytes 196640 | tf_op jit(solution)/shard_map/ppermute | solution.py:188
  58.1 0.0 collective-permute-done.5
  58.1 0.0 collective-permute-done.3
  58.1 1.2 %add_convert_fusion.2 = (bf16[768,128]{1,0:T(8,128)(2,1)S(1)}, bf16[768,128]{1,0:T(8,128)(2,1)S(1)}) fusion(bf16[1536,128]{1,0:T(8,128)(2,1)} %collective-permute-done.5, bf16[6144,128]{1,0:T(8,128)(2,1)S(1)} %shard_map.104, bf16[768,128]{1,0:T(8,128)(2,1)S(1)} %collective-permute-done.4, bf16[6144,128]{1,0:T(8,128)(2,1)S(1)} %collective-permute-done.1, ...), kind=kLoop, calls=%fused_computation.3 | loop fusion | flops 1769472 | bytes 1769474 | tf_op jit(solution)/shard_map/convert_element_type | solution.py:212
  59.4 1.9 %collective-permute-start.7 = (bf16[768,128]{1,0:T(8,128)(2,1)S(1)}, bf16[768,128]{1,0:T(8,128)(2,1)S(1)}, u32[]{:S(2)}, u32[]{:S(2)}) collective-permute-start(bf16[768,128]{1,0:T(8,128)(2,1)S(1)} %get-tuple-element.37), channel_id=1, source_target_pairs={{0,192},{16,208},{32,224},{48,240},{64,0},{80,16},{96,32},{112,48}... | collective-permute-start | bytes 589832 | tf_op jit(solution)/shard_map/ppermute | solution.py:188
  61.3 4.8 %collective-permute-start.6 = (bf16[768,128]{1,0:T(8,128)(2,1)S(1)}, bf16[768,128]{1,0:T(8,128)(2,1)S(1)}, u32[]{:S(2)}, u32[]{:S(2)}) collective-permute-start(bf16[768,128]{1,0:T(8,128)(2,1)S(1)} %get-tuple-element.36), channel_id=1, source_target_pairs={{0,64},{16,80},{32,96},{48,112},{64,128},{80,144},{96,160},{112,17... | collective-permute-start | bytes 589832 | tf_op jit(solution)/shard_map/ppermute | solution.py:188
  66.1 2.4 %collective-permute-done.7 = bf16[768,128]{1,0:T(8,128)(2,1)S(1)} collective-permute-done((bf16[768,128]{1,0:T(8,128)(2,1)S(1)}, bf16[768,128]{1,0:T(8,128)(2,1)S(1)}, u32[]{:S(2)}, u32[]{:S(2)}) %collective-permute-start.7) | collective-permute-done | bytes 196640 | tf_op jit(solution)/shard_map/ppermute | solution.py:188
  68.5 5.4 %collective-permute-done.6 = bf16[768,128]{1,0:T(8,128)(2,1)S(1)} collective-permute-done((bf16[768,128]{1,0:T(8,128)(2,1)S(1)}, bf16[768,128]{1,0:T(8,128)(2,1)S(1)}, u32[]{:S(2)}, u32[]{:S(2)}) %collective-permute-start.6) | collective-permute-done | bytes 196640 | tf_op jit(solution)/shard_map/ppermute | solution.py:188
  74.0 1.2 %fusion.1 = (bf16[768,128]{1,0:T(8,128)(2,1)S(1)}, f32[768,128]{1,0:T(8,128)S(1)}) fusion(bf16[768,128]{1,0:T(8,128)(2,1)S(1)} %collective-permute-done.7, bf16[768,128]{1,0:T(8,128)(2,1)S(1)} %collective-permute-done.6, bf16[1536,128]{1,0:T(8,128)(2,1)} %collective-permute-done.5, bf16[1536,128]{1,0:T(8,128)(2,1)} %collective-permute-done.3, ...), kind=kLoop, calls=%fused_computation.8 | loop fusion | flops 1179648 | bytes 1769472 | tf_op jit(solution)/shard_map/convert.1
  75.2 5.6 %collective-permute-start.9 = (bf16[256,128]{1,0:T(8,128)(2,1)S(1)}, bf16[256,128]{1,0:T(8,128)(2,1)S(1)}, u32[]{:S(2)}, u32[]{:S(2)}) collective-permute-start(bf16[256,128]{1,0:T(8,128)(2,1)S(1)} %get-tuple-element.45), channel_id=1, source_target_pairs={{0,512},{16,528},{32,544},{48,560},{64,576},{80,592},{96,608},{112... | collective-permute-start | bytes 196616 | tf_op jit(solution)/shard_map/ppermute | solution.py:188
  80.8 4.2 %collective-permute-start.8 = (bf16[256,128]{1,0:T(8,128)(2,1)S(1)}, bf16[256,128]{1,0:T(8,128)(2,1)S(1)}, u32[]{:S(2)}, u32[]{:S(2)}) collective-permute-start(bf16[256,128]{1,0:T(8,128)(2,1)S(1)} %get-tuple-element.44), channel_id=1, source_target_pairs={{0,256},{16,272},{32,288},{48,304},{64,320},{80,336},{96,352},{112... | collective-permute-start | bytes 196616 | tf_op jit(solution)/shard_map/ppermute | solution.py:188
  84.9 0.6 collective-permute-done.9
  85.5 8.9 %collective-permute-done.8 = bf16[256,128]{1,0:T(8,128)(2,1)S(1)} collective-permute-done((bf16[256,128]{1,0:T(8,128)(2,1)S(1)}, bf16[256,128]{1,0:T(8,128)(2,1)S(1)}, u32[]{:S(2)}, u32[]{:S(2)}) %collective-permute-start.8) | collective-permute-done | bytes 65568 | tf_op jit(solution)/shard_map/ppermute | solution.py:188
  94.4 0.7 fusion
  (2 shorter events, 0.0 us)
Async XLA Ops:
  4.3 6.3 %collective-permute-start = (bf16[256,128]{1,0:T(8,128)(2,1)S(1)}, bf16[256,128]{1,0:T(8,128)(2,1)S(1)}, u32[]{:S(2)}, u32[]{:S(2)}) collective-permute-start(bf16[256,128]{1,0:T(8,128)(2,1)S(1)} %get-tuple-element.24), channel_id=1, source_target_pairs={{0,16},{16,32},{32,48},{48,64},{64,80},{80,96},{96,112},{112,128},... | collective-permute-start | bytes 196616 | tf_op jit(solution)/shard_map/ppermute | solution.py:221
  10.5 1.4 %copy-start = (bf16[512,256]{1,0:T(8,128)(2,1)}, bf16[512,256]{1,0:T(8,128)(2,1)S(1)}, u32[]{:S(2)}) copy-start(bf16[512,256]{1,0:T(8,128)(2,1)S(1)} %shard_map.103.g_ref) | copy-start | bytes 786436
  12.0 20.5 %collective-permute-start.1 = (bf16[6144,128]{1,0:T(8,128)(2,1)S(1)}, bf16[6144,128]{1,0:T(8,128)(2,1)S(1)}, u32[]{:S(2)}, u32[]{:S(2)}) collective-permute-start(bf16[6144,128]{1,0:T(8,128)(2,1)S(1)} %shard_map.105), channel_id=1, source_target_pairs={{0,16},{16,0},{32,48},{48,32},{64,80},{80,64},{96,112},{112,96},{1... | collective-permute-start | bytes 4718600 | tf_op jit(solution)/shard_map/ppermute | solution.py:188
  15.6 16.9 %collective-permute-start.2 = (bf16[128,256]{1,0:T(8,128)(2,1)S(1)}, bf16[128,256]{1,0:T(8,128)(2,1)S(1)}, u32[]{:S(2)}, u32[]{:S(2)}) collective-permute-start(bf16[128,256]{1,0:T(8,128)(2,1)S(1)} %slice.63), channel_id=1, source_target_pairs={{16,0},{32,16},{48,32},{64,48},{80,64},{96,80},{112,96},{128,112},... | collective-permute-start | bytes 196616 | tf_op jit(solution)/shard_map/ppermute | solution.py:229
  32.5 11.3 %copy-start.1 = (bf16[128,256]{1,0:T(8,128)(2,1)}, bf16[128,256]{1,0:T(8,128)(2,1)S(1)}, u32[]{:S(2)}) copy-start(bf16[128,256]{1,0:T(8,128)(2,1)S(1)} %collective-permute-done.2.back_ref) | copy-start | bytes 196612
  33.6 24.5 %collective-permute-start.5 = (bf16[1536,128]{1,0:T(8,128)(2,1)}, bf16[1536,128]{1,0:T(8,128)(2,1)}, u32[]{:S(2)}, u32[]{:S(2)}) collective-permute-start(bf16[1536,128]{1,0:T(8,128)(2,1)} %get-tuple-element.42), channel_id=1, source_target_pairs={{0,224},{16,240},{32,0},{48,16},{64,32},{80,48},{96,64},{112,80},{... | collective-permute-start | bytes 1179656 | tf_op jit(solution)/shard_map/ppermute | solution.py:188
  39.2 19.0 %collective-permute-start.3 = (bf16[1536,128]{1,0:T(8,128)(2,1)}, bf16[1536,128]{1,0:T(8,128)(2,1)}, u32[]{:S(2)}, u32[]{:S(2)}) collective-permute-start(bf16[1536,128]{1,0:T(8,128)(2,1)} %get-tuple-element.43), channel_id=1, source_target_pairs={{0,32},{16,48},{32,64},{48,80},{64,96},{80,112},{96,128},{112,144}... | collective-permute-start | bytes 1179656 | tf_op jit(solution)/shard_map/ppermute | solution.py:188
  41.8 16.3 %collective-permute-start.4 = (bf16[768,128]{1,0:T(8,128)(2,1)}, bf16[768,128]{1,0:T(8,128)(2,1)S(1)}, u32[]{:S(2)}, u32[]{:S(2)}) collective-permute-start(bf16[768,128]{1,0:T(8,128)(2,1)} %add_convert_fusion.4), channel_id=1, source_target_pairs={{0,64},{16,208},{32,96},{48,240},{64,128},{80,16},{96,160},{112,48... | collective-permute-start | bytes 589832 | tf_op jit(solution)/shard_map/ppermute | solution.py:188
  59.4 9.1 %collective-permute-start.7 = (bf16[768,128]{1,0:T(8,128)(2,1)S(1)}, bf16[768,128]{1,0:T(8,128)(2,1)S(1)}, u32[]{:S(2)}, u32[]{:S(2)}) collective-permute-start(bf16[768,128]{1,0:T(8,128)(2,1)S(1)} %get-tuple-element.37), channel_id=1, source_target_pairs={{0,192},{16,208},{32,224},{48,240},{64,0},{80,16},{96,32},{112,48}... | collective-permute-start | bytes 589832 | tf_op jit(solution)/shard_map/ppermute | solution.py:188
  61.3 12.6 %collective-permute-start.6 = (bf16[768,128]{1,0:T(8,128)(2,1)S(1)}, bf16[768,128]{1,0:T(8,128)(2,1)S(1)}, u32[]{:S(2)}, u32[]{:S(2)}) collective-permute-start(bf16[768,128]{1,0:T(8,128)(2,1)S(1)} %get-tuple-element.36), channel_id=1, source_target_pairs={{0,64},{16,80},{32,96},{48,112},{64,128},{80,144},{96,160},{112,17... | collective-permute-start | bytes 589832 | tf_op jit(solution)/shard_map/ppermute | solution.py:188
  75.2 10.4 %collective-permute-start.9 = (bf16[256,128]{1,0:T(8,128)(2,1)S(1)}, bf16[256,128]{1,0:T(8,128)(2,1)S(1)}, u32[]{:S(2)}, u32[]{:S(2)}) collective-permute-start(bf16[256,128]{1,0:T(8,128)(2,1)S(1)} %get-tuple-element.45), channel_id=1, source_target_pairs={{0,512},{16,528},{32,544},{48,560},{64,576},{80,592},{96,608},{112... | collective-permute-start | bytes 196616 | tf_op jit(solution)/shard_map/ppermute | solution.py:188
  80.8 13.7 %collective-permute-start.8 = (bf16[256,128]{1,0:T(8,128)(2,1)S(1)}, bf16[256,128]{1,0:T(8,128)(2,1)S(1)}, u32[]{:S(2)}, u32[]{:S(2)}) collective-permute-start(bf16[256,128]{1,0:T(8,128)(2,1)S(1)} %get-tuple-element.44), channel_id=1, source_target_pairs={{0,256},{16,272},{32,288},{48,304},{64,320},{80,336},{96,352},{112... | collective-permute-start | bytes 196616 | tf_op jit(solution)/shard_map/ppermute | solution.py:188

commit v4 on v2

--- a/solution.py
+++ b/solution.py
@@ -10,7 +10,6 @@
 HD = 128
 UNIT = 128
 NZ, NY, NC = 3, 8, 2
-ORDER = (4, 3, 5, 2, 6, 1, 7, 0)
 SMEM = pl.BlockSpec(memory_space=pltpu.SMEM)
 VMEM = pl.BlockSpec(memory_space=pltpu.VMEM)
 PARAMS = pltpu.CompilerParams(vmem_limit_bytes=16 * 1024 * 1024)
@@ -37,10 +36,10 @@
     return softmax(jnp.where(mask, dot(q, k, ((1,), (1,))) * HD**-0.5, -jnp.inf))
 
 
-def context_kernel(ids_hbm, slot_hbm, q_hbm, k_hbm, v_hbm, g_hbm, w_hbm, stay_ref, leave_ref, g_ref, w_ref,
+def context_kernel(ids_hbm, slot_hbm, q_hbm, k_hbm, v_hbm, g_hbm, stay_ref, leave_ref, g_ref,
                    ids_ref, slot_ref, q_ref, k_ref, v_ref, sems):
     pairs = [(ids_hbm, ids_ref), (slot_hbm, slot_ref), (q_hbm, q_ref), (k_hbm, k_ref), (v_hbm, v_ref),
-             (g_hbm, g_ref), (w_hbm, w_ref)]
+             (g_hbm, g_ref)]
     copies = [pltpu.make_async_copy(src, dst, sems.at[i]) for i, (src, dst) in enumerate(pairs)]
     for copy in copies:
         copy.start()
@@ -60,41 +59,49 @@
             stay_ref[cols, rows] = jnp.where(stays, ctx, 0.0).astype(jnp.bfloat16)
             leave = jnp.where(stays, leave, ctx)
         leave_ref[cols, :] = leave.astype(jnp.bfloat16)
-    for copy in copies[5:]:
-        copy.wait()
+    copies[5].wait()
+
+
+def in_hbm(x):
+    return pltpu.with_memory_space_constraint(x, pltpu.HBM)
 
 
 def whole(shape):
     return pl.BlockSpec(shape, lambda i: (0,) * len(shape))
 
 
-def contexts(image_ids, send_slot, q, k, v, grad_out, out_weight):
+def contexts(image_ids, send_slot, q, k, v, grad_out):
     rows, width = q.shape
-    shapes = [(width, rows), (width, UNIT), grad_out.shape, out_weight.shape]
+    shapes = [(width, rows), (width, UNIT), grad_out.shape]
     return pl.pallas_call(
         context_kernel,
-        in_specs=[pl.BlockSpec(memory_space=pltpu.HBM)] * 7,
-        out_specs=[VMEM] * 4,
+        in_specs=[pl.BlockSpec(memory_space=pltpu.HBM)] * 6,
+        out_specs=[VMEM] * 3,
         out_shape=[jax.ShapeDtypeStruct(shape, jnp.bfloat16) for shape in shapes],
         scratch_shapes=[pltpu.SMEM(image_ids.shape, jnp.int32), pltpu.SMEM(send_slot.shape, jnp.int32)]
         + [pltpu.VMEM(q.shape, jnp.bfloat16)] * 3
-        + [pltpu.SemaphoreType.DMA((7,))],
+        + [pltpu.SemaphoreType.DMA((6,))],
         compiler_params=PARAMS,
-    )(*[pltpu.with_memory_space_constraint(x, pltpu.HBM) for x in (image_ids, send_slot, q, k, v, grad_out, out_weight)])
+    )(*[in_hbm(x) for x in (image_ids, send_slot, q, k, v, grad_out)])
 
 
 def partial_kernel(other, stay_ref, came_ref, g_ref, out_ref):
     me = lax.axis_index("dp")
-    z, y, c = me // (NY * NC), (me // NC) % NY, me % NC
+    y, c = (me // NC) % NY, me % NC
     core = 1 - c if other else c
     ctx_t = jnp.concatenate([stay_ref[...], came_ref[...]], axis=1)
     width = ctx_t.shape[0]
-    for n, distance in enumerate(ORDER):
-        dest = [((z + i) % NZ * NY + (y + distance) % NY) * NC + core for i in range(NZ)]
+    blocks = NY * NZ
+    group = 4
+    for n in range(0, blocks, group):
+        dest = []
+        for i in range(n, n + group):
+            odd = (y + (i < blocks // 2)) % 2
+            dest.append((i % (blocks // 2) * 2 + odd) * NC + core)
         g = jnp.concatenate([g_ref[:, pl.ds(pl.multiple_of(d * UNIT, UNIT), UNIT)] for d in dest], axis=1)
         part = dot(ctx_t, g, ((1,), (0,))).astype(jnp.bfloat16)
-        for i in range(NZ):
-            out_ref[pl.ds((n * NZ + i) * width, width), :] = part[:, i * UNIT : (i + 1) * UNIT]
+        for i in range(group):
+            out_ref[pl.ds((n + i) * width, width), :] = part[:, i * UNIT : (i + 1) * UNIT]
 
 
 def partial_grad(other, stay, came, grad_out):
@@ -172,16 +179,12 @@
     return lax.ppermute(block, "dp", [(index(*p), index(*to(*p))) for p in PLACES])
 
 
-def along_y(step):
-    return lambda z, y, c: (z, y + step, c)
-
-
-def apart_y(step):
-    return lambda z, y, c: (z, y + step * (1 - 2 * c), c)
-
-
-def along_z(step):
-    return lambda z, y, c: (z + step, y, c)
+def paired(z, y, c):
+    return (z, y + 1 - (y + c) % 2 * 2, c)
+
+
+def same_parity():
+    return [[index(z, y, c) for z in range(NZ) for y in range(odd, NY, 2)] for odd in range(2) for c in range(NC)]
 
 
 def sibling(z, y, c):
@@ -199,38 +202,22 @@
 def local(queries, key_rows, value_rows, image_ids, send_slot, out_weight, grad_out):
     row_count, width = queries.shape
     ranks = lax.axis_size("dp")
-    core = lax.axis_index("dp") % NC
-
-    stay, leave, g_near, w_near = contexts(
-        image_ids, send_slot, queries, key_rows, value_rows, grad_out, out_weight
-    )
+    stay, leave, g_near = contexts(image_ids, send_slot, queries, key_rows, value_rows, grad_out)
     came = lax.ppermute(leave, "dp", [(i, (i + 1) % ranks) for i in range(ranks)])
-    grad_ctx = grad_context(g_near, w_near)
-    stay, grad_ctx = lax.optimization_barrier((stay, grad_ctx))
 
     given = partial_grad(True, stay, came, g_near)
     got = send(given, sibling)
     own = partial_grad(False, stay, came, g_near)
 
-    size = NZ * width
-    mine = {d: own[i * size : (i + 1) * size] for i, d in enumerate(ORDER)}
-    theirs = {d: got[i * size : (i + 1) * size] for i, d in enumerate(ORDER)}
-    part = {d: rounded_total(mine[d], theirs[d]) for d in (4, 3, 5, 1, 7)}
-
-    far = send(part[4], apart_y(2))
-    up, down = send(part[3], along_y(1)), send(part[5], along_y(-1))
-    near_up, near_down = send(part[1], along_y(1)), send(part[7], along_y(-1))
-    none = jnp.zeros_like(far)
-    up = rounded_total(mine[2], theirs[2], up, jnp.where(core == 0, far, none))
-    down = rounded_total(mine[6], theirs[6], down, jnp.where(core == 1, far, none))
-    up, down = send(up, along_y(2)), send(down, along_y(-2))
-    ring = total(mine[0], theirs[0], near_up, near_down, up, down)
-    above = send(ring[width : 2 * width].astype(jnp.bfloat16), along_z(1))
-    below = send(ring[2 * width :].astype(jnp.bfloat16), along_z(-1))
-    grad_weight = total(ring[:width], above, below)
-
+    half = NY * NZ * width // 2
+    met = send(rounded_total(own[:half], got[:half]), paired)
+    grad_ctx = grad_context(g_near, out_weight)
     back = lax.ppermute(grad_ctx[row_count:], "dp", [((i + 1) % ranks, i) for i in range(ranks)])
+    met, back = lax.optimization_barrier((met, back))
+    sums = rounded_total(own[half:], got[half:], met).reshape(-1, width, UNIT)
+    sums = lax.all_to_all(sums, "dp", 0, 0, axis_index_groups=same_parity())
     grads = backward(image_ids, send_slot, queries, key_rows, value_rows, grad_ctx, back)
+    grad_weight = jnp.sum(sums.astype(jnp.float32), axis=0)
     return (*grads, grad_weight)
 
 

time: 90.2 us -> 91.9 us (1.019)
  waiting for transfers between devices: 20.6 us -> 52.7 us
  starting transfers between devices: 48.4 us -> 22.3 us
  other arithmetic: 4.88 us -> 2.16 us
    ppermute x10 -> x2, starting transfers between devices: 38.1 us -> 3.84 us  [send(): lax.ppermute(block, 'dp', [(index(*p), index(*to(*p))) for p in PLACES])]
    all_to_all x0 -> x1, waiting for transfers between devices: none -> 31.6 us  [local(): sums = lax.all_to_all(sums, 'dp', 0, 0, axis_index_groups=same_parity())]
    all_to_all x0 -> x1, starting transfers between devices: none -> 5.44 us  [local(): sums = lax.all_to_all(sums, 'dp', 0, 0, axis_index_groups=same_parity())]
    ppermute x10 -> x2, waiting for transfers between devices: 5.31 us -> 2.11 us  [send(): lax.ppermute(block, 'dp', [(index(*p), index(*to(*p))) for p in PLACES])]
    ppermute x1, starting transfers between devices: 8.35 us -> 11.1 us  [local(): lax.ppermute(grad_ctx[row_count:], 'dp', [((i + 1) % ranks, i) for i in r...]
    ppermute x1, waiting for transfers between devices: 0.01 us -> 1.88 us  [local(): lax.ppermute(grad_ctx[row_count:], 'dp', [((i + 1) % ranks, i) for i in r...]
    ppermute x1, waiting for transfers between devices: 15.3 us -> 17.2 us  [local(): lax.ppermute(leave, 'dp', [(i, (i + 1) % ranks) for i in range(ranks)])]
    add x1 -> x0, other arithmetic: 1.58 us -> none  [total(): return sum((t.astype(jnp.float32) for t in terms))]
  transfers between devices with their start and end apart: 12 -> 5, of which waited for: 3 -> 4; matrix products, arithmetic and copies ran while one was open for 3% -> 0% of each run, Pallas kernels for 9% -> 9%
where the time goes in v4:
time: 91.9 us; the launch traced here: 90.9 us
  waiting for transfers between devices  52.7 us (57%)
  starting transfers between devices  22.3 us (24%)
  Pallas kernels  13 us (14%)
  other arithmetic  2.16 us (2%)
    all_to_all x1, waiting for transfers between devices, local(): sums = lax.all_to_all(sums, 'dp', 0, 0, axis_index_groups=same_parity())  31.6 us
    ppermute x1, waiting for transfers between devices, local(): lax.ppermute(leave, 'dp', [(i, (i + 1) % ranks) for i in range(ranks)])  17.2 us
    ppermute x1, starting transfers between devices, local(): lax.ppermute(grad_ctx[row_count:], 'dp', [((i + 1) % ranks, i) for i in r...  11.1 us
    all_to_all x1, starting transfers between devices, local(): sums = lax.all_to_all(sums, 'dp', 0, 0, axis_index_groups=same_parity())  5.44 us
    pallas_call x1, Pallas kernels, backward(): pl.pallas_call(backward_kernel, grid=(1,), in_specs=[SMEM, SMEM] + [whole...  4.98 us
    ppermute x2, starting transfers between devices, send(): lax.ppermute(block, 'dp', [(index(*p), index(*to(*p))) for p in PLACES])  3.84 us
    pallas_call x1, Pallas kernels, contexts(): pl.pallas_call(context_kernel, in_specs=[pl.BlockSpec(memory_space=pltpu....  3.62 us
    pallas_call x2, Pallas kernels, partial_grad(): pl.pallas_call(functools.partial(partial_kernel, other), in_specs=[VMEM,...  2.52 us
  transfers between devices with their start and end apart: 5, of which 4 were waited for; matrix products, arithmetic and copies ran while one was open for 0% of the time, Pallas kernels for 9%

profile of v4, /device:TPU:6, one launch (start us, length us, event | category | flops | bytes accessed | tf_op | source)
XLA Modules:
  0.0 90.9 jit_solution(14355166523127084879)
XLA Ops:
  0.6 3.6 %shard_map.102 = (bf16[256,384]{1,0:T(8,128)(2,1)S(1)}, bf16[256,128]{1,0:T(8,128)(2,1)S(1)}, bf16[512,6144]{1,0:T(8,128)(2,1)S(1)}) custom-call(s32[384]{0:T(512)} %ids_ref.1, s32[384]{0:T(512)} %slot_ref.1, bf16[384,256]{1,0:T(8,128)(2,1)} %q_ref.1, bf16[384,256]{1,0:T(8,128)(2,1)} %k_ref.1, bf16[384,256]{1,0:T(8,128)(2,1)} %v_ref.1, bf16[512,6144]{1,0:T(8,128)(2,1)} %g_hbm.1), custom_call_target="tpu_custom_call" | custom-call | tf_op jit(solution)/shard_map/pallas_call | solution.py:76
  4.3 1.9 %collective-permute-start = (bf16[256,128]{1,0:T(8,128)(2,1)S(1)}, bf16[256,128]{1,0:T(8,128)(2,1)S(1)}, u32[]{:S(2)}, u32[]{:S(2)}) collective-permute-start(bf16[256,128]{1,0:T(8,128)(2,1)S(1)} %get-tuple-element.14), channel_id=1, source_target_pairs={{0,16},{16,32},{32,48},{48,64},{64,80},{80,96},{96,112},{112,128},... | collective-permute-start | bytes 196616 | tf_op jit(solution)/shard_map/ppermute | solution.py:206
  6.2 17.2 %collective-permute-done.came_ref = bf16[256,128]{1,0:T(8,128)(2,1)S(1)} collective-permute-done((bf16[256,128]{1,0:T(8,128)(2,1)S(1)}, bf16[256,128]{1,0:T(8,128)(2,1)S(1)}, u32[]{:S(2)}, u32[]{:S(2)}) %collective-permute-start) | collective-permute-done | bytes 65568 | tf_op jit(solution)/shard_map/ppermute | solution.py:206
  23.3 1.3 %shard_map.105 = bf16[6144,128]{1,0:T(8,128)(2,1)S(1)} custom-call(bf16[256,384]{1,0:T(8,128)(2,1)S(1)} %get-tuple-element.13.stay_ref, bf16[256,128]{1,0:T(8,128)(2,1)S(1)} %collective-permute-done.came_ref, bf16[512,6144]{1,0:T(8,128)(2,1)S(1)} %get-tuple-element.12.g_ref), custom_call_target="tpu_custom_call" | custom-call | tf_op jit(solution)/shard_map/pallas_call | solution.py:109
  24.6 1.9 %collective-permute-start.1 = (bf16[6144,128]{1,0:T(8,128)(2,1)S(1)}, bf16[6144,128]{1,0:T(8,128)(2,1)S(1)}, u32[]{:S(2)}, u32[]{:S(2)}) collective-permute-start(bf16[6144,128]{1,0:T(8,128)(2,1)S(1)} %shard_map.105), channel_id=1, source_target_pairs={{0,16},{16,0},{32,48},{48,32},{64,80},{80,64},{96,112},{112,96},{1... | collective-permute-start | bytes 4718600 | tf_op jit(solution)/shard_map/ppermute | solution.py:179
  26.6 0.0 copy-start
  26.6 1.3 %shard_map.104 = bf16[6144,128]{1,0:T(8,128)(2,1)S(1)} custom-call(bf16[256,384]{1,0:T(8,128)(2,1)S(1)} %get-tuple-element.13.stay_ref, bf16[256,128]{1,0:T(8,128)(2,1)S(1)} %collective-permute-done.came_ref, bf16[512,6144]{1,0:T(8,128)(2,1)S(1)} %get-tuple-element.12.g_ref), custom_call_target="tpu_custom_call" | custom-call | tf_op jit(solution)/shard_map/pallas_call | solution.py:109
  27.8 2.1 %collective-permute-done.1 = bf16[6144,128]{1,0:T(8,128)(2,1)S(1)} collective-permute-done((bf16[6144,128]{1,0:T(8,128)(2,1)S(1)}, bf16[6144,128]{1,0:T(8,128)(2,1)S(1)}, u32[]{:S(2)}, u32[]{:S(2)}) %collective-permute-start.1) | collective-permute-done | bytes 1572896 | tf_op jit(solution)/shard_map/ppermute | solution.py:179
  29.9 0.2 add_convert_fusion.1
  30.1 1.9 %collective-permute-start.2 = (bf16[3072,128]{1,0:T(8,128)(2,1)S(1)}, bf16[3072,128]{1,0:T(8,128)(2,1)S(1)}, u32[]{:S(2)}, u32[]{:S(2)}) collective-permute-start(bf16[3072,128]{1,0:T(8,128)(2,1)S(1)} %add_convert_fusion.1), channel_id=1, source_target_pairs={{0,32},{16,240},{32,0},{48,80},{64,96},{80,48},{96,64},{112,144},{... | collective-permute-start | bytes 2359304 | tf_op jit(solution)/shard_map/ppermute | solution.py:179
  32.1 0.0 copy-done
  32.1 1.9 %shard_map.103.g_ref = bf16[512,256]{1,0:T(8,128)(2,1)S(1)} custom-call(bf16[512,6144]{1,0:T(8,128)(2,1)S(1)} %get-tuple-element.12.g_ref, bf16[256,6144]{1,0:T(8,128)(2,1)S(1)} %copy-done), custom_call_target="tpu_custom_call" | custom-call | tf_op jit(solution)/shard_map/pallas_call | solution.py:128
  33.9 0.0 copy-start.1
  34.0 11.1 %collective-permute-start.3 = (bf16[128,256]{1,0:T(8,128)(2,1)S(1)}, bf16[128,256]{1,0:T(8,128)(2,1)S(1)}, u32[]{:S(2)}, u32[]{:S(2)}) collective-permute-start(bf16[128,256]{1,0:T(8,128)(2,1)S(1)} %slice.22), channel_id=1, source_target_pairs={{16,0},{32,16},{48,32},{64,48},{80,64},{96,80},{112,96},{128,112},... | collective-permute-start | bytes 196616 | tf_op jit(solution)/shard_map/ppermute | solution.py:215
  45.0 1.9 %collective-permute-done.3.back_ref = bf16[128,256]{1,0:T(8,128)(2,1)S(1)} collective-permute-done((bf16[128,256]{1,0:T(8,128)(2,1)S(1)}, bf16[128,256]{1,0:T(8,128)(2,1)S(1)}, u32[]{:S(2)}, u32[]{:S(2)}) %collective-permute-start.3) | collective-permute-done | bytes 65568 | tf_op jit(solution)/shard_map/ppermute | solution.py:215
  46.9 0.0 copy-start.2
  46.9 0.0 collective-permute-done.2
  46.9 1.2 %add_convert_fusion = bf16[3072,128]{1,0:T(8,128)(2,1)} fusion(bf16[3072,128]{1,0:T(8,128)(2,1)S(1)} %collective-permute-done.2, bf16[6144,128]{1,0:T(8,128)(2,1)S(1)} %collective-permute-done.1, bf16[6144,128]{1,0:T(8,128)(2,1)S(1)} %shard_map.104), kind=kLoop, calls=%fused_computation.1 | loop fusion | flops 2359296 | bytes 3145728 | tf_op jit(solution)/shard_map/convert_element_type | solution.py:199
  48.1 0.0 copy-done.1
  48.1 0.0 copy-done.2
  48.1 5.4 %all-to-all-start = ((bf16[12,256,128]{2,1,0:T(8,128)(2,1)}), bf16[12,256,128]{2,1,0:T(8,128)(2,1)S(1)}, u32[]{:S(2)}, u32[]{:S(2)}) async-start(bf16[12,256,128]{2,1,0:T(8,128)(2,1)} %bitcast), calls=%async_computation | async-start | bytes 1572864 | tf_op jit(solution)/shard_map/all_to_all | solution.py:218
  53.6 5.0 %shard_map.106 = (bf16[384,256]{1,0:T(8,128)(2,1)}, bf16[384,256]{1,0:T(8,128)(2,1)}, bf16[384,256]{1,0:T(8,128)(2,1)}) custom-call(s32[384]{0:T(512)} %ids_ref.1, s32[384]{0:T(512)} %slot_ref.1, bf16[384,256]{1,0:T(8,128)(2,1)} %q_ref.1, bf16[384,256]{1,0:T(8,128)(2,1)} %k_ref.1, bf16[384,256]{1,0:T(8,128)(2,1)} %v_ref.1, bf16[512,256]{1,0:T(8,128)(2,1)} %copy-done.1, ...), custom_call_target="tpu_custom_call" | custom-call | tf_op jit(solution)/shard_map/pallas_call | solution.py:162
  58.6 31.6 %all-to-all-done = bf16[12,256,128]{2,1,0:T(8,128)(2,1)S(1)} async-done(((bf16[12,256,128]{2,1,0:T(8,128)(2,1)}), bf16[12,256,128]{2,1,0:T(8,128)(2,1)S(1)}, u32[]{:S(2)}, u32[]{:S(2)}) %all-to-all-start) | async-done | bytes 786464 | tf_op jit(solution)/shard_map/all_to_all | solution.py:218
  90.1 0.8 convert_reduce_fusion
  (1 shorter events, 0.0 us)
Async XLA Ops:
  4.3 19.1 %collective-permute-start = (bf16[256,128]{1,0:T(8,128)(2,1)S(1)}, bf16[256,128]{1,0:T(8,128)(2,1)S(1)}, u32[]{:S(2)}, u32[]{:S(2)}) collective-permute-start(bf16[256,128]{1,0:T(8,128)(2,1)S(1)} %get-tuple-element.14), channel_id=1, source_target_pairs={{0,16},{16,32},{32,48},{48,64},{64,80},{80,96},{96,112},{112,128},... | collective-permute-start | bytes 196616 | tf_op jit(solution)/shard_map/ppermute | solution.py:206
  24.6 5.3 %collective-permute-start.1 = (bf16[6144,128]{1,0:T(8,128)(2,1)S(1)}, bf16[6144,128]{1,0:T(8,128)(2,1)S(1)}, u32[]{:S(2)}, u32[]{:S(2)}) collective-permute-start(bf16[6144,128]{1,0:T(8,128)(2,1)S(1)} %shard_map.105), channel_id=1, source_target_pairs={{0,16},{16,0},{32,48},{48,32},{64,80},{80,64},{96,112},{112,96},{1... | collective-permute-start | bytes 4718600 | tf_op jit(solution)/shard_map/ppermute | solution.py:179
  26.6 5.5 %copy-start = (bf16[256,6144]{1,0:T(8,128)(2,1)S(1)}, bf16[256,6144]{1,0:T(8,128)(2,1)}, u32[]{:S(2)}) copy-start(bf16[256,6144]{1,0:T(8,128)(2,1)} %w_ref.1) | copy-start | bytes 9437188
  30.1 16.8 %collective-permute-start.2 = (bf16[3072,128]{1,0:T(8,128)(2,1)S(1)}, bf16[3072,128]{1,0:T(8,128)(2,1)S(1)}, u32[]{:S(2)}, u32[]{:S(2)}) collective-permute-start(bf16[3072,128]{1,0:T(8,128)(2,1)S(1)} %add_convert_fusion.1), channel_id=1, source_target_pairs={{0,32},{16,240},{32,0},{48,80},{64,96},{80,48},{96,64},{112,144},{... | collective-permute-start | bytes 2359304 | tf_op jit(solution)/shard_map/ppermute | solution.py:179
  33.9 14.2 %copy-start.1 = (bf16[512,256]{1,0:T(8,128)(2,1)}, bf16[512,256]{1,0:T(8,128)(2,1)S(1)}, u32[]{:S(2)}) copy-start(bf16[512,256]{1,0:T(8,128)(2,1)S(1)} %shard_map.103.g_ref) | copy-start | bytes 786436
  34.0 13.0 %collective-permute-start.3 = (bf16[128,256]{1,0:T(8,128)(2,1)S(1)}, bf16[128,256]{1,0:T(8,128)(2,1)S(1)}, u32[]{:S(2)}, u32[]{:S(2)}) collective-permute-start(bf16[128,256]{1,0:T(8,128)(2,1)S(1)} %slice.22), channel_id=1, source_target_pairs={{16,0},{32,16},{48,32},{64,48},{80,64},{96,80},{112,96},{128,112},... | collective-permute-start | bytes 196616 | tf_op jit(solution)/shard_map/ppermute | solution.py:215
  46.9 1.2 %copy-start.2 = (bf16[128,256]{1,0:T(8,128)(2,1)}, bf16[128,256]{1,0:T(8,128)(2,1)S(1)}, u32[]{:S(2)}) copy-start(bf16[128,256]{1,0:T(8,128)(2,1)S(1)} %collective-permute-done.3.back_ref) | copy-start | bytes 196612
  48.1 42.0 %all-to-all-start = ((bf16[12,256,128]{2,1,0:T(8,128)(2,1)}), bf16[12,256,128]{2,1,0:T(8,128)(2,1)S(1)}, u32[]{:S(2)}, u32[]{:S(2)}) async-start(bf16[12,256,128]{2,1,0:T(8,128)(2,1)} %bitcast), calls=%async_computation | async-start | bytes 1572864 | tf_op jit(solution)/shard_map/all_to_all | solution.py:218

commit v5 on v4

v5 whole, which is shorter than its diff:
```python
import functools

import jax
import jax.numpy as jnp
from jax import lax
from jax.experimental import pallas as pl
from jax.experimental.pallas import tpu as pltpu
from jax.sharding import PartitionSpec as P

HD = 128
UNIT = 128
NZ, NY, NC = 3, 8, 2
VMEM = pl.BlockSpec(memory_space=pltpu.VMEM)
PARAMS = pltpu.CompilerParams(vmem_limit_bytes=16 * 1024 * 1024)


def dot(a, b, dims):
    return lax.dot_general(a, b, (dims, ((), ())), preferred_element_type=jnp.float32)


def softmax(scores):
    expo = jnp.exp(scores - jnp.max(scores, axis=-1, keepdims=True))
    return expo / jnp.sum(expo, axis=-1, keepdims=True)


def unit_weights(q, k, mask):
    return softmax(jnp.where(mask, dot(q, k, ((1,), (1,))) * HD**-0.5, -jnp.inf))


def leaving_kernel(ids_hbm, slot_hbm, q_hbm, k_hbm, v_hbm, leave_ref, same_ref, stays_ref, q_ref, k_ref, v_ref,
                   ids_ref, slot_ref, sems):
    pairs = [(ids_hbm, ids_ref), (slot_hbm, slot_ref), (q_hbm, q_ref), (k_hbm, k_ref), (v_hbm, v_ref)]
    copies = [pltpu.make_async_copy(src, dst, sems.at[i]) for i, (src, dst) in enumerate(pairs)]
    for copy in copies:
        copy.start()
    for copy in copies:
        copy.wait()
    rows, width = q_ref.shape
    units = rows // UNIT
    stays = [slot_ref[u * UNIT] < rows for u in range(units)]
    first = jnp.int32(0)
    for u in range(1, units):
        first = jnp.where(stays[u], first, u * UNIT)
    moves = slot_ref[first] >= rows
    moved = pl.ds(pl.multiple_of(first, UNIT), UNIT)
    for h in range(width // HD):
        cols = pl.ds(h * HD, HD)
        w = softmax(dot(q_ref[moved, cols], k_ref[moved, cols], ((1,), (1,))) * HD**-0.5)
        ctx = dot(v_ref[moved, cols].T, w.astype(jnp.bfloat16), ((1,), (1,)))
        leave_ref[cols, :] = jnp.where(moves, ctx, 0.0).astype(jnp.bfloat16)
    lane_unit = lax.broadcasted_iota(jnp.int32, (1, rows), 1) // UNIT
    lane_ids = jnp.full((1, rows), ids_ref[0], jnp.int32)
    for u in range(1, units):
        lane_ids = jnp.where(lane_unit == u, ids_ref[u * UNIT], lane_ids)
    for u in range(units):
        same_ref[pl.ds(u, 1), :] = (lane_ids == ids_ref[u * UNIT]).astype(jnp.int32)
        stays_ref[pl.ds(u, 1), :] = jnp.full((1, UNIT), stays[u].astype(jnp.int32), jnp.int32)


def leaving_context(image_ids, send_slot, q, k, v):
    rows, width = q.shape
    shapes = [
        jax.ShapeDtypeStruct((width, UNIT), jnp.bfloat16),
        jax.ShapeDtypeStruct((8, rows), jnp.int32),
        jax.ShapeDtypeStruct((8, UNIT), jnp.int32),
    ] + [jax.ShapeDtypeStruct(q.shape, jnp.bfloat16)] * 3
    return pl.pallas_call(
        leaving_kernel,
        in_specs=[pl.BlockSpec(memory_space=pltpu.HBM)] * 5,
        out_specs=[VMEM] * 6,
        out_shape=shapes,
        scratch_shapes=[
            pltpu.SMEM(image_ids.shape, jnp.int32),
            pltpu.SMEM(send_slot.shape, jnp.int32),
            pltpu.SemaphoreType.DMA((5,)),
        ],
        compiler_params=PARAMS,
    )(*[in_hbm(x) for x in (image_ids, send_slot, q, k, v)])


def context_kernel(same_ref, stays_ref, q_ref, k_ref, v_ref, g_hbm, stay_ref, g_ref, sem):
    copy = pltpu.make_async_copy(g_hbm, g_ref, sem)
    copy.start()
    for h in range(q_ref.shape[1] // HD):
        cols = pl.ds(h * HD, HD)
        v_t = v_ref[:, cols].T
        for u in range(q_ref.shape[0] // UNIT):
            rows = pl.ds(u * UNIT, UNIT)
            w = unit_weights(q_ref[rows, cols], k_ref[:, cols], same_ref[u : u + 1, :] != 0)
            ctx = dot(v_t, w.astype(jnp.bfloat16), ((1,), (1,)))
            stay_ref[cols, rows] = jnp.where(stays_ref[u : u + 1, :] != 0, ctx, 0.0).astype(jnp.bfloat16)
    copy.wait()


def staying_context(same, stays, q, k, v, grad_out):
    shapes = [q.shape[::-1], grad_out.shape]
    return pl.pallas_call(
        context_kernel,
        in_specs=[VMEM] * 5 + [pl.BlockSpec(memory_space=pltpu.HBM)],
        out_specs=[VMEM] * 2,
        out_shape=[jax.ShapeDtypeStruct(shape, jnp.bfloat16) for shape in shapes],
        scratch_shapes=[pltpu.SemaphoreType.DMA],
        compiler_params=PARAMS,
    )(same, stays, q, k, v, in_hbm(grad_out))


def in_hbm(x):
    return pltpu.with_memory_space_constraint(x, pltpu.HBM)


def partial_kernel(crossing, other, stay_ref, came_ref, g_ref, out_ref):
    me = lax.axis_index("dp")
    y, c = (me // NC) % NY, me % NC
    core = 1 - c if other else c
    odd = (y + crossing) % 2
    ctx_t = jnp.concatenate([stay_ref[...], came_ref[...]], axis=1)
    width = ctx_t.shape[0]
    group = 4
    for n in range(0, NY * NZ // 2, group):
        dest = [(i * 2 + odd) * NC + core for i in range(n, n + group)]
        g = jnp.concatenate([g_ref[:, pl.ds(pl.multiple_of(d * UNIT, UNIT), UNIT)] for d in dest], axis=1)
        part = dot(ctx_t, g, ((1,), (0,))).astype(jnp.bfloat16)
        for i in range(group):
            out_ref[pl.ds((n + i) * width, width), :] = part[:, i * UNIT : (i + 1) * UNIT]


def partial_grad(crossing, other, stay, came, grad_out):
    shape = (NY * NZ // 2 * stay.shape[0], UNIT)
    return pl.pallas_call(
        functools.partial(partial_kernel, crossing, other),
        in_specs=[VMEM, VMEM, VMEM],
        out_specs=VMEM,
        out_shape=jax.ShapeDtypeStruct(shape, jnp.bfloat16),
        compiler_params=PARAMS,
    )(stay, came, grad_out)


def grad_context_kernel(g_ref, w_ref, out_ref):
    step = 1024
    acc = jnp.zeros(out_ref.shape, jnp.float32)
    for i in range(0, g_ref.shape[1], step):
        acc += dot(g_ref[:, i : i + step], w_ref[:, i : i + step], ((1,), (1,)))
    out_ref[...] = acc.astype(jnp.bfloat16)


def grad_context(grad_out, out_weight):
    shape = (grad_out.shape[0], out_weight.shape[0])
    return pl.pallas_call(
        grad_context_kernel,
        in_specs=[VMEM] * 2,
        out_specs=VMEM,
        out_shape=jax.ShapeDtypeStruct(shape, jnp.bfloat16),
        compiler_params=PARAMS,
    )(grad_out, out_weight)


def backward_kernel(same_ref, stays_ref, q_ref, k_ref, v_ref, g_ref, back_ref, dq_ref, dk_ref, dv_ref):
    for h in range(q_ref.shape[1] // HD):
        cols = pl.ds(h * HD, HD)
        k, v = k_ref[:, cols], v_ref[:, cols]
        dk = jnp.zeros(k.shape, jnp.float32)
        dv = jnp.zeros(v.shape, jnp.float32)
        for u in range(q_ref.shape[0] // UNIT):
            rows = pl.ds(u * UNIT, UNIT)
            q = q_ref[rows, cols]
            w = unit_weights(q, k, same_ref[u : u + 1, :] != 0)
            stays = stays_ref[u : u + 1, :] != 0
            g = jnp.where(stays, g_ref[rows, cols].astype(jnp.float32), back_ref[:, cols].astype(jnp.float32))
            g = g.astype(jnp.bfloat16)
            dv += dot(w.astype(jnp.bfloat16), g, ((0,), (0,)))
            dw = dot(g, v, ((1,), (1,)))
            ds = (w * (dw - jnp.sum(w * dw, axis=-1, keepdims=True))).astype(jnp.bfloat16)
            dq_ref[rows, cols] = (dot(ds, k, ((1,), (0,))) * HD**-0.5).astype(jnp.bfloat16)
            dk += dot(ds, q, ((0,), (0,)))
        dk_ref[:, cols] = (dk * HD**-0.5).astype(jnp.bfloat16)
        dv_ref[:, cols] = dv.astype(jnp.bfloat16)


def backward(same, stays, q, k, v, g, back):
    return pl.pallas_call(
        backward_kernel,
        in_specs=[VMEM] * 7,
        out_specs=[VMEM] * 3,
        out_shape=[jax.ShapeDtypeStruct(q.shape, jnp.bfloat16)] * 3,
        compiler_params=PARAMS,
    )(same, stays, q, k, v, g, back)


PLACES = [(z, y, c) for z in range(NZ) for y in range(NY) for c in range(NC)]


def index(z, y, c):
    return (z % NZ * NY + y % NY) * NC + c


def send(block, to):
    return lax.ppermute(block, "dp", [(index(*p), index(*to(*p))) for p in PLACES])


def paired(z, y, c):
    return (z, y + 1 - (y + c) % 2 * 2, c)


def same_parity():
    return [[index(z, y, c) for z in range(NZ) for y in range(odd, NY, 2)] for odd in range(2) for c in range(NC)]


def sibling(z, y, c):
    return (z, y, 1 - c)


def total(*terms):
    return sum(t.astype(jnp.float32) for t in terms)


def rounded_total(*terms):
    return total(*terms).astype(jnp.bfloat16)


def local(queries, key_rows, value_rows, image_ids, send_slot, out_weight, grad_out):
    row_count, width = queries.shape
    ranks = lax.axis_size("dp")
    leave, same, stays, q, k, v = leaving_context(image_ids, send_slot, queries, key_rows, value_rows)
    came = lax.ppermute(leave, "dp", [(i, (i + 1) % ranks) for i in range(ranks)])
    stay, g_near = staying_context(same, stays, q, k, v, grad_out)

    got = send(partial_grad(True, True, stay, came, g_near), sibling)
    own = partial_grad(True, False, stay, came, g_near)
    first, stay = lax.optimization_barrier((rounded_total(own, got), stay))
    met = send(first, paired)

    got = send(partial_grad(False, True, stay, came, g_near), sibling)
    own = partial_grad(False, False, stay, came, g_near)
    grad_ctx = grad_context(g_near, out_weight)
    sums = rounded_total(own, got, met).reshape(-1, width, UNIT)
    sums, grad_ctx = lax.optimization_barrier((sums, grad_ctx))
    sums = lax.all_to_all(sums, "dp", 0, 0, axis_index_groups=same_parity())

    back = lax.ppermute(grad_ctx[row_count:], "dp", [((i + 1) % ranks, i) for i in range(ranks)])
    grads = backward(same, stays, q, k, v, grad_ctx, back)
    grad_weight = jnp.sum(sums.astype(jnp.float32), axis=0)
    return (*grads, grad_weight)


def solution(mesh):
    placed = (
        P("dp", "fsdp"),
        P("dp", "fsdp"),
        P("dp", "fsdp"),
        P("dp"),
        P("dp"),
        P("fsdp", None),
        P("dp", None),
    )
    return jax.shard_map(
        local,
        mesh=mesh,
        in_specs=placed,
        out_specs=(P("dp", "fsdp"), P("dp", "fsdp"), P("dp", "fsdp"), P("fsdp", "dp")),
        check_vma=False,
    )
```

time: 91.9 us -> 88.6 us (0.964)
  waiting for transfers between devices: 52.7 us -> 45.6 us
  starting transfers between devices: 22.3 us -> 26 us
    all_to_all x1, waiting for transfers between devices: 31.6 us -> 3.64 us  [local(): sums = lax.all_to_all(sums, 'dp', 0, 0, axis_index_groups=same_parity())]
    ppermute x1, waiting for transfers between devices: 1.88 us -> 19.7 us  [local(): lax.ppermute(grad_ctx[row_count:], 'dp', [((i + 1) % ranks, i) for i in r...]
    ppermute x2 -> x3, waiting for transfers between devices: 2.11 us -> 7.88 us  [send(): lax.ppermute(block, 'dp', [(index(*p), index(*to(*p))) for p in PLACES])]
    all_to_all x1, starting transfers between devices: 5.44 us -> 8.36 us  [local(): sums = lax.all_to_all(sums, 'dp', 0, 0, axis_index_groups=same_parity())]
    ppermute x1, waiting for transfers between devices: 17.2 us -> 14.3 us  [local(): lax.ppermute(leave, 'dp', [(i, (i + 1) % ranks) for i in range(ranks)])]
    ppermute x2 -> x3, starting transfers between devices: 3.84 us -> 5.99 us  [send(): lax.ppermute(block, 'dp', [(index(*p), index(*to(*p))) for p in PLACES])]
    ppermute x1, starting transfers between devices: 11.1 us -> 9.78 us  [local(): lax.ppermute(grad_ctx[row_count:], 'dp', [((i + 1) % ranks, i) for i in r...]
    pallas_call x4 -> x7, Pallas kernels: 11.1 us -> 11.3 us  [the longest x1 3.75 us: backward(): pl.pallas_call(backward_kernel, in_specs=[VMEM] * 7, out_specs=[VMEM] * 3...]
  transfers between devices with their start and end apart: 5 -> 6, of which waited for: 4 -> 5; matrix products, arithmetic and copies ran while one was open for 0% -> 0% of each run, Pallas kernels for 9% -> 12%
where the time goes in v5:
time: 88.6 us; the launch traced here: 87.7 us
  waiting for transfers between devices  45.6 us (51%)
  starting transfers between devices  26 us (29%)
  Pallas kernels  13.1 us (15%)
  other arithmetic  2.16 us (2%)
    ppermute x1, waiting for transfers between devices, local(): lax.ppermute(grad_ctx[row_count:], 'dp', [((i + 1) % ranks, i) for i in r...  19.7 us
    ppermute x1, waiting for transfers between devices, local(): lax.ppermute(leave, 'dp', [(i, (i + 1) % ranks) for i in range(ranks)])  14.3 us
    ppermute x1, starting transfers between devices, local(): lax.ppermute(grad_ctx[row_count:], 'dp', [((i + 1) % ranks, i) for i in r...  9.78 us
    all_to_all x1, starting transfers between devices, local(): sums = lax.all_to_all(sums, 'dp', 0, 0, axis_index_groups=same_parity())  8.36 us
    ppermute x3, waiting for transfers between devices, send(): lax.ppermute(block, 'dp', [(index(*p), index(*to(*p))) for p in PLACES])  7.88 us
    ppermute x3, starting transfers between devices, send(): lax.ppermute(block, 'dp', [(index(*p), index(*to(*p))) for p in PLACES])  5.99 us
    pallas_call x1, Pallas kernels, backward(): pl.pallas_call(backward_kernel, in_specs=[VMEM] * 7, out_specs=[VMEM] * 3...  3.75 us
    all_to_all x1, waiting for transfers between devices, local(): sums = lax.all_to_all(sums, 'dp', 0, 0, axis_index_groups=same_parity())  3.64 us
  transfers between devices with their start and end apart: 6, of which 5 were waited for; matrix products, arithmetic and copies ran while one was open for 0% of the time, Pallas kernels for 12%

profile of v5, /device:TPU:6, one launch (start us, length us, event | category | flops | bytes accessed | tf_op | source)
XLA Modules:
  0.0 87.7 jit_solution(2157201310238709655)
XLA Ops:
  0.6 1.7 %shard_map.102 = (bf16[256,128]{1,0:T(8,128)(2,1)S(1)}, s32[8,384]{1,0:T(8,128)S(1)}, s32[8,128]{1,0:T(8,128)S(1)}, bf16[384,256]{1,0:T(8,128)(2,1)S(1)}, bf16[3...) custom-call(s32[384]{0:T(512)} %ids_hbm.1, s32[384]{0:T(512)} %slot_hbm.1, bf16[384,256]{1,0:T(8,128)(2,1)} %q_hbm.1, ...), custom_call_target="tpu_custom_call" | custom-call | tf_op jit(solution)/shard_map/pallas_call | solution.py:67
  2.4 1.9 %collective-permute-start = (bf16[256,128]{1,0:T(8,128)(2,1)S(1)}, bf16[256,128]{1,0:T(8,128)(2,1)S(1)}, u32[]{:S(2)}, u32[]{:S(2)}) collective-permute-start(bf16[256,128]{1,0:T(8,128)(2,1)S(1)} %get-tuple-element.25), channel_id=1, source_target_pairs={{0,16},{16,32},{32,48},{48,64},{64,80},{80,96},{96,112},{112,128},... | collective-permute-start | bytes 196616 | tf_op jit(solution)/shard_map/ppermute | solution.py:224
  4.3 2.8 %shard_map.103 = (bf16[256,384]{1,0:T(8,128)(2,1)S(1)}, bf16[512,6144]{1,0:T(8,128)(2,1)S(1)}) custom-call(s32[8,384]{1,0:T(8,128)S(1)} %get-tuple-element.19.same_ref, s32[8,128]{1,0:T(8,128)S(1)} %get-tuple-element.20.stays_ref, bf16[384,256]{1,0:T(8,128)(2,1)S(1)} %get-tuple-element.21.q_ref, bf16[384,256]{1,0:T(8,128)(2,1)S(1)} %get-tuple-element.22.k_ref, ...), custom_call_target="tpu_custom_call" | custom-call | tf_op jit(solution)/shard_map/pallas_call | solution.py:97
  7.1 14.3 %collective-permute-done.came_ref = bf16[256,128]{1,0:T(8,128)(2,1)S(1)} collective-permute-done((bf16[256,128]{1,0:T(8,128)(2,1)S(1)}, bf16[256,128]{1,0:T(8,128)(2,1)S(1)}, u32[]{:S(2)}, u32[]{:S(2)}) %collective-permute-start) | collective-permute-done | bytes 65568 | tf_op jit(solution)/shard_map/ppermute | solution.py:224
  21.5 0.7 shard_map.105
  22.2 1.9 %collective-permute-start.1 = (bf16[3072,128]{1,0:T(8,128)(2,1)S(1)}, bf16[3072,128]{1,0:T(8,128)(2,1)S(1)}, u32[]{:S(2)}, u32[]{:S(2)}) collective-permute-start(bf16[3072,128]{1,0:T(8,128)(2,1)S(1)} %shard_map.105), channel_id=1, source_target_pairs={{0,16},{16,0},{32,48},{48,32},{64,80},{80,64},{96,112},{112,96},{1... | collective-permute-start | bytes 2359304 | tf_op jit(solution)/shard_map/ppermute | solution.py:197
  24.1 0.8 shard_map.104
  24.9 1.5 %collective-permute-done.1 = bf16[3072,128]{1,0:T(8,128)(2,1)S(1)} collective-permute-done((bf16[3072,128]{1,0:T(8,128)(2,1)S(1)}, bf16[3072,128]{1,0:T(8,128)(2,1)S(1)}, u32[]{:S(2)}, u32[]{:S(2)}) %collective-permute-start.1) | collective-permute-done | bytes 786464 | tf_op jit(solution)/shard_map/ppermute | solution.py:197
  26.4 0.2 add_convert_fusion.1
  26.6 1.9 %collective-permute-start.3 = (bf16[3072,128]{1,0:T(8,128)(2,1)S(1)}, bf16[3072,128]{1,0:T(8,128)(2,1)S(1)}, u32[]{:S(2)}, u32[]{:S(2)}) collective-permute-start(bf16[3072,128]{1,0:T(8,128)(2,1)S(1)} %add_convert_fusion.1), channel_id=1, source_target_pairs={{0,32},{16,240},{32,0},{48,80},{64,96},{80,48},{96,64},{112,144},{... | collective-permute-start | bytes 2359304 | tf_op jit(solution)/shard_map/ppermute | solution.py:197
  28.5 0.0 copy-start
  28.5 0.8 shard_map.107
  29.3 2.1 %collective-permute-start.2 = (bf16[3072,128]{1,0:T(8,128)(2,1)S(1)}, bf16[3072,128]{1,0:T(8,128)(2,1)S(1)}, u32[]{:S(2)}, u32[]{:S(2)}) collective-permute-start(bf16[3072,128]{1,0:T(8,128)(2,1)S(1)} %shard_map.107), channel_id=1, source_target_pairs={{0,16},{16,0},{32,48},{48,32},{64,80},{80,64},{96,112},{112,96},{1... | collective-permute-start | bytes 2359304 | tf_op jit(solution)/shard_map/ppermute | solution.py:197
  31.5 0.0 copy-done
  31.5 1.8 %shard_map.108.g_ref = bf16[512,256]{1,0:T(8,128)(2,1)S(1)} custom-call(bf16[512,6144]{1,0:T(8,128)(2,1)S(1)} %get-tuple-element.26.g_ref, bf16[256,6144]{1,0:T(8,128)(2,1)S(1)} %copy-done), custom_call_target="tpu_custom_call" | custom-call | tf_op jit(solution)/shard_map/pallas_call | solution.py:148
  33.3 0.8 shard_map.106
  34.1 6.4 %collective-permute-done.3 = bf16[3072,128]{1,0:T(8,128)(2,1)S(1)} collective-permute-done((bf16[3072,128]{1,0:T(8,128)(2,1)S(1)}, bf16[3072,128]{1,0:T(8,128)(2,1)S(1)}, u32[]{:S(2)}, u32[]{:S(2)}) %collective-permute-start.3) | collective-permute-done | bytes 786464 | tf_op jit(solution)/shard_map/ppermute | solution.py:197
  40.5 0.0 collective-permute-done.2
  40.5 1.2 %add_convert_fusion = bf16[3072,128]{1,0:T(8,128)(2,1)} fusion(bf16[3072,128]{1,0:T(8,128)(2,1)S(1)} %collective-permute-done.3, bf16[3072,128]{1,0:T(8,128)(2,1)S(1)} %collective-permute-done.2, bf16[3072,128]{1,0:T(8,128)(2,1)S(1)} %shard_map.106), kind=kLoop, calls=%fused_computation.1 | loop fusion | flops 2359296 | bytes 3145728 | tf_op jit(solution)/shard_map/convert_element_type | solution.py:217
  41.7 8.4 %all-to-all-start = ((bf16[12,256,128]{2,1,0:T(8,128)(2,1)}), bf16[12,256,128]{2,1,0:T(8,128)(2,1)S(1)}, u32[]{:S(2)}, u32[]{:S(2)}) async-start(bf16[12,256,128]{2,1,0:T(8,128)(2,1)} %bitcast), calls=%async_computation | async-start | bytes 1572864 | tf_op jit(solution)/shard_map/all_to_all | solution.py:237
  50.0 9.8 %collective-permute-start.4 = (bf16[128,256]{1,0:T(8,128)(2,1)S(1)}, bf16[128,256]{1,0:T(8,128)(2,1)S(1)}, u32[]{:S(2)}, u32[]{:S(2)}) collective-permute-start(bf16[128,256]{1,0:T(8,128)(2,1)S(1)} %slice.3), channel_id=1, source_target_pairs={{16,0},{32,16},{48,32},{64,48},{80,64},{96,80},{112,96},{128,112},... | collective-permute-start | bytes 196616 | tf_op jit(solution)/shard_map/ppermute | solution.py:239
  59.8 19.7 %collective-permute-done.4.back_ref = bf16[128,256]{1,0:T(8,128)(2,1)S(1)} collective-permute-done((bf16[128,256]{1,0:T(8,128)(2,1)S(1)}, bf16[128,256]{1,0:T(8,128)(2,1)S(1)}, u32[]{:S(2)}, u32[]{:S(2)}) %collective-permute-start.4) | collective-permute-done | bytes 65568 | tf_op jit(solution)/shard_map/ppermute | solution.py:239
  79.6 3.8 %shard_map.109 = (bf16[384,256]{1,0:T(8,128)(2,1)}, bf16[384,256]{1,0:T(8,128)(2,1)}, bf16[384,256]{1,0:T(8,128)(2,1)}) custom-call(s32[8,384]{1,0:T(8,128)S(1)} %get-tuple-element.19.same_ref, s32[8,128]{1,0:T(8,128)S(1)} %get-tuple-element.20.stays_ref, bf16[384,256]{1,0:T(8,128)(2,1)S(1)} %get-tuple-element.21.q_ref, ...), custom_call_target="tpu_custom_call" | custom-call | tf_op jit(solution)/shard_map/pallas_call | solution.py:180
  83.3 3.6 %all-to-all-done = bf16[12,256,128]{2,1,0:T(8,128)(2,1)S(1)} async-done(((bf16[12,256,128]{2,1,0:T(8,128)(2,1)}), bf16[12,256,128]{2,1,0:T(8,128)(2,1)S(1)}, u32[]{:S(2)}, u32[]{:S(2)}) %all-to-all-start) | async-done | bytes 786464 | tf_op jit(solution)/shard_map/all_to_all | solution.py:237
  87.0 0.8 convert_reduce_fusion
  (1 shorter events, 0.0 us)
Async XLA Ops:
  2.4 19.1 %collective-permute-start = (bf16[256,128]{1,0:T(8,128)(2,1)S(1)}, bf16[256,128]{1,0:T(8,128)(2,1)S(1)}, u32[]{:S(2)}, u32[]{:S(2)}) collective-permute-start(bf16[256,128]{1,0:T(8,128)(2,1)S(1)} %get-tuple-element.25), channel_id=1, source_target_pairs={{0,16},{16,32},{32,48},{48,64},{64,80},{80,96},{96,112},{112,128},... | collective-permute-start | bytes 196616 | tf_op jit(solution)/shard_map/ppermute | solution.py:224
  22.2 4.2 %collective-permute-start.1 = (bf16[3072,128]{1,0:T(8,128)(2,1)S(1)}, bf16[3072,128]{1,0:T(8,128)(2,1)S(1)}, u32[]{:S(2)}, u32[]{:S(2)}) collective-permute-start(bf16[3072,128]{1,0:T(8,128)(2,1)S(1)} %shard_map.105), channel_id=1, source_target_pairs={{0,16},{16,0},{32,48},{48,32},{64,80},{80,64},{96,112},{112,96},{1... | collective-permute-start | bytes 2359304 | tf_op jit(solution)/shard_map/ppermute | solution.py:197
  26.6 13.9 %collective-permute-start.3 = (bf16[3072,128]{1,0:T(8,128)(2,1)S(1)}, bf16[3072,128]{1,0:T(8,128)(2,1)S(1)}, u32[]{:S(2)}, u32[]{:S(2)}) collective-permute-start(bf16[3072,128]{1,0:T(8,128)(2,1)S(1)} %add_convert_fusion.1), channel_id=1, source_target_pairs={{0,32},{16,240},{32,0},{48,80},{64,96},{80,48},{96,64},{112,144},{... | collective-permute-start | bytes 2359304 | tf_op jit(solution)/shard_map/ppermute | solution.py:197
  28.5 3.0 %copy-start = (bf16[256,6144]{1,0:T(8,128)(2,1)S(1)}, bf16[256,6144]{1,0:T(8,128)(2,1)}, u32[]{:S(2)}) copy-start(bf16[256,6144]{1,0:T(8,128)(2,1)} %w_ref.1) | copy-start | bytes 9437188
  29.3 11.2 %collective-permute-start.2 = (bf16[3072,128]{1,0:T(8,128)(2,1)S(1)}, bf16[3072,128]{1,0:T(8,128)(2,1)S(1)}, u32[]{:S(2)}, u32[]{:S(2)}) collective-permute-start(bf16[3072,128]{1,0:T(8,128)(2,1)S(1)} %shard_map.107), channel_id=1, source_target_pairs={{0,16},{16,0},{32,48},{48,32},{64,80},{80,64},{96,112},{112,96},{1... | collective-permute-start | bytes 2359304 | tf_op jit(solution)/shard_map/ppermute | solution.py:197
  41.7 45.3 %all-to-all-start = ((bf16[12,256,128]{2,1,0:T(8,128)(2,1)}), bf16[12,256,128]{2,1,0:T(8,128)(2,1)S(1)}, u32[]{:S(2)}, u32[]{:S(2)}) async-start(bf16[12,256,128]{2,1,0:T(8,128)(2,1)} %bitcast), calls=%async_computation | async-start | bytes 1572864 | tf_op jit(solution)/shard_map/all_to_all | solution.py:237
  50.0 29.5 %collective-permute-start.4 = (bf16[128,256]{1,0:T(8,128)(2,1)S(1)}, bf16[128,256]{1,0:T(8,128)(2,1)S(1)}, u32[]{:S(2)}, u32[]{:S(2)}) collective-permute-start(bf16[128,256]{1,0:T(8,128)(2,1)S(1)} %slice.3), channel_id=1, source_target_pairs={{16,0},{32,16},{48,32},{64,48},{80,64},{96,80},{112,96},{128,112},... | collective-permute-start | bytes 196616 | tf_op jit(solution)/shard_map/ppermute | solution.py:239

commit v6 on v5

--- a/solution.py
+++ b/solution.py
@@ -110,14 +110,16 @@
 
 def partial_kernel(crossing, other, stay_ref, came_ref, g_ref, out_ref):
     me = lax.axis_index("dp")
-    y, c = (me // NC) % NY, me % NC
+    z, y, c = me // (NY * NC), (me // NC) % NY, me % NC
     core = 1 - c if other else c
     odd = (y + crossing) % 2
+    places = [((z + i) % NZ, j * 2 + odd) for j in range(NY // 2) for i in range(1, NZ)]
+    places += [(z, j * 2 + odd) for j in range(NY // 2)]
     ctx_t = jnp.concatenate([stay_ref[...], came_ref[...]], axis=1)
     width = ctx_t.shape[0]
     group = 4
-    for n in range(0, NY * NZ // 2, group):
-        dest = [(i * 2 + odd) * NC + core for i in range(n, n + group)]
+    for n in range(0, len(places), group):
+        dest = [(z_to * NY + y_to) * NC + core for z_to, y_to in places[n : n + group]]
         g = jnp.concatenate([g_ref[:, pl.ds(pl.multiple_of(d * UNIT, UNIT), UNIT)] for d in dest], axis=1)
         part = dot(ctx_t, g, ((1,), (0,))).astype(jnp.bfloat16)
         for i in range(group):
@@ -202,7 +204,11 @@
 
 
 def same_parity():
-    return [[index(z, y, c) for z in range(NZ) for y in range(odd, NY, 2)] for odd in range(2) for c in range(NC)]
+    return [[index(z, y, c) for y in range(odd, NY, 2)] for z in range(NZ) for odd in range(2) for c in range(NC)]
+
+
+def along_z(step):
+    return lambda z, y, c: (z + step, y, c)
 
 
 def sibling(z, y, c):
@@ -223,22 +229,28 @@
     leave, same, stays, q, k, v = leaving_context(image_ids, send_slot, queries, key_rows, value_rows)
     came = lax.ppermute(leave, "dp", [(i, (i + 1) % ranks) for i in range(ranks)])
     stay, g_near = staying_context(same, stays, q, k, v, grad_out)
+    grad_ctx = grad_context(g_near, out_weight)
+    stay, tail = lax.optimization_barrier((stay, grad_ctx[row_count:]))
+    back = lax.ppermute(tail, "dp", [((i + 1) % ranks, i) for i in range(ranks)])
 
     got = send(partial_grad(True, True, stay, came, g_near), sibling)
     own = partial_grad(True, False, stay, came, g_near)
+    got, back = lax.optimization_barrier((got, back))
     first, stay = lax.optimization_barrier((rounded_total(own, got), stay))
     met = send(first, paired)
 
     got = send(partial_grad(False, True, stay, came, g_near), sibling)
     own = partial_grad(False, False, stay, came, g_near)
-    grad_ctx = grad_context(g_near, out_weight)
-    sums = rounded_total(own, got, met).reshape(-1, width, UNIT)
-    sums, grad_ctx = lax.optimization_barrier((sums, grad_ctx))
-    sums = lax.all_to_all(sums, "dp", 0, 0, axis_index_groups=same_parity())
-
-    back = lax.ppermute(grad_ctx[row_count:], "dp", [((i + 1) % ranks, i) for i in range(ranks)])
+    far = (NZ - 1) * (NY // 2) * width
+    away = rounded_total(own[:far], got[:far], met[:far]).reshape(NY // 2, -1, UNIT)
+    here = rounded_total(own[far:], got[far:], met[far:]).reshape(NY // 2, -1, UNIT)
+    away, here = lax.optimization_barrier((away, here))
+    away = lax.all_to_all(away, "dp", 0, 0, axis_index_groups=same_parity())
+    away, here = lax.optimization_barrier((rounded_total(*away), here))
+    here = lax.all_to_all(here, "dp", 0, 0, axis_index_groups=same_parity())
+    above, below = send(away[:width], along_z(1)), send(away[width:], along_z(-1))
     grads = backward(same, stays, q, k, v, grad_ctx, back)
-    grad_weight = jnp.sum(sums.astype(jnp.float32), axis=0)
+    grad_weight = total(*here, above, below)
     return (*grads, grad_weight)
 
 

time: 88.6 us -> 89.3 us (level)
  waiting for transfers between devices: 45.6 us -> 20.4 us
  blocking collectives: 0 us -> 19.2 us
  starting transfers between devices: 26 us -> 31 us
    all_to_all x0 -> x1, blocking collectives: none -> 19.2 us  [local(): away = lax.all_to_all(away, 'dp', 0, 0, axis_index_groups=same_parity())]
    ppermute x1, waiting for transfers between devices: 19.7 us -> 1.09 us  [local(): lax.ppermute(tail, 'dp', [((i + 1) % ranks, i) for i in range(ranks)])]
    ppermute x3 -> x5, starting transfers between devices: 5.99 us -> 19.1 us  [send(): lax.ppermute(block, 'dp', [(index(*p), index(*to(*p))) for p in PLACES])]
    all_to_all x1, starting transfers between devices: 8.36 us -> 3.89 us  [local(): here = lax.all_to_all(here, 'dp', 0, 0, axis_index_groups=same_parity())]
    ppermute x1, starting transfers between devices: 9.78 us -> 6.01 us  [local(): lax.ppermute(tail, 'dp', [((i + 1) % ranks, i) for i in range(ranks)])]
    all_to_all x1, waiting for transfers between devices: 3.64 us -> 0.01 us  [local(): here = lax.all_to_all(here, 'dp', 0, 0, axis_index_groups=same_parity())]
    ppermute x1, waiting for transfers between devices: 14.3 us -> 11.6 us  [local(): lax.ppermute(leave, 'dp', [(i, (i + 1) % ranks) for i in range(ranks)])]
    ppermute x3 -> x5, waiting for transfers between devices: 7.88 us -> 7.73 us  [send(): lax.ppermute(block, 'dp', [(index(*p), index(*to(*p))) for p in PLACES])]
  transfers between devices with their start and end apart: 6 -> 8, of which waited for: 5 -> 4; matrix products, arithmetic and copies ran while one was open for 0% -> 0% of each run, Pallas kernels for 12% -> 12%
where the time goes in v6:
time: 89.3 us; the launch traced here: 87.5 us
  starting transfers between devices  31 us (35%)
  waiting for transfers between devices  20.4 us (23%)
  blocking collectives  19.2 us (22%)
  Pallas kernels  13.4 us (15%)
  other arithmetic  1.99 us (2%)
    all_to_all x1, blocking collectives, local(): away = lax.all_to_all(away, 'dp', 0, 0, axis_index_groups=same_parity())  19.2 us
    ppermute x5, starting transfers between devices, send(): lax.ppermute(block, 'dp', [(index(*p), index(*to(*p))) for p in PLACES])  19.1 us
    ppermute x1, waiting for transfers between devices, local(): lax.ppermute(leave, 'dp', [(i, (i + 1) % ranks) for i in range(ranks)])  11.6 us
    ppermute x5, waiting for transfers between devices, send(): lax.ppermute(block, 'dp', [(index(*p), index(*to(*p))) for p in PLACES])  7.73 us
    ppermute x1, starting transfers between devices, local(): lax.ppermute(tail, 'dp', [((i + 1) % ranks, i) for i in range(ranks)])  6.01 us
    all_to_all x1, starting transfers between devices, local(): here = lax.all_to_all(here, 'dp', 0, 0, axis_index_groups=same_parity())  3.89 us
    pallas_call x1, Pallas kernels, backward(): pl.pallas_call(backward_kernel, in_specs=[VMEM] * 7, out_specs=[VMEM] * 3...  3.76 us
    pallas_call x4, Pallas kernels, partial_grad(): pl.pallas_call(functools.partial(partial_kernel, crossing, other), in_spe...  3.15 us
  transfers between devices with their start and end apart: 8, of which 4 were waited for; matrix products, arithmetic and copies ran while one was open for 0% of the time, Pallas kernels for 12%

profile of v6, /device:TPU:6, one launch (start us, length us, event | category | flops | bytes accessed | tf_op | source)
XLA Modules:
  0.0 87.5 jit_solution(3708824138434163049)
XLA Ops:
  0.6 1.7 %shard_map.102 = (bf16[256,128]{1,0:T(8,128)(2,1)S(1)}, s32[8,384]{1,0:T(8,128)S(1)}, s32[8,128]{1,0:T(8,128)S(1)}, bf16[384,256]{1,0:T(8,128)(2,1)S(1)}, bf16[3...) custom-call(s32[384]{0:T(512)} %ids_hbm.1, s32[384]{0:T(512)} %slot_hbm.1, bf16[384,256]{1,0:T(8,128)(2,1)} %q_hbm.1, ...), custom_call_target="tpu_custom_call" | custom-call | tf_op jit(solution)/shard_map/pallas_call | solution.py:67
  2.4 1.9 %collective-permute-start = (bf16[256,128]{1,0:T(8,128)(2,1)S(1)}, bf16[256,128]{1,0:T(8,128)(2,1)S(1)}, u32[]{:S(2)}, u32[]{:S(2)}) collective-permute-start(bf16[256,128]{1,0:T(8,128)(2,1)S(1)} %get-tuple-element.33), channel_id=1, source_target_pairs={{0,16},{16,32},{32,48},{48,64},{64,80},{80,96},{96,112},{112,128},... | collective-permute-start | bytes 196616 | tf_op jit(solution)/shard_map/ppermute | solution.py:230
  4.3 0.0 copy-start
  4.3 2.9 %shard_map.103 = (bf16[256,384]{1,0:T(8,128)(2,1)S(1)}, bf16[512,6144]{1,0:T(8,128)(2,1)S(1)}) custom-call(s32[8,384]{1,0:T(8,128)S(1)} %get-tuple-element.25.same_ref, s32[8,128]{1,0:T(8,128)S(1)} %get-tuple-element.26.stays_ref, bf16[384,256]{1,0:T(8,128)(2,1)S(1)} %get-tuple-element.27.q_ref, bf16[384,256]{1,0:T(8,128)(2,1)S(1)} %get-tuple-element.28.k_ref, ...), custom_call_target="tpu_custom_call" | custom-call | tf_op jit(solution)/shard_map/pallas_call | solution.py:97
  7.3 0.7 copy-done
  8.0 1.8 %shard_map.104.g_ref = bf16[512,256]{1,0:T(8,128)(2,1)S(1)} custom-call(bf16[512,6144]{1,0:T(8,128)(2,1)S(1)} %get-tuple-element.30.g_ref, bf16[256,6144]{1,0:T(8,128)(2,1)S(1)} %copy-done), custom_call_target="tpu_custom_call" | custom-call | tf_op jit(solution)/shard_map/pallas_call | solution.py:150
  9.9 11.6 %collective-permute-done.came_ref = bf16[256,128]{1,0:T(8,128)(2,1)S(1)} collective-permute-done((bf16[256,128]{1,0:T(8,128)(2,1)S(1)}, bf16[256,128]{1,0:T(8,128)(2,1)S(1)}, u32[]{:S(2)}, u32[]{:S(2)}) %collective-permute-start) | collective-permute-done | bytes 65568 | tf_op jit(solution)/shard_map/ppermute | solution.py:230
  21.5 0.8 shard_map.105
  22.2 1.9 %collective-permute-start.1 = (bf16[3072,128]{1,0:T(8,128)(2,1)S(1)}, bf16[3072,128]{1,0:T(8,128)(2,1)S(1)}, u32[]{:S(2)}, u32[]{:S(2)}) collective-permute-start(bf16[3072,128]{1,0:T(8,128)(2,1)S(1)} %shard_map.105), channel_id=1, source_target_pairs={{0,16},{16,0},{32,48},{48,32},{64,80},{80,64},{96,112},{112,96},{1... | collective-permute-start | bytes 2359304 | tf_op jit(solution)/shard_map/ppermute | solution.py:199
  24.2 6.0 %collective-permute-start.2 = (bf16[128,256]{1,0:T(8,128)(2,1)S(1)}, bf16[128,256]{1,0:T(8,128)(2,1)S(1)}, u32[]{:S(2)}, u32[]{:S(2)}) collective-permute-start(bf16[128,256]{1,0:T(8,128)(2,1)S(1)} %slice.36), channel_id=1, source_target_pairs={{16,0},{32,16},{48,32},{64,48},{80,64},{96,80},{112,96},{128,112},... | collective-permute-start | bytes 196616 | tf_op jit(solution)/shard_map/ppermute | solution.py:234
  30.2 0.8 shard_map.107
  31.0 1.1 %collective-permute-done.2.back_ref = bf16[128,256]{1,0:T(8,128)(2,1)S(1)} collective-permute-done((bf16[128,256]{1,0:T(8,128)(2,1)S(1)}, bf16[128,256]{1,0:T(8,128)(2,1)S(1)}, u32[]{:S(2)}, u32[]{:S(2)}) %collective-permute-start.2) | collective-permute-done | bytes 65568 | tf_op jit(solution)/shard_map/ppermute | solution.py:234
  32.1 0.0 collective-permute-done.1
  32.1 0.2 add_convert_fusion
  32.3 1.9 %collective-permute-start.4 = (bf16[3072,128]{1,0:T(8,128)(2,1)S(1)}, bf16[3072,128]{1,0:T(8,128)(2,1)S(1)}, u32[]{:S(2)}, u32[]{:S(2)}) collective-permute-start(bf16[3072,128]{1,0:T(8,128)(2,1)S(1)} %add_convert_fusion), channel_id=1, source_target_pairs={{0,32},{16,240},{32,0},{48,80},{64,96},{80,48},{96,64},{112,144},{... | collective-permute-start | bytes 2359304 | tf_op jit(solution)/shard_map/ppermute | solution.py:199
  34.2 0.8 shard_map.109
  35.0 5.5 %collective-permute-start.3 = (bf16[3072,128]{1,0:T(8,128)(2,1)S(1)}, bf16[3072,128]{1,0:T(8,128)(2,1)S(1)}, u32[]{:S(2)}, u32[]{:S(2)}) collective-permute-start(bf16[3072,128]{1,0:T(8,128)(2,1)S(1)} %shard_map.109), channel_id=1, source_target_pairs={{0,16},{16,0},{32,48},{48,32},{64,80},{80,64},{96,112},{112,96},{1... | collective-permute-start | bytes 2359304 | tf_op jit(solution)/shard_map/ppermute | solution.py:199
  40.6 0.8 shard_map.108
  41.4 4.8 %collective-permute-done.4 = bf16[3072,128]{1,0:T(8,128)(2,1)S(1)} collective-permute-done((bf16[3072,128]{1,0:T(8,128)(2,1)S(1)}, bf16[3072,128]{1,0:T(8,128)(2,1)S(1)}, u32[]{:S(2)}, u32[]{:S(2)}) %collective-permute-start.4) | collective-permute-done | bytes 786464 | tf_op jit(solution)/shard_map/ppermute | solution.py:199
  46.2 0.0 collective-permute-done.3
  46.2 0.2 add_convert_fusion.1
  46.4 0.8 add_convert_fusion.2
  47.2 19.2 %all_to_all.10 = bf16[4,512,128]{2,1,0:T(8,128)(2,1)S(1)} all-to-all(bf16[4,512,128]{2,1,0:T(8,128)(2,1)S(1)} %bitcast.8), channel_id=1, replica_groups={{0,64,128,192},{16,80,144,208},{32,96,160,224},{48,112,176,240},{256,32..., dimensions={0} | all-to-all | bytes 1048576 | tf_op jit(solution)/shard_map/all_to_all | solution.py:248
  66.4 0.1 fusion
  66.5 3.9 %all-to-all-start.1 = ((bf16[4,256,128]{2,1,0:T(8,128)(2,1)}), bf16[4,256,128]{2,1,0:T(8,128)(2,1)S(1)}, u32[]{:S(2)}, u32[]{:S(2)}) async-start(bf16[4,256,128]{2,1,0:T(8,128)(2,1)} %bitcast.1), calls=%async_computation.1 | async-start | bytes 524288 | tf_op jit(solution)/shard_map/all_to_all | solution.py:250
  70.4 6.2 %collective-permute-start.6 = (bf16[256,128]{1,0:T(8,128)(2,1)S(1)}, bf16[256,128]{1,0:T(8,128)(2,1)S(1)}, u32[]{:S(2)}, u32[]{:S(2)}) collective-permute-start(bf16[256,128]{1,0:T(8,128)(2,1)S(1)} %get-tuple-element.47), channel_id=1, source_target_pairs={{0,512},{16,528},{32,544},{48,560},{64,576},{80,592},{96,608},{112... | collective-permute-start | bytes 196616 | tf_op jit(solution)/shard_map/ppermute | solution.py:199
  76.6 3.6 %collective-permute-start.5 = (bf16[256,128]{1,0:T(8,128)(2,1)S(1)}, bf16[256,128]{1,0:T(8,128)(2,1)S(1)}, u32[]{:S(2)}, u32[]{:S(2)}) collective-permute-start(bf16[256,128]{1,0:T(8,128)(2,1)S(1)} %get-tuple-element.46), channel_id=1, source_target_pairs={{0,256},{16,272},{32,288},{48,304},{64,320},{80,336},{96,352},{112... | collective-permute-start | bytes 196616 | tf_op jit(solution)/shard_map/ppermute | solution.py:199
  80.1 3.8 %shard_map.106 = (bf16[384,256]{1,0:T(8,128)(2,1)}, bf16[384,256]{1,0:T(8,128)(2,1)}, bf16[384,256]{1,0:T(8,128)(2,1)}) custom-call(s32[8,384]{1,0:T(8,128)S(1)} %get-tuple-element.25.same_ref, s32[8,128]{1,0:T(8,128)S(1)} %get-tuple-element.26.stays_ref, bf16[384,256]{1,0:T(8,128)(2,1)S(1)} %get-tuple-element.27.q_ref, ...), custom_call_target="tpu_custom_call" | custom-call | tf_op jit(solution)/shard_map/pallas_call | solution.py:182
  83.9 0.0 collective-permute-done.6
  83.9 2.9 %collective-permute-done.5 = bf16[256,128]{1,0:T(8,128)(2,1)S(1)} collective-permute-done((bf16[256,128]{1,0:T(8,128)(2,1)S(1)}, bf16[256,128]{1,0:T(8,128)(2,1)S(1)}, u32[]{:S(2)}, u32[]{:S(2)}) %collective-permute-start.5) | collective-permute-done | bytes 65568 | tf_op jit(solution)/shard_map/ppermute | solution.py:199
  86.8 0.0 all-to-all-done.1
  86.8 0.7 fusion.1
  (2 shorter events, 0.0 us)
Async XLA Ops:
  2.4 19.1 %collective-permute-start = (bf16[256,128]{1,0:T(8,128)(2,1)S(1)}, bf16[256,128]{1,0:T(8,128)(2,1)S(1)}, u32[]{:S(2)}, u32[]{:S(2)}) collective-permute-start(bf16[256,128]{1,0:T(8,128)(2,1)S(1)} %get-tuple-element.33), channel_id=1, source_target_pairs={{0,16},{16,32},{32,48},{48,64},{64,80},{80,96},{96,112},{112,128},... | collective-permute-start | bytes 196616 | tf_op jit(solution)/shard_map/ppermute | solution.py:230
  4.3 3.7 %copy-start = (bf16[256,6144]{1,0:T(8,128)(2,1)S(1)}, bf16[256,6144]{1,0:T(8,128)(2,1)}, u32[]{:S(2)}) copy-start(bf16[256,6144]{1,0:T(8,128)(2,1)} %w_ref.1) | copy-start | bytes 9437188
  22.2 9.8 %collective-permute-start.1 = (bf16[3072,128]{1,0:T(8,128)(2,1)S(1)}, bf16[3072,128]{1,0:T(8,128)(2,1)S(1)}, u32[]{:S(2)}, u32[]{:S(2)}) collective-permute-start(bf16[3072,128]{1,0:T(8,128)(2,1)S(1)} %shard_map.105), channel_id=1, source_target_pairs={{0,16},{16,0},{32,48},{48,32},{64,80},{80,64},{96,112},{112,96},{1... | collective-permute-start | bytes 2359304 | tf_op jit(solution)/shard_map/ppermute | solution.py:199
  24.2 7.9 %collective-permute-start.2 = (bf16[128,256]{1,0:T(8,128)(2,1)S(1)}, bf16[128,256]{1,0:T(8,128)(2,1)S(1)}, u32[]{:S(2)}, u32[]{:S(2)}) collective-permute-start(bf16[128,256]{1,0:T(8,128)(2,1)S(1)} %slice.36), channel_id=1, source_target_pairs={{16,0},{32,16},{48,32},{64,48},{80,64},{96,80},{112,96},{128,112},... | collective-permute-start | bytes 196616 | tf_op jit(solution)/shard_map/ppermute | solution.py:234
  32.3 13.9 %collective-permute-start.4 = (bf16[3072,128]{1,0:T(8,128)(2,1)S(1)}, bf16[3072,128]{1,0:T(8,128)(2,1)S(1)}, u32[]{:S(2)}, u32[]{:S(2)}) collective-permute-start(bf16[3072,128]{1,0:T(8,128)(2,1)S(1)} %add_convert_fusion), channel_id=1, source_target_pairs={{0,32},{16,240},{32,0},{48,80},{64,96},{80,48},{96,64},{112,144},{... | collective-permute-start | bytes 2359304 | tf_op jit(solution)/shard_map/ppermute | solution.py:199
  35.0 11.1 %collective-permute-start.3 = (bf16[3072,128]{1,0:T(8,128)(2,1)S(1)}, bf16[3072,128]{1,0:T(8,128)(2,1)S(1)}, u32[]{:S(2)}, u32[]{:S(2)}) collective-permute-start(bf16[3072,128]{1,0:T(8,128)(2,1)S(1)} %shard_map.109), channel_id=1, source_target_pairs={{0,16},{16,0},{32,48},{48,32},{64,80},{80,64},{96,112},{112,96},{1... | collective-permute-start | bytes 2359304 | tf_op jit(solution)/shard_map/ppermute | solution.py:199
  66.5 20.4 %all-to-all-start.1 = ((bf16[4,256,128]{2,1,0:T(8,128)(2,1)}), bf16[4,256,128]{2,1,0:T(8,128)(2,1)S(1)}, u32[]{:S(2)}, u32[]{:S(2)}) async-start(bf16[4,256,128]{2,1,0:T(8,128)(2,1)} %bitcast.1), calls=%async_computation.1 | async-start | bytes 524288 | tf_op jit(solution)/shard_map/all_to_all | solution.py:250
  70.4 13.5 %collective-permute-start.6 = (bf16[256,128]{1,0:T(8,128)(2,1)S(1)}, bf16[256,128]{1,0:T(8,128)(2,1)S(1)}, u32[]{:S(2)}, u32[]{:S(2)}) collective-permute-start(bf16[256,128]{1,0:T(8,128)(2,1)S(1)} %get-tuple-element.47), channel_id=1, source_target_pairs={{0,512},{16,528},{32,544},{48,560},{64,576},{80,592},{96,608},{112... | collective-permute-start | bytes 196616 | tf_op jit(solution)/shard_map/ppermute | solution.py:199
  76.6 10.3 %collective-permute-start.5 = (bf16[256,128]{1,0:T(8,128)(2,1)S(1)}, bf16[256,128]{1,0:T(8,128)(2,1)S(1)}, u32[]{:S(2)}, u32[]{:S(2)}) collective-permute-start(bf16[256,128]{1,0:T(8,128)(2,1)S(1)} %get-tuple-element.46), channel_id=1, source_target_pairs={{0,256},{16,272},{32,288},{48,304},{64,320},{80,336},{96,352},{112... | collective-permute-start | bytes 196616 | tf_op jit(solution)/shard_map/ppermute | solution.py:199

commit v7 on v5

--- a/solution.py
+++ b/solution.py
@@ -113,11 +113,12 @@
     y, c = (me // NC) % NY, me % NC
     core = 1 - c if other else c
     odd = (y + crossing) % 2
+    places = [(i, j * 2 + odd) for j in range(NY // 2) for i in range(NZ)]
     ctx_t = jnp.concatenate([stay_ref[...], came_ref[...]], axis=1)
     width = ctx_t.shape[0]
     group = 4
-    for n in range(0, NY * NZ // 2, group):
-        dest = [(i * 2 + odd) * NC + core for i in range(n, n + group)]
+    for n in range(0, len(places), group):
+        dest = [(z_to * NY + y_to) * NC + core for z_to, y_to in places[n : n + group]]
         g = jnp.concatenate([g_ref[:, pl.ds(pl.multiple_of(d * UNIT, UNIT), UNIT)] for d in dest], axis=1)
         part = dot(ctx_t, g, ((1,), (0,))).astype(jnp.bfloat16)
         for i in range(group):
@@ -202,7 +203,11 @@
 
 
 def same_parity():
-    return [[index(z, y, c) for z in range(NZ) for y in range(odd, NY, 2)] for odd in range(2) for c in range(NC)]
+    return [[index(z, y, c) for y in range(odd, NY, 2)] for z in range(NZ) for odd in range(2) for c in range(NC)]
+
+
+def same_place():
+    return [[index(z, y, c) for z in range(NZ)] for y in range(NY) for c in range(NC)]
 
 
 def sibling(z, y, c):
@@ -223,6 +228,7 @@
     leave, same, stays, q, k, v = leaving_context(image_ids, send_slot, queries, key_rows, value_rows)
     came = lax.ppermute(leave, "dp", [(i, (i + 1) % ranks) for i in range(ranks)])
     stay, g_near = staying_context(same, stays, q, k, v, grad_out)
+    grad_ctx = grad_context(g_near, out_weight)
 
     got = send(partial_grad(True, True, stay, came, g_near), sibling)
     own = partial_grad(True, False, stay, came, g_near)
@@ -231,14 +237,15 @@
 
     got = send(partial_grad(False, True, stay, came, g_near), sibling)
     own = partial_grad(False, False, stay, came, g_near)
-    grad_ctx = grad_context(g_near, out_weight)
-    sums = rounded_total(own, got, met).reshape(-1, width, UNIT)
-    sums, grad_ctx = lax.optimization_barrier((sums, grad_ctx))
+    sums = rounded_total(own, got, met).reshape(NY // 2, -1, UNIT)
+    sums, tail = lax.optimization_barrier((sums, grad_ctx[row_count:]))
     sums = lax.all_to_all(sums, "dp", 0, 0, axis_index_groups=same_parity())
-
-    back = lax.ppermute(grad_ctx[row_count:], "dp", [((i + 1) % ranks, i) for i in range(ranks)])
+    back = lax.ppermute(tail, "dp", [((i + 1) % ranks, i) for i in range(ranks)])
+    sums, back = lax.optimization_barrier((sums, back))
     grads = backward(same, stays, q, k, v, grad_ctx, back)
-    grad_weight = jnp.sum(sums.astype(jnp.float32), axis=0)
+    sums = rounded_total(*sums).reshape(NZ, -1, UNIT)
+    sums = lax.all_to_all(sums, "dp", 0, 0, axis_index_groups=same_place())
+    grad_weight = total(*sums)
     return (*grads, grad_weight)
 
 

time: 88.6 us -> 86.8 us (0.980)
  waiting for transfers between devices: 45.6 us -> 40 us
  starting transfers between devices: 26 us -> 29.6 us
    ppermute x1, waiting for transfers between devices: 19.7 us -> 1.88 us  [local(): lax.ppermute(tail, 'dp', [((i + 1) % ranks, i) for i in range(ranks)])]
    all_to_all x0 -> x1, starting transfers between devices: none -> 8.32 us  [local(): sums = lax.all_to_all(sums, 'dp', 0, 0, axis_index_groups=same_place())]
    all_to_all x1, waiting for transfers between devices: 3.64 us -> 9.9 us  [local(): sums = lax.all_to_all(sums, 'dp', 0, 0, axis_index_groups=same_parity())]
    all_to_all x0 -> x1, waiting for transfers between devices: none -> 6.05 us  [local(): sums = lax.all_to_all(sums, 'dp', 0, 0, axis_index_groups=same_place())]
    all_to_all x1, starting transfers between devices: 8.36 us -> 3.49 us  [local(): sums = lax.all_to_all(sums, 'dp', 0, 0, axis_index_groups=same_parity())]
  transfers between devices with their start and end apart: 6 -> 7, of which waited for: 5 -> 6; matrix products, arithmetic and copies ran while one was open for 0% -> 0% of each run, Pallas kernels for 12% -> 12%
where the time goes in v7:
time: 86.8 us; the launch traced here: 86.4 us
  waiting for transfers between devices  40 us (46%)
  starting transfers between devices  29.6 us (34%)
  Pallas kernels  13.2 us (15%)
  other arithmetic  2.86 us (3%)
    ppermute x1, waiting for transfers between devices, local(): lax.ppermute(leave, 'dp', [(i, (i + 1) % ranks) for i in range(ranks)])  14.3 us
    all_to_all x1, waiting for transfers between devices, local(): sums = lax.all_to_all(sums, 'dp', 0, 0, axis_index_groups=same_parity())  9.9 us
    ppermute x1, starting transfers between devices, local(): lax.ppermute(tail, 'dp', [((i + 1) % ranks, i) for i in range(ranks)])  9.82 us
    all_to_all x1, starting transfers between devices, local(): sums = lax.all_to_all(sums, 'dp', 0, 0, axis_index_groups=same_place())  8.32 us
    ppermute x3, waiting for transfers between devices, send(): lax.ppermute(block, 'dp', [(index(*p), index(*to(*p))) for p in PLACES])  7.82 us
    all_to_all x1, waiting for transfers between devices, local(): sums = lax.all_to_all(sums, 'dp', 0, 0, axis_index_groups=same_place())  6.05 us
    ppermute x3, starting transfers between devices, send(): lax.ppermute(block, 'dp', [(index(*p), index(*to(*p))) for p in PLACES])  6.02 us
    pallas_call x1, Pallas kernels, backward(): pl.pallas_call(backward_kernel, in_specs=[VMEM] * 7, out_specs=[VMEM] * 3...  3.75 us
  transfers between devices with their start and end apart: 7, of which 6 were waited for; matrix products, arithmetic and copies ran while one was open for 0% of the time, Pallas kernels for 12%

profile of v7, /device:TPU:6, one launch (start us, length us, event | category | flops | bytes accessed | tf_op | source)
XLA Modules:
  0.0 86.4 jit_solution(1548391526377297881)
XLA Ops:
  0.6 1.7 %shard_map.102 = (bf16[256,128]{1,0:T(8,128)(2,1)S(1)}, s32[8,384]{1,0:T(8,128)S(1)}, s32[8,128]{1,0:T(8,128)S(1)}, bf16[384,256]{1,0:T(8,128)(2,1)S(1)}, bf16[3...) custom-call(s32[384]{0:T(512)} %ids_hbm.1, s32[384]{0:T(512)} %slot_hbm.1, bf16[384,256]{1,0:T(8,128)(2,1)} %q_hbm.1, ...), custom_call_target="tpu_custom_call" | custom-call | tf_op jit(solution)/shard_map/pallas_call | solution.py:67
  2.4 1.9 %collective-permute-start = (bf16[256,128]{1,0:T(8,128)(2,1)S(1)}, bf16[256,128]{1,0:T(8,128)(2,1)S(1)}, u32[]{:S(2)}, u32[]{:S(2)}) collective-permute-start(bf16[256,128]{1,0:T(8,128)(2,1)S(1)} %get-tuple-element.28), channel_id=1, source_target_pairs={{0,16},{16,32},{32,48},{48,64},{64,80},{80,96},{96,112},{112,128},... | collective-permute-start | bytes 196616 | tf_op jit(solution)/shard_map/ppermute | solution.py:229
  4.3 2.8 %shard_map.103 = (bf16[256,384]{1,0:T(8,128)(2,1)S(1)}, bf16[512,6144]{1,0:T(8,128)(2,1)S(1)}) custom-call(s32[8,384]{1,0:T(8,128)S(1)} %get-tuple-element.21.same_ref, s32[8,128]{1,0:T(8,128)S(1)} %get-tuple-element.22.stays_ref, bf16[384,256]{1,0:T(8,128)(2,1)S(1)} %get-tuple-element.23.q_ref, bf16[384,256]{1,0:T(8,128)(2,1)S(1)} %get-tuple-element.24.k_ref, ...), custom_call_target="tpu_custom_call" | custom-call | tf_op jit(solution)/shard_map/pallas_call | solution.py:97
  7.1 14.3 %collective-permute-done.came_ref = bf16[256,128]{1,0:T(8,128)(2,1)S(1)} collective-permute-done((bf16[256,128]{1,0:T(8,128)(2,1)S(1)}, bf16[256,128]{1,0:T(8,128)(2,1)S(1)}, u32[]{:S(2)}, u32[]{:S(2)}) %collective-permute-start) | collective-permute-done | bytes 65568 | tf_op jit(solution)/shard_map/ppermute | solution.py:229
  21.5 0.8 shard_map.106
  22.2 1.9 %collective-permute-start.1 = (bf16[3072,128]{1,0:T(8,128)(2,1)S(1)}, bf16[3072,128]{1,0:T(8,128)(2,1)S(1)}, u32[]{:S(2)}, u32[]{:S(2)}) collective-permute-start(bf16[3072,128]{1,0:T(8,128)(2,1)S(1)} %shard_map.106), channel_id=1, source_target_pairs={{0,16},{16,0},{32,48},{48,32},{64,80},{80,64},{96,112},{112,96},{1... | collective-permute-start | bytes 2359304 | tf_op jit(solution)/shard_map/ppermute | solution.py:198
  24.1 0.8 shard_map.105
  24.9 1.5 %collective-permute-done.1 = bf16[3072,128]{1,0:T(8,128)(2,1)S(1)} collective-permute-done((bf16[3072,128]{1,0:T(8,128)(2,1)S(1)}, bf16[3072,128]{1,0:T(8,128)(2,1)S(1)}, u32[]{:S(2)}, u32[]{:S(2)}) %collective-permute-start.1) | collective-permute-done | bytes 786464 | tf_op jit(solution)/shard_map/ppermute | solution.py:198
  26.4 0.2 add_convert_fusion.1
  26.6 1.9 %collective-permute-start.3 = (bf16[3072,128]{1,0:T(8,128)(2,1)S(1)}, bf16[3072,128]{1,0:T(8,128)(2,1)S(1)}, u32[]{:S(2)}, u32[]{:S(2)}) collective-permute-start(bf16[3072,128]{1,0:T(8,128)(2,1)S(1)} %add_convert_fusion.1), channel_id=1, source_target_pairs={{0,32},{16,240},{32,0},{48,80},{64,96},{80,48},{96,64},{112,144},{... | collective-permute-start | bytes 2359304 | tf_op jit(solution)/shard_map/ppermute | solution.py:198
  28.5 0.0 copy-start
  28.5 0.8 shard_map.108
  29.3 2.2 %collective-permute-start.2 = (bf16[3072,128]{1,0:T(8,128)(2,1)S(1)}, bf16[3072,128]{1,0:T(8,128)(2,1)S(1)}, u32[]{:S(2)}, u32[]{:S(2)}) collective-permute-start(bf16[3072,128]{1,0:T(8,128)(2,1)S(1)} %shard_map.108), channel_id=1, source_target_pairs={{0,16},{16,0},{32,48},{48,32},{64,80},{80,64},{96,112},{112,96},{1... | collective-permute-start | bytes 2359304 | tf_op jit(solution)/shard_map/ppermute | solution.py:198
  31.5 0.0 copy-done
  31.5 1.8 %shard_map.104.g_ref = bf16[512,256]{1,0:T(8,128)(2,1)S(1)} custom-call(bf16[512,6144]{1,0:T(8,128)(2,1)S(1)} %get-tuple-element.26.g_ref, bf16[256,6144]{1,0:T(8,128)(2,1)S(1)} %copy-done), custom_call_target="tpu_custom_call" | custom-call | tf_op jit(solution)/shard_map/pallas_call | solution.py:149
  33.4 0.8 shard_map.107
  34.1 6.3 %collective-permute-done.3 = bf16[3072,128]{1,0:T(8,128)(2,1)S(1)} collective-permute-done((bf16[3072,128]{1,0:T(8,128)(2,1)S(1)}, bf16[3072,128]{1,0:T(8,128)(2,1)S(1)}, u32[]{:S(2)}, u32[]{:S(2)}) %collective-permute-start.3) | collective-permute-done | bytes 786464 | tf_op jit(solution)/shard_map/ppermute | solution.py:198
  40.5 0.0 collective-permute-done.2
  40.5 1.2 %add_convert_fusion = bf16[3072,128]{1,0:T(8,128)(2,1)} fusion(bf16[3072,128]{1,0:T(8,128)(2,1)S(1)} %collective-permute-done.3, bf16[3072,128]{1,0:T(8,128)(2,1)S(1)} %collective-permute-done.2, bf16[3072,128]{1,0:T(8,128)(2,1)S(1)} %shard_map.107), kind=kLoop, calls=%fused_computation | loop fusion | flops 2359296 | bytes 3145728 | tf_op jit(solution)/shard_map/convert_element_type | solution.py:222
  41.7 3.5 %all-to-all-start = ((bf16[4,768,128]{2,1,0:T(8,128)(2,1)}), bf16[4,768,128]{2,1,0:T(8,128)(2,1)S(1)}, u32[]{:S(2)}, u32[]{:S(2)}) async-start(bf16[4,768,128]{2,1,0:T(8,128)(2,1)} %bitcast), calls=%async_computation | async-start | bytes 1572864 | tf_op jit(solution)/shard_map/all_to_all | solution.py:242
  45.2 9.8 %collective-permute-start.4 = (bf16[128,256]{1,0:T(8,128)(2,1)S(1)}, bf16[128,256]{1,0:T(8,128)(2,1)S(1)}, u32[]{:S(2)}, u32[]{:S(2)}) collective-permute-start(bf16[128,256]{1,0:T(8,128)(2,1)S(1)} %slice.4), channel_id=1, source_target_pairs={{16,0},{32,16},{48,32},{64,48},{80,64},{96,80},{112,96},{128,112},... | collective-permute-start | bytes 196616 | tf_op jit(solution)/shard_map/ppermute | solution.py:243
  55.0 1.9 %collective-permute-done.4.back_ref = bf16[128,256]{1,0:T(8,128)(2,1)S(1)} collective-permute-done((bf16[128,256]{1,0:T(8,128)(2,1)S(1)}, bf16[128,256]{1,0:T(8,128)(2,1)S(1)}, u32[]{:S(2)}, u32[]{:S(2)}) %collective-permute-start.4) | collective-permute-done | bytes 65568 | tf_op jit(solution)/shard_map/ppermute | solution.py:243
  56.9 9.9 %all-to-all-done = bf16[4,768,128]{2,1,0:T(8,128)(2,1)S(1)} async-done(((bf16[4,768,128]{2,1,0:T(8,128)(2,1)}), bf16[4,768,128]{2,1,0:T(8,128)(2,1)S(1)}, u32[]{:S(2)}, u32[]{:S(2)}) %all-to-all-start) | async-done | bytes 786464 | tf_op jit(solution)/shard_map/all_to_all | solution.py:242
  66.8 0.8 add_convert_fusion.2
  67.6 8.3 %all-to-all-start.1 = ((bf16[3,256,128]{2,1,0:T(8,128)(2,1)}), bf16[3,256,128]{2,1,0:T(8,128)(2,1)S(1)}, u32[]{:S(2)}, u32[]{:S(2)}) async-start(bf16[3,256,128]{2,1,0:T(8,128)(2,1)} %bitcast.1), calls=%async_computation.1 | async-start | bytes 393216 | tf_op jit(solution)/shard_map/all_to_all | solution.py:247
  75.9 3.8 %shard_map.109 = (bf16[384,256]{1,0:T(8,128)(2,1)}, bf16[384,256]{1,0:T(8,128)(2,1)}, bf16[384,256]{1,0:T(8,128)(2,1)}) custom-call(s32[8,384]{1,0:T(8,128)S(1)} %get-tuple-element.21.same_ref, s32[8,128]{1,0:T(8,128)S(1)} %get-tuple-element.22.stays_ref, bf16[384,256]{1,0:T(8,128)(2,1)S(1)} %get-tuple-element.23.q_ref, ...), custom_call_target="tpu_custom_call" | custom-call | tf_op jit(solution)/shard_map/pallas_call | solution.py:181
  79.7 6.1 %all-to-all-done.1 = bf16[3,256,128]{2,1,0:T(8,128)(2,1)S(1)} async-done(((bf16[3,256,128]{2,1,0:T(8,128)(2,1)}), bf16[3,256,128]{2,1,0:T(8,128)(2,1)S(1)}, u32[]{:S(2)}, u32[]{:S(2)}) %all-to-all-start.1) | async-done | bytes 196640 | tf_op jit(solution)/shard_map/all_to_all | solution.py:247
  85.7 0.7 add_bitcast_fusion
  (1 shorter events, 0.0 us)
Async XLA Ops:
  2.4 19.1 %collective-permute-start = (bf16[256,128]{1,0:T(8,128)(2,1)S(1)}, bf16[256,128]{1,0:T(8,128)(2,1)S(1)}, u32[]{:S(2)}, u32[]{:S(2)}) collective-permute-start(bf16[256,128]{1,0:T(8,128)(2,1)S(1)} %get-tuple-element.28), channel_id=1, source_target_pairs={{0,16},{16,32},{32,48},{48,64},{64,80},{80,96},{96,112},{112,128},... | collective-permute-start | bytes 196616 | tf_op jit(solution)/shard_map/ppermute | solution.py:229
  22.2 4.2 %collective-permute-start.1 = (bf16[3072,128]{1,0:T(8,128)(2,1)S(1)}, bf16[3072,128]{1,0:T(8,128)(2,1)S(1)}, u32[]{:S(2)}, u32[]{:S(2)}) collective-permute-start(bf16[3072,128]{1,0:T(8,128)(2,1)S(1)} %shard_map.106), channel_id=1, source_target_pairs={{0,16},{16,0},{32,48},{48,32},{64,80},{80,64},{96,112},{112,96},{1... | collective-permute-start | bytes 2359304 | tf_op jit(solution)/shard_map/ppermute | solution.py:198
  26.6 13.9 %collective-permute-start.3 = (bf16[3072,128]{1,0:T(8,128)(2,1)S(1)}, bf16[3072,128]{1,0:T(8,128)(2,1)S(1)}, u32[]{:S(2)}, u32[]{:S(2)}) collective-permute-start(bf16[3072,128]{1,0:T(8,128)(2,1)S(1)} %add_convert_fusion.1), channel_id=1, source_target_pairs={{0,32},{16,240},{32,0},{48,80},{64,96},{80,48},{96,64},{112,144},{... | collective-permute-start | bytes 2359304 | tf_op jit(solution)/shard_map/ppermute | solution.py:198
  28.5 3.0 %copy-start = (bf16[256,6144]{1,0:T(8,128)(2,1)S(1)}, bf16[256,6144]{1,0:T(8,128)(2,1)}, u32[]{:S(2)}) copy-start(bf16[256,6144]{1,0:T(8,128)(2,1)} %w_ref.1) | copy-start | bytes 9437188
  29.3 11.2 %collective-permute-start.2 = (bf16[3072,128]{1,0:T(8,128)(2,1)S(1)}, bf16[3072,128]{1,0:T(8,128)(2,1)S(1)}, u32[]{:S(2)}, u32[]{:S(2)}) collective-permute-start(bf16[3072,128]{1,0:T(8,128)(2,1)S(1)} %shard_map.108), channel_id=1, source_target_pairs={{0,16},{16,0},{32,48},{48,32},{64,80},{80,64},{96,112},{112,96},{1... | collective-permute-start | bytes 2359304 | tf_op jit(solution)/shard_map/ppermute | solution.py:198
  41.7 25.1 %all-to-all-start = ((bf16[4,768,128]{2,1,0:T(8,128)(2,1)}), bf16[4,768,128]{2,1,0:T(8,128)(2,1)S(1)}, u32[]{:S(2)}, u32[]{:S(2)}) async-start(bf16[4,768,128]{2,1,0:T(8,128)(2,1)} %bitcast), calls=%async_computation | async-start | bytes 1572864 | tf_op jit(solution)/shard_map/all_to_all | solution.py:242
  45.2 11.7 %collective-permute-start.4 = (bf16[128,256]{1,0:T(8,128)(2,1)S(1)}, bf16[128,256]{1,0:T(8,128)(2,1)S(1)}, u32[]{:S(2)}, u32[]{:S(2)}) collective-permute-start(bf16[128,256]{1,0:T(8,128)(2,1)S(1)} %slice.4), channel_id=1, source_target_pairs={{16,0},{32,16},{48,32},{64,48},{80,64},{96,80},{112,96},{128,112},... | collective-permute-start | bytes 196616 | tf_op jit(solution)/shard_map/ppermute | solution.py:243
  67.6 18.1 %all-to-all-start.1 = ((bf16[3,256,128]{2,1,0:T(8,128)(2,1)}), bf16[3,256,128]{2,1,0:T(8,128)(2,1)S(1)}, u32[]{:S(2)}, u32[]{:S(2)}) async-start(bf16[3,256,128]{2,1,0:T(8,128)(2,1)} %bitcast.1), calls=%async_computation.1 | async-start | bytes 393216 | tf_op jit(solution)/shard_map/all_to_all | solution.py:247

commit v8 on v7

--- a/solution.py
+++ b/solution.py
@@ -10,8 +10,9 @@
 HD = 128
 UNIT = 128
 NZ, NY, NC = 3, 8, 2
+ORDER = (4, 3, 5, 2, 6, 1, 7, 0)
 VMEM = pl.BlockSpec(memory_space=pltpu.VMEM)
-PARAMS = pltpu.CompilerParams(vmem_limit_bytes=16 * 1024 * 1024)
+PARAMS = pltpu.CompilerParams(vmem_limit_bytes=8 * 1024 * 1024)
 
 
 def dot(a, b, dims):
@@ -108,27 +109,24 @@
     return pltpu.with_memory_space_constraint(x, pltpu.HBM)
 
 
-def partial_kernel(crossing, other, stay_ref, came_ref, g_ref, out_ref):
+def partial_kernel(other, stay_ref, came_ref, g_ref, out_ref):
     me = lax.axis_index("dp")
     y, c = (me // NC) % NY, me % NC
     core = 1 - c if other else c
-    odd = (y + crossing) % 2
-    places = [(i, j * 2 + odd) for j in range(NY // 2) for i in range(NZ)]
     ctx_t = jnp.concatenate([stay_ref[...], came_ref[...]], axis=1)
     width = ctx_t.shape[0]
-    group = 4
-    for n in range(0, len(places), group):
-        dest = [(z_to * NY + y_to) * NC + core for z_to, y_to in places[n : n + group]]
+    for n, distance in enumerate(ORDER):
+        dest = [(i * NY + (y + distance) % NY) * NC + core for i in range(NZ)]
         g = jnp.concatenate([g_ref[:, pl.ds(pl.multiple_of(d * UNIT, UNIT), UNIT)] for d in dest], axis=1)
         part = dot(ctx_t, g, ((1,), (0,))).astype(jnp.bfloat16)
-        for i in range(group):
-            out_ref[pl.ds((n + i) * width, width), :] = part[:, i * UNIT : (i + 1) * UNIT]
-
-
-def partial_grad(crossing, other, stay, came, grad_out):
-    shape = (NY * NZ // 2 * stay.shape[0], UNIT)
-    return pl.pallas_call(
-        functools.partial(partial_kernel, crossing, other),
+        for i in range(NZ):
+            out_ref[pl.ds((n * NZ + i) * width, width), :] = part[:, i * UNIT : (i + 1) * UNIT]
+
+
+def partial_grad(other, stay, came, grad_out):
+    shape = (NY * NZ * stay.shape[0], UNIT)
+    return pl.pallas_call(
+        functools.partial(partial_kernel, other),
         in_specs=[VMEM, VMEM, VMEM],
         out_specs=VMEM,
         out_shape=jax.ShapeDtypeStruct(shape, jnp.bfloat16),
@@ -198,12 +196,12 @@
     return lax.ppermute(block, "dp", [(index(*p), index(*to(*p))) for p in PLACES])
 
 
-def paired(z, y, c):
-    return (z, y + 1 - (y + c) % 2 * 2, c)
-
-
-def same_parity():
-    return [[index(z, y, c) for y in range(odd, NY, 2)] for z in range(NZ) for odd in range(2) for c in range(NC)]
+def along_y(step):
+    return lambda z, y, c: (z, y + step, c)
+
+
+def apart_y(step):
+    return lambda z, y, c: (z, y + step * (1 - 2 * c), c)
 
 
 def same_place():
@@ -229,22 +227,32 @@
     came = lax.ppermute(leave, "dp", [(i, (i + 1) % ranks) for i in range(ranks)])
     stay, g_near = staying_context(same, stays, q, k, v, grad_out)
     grad_ctx = grad_context(g_near, out_weight)
-
-    got = send(partial_grad(True, True, stay, came, g_near), sibling)
-    own = partial_grad(True, False, stay, came, g_near)
-    first, stay = lax.optimization_barrier((rounded_total(own, got), stay))
-    met = send(first, paired)
-
-    got = send(partial_grad(False, True, stay, came, g_near), sibling)
-    own = partial_grad(False, False, stay, came, g_near)
-    sums = rounded_total(own, got, met).reshape(NY // 2, -1, UNIT)
+    stay, grad_ctx = lax.optimization_barrier((stay, grad_ctx))
+
+    size = NZ * width
+
+    def cut(x):
+        return [x[i : i + size] for i in range(0, x.shape[0], size)]
+
+    got = send(partial_grad(True, stay, came, g_near), sibling)
+    own = partial_grad(False, stay, came, g_near)
+    parts = [rounded_total(*pair) for pair in zip(cut(own), cut(got), strict=True)]
+    part = dict(zip(ORDER, lax.optimization_barrier(parts), strict=True))
+    far, up, down = send(part[4], apart_y(2)), send(part[3], along_y(1)), send(part[5], along_y(-1))
+
+    core = lax.axis_index("dp") % NC
+    none = jnp.zeros_like(far)
+    up = rounded_total(part[2], up, jnp.where(core == 0, far, none))
+    down = rounded_total(part[6], down, jnp.where(core == 1, far, none))
+    near = part[1], part[7]
+    up, down, *near = lax.optimization_barrier((up, down, *near))
+    up, down = send(up, along_y(2)), send(down, along_y(-2))
+    near = send(near[0], along_y(1)), send(near[1], along_y(-1))
+    sums = rounded_total(part[0], up, down, *near).reshape(NZ, -1, UNIT)
     sums, tail = lax.optimization_barrier((sums, grad_ctx[row_count:]))
-    sums = lax.all_to_all(sums, "dp", 0, 0, axis_index_groups=same_parity())
+    sums = lax.all_to_all(sums, "dp", 0, 0, axis_index_groups=same_place())
     back = lax.ppermute(tail, "dp", [((i + 1) % ranks, i) for i in range(ranks)])
-    sums, back = lax.optimization_barrier((sums, back))
-    grads = backward(same, stays, q, k, v, grad_ctx, back)
-    sums = rounded_total(*sums).reshape(NZ, -1, UNIT)
-    sums = lax.all_to_all(sums, "dp", 0, 0, axis_index_groups=same_place())
+    grads = backward(same, stays, queries, key_rows, value_rows, grad_ctx, back)
     grad_weight = total(*sums)
     return (*grads, grad_weight)
 

time: 86.8 us -> 92.9 us (1.070)
  the two profiles are of different devices: /device:TPU:6 before, /device:TPU:59 now
where the time goes in v8:
time: 92.9 us; the launch traced here: 92.4 us
  starting transfers between devices  43.9 us (47%)
  waiting for transfers between devices  31.8 us (34%)
  Pallas kernels  13 us (14%)
  other arithmetic  2.08 us (2%)
    ppermute x8, starting transfers between devices, send(): lax.ppermute(block, 'dp', [(index(*p), index(*to(*p))) for p in PLACES])  22.3 us
    ppermute x8, waiting for transfers between devices, send(): lax.ppermute(block, 'dp', [(index(*p), index(*to(*p))) for p in PLACES])  20.9 us
    ppermute x1, waiting for transfers between devices, local(): lax.ppermute(tail, 'dp', [((i + 1) % ranks, i) for i in range(ranks)])  10.8 us
    ppermute x1, starting transfers between devices, local(): lax.ppermute(leave, 'dp', [(i, (i + 1) % ranks) for i in range(ranks)])  10.4 us
    all_to_all x1, starting transfers between devices, local(): sums = lax.all_to_all(sums, 'dp', 0, 0, axis_index_groups=same_place())  8.65 us
    pallas_call x1, Pallas kernels, backward(): pl.pallas_call(backward_kernel, in_specs=[VMEM] * 7, out_specs=[VMEM] * 3...  3.76 us
    pallas_call x1, Pallas kernels, staying_context(): pl.pallas_call(context_kernel, in_specs=[VMEM] * 5 + [pl.BlockSpec(memory...  2.95 us
    pallas_call x2, Pallas kernels, partial_grad(): pl.pallas_call(functools.partial(partial_kernel, other), in_specs=[VMEM,...  2.79 us
  transfers between devices with their start and end apart: 11, of which 8 were waited for; matrix products, arithmetic and copies ran while one was open for 0% of the time, Pallas kernels for 11%

profile of v8, /device:TPU:59, one launch (start us, length us, event | category | flops | bytes accessed | tf_op | source)
XLA Modules:
  0.0 92.4 jit_solution(3681096545403976073)
XLA Ops:
  0.6 1.7 %shard_map.102 = (bf16[256,128]{1,0:T(8,128)(2,1)S(1)}, s32[8,384]{1,0:T(8,128)S(1)}, s32[8,128]{1,0:T(8,128)S(1)}, bf16[384,256]{1,0:T(8,128)(2,1)S(1)}, bf16[3...) custom-call(s32[384]{0:T(512)} %ids_hbm.1, s32[384]{0:T(512)} %slot_hbm.1, bf16[384,256]{1,0:T(8,128)(2,1)} %q_ref.1, ...), custom_call_target="tpu_custom_call" | custom-call | tf_op jit(solution)/shard_map/pallas_call | solution.py:68
  2.4 10.4 %collective-permute-start = (bf16[256,128]{1,0:T(8,128)(2,1)S(1)}, bf16[256,128]{1,0:T(8,128)(2,1)S(1)}, u32[]{:S(2)}, u32[]{:S(2)}) collective-permute-start(bf16[256,128]{1,0:T(8,128)(2,1)S(1)} %get-tuple-element.40), channel_id=1, source_target_pairs={{0,16},{16,32},{32,48},{48,64},{64,80},{80,96},{96,112},{112,128},... | collective-permute-start | bytes 196616 | tf_op jit(solution)/shard_map/ppermute | solution.py:227
  12.8 0.0 copy-start
  12.8 2.9 %shard_map.103 = (bf16[256,384]{1,0:T(8,128)(2,1)S(1)}, bf16[512,6144]{1,0:T(8,128)(2,1)S(1)}) custom-call(s32[8,384]{1,0:T(8,128)S(1)} %get-tuple-element.31.same_ref, s32[8,128]{1,0:T(8,128)S(1)} %get-tuple-element.32.stays_ref, bf16[384,256]{1,0:T(8,128)(2,1)S(1)} %get-tuple-element.33.q_ref, bf16[384,256]{1,0:T(8,128)(2,1)S(1)} %get-tuple-element.34.k_ref, ...), custom_call_target="tpu_custom_call" | custom-call | tf_op jit(solution)/shard_map/pallas_call | solution.py:98
  15.8 0.7 copy-done
  16.5 1.8 %shard_map.104.g_ref = bf16[512,256]{1,0:T(8,128)(2,1)S(1)} custom-call(bf16[512,6144]{1,0:T(8,128)(2,1)S(1)} %get-tuple-element.37.g_ref, bf16[256,6144]{1,0:T(8,128)(2,1)S(1)} %copy-done), custom_call_target="tpu_custom_call" | custom-call | tf_op jit(solution)/shard_map/pallas_call | solution.py:147
  18.3 0.0 collective-permute-done.came_ref
  18.3 1.4 %shard_map.106 = bf16[6144,128]{1,0:T(8,128)(2,1)S(1)} custom-call(bf16[256,384]{1,0:T(8,128)(2,1)S(1)} %get-tuple-element.39.stay_ref, bf16[256,128]{1,0:T(8,128)(2,1)S(1)} %collective-permute-done.came_ref, bf16[512,6144]{1,0:T(8,128)(2,1)S(1)} %get-tuple-element.37.g_ref), custom_call_target="tpu_custom_call" | custom-call | tf_op jit(solution)/shard_map/pallas_call | solution.py:128
  19.7 1.9 %collective-permute-start.1 = (bf16[6144,128]{1,0:T(8,128)(2,1)S(1)}, bf16[6144,128]{1,0:T(8,128)(2,1)S(1)}, u32[]{:S(2)}, u32[]{:S(2)}) collective-permute-start(bf16[6144,128]{1,0:T(8,128)(2,1)S(1)} %shard_map.106), channel_id=1, source_target_pairs={{0,16},{16,0},{32,48},{48,32},{64,80},{80,64},{96,112},{112,96},{1... | collective-permute-start | bytes 4718600 | tf_op jit(solution)/shard_map/ppermute | solution.py:196
  21.7 1.4 %shard_map.105 = bf16[6144,128]{1,0:T(8,128)(2,1)S(1)} custom-call(bf16[256,384]{1,0:T(8,128)(2,1)S(1)} %get-tuple-element.39.stay_ref, bf16[256,128]{1,0:T(8,128)(2,1)S(1)} %collective-permute-done.came_ref, bf16[512,6144]{1,0:T(8,128)(2,1)S(1)} %get-tuple-element.37.g_ref), custom_call_target="tpu_custom_call" | custom-call | tf_op jit(solution)/shard_map/pallas_call | solution.py:128
  23.1 2.0 %collective-permute-done.1 = bf16[6144,128]{1,0:T(8,128)(2,1)S(1)} collective-permute-done((bf16[6144,128]{1,0:T(8,128)(2,1)S(1)}, bf16[6144,128]{1,0:T(8,128)(2,1)S(1)}, u32[]{:S(2)}, u32[]{:S(2)}) %collective-permute-start.1) | collective-permute-done | bytes 1572896 | tf_op jit(solution)/shard_map/ppermute | solution.py:196
  25.0 0.4 add_convert_fusion.3
  25.4 0.0 copy-start.1
  25.5 0.0 copy-start.2
  25.5 0.0 copy-start.3
  25.5 4.9 %collective-permute-start.2 = (bf16[768,128]{1,0:T(8,128)(2,1)S(1)}, bf16[768,128]{1,0:T(8,128)(2,1)S(1)}, u32[]{:S(2)}, u32[]{:S(2)}) collective-permute-start(bf16[768,128]{1,0:T(8,128)(2,1)S(1)} %get-tuple-element.43), channel_id=1, source_target_pairs={{0,32},{16,48},{32,64},{48,80},{64,96},{80,112},{96,128},{112,144}... | collective-permute-start | bytes 589832 | tf_op jit(solution)/shard_map/ppermute | solution.py:196
  30.4 1.9 %collective-permute-start.3 = (bf16[768,128]{1,0:T(8,128)(2,1)S(1)}, bf16[768,128]{1,0:T(8,128)(2,1)S(1)}, u32[]{:S(2)}, u32[]{:S(2)}) collective-permute-start(bf16[768,128]{1,0:T(8,128)(2,1)S(1)} %get-tuple-element.44), channel_id=1, source_target_pairs={{0,64},{16,208},{32,96},{48,240},{64,128},{80,16},{96,160},{112,48... | collective-permute-start | bytes 589832 | tf_op jit(solution)/shard_map/ppermute | solution.py:196
  32.3 1.9 %collective-permute-start.4 = (bf16[768,128]{1,0:T(8,128)(2,1)S(1)}, bf16[768,128]{1,0:T(8,128)(2,1)S(1)}, u32[]{:S(2)}, u32[]{:S(2)}) collective-permute-start(bf16[768,128]{1,0:T(8,128)(2,1)S(1)} %get-tuple-element.46), channel_id=1, source_target_pairs={{0,224},{16,240},{32,0},{48,16},{64,32},{80,48},{96,64},{112,80},{... | collective-permute-start | bytes 589832 | tf_op jit(solution)/shard_map/ppermute | solution.py:196
  34.3 0.0 collective-permute-done.2
  34.3 7.3 %collective-permute-done.3 = bf16[768,128]{1,0:T(8,128)(2,1)S(1)} collective-permute-done((bf16[768,128]{1,0:T(8,128)(2,1)S(1)}, bf16[768,128]{1,0:T(8,128)(2,1)S(1)}, u32[]{:S(2)}, u32[]{:S(2)}) %collective-permute-start.3) | collective-permute-done | bytes 196640 | tf_op jit(solution)/shard_map/ppermute | solution.py:196
  41.6 2.0 %collective-permute-done.4 = bf16[768,128]{1,0:T(8,128)(2,1)S(1)} collective-permute-done((bf16[768,128]{1,0:T(8,128)(2,1)S(1)}, bf16[768,128]{1,0:T(8,128)(2,1)S(1)}, u32[]{:S(2)}, u32[]{:S(2)}) %collective-permute-start.4) | collective-permute-done | bytes 196640 | tf_op jit(solution)/shard_map/ppermute | solution.py:196
  43.7 0.2 add_convert_fusion.1
  43.8 1.9 %collective-permute-start.5 = (bf16[768,128]{1,0:T(8,128)(2,1)S(1)}, bf16[768,128]{1,0:T(8,128)(2,1)S(1)}, u32[]{:S(2)}, u32[]{:S(2)}) collective-permute-start(bf16[768,128]{1,0:T(8,128)(2,1)S(1)} %get-tuple-element.49), channel_id=1, source_target_pairs={{0,64},{16,80},{32,96},{48,112},{64,128},{80,144},{96,160},{112,17... | collective-permute-start | bytes 589832 | tf_op jit(solution)/shard_map/ppermute | solution.py:196
  45.8 4.3 %collective-permute-start.6 = (bf16[768,128]{1,0:T(8,128)(2,1)S(1)}, bf16[768,128]{1,0:T(8,128)(2,1)S(1)}, u32[]{:S(2)}, u32[]{:S(2)}) collective-permute-start(bf16[768,128]{1,0:T(8,128)(2,1)S(1)} %get-tuple-element.50), channel_id=1, source_target_pairs={{0,192},{16,208},{32,224},{48,240},{64,0},{80,16},{96,32},{112,48}... | collective-permute-start | bytes 589832 | tf_op jit(solution)/shard_map/ppermute | solution.py:196
  50.0 3.5 %collective-permute-start.7 = (bf16[768,128]{1,0:T(8,128)(2,1)S(1)}, bf16[768,128]{1,0:T(8,128)(2,1)S(1)}, u32[]{:S(2)}, u32[]{:S(2)}) collective-permute-start(bf16[768,128]{1,0:T(8,128)(2,1)S(1)} %get-tuple-element.51), channel_id=1, source_target_pairs={{0,32},{16,48},{32,64},{48,80},{64,96},{80,112},{96,128},{112,144}... | collective-permute-start | bytes 589832 | tf_op jit(solution)/shard_map/ppermute | solution.py:196
  53.5 1.9 %collective-permute-start.8 = (bf16[768,128]{1,0:T(8,128)(2,1)S(1)}, bf16[768,128]{1,0:T(8,128)(2,1)S(1)}, u32[]{:S(2)}, u32[]{:S(2)}) collective-permute-start(bf16[768,128]{1,0:T(8,128)(2,1)S(1)} %get-tuple-element.52), channel_id=1, source_target_pairs={{0,224},{16,240},{32,0},{48,16},{64,32},{80,48},{96,64},{112,80},{... | collective-permute-start | bytes 589832 | tf_op jit(solution)/shard_map/ppermute | solution.py:196
  55.5 1.4 %collective-permute-done.5 = bf16[768,128]{1,0:T(8,128)(2,1)S(1)} collective-permute-done((bf16[768,128]{1,0:T(8,128)(2,1)S(1)}, bf16[768,128]{1,0:T(8,128)(2,1)S(1)}, u32[]{:S(2)}, u32[]{:S(2)}) %collective-permute-start.5) | collective-permute-done | bytes 196640 | tf_op jit(solution)/shard_map/ppermute | solution.py:196
  56.8 3.3 %collective-permute-done.6 = bf16[768,128]{1,0:T(8,128)(2,1)S(1)} collective-permute-done((bf16[768,128]{1,0:T(8,128)(2,1)S(1)}, bf16[768,128]{1,0:T(8,128)(2,1)S(1)}, u32[]{:S(2)}, u32[]{:S(2)}) %collective-permute-start.6) | collective-permute-done | bytes 196640 | tf_op jit(solution)/shard_map/ppermute | solution.py:196
  60.1 0.1 collective-permute-done.7
  60.3 4.8 %collective-permute-done.8 = bf16[768,128]{1,0:T(8,128)(2,1)S(1)} collective-permute-done((bf16[768,128]{1,0:T(8,128)(2,1)S(1)}, bf16[768,128]{1,0:T(8,128)(2,1)S(1)}, u32[]{:S(2)}, u32[]{:S(2)}) %collective-permute-start.8) | collective-permute-done | bytes 196640 | tf_op jit(solution)/shard_map/ppermute | solution.py:196
  65.0 0.8 add_convert_fusion
  65.9 8.6 %all-to-all-start = ((bf16[3,256,128]{2,1,0:T(8,128)(2,1)}), bf16[3,256,128]{2,1,0:T(8,128)(2,1)S(1)}, u32[]{:S(2)}, u32[]{:S(2)}) async-start(bf16[3,256,128]{2,1,0:T(8,128)(2,1)} %bitcast), calls=%async_computation | async-start | bytes 393216 | tf_op jit(solution)/shard_map/all_to_all | solution.py:253
  74.5 2.6 %collective-permute-start.9 = (bf16[128,256]{1,0:T(8,128)(2,1)S(1)}, bf16[128,256]{1,0:T(8,128)(2,1)S(1)}, u32[]{:S(2)}, u32[]{:S(2)}) collective-permute-start(bf16[128,256]{1,0:T(8,128)(2,1)S(1)} %slice.67), channel_id=1, source_target_pairs={{16,0},{32,16},{48,32},{64,48},{80,64},{96,80},{112,96},{128,112},... | collective-permute-start | bytes 196616 | tf_op jit(solution)/shard_map/ppermute | solution.py:254
  77.1 10.8 %collective-permute-done.9.back_ref = bf16[128,256]{1,0:T(8,128)(2,1)S(1)} collective-permute-done((bf16[128,256]{1,0:T(8,128)(2,1)S(1)}, bf16[128,256]{1,0:T(8,128)(2,1)S(1)}, u32[]{:S(2)}, u32[]{:S(2)}) %collective-permute-start.9) | collective-permute-done | bytes 65568 | tf_op jit(solution)/shard_map/ppermute | solution.py:254
  88.0 0.0 copy-done.1
  88.0 0.0 copy-done.2
  88.0 0.0 copy-done.3
  88.0 3.8 %shard_map.107 = (bf16[384,256]{1,0:T(8,128)(2,1)}, bf16[384,256]{1,0:T(8,128)(2,1)}, bf16[384,256]{1,0:T(8,128)(2,1)}) custom-call(s32[8,384]{1,0:T(8,128)S(1)} %get-tuple-element.31.same_ref, s32[8,128]{1,0:T(8,128)S(1)} %get-tuple-element.32.stays_ref, bf16[384,256]{1,0:T(8,128)(2,1)S(1)} %copy-done.1, bf16[384,256]{1,0:T(8,128)(2,1)S(1)} %copy-done.2, ...), custom_call_target="tpu_custom_call" | custom-call | tf_op jit(solution)/shard_map/pallas_call | solution.py:179
  91.7 0.0 all-to-all-done
  91.7 0.7 add_bitcast_fusion
  (1 shorter events, 0.0 us)
Async XLA Ops:
  2.4 15.9 %collective-permute-start = (bf16[256,128]{1,0:T(8,128)(2,1)S(1)}, bf16[256,128]{1,0:T(8,128)(2,1)S(1)}, u32[]{:S(2)}, u32[]{:S(2)}) collective-permute-start(bf16[256,128]{1,0:T(8,128)(2,1)S(1)} %get-tuple-element.40), channel_id=1, source_target_pairs={{0,16},{16,32},{32,48},{48,64},{64,80},{80,96},{96,112},{112,128},... | collective-permute-start | bytes 196616 | tf_op jit(solution)/shard_map/ppermute | solution.py:227
  12.8 3.7 %copy-start = (bf16[256,6144]{1,0:T(8,128)(2,1)S(1)}, bf16[256,6144]{1,0:T(8,128)(2,1)}, u32[]{:S(2)}) copy-start(bf16[256,6144]{1,0:T(8,128)(2,1)} %w_ref.1) | copy-start | bytes 9437188
  19.7 5.3 %collective-permute-start.1 = (bf16[6144,128]{1,0:T(8,128)(2,1)S(1)}, bf16[6144,128]{1,0:T(8,128)(2,1)S(1)}, u32[]{:S(2)}, u32[]{:S(2)}) collective-permute-start(bf16[6144,128]{1,0:T(8,128)(2,1)S(1)} %shard_map.106), channel_id=1, source_target_pairs={{0,16},{16,0},{32,48},{48,32},{64,80},{80,64},{96,112},{112,96},{1... | collective-permute-start | bytes 4718600 | tf_op jit(solution)/shard_map/ppermute | solution.py:196
  25.4 62.5 %copy-start.1 = (bf16[384,256]{1,0:T(8,128)(2,1)S(1)}, bf16[384,256]{1,0:T(8,128)(2,1)}, u32[]{:S(2)}) copy-start(bf16[384,256]{1,0:T(8,128)(2,1)} %q_ref.1) | copy-start | bytes 589828
  25.5 62.5 %copy-start.2 = (bf16[384,256]{1,0:T(8,128)(2,1)S(1)}, bf16[384,256]{1,0:T(8,128)(2,1)}, u32[]{:S(2)}) copy-start(bf16[384,256]{1,0:T(8,128)(2,1)} %k_ref.1) | copy-start | bytes 589828
  25.5 62.5 %copy-start.3 = (bf16[384,256]{1,0:T(8,128)(2,1)S(1)}, bf16[384,256]{1,0:T(8,128)(2,1)}, u32[]{:S(2)}) copy-start(bf16[384,256]{1,0:T(8,128)(2,1)} %v_ref.1) | copy-start | bytes 589828
  25.5 8.8 %collective-permute-start.2 = (bf16[768,128]{1,0:T(8,128)(2,1)S(1)}, bf16[768,128]{1,0:T(8,128)(2,1)S(1)}, u32[]{:S(2)}, u32[]{:S(2)}) collective-permute-start(bf16[768,128]{1,0:T(8,128)(2,1)S(1)} %get-tuple-element.43), channel_id=1, source_target_pairs={{0,32},{16,48},{32,64},{48,80},{64,96},{80,112},{96,128},{112,144}... | collective-permute-start | bytes 589832 | tf_op jit(solution)/shard_map/ppermute | solution.py:196
  30.4 11.2 %collective-permute-start.3 = (bf16[768,128]{1,0:T(8,128)(2,1)S(1)}, bf16[768,128]{1,0:T(8,128)(2,1)S(1)}, u32[]{:S(2)}, u32[]{:S(2)}) collective-permute-start(bf16[768,128]{1,0:T(8,128)(2,1)S(1)} %get-tuple-element.44), channel_id=1, source_target_pairs={{0,64},{16,208},{32,96},{48,240},{64,128},{80,16},{96,160},{112,48... | collective-permute-start | bytes 589832 | tf_op jit(solution)/shard_map/ppermute | solution.py:196
  32.3 11.3 %collective-permute-start.4 = (bf16[768,128]{1,0:T(8,128)(2,1)S(1)}, bf16[768,128]{1,0:T(8,128)(2,1)S(1)}, u32[]{:S(2)}, u32[]{:S(2)}) collective-permute-start(bf16[768,128]{1,0:T(8,128)(2,1)S(1)} %get-tuple-element.46), channel_id=1, source_target_pairs={{0,224},{16,240},{32,0},{48,16},{64,32},{80,48},{96,64},{112,80},{... | collective-permute-start | bytes 589832 | tf_op jit(solution)/shard_map/ppermute | solution.py:196
  43.8 13.0 %collective-permute-start.5 = (bf16[768,128]{1,0:T(8,128)(2,1)S(1)}, bf16[768,128]{1,0:T(8,128)(2,1)S(1)}, u32[]{:S(2)}, u32[]{:S(2)}) collective-permute-start(bf16[768,128]{1,0:T(8,128)(2,1)S(1)} %get-tuple-element.49), channel_id=1, source_target_pairs={{0,64},{16,80},{32,96},{48,112},{64,128},{80,144},{96,160},{112,17... | collective-permute-start | bytes 589832 | tf_op jit(solution)/shard_map/ppermute | solution.py:196
  45.8 14.4 %collective-permute-start.6 = (bf16[768,128]{1,0:T(8,128)(2,1)S(1)}, bf16[768,128]{1,0:T(8,128)(2,1)S(1)}, u32[]{:S(2)}, u32[]{:S(2)}) collective-permute-start(bf16[768,128]{1,0:T(8,128)(2,1)S(1)} %get-tuple-element.50), channel_id=1, source_target_pairs={{0,192},{16,208},{32,224},{48,240},{64,0},{80,16},{96,32},{112,48}... | collective-permute-start | bytes 589832 | tf_op jit(solution)/shard_map/ppermute | solution.py:196
  50.0 10.2 %collective-permute-start.7 = (bf16[768,128]{1,0:T(8,128)(2,1)S(1)}, bf16[768,128]{1,0:T(8,128)(2,1)S(1)}, u32[]{:S(2)}, u32[]{:S(2)}) collective-permute-start(bf16[768,128]{1,0:T(8,128)(2,1)S(1)} %get-tuple-element.51), channel_id=1, source_target_pairs={{0,32},{16,48},{32,64},{48,80},{64,96},{80,112},{96,128},{112,144}... | collective-permute-start | bytes 589832 | tf_op jit(solution)/shard_map/ppermute | solution.py:196
  53.5 11.5 %collective-permute-start.8 = (bf16[768,128]{1,0:T(8,128)(2,1)S(1)}, bf16[768,128]{1,0:T(8,128)(2,1)S(1)}, u32[]{:S(2)}, u32[]{:S(2)}) collective-permute-start(bf16[768,128]{1,0:T(8,128)(2,1)S(1)} %get-tuple-element.52), channel_id=1, source_target_pairs={{0,224},{16,240},{32,0},{48,16},{64,32},{80,48},{96,64},{112,80},{... | collective-permute-start | bytes 589832 | tf_op jit(solution)/shard_map/ppermute | solution.py:196
  65.9 25.9 %all-to-all-start = ((bf16[3,256,128]{2,1,0:T(8,128)(2,1)}), bf16[3,256,128]{2,1,0:T(8,128)(2,1)S(1)}, u32[]{:S(2)}, u32[]{:S(2)}) async-start(bf16[3,256,128]{2,1,0:T(8,128)(2,1)} %bitcast), calls=%async_computation | async-start | bytes 393216 | tf_op jit(solution)/shard_map/all_to_all | solution.py:253
  74.5 13.5 %collective-permute-start.9 = (bf16[128,256]{1,0:T(8,128)(2,1)S(1)}, bf16[128,256]{1,0:T(8,128)(2,1)S(1)}, u32[]{:S(2)}, u32[]{:S(2)}) collective-permute-start(bf16[128,256]{1,0:T(8,128)(2,1)S(1)} %slice.67), channel_id=1, source_target_pairs={{16,0},{32,16},{48,32},{64,48},{80,64},{96,80},{112,96},{128,112},... | collective-permute-start | bytes 196616 | tf_op jit(solution)/shard_map/ppermute | solution.py:254

commit v9 on v8

--- a/solution.py
+++ b/solution.py
@@ -239,19 +239,18 @@
     parts = [rounded_total(*pair) for pair in zip(cut(own), cut(got), strict=True)]
     part = dict(zip(ORDER, lax.optimization_barrier(parts), strict=True))
     far, up, down = send(part[4], apart_y(2)), send(part[3], along_y(1)), send(part[5], along_y(-1))
+    near = send(part[1], along_y(1)), send(part[7], along_y(-1))
 
     core = lax.axis_index("dp") % NC
     none = jnp.zeros_like(far)
     up = rounded_total(part[2], up, jnp.where(core == 0, far, none))
     down = rounded_total(part[6], down, jnp.where(core == 1, far, none))
-    near = part[1], part[7]
-    up, down, *near = lax.optimization_barrier((up, down, *near))
+    up, down, tail = lax.optimization_barrier((up, down, grad_ctx[row_count:]))
     up, down = send(up, along_y(2)), send(down, along_y(-2))
-    near = send(near[0], along_y(1)), send(near[1], along_y(-1))
+    back = lax.ppermute(tail, "dp", [((i + 1) % ranks, i) for i in range(ranks)])
     sums = rounded_total(part[0], up, down, *near).reshape(NZ, -1, UNIT)
-    sums, tail = lax.optimization_barrier((sums, grad_ctx[row_count:]))
+    sums, back = lax.optimization_barrier((sums, back))
     sums = lax.all_to_all(sums, "dp", 0, 0, axis_index_groups=same_place())
-    back = lax.ppermute(tail, "dp", [((i + 1) % ranks, i) for i in range(ranks)])
     grads = backward(same, stays, queries, key_rows, value_rows, grad_ctx, back)
     grad_weight = total(*sums)
     return (*grads, grad_weight)

time: 92.9 us -> 83.8 us (0.902)
  the two profiles are of different devices: /device:TPU:59 before, /device:TPU:57 now
where the time goes in v9:
time: 83.8 us; the launch traced here: 83.3 us
  starting transfers between devices  47.3 us (56%)
  waiting for transfers between devices  19.3 us (23%)
  Pallas kernels  13 us (16%)
  other arithmetic  2.08 us (2%)
  between operations  0.85 us (1%)
    ppermute x8, starting transfers between devices, send(): lax.ppermute(block, 'dp', [(index(*p), index(*to(*p))) for p in PLACES])  24.9 us
    ppermute x8, waiting for transfers between devices, send(): lax.ppermute(block, 'dp', [(index(*p), index(*to(*p))) for p in PLACES])  11.5 us
    ppermute x1, starting transfers between devices, local(): lax.ppermute(leave, 'dp', [(i, (i + 1) % ranks) for i in range(ranks)])  10.4 us
    all_to_all x1, starting transfers between devices, local(): sums = lax.all_to_all(sums, 'dp', 0, 0, axis_index_groups=same_place())  8.59 us
    all_to_all x1, waiting for transfers between devices, local(): sums = lax.all_to_all(sums, 'dp', 0, 0, axis_index_groups=same_place())  7 us
    pallas_call x1, Pallas kernels, backward(): pl.pallas_call(backward_kernel, in_specs=[VMEM] * 7, out_specs=[VMEM] * 3...  3.75 us
    ppermute x1, starting transfers between devices, local(): lax.ppermute(tail, 'dp', [((i + 1) % ranks, i) for i in range(ranks)])  3.43 us
    pallas_call x1, Pallas kernels, staying_context(): pl.pallas_call(context_kernel, in_specs=[VMEM] * 5 + [pl.BlockSpec(memory...  2.95 us
  transfers between devices with their start and end apart: 11, of which 7 were waited for; matrix products, arithmetic and copies ran while one was open for 1% of the time, Pallas kernels for 12%

profile of v9, /device:TPU:57, one launch (start us, length us, event | category | flops | bytes accessed | tf_op | source)
XLA Modules:
  0.0 83.3 jit_solution(9766544376463140501)
XLA Ops:
  0.6 1.7 %shard_map.102 = (bf16[256,128]{1,0:T(8,128)(2,1)S(1)}, s32[8,384]{1,0:T(8,128)S(1)}, s32[8,128]{1,0:T(8,128)S(1)}, bf16[384,256]{1,0:T(8,128)(2,1)S(1)}, bf16[3...) custom-call(s32[384]{0:T(512)} %ids_hbm.1, s32[384]{0:T(512)} %slot_hbm.1, bf16[384,256]{1,0:T(8,128)(2,1)} %q_ref.1, ...), custom_call_target="tpu_custom_call" | custom-call | tf_op jit(solution)/shard_map/pallas_call | solution.py:68
  2.4 10.4 %collective-permute-start = (bf16[256,128]{1,0:T(8,128)(2,1)S(1)}, bf16[256,128]{1,0:T(8,128)(2,1)S(1)}, u32[]{:S(2)}, u32[]{:S(2)}) collective-permute-start(bf16[256,128]{1,0:T(8,128)(2,1)S(1)} %get-tuple-element.39), channel_id=1, source_target_pairs={{0,16},{16,32},{32,48},{48,64},{64,80},{80,96},{96,112},{112,128},... | collective-permute-start | bytes 196616 | tf_op jit(solution)/shard_map/ppermute | solution.py:227
  12.8 0.0 copy-start
  12.8 2.9 %shard_map.103 = (bf16[256,384]{1,0:T(8,128)(2,1)S(1)}, bf16[512,6144]{1,0:T(8,128)(2,1)S(1)}) custom-call(s32[8,384]{1,0:T(8,128)S(1)} %get-tuple-element.30.same_ref, s32[8,128]{1,0:T(8,128)S(1)} %get-tuple-element.31.stays_ref, bf16[384,256]{1,0:T(8,128)(2,1)S(1)} %get-tuple-element.32.q_ref, bf16[384,256]{1,0:T(8,128)(2,1)S(1)} %get-tuple-element.33.k_ref, ...), custom_call_target="tpu_custom_call" | custom-call | tf_op jit(solution)/shard_map/pallas_call | solution.py:98
  15.8 0.7 copy-done
  16.5 1.8 %shard_map.104.g_ref = bf16[512,256]{1,0:T(8,128)(2,1)S(1)} custom-call(bf16[512,6144]{1,0:T(8,128)(2,1)S(1)} %get-tuple-element.36.g_ref, bf16[256,6144]{1,0:T(8,128)(2,1)S(1)} %copy-done), custom_call_target="tpu_custom_call" | custom-call | tf_op jit(solution)/shard_map/pallas_call | solution.py:147
  18.3 0.0 collective-permute-done.came_ref
  18.3 1.4 %shard_map.106 = bf16[6144,128]{1,0:T(8,128)(2,1)S(1)} custom-call(bf16[256,384]{1,0:T(8,128)(2,1)S(1)} %get-tuple-element.38.stay_ref, bf16[256,128]{1,0:T(8,128)(2,1)S(1)} %collective-permute-done.came_ref, bf16[512,6144]{1,0:T(8,128)(2,1)S(1)} %get-tuple-element.36.g_ref), custom_call_target="tpu_custom_call" | custom-call | tf_op jit(solution)/shard_map/pallas_call | solution.py:128
  19.7 1.9 %collective-permute-start.1 = (bf16[6144,128]{1,0:T(8,128)(2,1)S(1)}, bf16[6144,128]{1,0:T(8,128)(2,1)S(1)}, u32[]{:S(2)}, u32[]{:S(2)}) collective-permute-start(bf16[6144,128]{1,0:T(8,128)(2,1)S(1)} %shard_map.106), channel_id=1, source_target_pairs={{0,16},{16,0},{32,48},{48,32},{64,80},{80,64},{96,112},{112,96},{1... | collective-permute-start | bytes 4718600 | tf_op jit(solution)/shard_map/ppermute | solution.py:196
  21.7 1.4 %shard_map.105 = bf16[6144,128]{1,0:T(8,128)(2,1)S(1)} custom-call(bf16[256,384]{1,0:T(8,128)(2,1)S(1)} %get-tuple-element.38.stay_ref, bf16[256,128]{1,0:T(8,128)(2,1)S(1)} %collective-permute-done.came_ref, bf16[512,6144]{1,0:T(8,128)(2,1)S(1)} %get-tuple-element.36.g_ref), custom_call_target="tpu_custom_call" | custom-call | tf_op jit(solution)/shard_map/pallas_call | solution.py:128
  23.1 2.0 %collective-permute-done.1 = bf16[6144,128]{1,0:T(8,128)(2,1)S(1)} collective-permute-done((bf16[6144,128]{1,0:T(8,128)(2,1)S(1)}, bf16[6144,128]{1,0:T(8,128)(2,1)S(1)}, u32[]{:S(2)}, u32[]{:S(2)}) %collective-permute-start.1) | collective-permute-done | bytes 1572896 | tf_op jit(solution)/shard_map/ppermute | solution.py:196
  25.0 0.4 add_convert_fusion.3
  25.4 0.0 copy-start.1
  25.5 0.0 copy-start.2
  25.5 0.0 copy-start.3
  25.5 6.4 %collective-permute-start.2 = (bf16[768,128]{1,0:T(8,128)(2,1)S(1)}, bf16[768,128]{1,0:T(8,128)(2,1)S(1)}, u32[]{:S(2)}, u32[]{:S(2)}) collective-permute-start(bf16[768,128]{1,0:T(8,128)(2,1)S(1)} %get-tuple-element.42), channel_id=1, source_target_pairs={{0,32},{16,48},{32,64},{48,80},{64,96},{80,112},{96,128},{112,144}... | collective-permute-start | bytes 589832 | tf_op jit(solution)/shard_map/ppermute | solution.py:196
  31.9 1.9 %collective-permute-start.3 = (bf16[768,128]{1,0:T(8,128)(2,1)S(1)}, bf16[768,128]{1,0:T(8,128)(2,1)S(1)}, u32[]{:S(2)}, u32[]{:S(2)}) collective-permute-start(bf16[768,128]{1,0:T(8,128)(2,1)S(1)} %get-tuple-element.43), channel_id=1, source_target_pairs={{0,64},{16,208},{32,96},{48,240},{64,128},{80,16},{96,160},{112,48... | collective-permute-start | bytes 589832 | tf_op jit(solution)/shard_map/ppermute | solution.py:196
  33.9 1.9 %collective-permute-start.4 = (bf16[768,128]{1,0:T(8,128)(2,1)S(1)}, bf16[768,128]{1,0:T(8,128)(2,1)S(1)}, u32[]{:S(2)}, u32[]{:S(2)}) collective-permute-start(bf16[768,128]{1,0:T(8,128)(2,1)S(1)} %get-tuple-element.45), channel_id=1, source_target_pairs={{0,224},{16,240},{32,0},{48,16},{64,32},{80,48},{96,64},{112,80},{... | collective-permute-start | bytes 589832 | tf_op jit(solution)/shard_map/ppermute | solution.py:196
  35.8 4.6 %collective-permute-start.7 = (bf16[768,128]{1,0:T(8,128)(2,1)S(1)}, bf16[768,128]{1,0:T(8,128)(2,1)S(1)}, u32[]{:S(2)}, u32[]{:S(2)}) collective-permute-start(bf16[768,128]{1,0:T(8,128)(2,1)S(1)} %get-tuple-element.48), channel_id=1, source_target_pairs={{0,32},{16,48},{32,64},{48,80},{64,96},{80,112},{96,128},{112,144}... | collective-permute-start | bytes 589832 | tf_op jit(solution)/shard_map/ppermute | solution.py:196
  40.4 1.9 %collective-permute-start.8 = (bf16[768,128]{1,0:T(8,128)(2,1)S(1)}, bf16[768,128]{1,0:T(8,128)(2,1)S(1)}, u32[]{:S(2)}, u32[]{:S(2)}) collective-permute-start(bf16[768,128]{1,0:T(8,128)(2,1)S(1)} %get-tuple-element.49), channel_id=1, source_target_pairs={{0,224},{16,240},{32,0},{48,16},{64,32},{80,48},{96,64},{112,80},{... | collective-permute-start | bytes 589832 | tf_op jit(solution)/shard_map/ppermute | solution.py:196
  42.3 0.0 collective-permute-done.2
  42.3 0.8 collective-permute-done.3
  43.2 2.0 %collective-permute-done.4 = bf16[768,128]{1,0:T(8,128)(2,1)S(1)} collective-permute-done((bf16[768,128]{1,0:T(8,128)(2,1)S(1)}, bf16[768,128]{1,0:T(8,128)(2,1)S(1)}, u32[]{:S(2)}, u32[]{:S(2)}) %collective-permute-start.4) | collective-permute-done | bytes 196640 | tf_op jit(solution)/shard_map/ppermute | solution.py:196
  45.2 0.2 add_convert_fusion.1
  45.4 1.9 %collective-permute-start.5 = (bf16[768,128]{1,0:T(8,128)(2,1)S(1)}, bf16[768,128]{1,0:T(8,128)(2,1)S(1)}, u32[]{:S(2)}, u32[]{:S(2)}) collective-permute-start(bf16[768,128]{1,0:T(8,128)(2,1)S(1)} %get-tuple-element.46), channel_id=1, source_target_pairs={{0,64},{16,80},{32,96},{48,112},{64,128},{80,144},{96,160},{112,17... | collective-permute-start | bytes 589832 | tf_op jit(solution)/shard_map/ppermute | solution.py:196
  47.3 4.3 %collective-permute-start.6 = (bf16[768,128]{1,0:T(8,128)(2,1)S(1)}, bf16[768,128]{1,0:T(8,128)(2,1)S(1)}, u32[]{:S(2)}, u32[]{:S(2)}) collective-permute-start(bf16[768,128]{1,0:T(8,128)(2,1)S(1)} %get-tuple-element.47), channel_id=1, source_target_pairs={{0,192},{16,208},{32,224},{48,240},{64,0},{80,16},{96,32},{112,48}... | collective-permute-start | bytes 589832 | tf_op jit(solution)/shard_map/ppermute | solution.py:196
  51.6 3.4 %collective-permute-start.9 = (bf16[128,256]{1,0:T(8,128)(2,1)S(1)}, bf16[128,256]{1,0:T(8,128)(2,1)S(1)}, u32[]{:S(2)}, u32[]{:S(2)}) collective-permute-start(bf16[128,256]{1,0:T(8,128)(2,1)S(1)} %slice.67), channel_id=1, source_target_pairs={{16,0},{32,16},{48,32},{64,48},{80,64},{96,80},{112,96},{128,112},... | collective-permute-start | bytes 196616 | tf_op jit(solution)/shard_map/ppermute | solution.py:250
  55.0 0.0 collective-permute-done.7
  55.0 0.0 collective-permute-done.8
  55.0 2.6 %collective-permute-done.5 = bf16[768,128]{1,0:T(8,128)(2,1)S(1)} collective-permute-done((bf16[768,128]{1,0:T(8,128)(2,1)S(1)}, bf16[768,128]{1,0:T(8,128)(2,1)S(1)}, u32[]{:S(2)}, u32[]{:S(2)}) %collective-permute-start.5) | collective-permute-done | bytes 196640 | tf_op jit(solution)/shard_map/ppermute | solution.py:196
  57.7 4.0 %collective-permute-done.6 = bf16[768,128]{1,0:T(8,128)(2,1)S(1)} collective-permute-done((bf16[768,128]{1,0:T(8,128)(2,1)S(1)}, bf16[768,128]{1,0:T(8,128)(2,1)S(1)}, u32[]{:S(2)}, u32[]{:S(2)}) %collective-permute-start.6) | collective-permute-done | bytes 196640 | tf_op jit(solution)/shard_map/ppermute | solution.py:196
  61.7 0.8 add_convert_fusion
  62.5 0.8 collective-permute-done.9.back_ref
  63.3 8.6 %all-to-all-start = ((bf16[3,256,128]{2,1,0:T(8,128)(2,1)}), bf16[3,256,128]{2,1,0:T(8,128)(2,1)S(1)}, u32[]{:S(2)}, u32[]{:S(2)}) async-start(bf16[3,256,128]{2,1,0:T(8,128)(2,1)} %bitcast), calls=%async_computation | async-start | bytes 393216 | tf_op jit(solution)/shard_map/all_to_all | solution.py:253
  71.9 0.0 copy-done.1
  71.9 0.0 copy-done.2
  71.9 0.0 copy-done.3
  71.9 3.8 %shard_map.107 = (bf16[384,256]{1,0:T(8,128)(2,1)}, bf16[384,256]{1,0:T(8,128)(2,1)}, bf16[384,256]{1,0:T(8,128)(2,1)}) custom-call(s32[8,384]{1,0:T(8,128)S(1)} %get-tuple-element.30.same_ref, s32[8,128]{1,0:T(8,128)S(1)} %get-tuple-element.31.stays_ref, bf16[384,256]{1,0:T(8,128)(2,1)S(1)} %copy-done.1, bf16[384,256]{1,0:T(8,128)(2,1)S(1)} %copy-done.2, ...), custom_call_target="tpu_custom_call" | custom-call | tf_op jit(solution)/shard_map/pallas_call | solution.py:179
  75.6 7.0 %all-to-all-done = bf16[3,256,128]{2,1,0:T(8,128)(2,1)S(1)} async-done(((bf16[3,256,128]{2,1,0:T(8,128)(2,1)}), bf16[3,256,128]{2,1,0:T(8,128)(2,1)S(1)}, u32[]{:S(2)}, u32[]{:S(2)}) %all-to-all-start) | async-done | bytes 196640 | tf_op jit(solution)/shard_map/all_to_all | solution.py:253
  82.6 0.7 add_bitcast_fusion
  (1 shorter events, 0.0 us)
Async XLA Ops:
  2.4 15.9 %collective-permute-start = (bf16[256,128]{1,0:T(8,128)(2,1)S(1)}, bf16[256,128]{1,0:T(8,128)(2,1)S(1)}, u32[]{:S(2)}, u32[]{:S(2)}) collective-permute-start(bf16[256,128]{1,0:T(8,128)(2,1)S(1)} %get-tuple-element.39), channel_id=1, source_target_pairs={{0,16},{16,32},{32,48},{48,64},{64,80},{80,96},{96,112},{112,128},... | collective-permute-start | bytes 196616 | tf_op jit(solution)/shard_map/ppermute | solution.py:227
  12.8 3.7 %copy-start = (bf16[256,6144]{1,0:T(8,128)(2,1)S(1)}, bf16[256,6144]{1,0:T(8,128)(2,1)}, u32[]{:S(2)}) copy-start(bf16[256,6144]{1,0:T(8,128)(2,1)} %w_ref.1) | copy-start | bytes 9437188
  19.7 5.3 %collective-permute-start.1 = (bf16[6144,128]{1,0:T(8,128)(2,1)S(1)}, bf16[6144,128]{1,0:T(8,128)(2,1)S(1)}, u32[]{:S(2)}, u32[]{:S(2)}) collective-permute-start(bf16[6144,128]{1,0:T(8,128)(2,1)S(1)} %shard_map.106), channel_id=1, source_target_pairs={{0,16},{16,0},{32,48},{48,32},{64,80},{80,64},{96,112},{112,96},{1... | collective-permute-start | bytes 4718600 | tf_op jit(solution)/shard_map/ppermute | solution.py:196
  25.4 46.4 %copy-start.1 = (bf16[384,256]{1,0:T(8,128)(2,1)S(1)}, bf16[384,256]{1,0:T(8,128)(2,1)}, u32[]{:S(2)}) copy-start(bf16[384,256]{1,0:T(8,128)(2,1)} %q_ref.1) | copy-start | bytes 589828
  25.5 46.4 %copy-start.2 = (bf16[384,256]{1,0:T(8,128)(2,1)S(1)}, bf16[384,256]{1,0:T(8,128)(2,1)}, u32[]{:S(2)}) copy-start(bf16[384,256]{1,0:T(8,128)(2,1)} %k_ref.1) | copy-start | bytes 589828
  25.5 46.4 %copy-start.3 = (bf16[384,256]{1,0:T(8,128)(2,1)S(1)}, bf16[384,256]{1,0:T(8,128)(2,1)}, u32[]{:S(2)}) copy-start(bf16[384,256]{1,0:T(8,128)(2,1)} %v_ref.1) | copy-start | bytes 589828
  25.5 16.9 %collective-permute-start.2 = (bf16[768,128]{1,0:T(8,128)(2,1)S(1)}, bf16[768,128]{1,0:T(8,128)(2,1)S(1)}, u32[]{:S(2)}, u32[]{:S(2)}) collective-permute-start(bf16[768,128]{1,0:T(8,128)(2,1)S(1)} %get-tuple-element.42), channel_id=1, source_target_pairs={{0,32},{16,48},{32,64},{48,80},{64,96},{80,112},{96,128},{112,144}... | collective-permute-start | bytes 589832 | tf_op jit(solution)/shard_map/ppermute | solution.py:196
  31.9 11.2 %collective-permute-start.3 = (bf16[768,128]{1,0:T(8,128)(2,1)S(1)}, bf16[768,128]{1,0:T(8,128)(2,1)S(1)}, u32[]{:S(2)}, u32[]{:S(2)}) collective-permute-start(bf16[768,128]{1,0:T(8,128)(2,1)S(1)} %get-tuple-element.43), channel_id=1, source_target_pairs={{0,64},{16,208},{32,96},{48,240},{64,128},{80,16},{96,160},{112,48... | collective-permute-start | bytes 589832 | tf_op jit(solution)/shard_map/ppermute | solution.py:196
  33.9 11.3 %collective-permute-start.4 = (bf16[768,128]{1,0:T(8,128)(2,1)S(1)}, bf16[768,128]{1,0:T(8,128)(2,1)S(1)}, u32[]{:S(2)}, u32[]{:S(2)}) collective-permute-start(bf16[768,128]{1,0:T(8,128)(2,1)S(1)} %get-tuple-element.45), channel_id=1, source_target_pairs={{0,224},{16,240},{32,0},{48,16},{64,32},{80,48},{96,64},{112,80},{... | collective-permute-start | bytes 589832 | tf_op jit(solution)/shard_map/ppermute | solution.py:196
  35.8 19.2 %collective-permute-start.7 = (bf16[768,128]{1,0:T(8,128)(2,1)S(1)}, bf16[768,128]{1,0:T(8,128)(2,1)S(1)}, u32[]{:S(2)}, u32[]{:S(2)}) collective-permute-start(bf16[768,128]{1,0:T(8,128)(2,1)S(1)} %get-tuple-element.48), channel_id=1, source_target_pairs={{0,32},{16,48},{32,64},{48,80},{64,96},{80,112},{96,128},{112,144}... | collective-permute-start | bytes 589832 | tf_op jit(solution)/shard_map/ppermute | solution.py:196
  40.4 14.6 %collective-permute-start.8 = (bf16[768,128]{1,0:T(8,128)(2,1)S(1)}, bf16[768,128]{1,0:T(8,128)(2,1)S(1)}, u32[]{:S(2)}, u32[]{:S(2)}) collective-permute-start(bf16[768,128]{1,0:T(8,128)(2,1)S(1)} %get-tuple-element.49), channel_id=1, source_target_pairs={{0,224},{16,240},{32,0},{48,16},{64,32},{80,48},{96,64},{112,80},{... | collective-permute-start | bytes 589832 | tf_op jit(solution)/shard_map/ppermute | solution.py:196
  45.4 12.3 %collective-permute-start.5 = (bf16[768,128]{1,0:T(8,128)(2,1)S(1)}, bf16[768,128]{1,0:T(8,128)(2,1)S(1)}, u32[]{:S(2)}, u32[]{:S(2)}) collective-permute-start(bf16[768,128]{1,0:T(8,128)(2,1)S(1)} %get-tuple-element.46), channel_id=1, source_target_pairs={{0,64},{16,80},{32,96},{48,112},{64,128},{80,144},{96,160},{112,17... | collective-permute-start | bytes 589832 | tf_op jit(solution)/shard_map/ppermute | solution.py:196
  47.3 14.4 %collective-permute-start.6 = (bf16[768,128]{1,0:T(8,128)(2,1)S(1)}, bf16[768,128]{1,0:T(8,128)(2,1)S(1)}, u32[]{:S(2)}, u32[]{:S(2)}) collective-permute-start(bf16[768,128]{1,0:T(8,128)(2,1)S(1)} %get-tuple-element.47), channel_id=1, source_target_pairs={{0,192},{16,208},{32,224},{48,240},{64,0},{80,16},{96,32},{112,48}... | collective-permute-start | bytes 589832 | tf_op jit(solution)/shard_map/ppermute | solution.py:196
  51.6 11.7 %collective-permute-start.9 = (bf16[128,256]{1,0:T(8,128)(2,1)S(1)}, bf16[128,256]{1,0:T(8,128)(2,1)S(1)}, u32[]{:S(2)}, u32[]{:S(2)}) collective-permute-start(bf16[128,256]{1,0:T(8,128)(2,1)S(1)} %slice.67), channel_id=1, source_target_pairs={{16,0},{32,16},{48,32},{64,48},{80,64},{96,80},{112,96},{128,112},... | collective-permute-start | bytes 196616 | tf_op jit(solution)/shard_map/ppermute | solution.py:250
  63.3 19.3 %all-to-all-start = ((bf16[3,256,128]{2,1,0:T(8,128)(2,1)}), bf16[3,256,128]{2,1,0:T(8,128)(2,1)S(1)}, u32[]{:S(2)}, u32[]{:S(2)}) async-start(bf16[3,256,128]{2,1,0:T(8,128)(2,1)} %bitcast), calls=%async_computation | async-start | bytes 393216 | tf_op jit(solution)/shard_map/all_to_all | solution.py:253

commit v10 on v9

--- a/solution.py
+++ b/solution.py
@@ -10,7 +10,7 @@
 HD = 128
 UNIT = 128
 NZ, NY, NC = 3, 8, 2
-ORDER = (4, 3, 5, 2, 6, 1, 7, 0)
+ORDER = (4, 3, -3, 2, -2, 1, -1, 0)
 VMEM = pl.BlockSpec(memory_space=pltpu.VMEM)
 PARAMS = pltpu.CompilerParams(vmem_limit_bytes=8 * 1024 * 1024)
 
@@ -116,7 +116,8 @@
     ctx_t = jnp.concatenate([stay_ref[...], came_ref[...]], axis=1)
     width = ctx_t.shape[0]
     for n, distance in enumerate(ORDER):
-        dest = [(i * NY + (y + distance) % NY) * NC + core for i in range(NZ)]
+        y_to = (y + NY + distance * (1 - 2 * core)) % NY
+        dest = [(i * NY + y_to) * NC + core for i in range(NZ)]
         g = jnp.concatenate([g_ref[:, pl.ds(pl.multiple_of(d * UNIT, UNIT), UNIT)] for d in dest], axis=1)
         part = dot(ctx_t, g, ((1,), (0,))).astype(jnp.bfloat16)
         for i in range(NZ):
@@ -197,10 +198,6 @@
 
 
 def along_y(step):
-    return lambda z, y, c: (z, y + step, c)
-
-
-def apart_y(step):
     return lambda z, y, c: (z, y + step * (1 - 2 * c), c)
 
 
@@ -238,13 +235,10 @@
     own = partial_grad(False, stay, came, g_near)
     parts = [rounded_total(*pair) for pair in zip(cut(own), cut(got), strict=True)]
     part = dict(zip(ORDER, lax.optimization_barrier(parts), strict=True))
-    far, up, down = send(part[4], apart_y(2)), send(part[3], along_y(1)), send(part[5], along_y(-1))
-    near = send(part[1], along_y(1)), send(part[7], along_y(-1))
-
-    core = lax.axis_index("dp") % NC
-    none = jnp.zeros_like(far)
-    up = rounded_total(part[2], up, jnp.where(core == 0, far, none))
-    down = rounded_total(part[6], down, jnp.where(core == 1, far, none))
+    far, up, down = send(part[4], along_y(2)), send(part[3], along_y(1)), send(part[-3], along_y(-1))
+    near = send(part[1], along_y(1)), send(part[-1], along_y(-1))
+
+    up, down = rounded_total(part[2], up, far), rounded_total(part[-2], down)
     up, down, tail = lax.optimization_barrier((up, down, grad_ctx[row_count:]))
     up, down = send(up, along_y(2)), send(down, along_y(-2))
     back = lax.ppermute(tail, "dp", [((i + 1) % ranks, i) for i in range(ranks)])

time: 83.8 us -> 81.3 us (0.970)
  the two profiles are of different devices: /device:TPU:57 before, /device:TPU:6 now
where the time goes in v10:
time: 81.3 us; the launch traced here: 80.5 us
  starting transfers between devices  39 us (48%)
  waiting for transfers between devices  24.9 us (31%)
  Pallas kernels  13 us (16%)
  other arithmetic  2.03 us (2%)
  between operations  0.84 us (1%)
    ppermute x8, starting transfers between devices, send(): lax.ppermute(block, 'dp', [(index(*p), index(*to(*p))) for p in PLACES])  24.8 us
    ppermute x1, waiting for transfers between devices, local(): lax.ppermute(leave, 'dp', [(i, (i + 1) % ranks) for i in range(ranks)])  11.6 us
    all_to_all x1, starting transfers between devices, local(): sums = lax.all_to_all(sums, 'dp', 0, 0, axis_index_groups=same_place())  7.48 us
    ppermute x8, waiting for transfers between devices, send(): lax.ppermute(block, 'dp', [(index(*p), index(*to(*p))) for p in PLACES])  7.27 us
    all_to_all x1, waiting for transfers between devices, local(): sums = lax.all_to_all(sums, 'dp', 0, 0, axis_index_groups=same_place())  5.97 us
    ppermute x1, starting transfers between devices, local(): lax.ppermute(tail, 'dp', [((i + 1) % ranks, i) for i in range(ranks)])  4.78 us
    pallas_call x1, Pallas kernels, backward(): pl.pallas_call(backward_kernel, in_specs=[VMEM] * 7, out_specs=[VMEM] * 3...  3.76 us
    pallas_call x1, Pallas kernels, staying_context(): pl.pallas_call(context_kernel, in_specs=[VMEM] * 5 + [pl.BlockSpec(memory...  2.95 us
  transfers between devices with their start and end apart: 11, of which 5 were waited for; matrix products, arithmetic and copies ran while one was open for 1% of the time, Pallas kernels for 12%

profile of v10, /device:TPU:6, one launch (start us, length us, event | category | flops | bytes accessed | tf_op | source)
XLA Modules:
  0.0 80.5 jit_solution(7334432591902900880)
XLA Ops:
  0.6 1.7 %shard_map.102 = (bf16[256,128]{1,0:T(8,128)(2,1)S(1)}, s32[8,384]{1,0:T(8,128)S(1)}, s32[8,128]{1,0:T(8,128)S(1)}, bf16[384,256]{1,0:T(8,128)(2,1)S(1)}, bf16[3...) custom-call(s32[384]{0:T(512)} %ids_hbm.1, s32[384]{0:T(512)} %slot_hbm.1, bf16[384,256]{1,0:T(8,128)(2,1)} %q_ref.1, ...), custom_call_target="tpu_custom_call" | custom-call | tf_op jit(solution)/shard_map/pallas_call | solution.py:68
  2.4 1.9 %collective-permute-start = (bf16[256,128]{1,0:T(8,128)(2,1)S(1)}, bf16[256,128]{1,0:T(8,128)(2,1)S(1)}, u32[]{:S(2)}, u32[]{:S(2)}) collective-permute-start(bf16[256,128]{1,0:T(8,128)(2,1)S(1)} %get-tuple-element.39), channel_id=1, source_target_pairs={{0,16},{16,32},{32,48},{48,64},{64,80},{80,96},{96,112},{112,128},... | collective-permute-start | bytes 196616 | tf_op jit(solution)/shard_map/ppermute | solution.py:224
  4.3 0.0 copy-start
  4.3 2.9 %shard_map.103 = (bf16[256,384]{1,0:T(8,128)(2,1)S(1)}, bf16[512,6144]{1,0:T(8,128)(2,1)S(1)}) custom-call(s32[8,384]{1,0:T(8,128)S(1)} %get-tuple-element.30.same_ref, s32[8,128]{1,0:T(8,128)S(1)} %get-tuple-element.31.stays_ref, bf16[384,256]{1,0:T(8,128)(2,1)S(1)} %get-tuple-element.32.q_ref, bf16[384,256]{1,0:T(8,128)(2,1)S(1)} %get-tuple-element.33.k_ref, ...), custom_call_target="tpu_custom_call" | custom-call | tf_op jit(solution)/shard_map/pallas_call | solution.py:98
  7.3 0.7 copy-done
  8.0 1.8 %shard_map.104.g_ref = bf16[512,256]{1,0:T(8,128)(2,1)S(1)} custom-call(bf16[512,6144]{1,0:T(8,128)(2,1)S(1)} %get-tuple-element.36.g_ref, bf16[256,6144]{1,0:T(8,128)(2,1)S(1)} %copy-done), custom_call_target="tpu_custom_call" | custom-call | tf_op jit(solution)/shard_map/pallas_call | solution.py:148
  9.8 11.6 %collective-permute-done.came_ref = bf16[256,128]{1,0:T(8,128)(2,1)S(1)} collective-permute-done((bf16[256,128]{1,0:T(8,128)(2,1)S(1)}, bf16[256,128]{1,0:T(8,128)(2,1)S(1)}, u32[]{:S(2)}, u32[]{:S(2)}) %collective-permute-start) | collective-permute-done | bytes 65568 | tf_op jit(solution)/shard_map/ppermute | solution.py:224
  21.5 1.3 %shard_map.106 = bf16[6144,128]{1,0:T(8,128)(2,1)S(1)} custom-call(bf16[256,384]{1,0:T(8,128)(2,1)S(1)} %get-tuple-element.38.stay_ref, bf16[256,128]{1,0:T(8,128)(2,1)S(1)} %collective-permute-done.came_ref, bf16[512,6144]{1,0:T(8,128)(2,1)S(1)} %get-tuple-element.36.g_ref), custom_call_target="tpu_custom_call" | custom-call | tf_op jit(solution)/shard_map/pallas_call | solution.py:129
  22.8 1.9 %collective-permute-start.1 = (bf16[6144,128]{1,0:T(8,128)(2,1)S(1)}, bf16[6144,128]{1,0:T(8,128)(2,1)S(1)}, u32[]{:S(2)}, u32[]{:S(2)}) collective-permute-start(bf16[6144,128]{1,0:T(8,128)(2,1)S(1)} %shard_map.106), channel_id=1, source_target_pairs={{0,16},{16,0},{32,48},{48,32},{64,80},{80,64},{96,112},{112,96},{1... | collective-permute-start | bytes 4718600 | tf_op jit(solution)/shard_map/ppermute | solution.py:197
  24.7 1.4 %shard_map.105 = bf16[6144,128]{1,0:T(8,128)(2,1)S(1)} custom-call(bf16[256,384]{1,0:T(8,128)(2,1)S(1)} %get-tuple-element.38.stay_ref, bf16[256,128]{1,0:T(8,128)(2,1)S(1)} %collective-permute-done.came_ref, bf16[512,6144]{1,0:T(8,128)(2,1)S(1)} %get-tuple-element.36.g_ref), custom_call_target="tpu_custom_call" | custom-call | tf_op jit(solution)/shard_map/pallas_call | solution.py:129
  26.1 2.0 %collective-permute-done.1 = bf16[6144,128]{1,0:T(8,128)(2,1)S(1)} collective-permute-done((bf16[6144,128]{1,0:T(8,128)(2,1)S(1)}, bf16[6144,128]{1,0:T(8,128)(2,1)S(1)}, u32[]{:S(2)}, u32[]{:S(2)}) %collective-permute-start.1) | collective-permute-done | bytes 1572896 | tf_op jit(solution)/shard_map/ppermute | solution.py:197
  28.1 0.4 add_convert_fusion.3
  28.5 0.0 copy-start.1
  28.5 0.0 copy-start.2
  28.6 0.0 copy-start.3
  28.6 2.1 %collective-permute-start.4 = (bf16[768,128]{1,0:T(8,128)(2,1)S(1)}, bf16[768,128]{1,0:T(8,128)(2,1)S(1)}, u32[]{:S(2)}, u32[]{:S(2)}) collective-permute-start(bf16[768,128]{1,0:T(8,128)(2,1)S(1)} %get-tuple-element.45), channel_id=1, source_target_pairs={{0,224},{16,48},{32,0},{48,80},{64,32},{80,112},{96,64},{112,144},... | collective-permute-start | bytes 589832 | tf_op jit(solution)/shard_map/ppermute | solution.py:197
  30.6 3.9 %collective-permute-start.2 = (bf16[768,128]{1,0:T(8,128)(2,1)S(1)}, bf16[768,128]{1,0:T(8,128)(2,1)S(1)}, u32[]{:S(2)}, u32[]{:S(2)}) collective-permute-start(bf16[768,128]{1,0:T(8,128)(2,1)S(1)} %get-tuple-element.42), channel_id=1, source_target_pairs={{0,32},{16,240},{32,64},{48,16},{64,96},{80,48},{96,128},{112,80},... | collective-permute-start | bytes 589832 | tf_op jit(solution)/shard_map/ppermute | solution.py:197
  34.6 1.9 %collective-permute-start.3 = (bf16[768,128]{1,0:T(8,128)(2,1)S(1)}, bf16[768,128]{1,0:T(8,128)(2,1)S(1)}, u32[]{:S(2)}, u32[]{:S(2)}) collective-permute-start(bf16[768,128]{1,0:T(8,128)(2,1)S(1)} %get-tuple-element.43), channel_id=1, source_target_pairs={{0,64},{16,208},{32,96},{48,240},{64,128},{80,16},{96,160},{112,48... | collective-permute-start | bytes 589832 | tf_op jit(solution)/shard_map/ppermute | solution.py:197
  36.5 1.9 %collective-permute-start.7 = (bf16[768,128]{1,0:T(8,128)(2,1)S(1)}, bf16[768,128]{1,0:T(8,128)(2,1)S(1)}, u32[]{:S(2)}, u32[]{:S(2)}) collective-permute-start(bf16[768,128]{1,0:T(8,128)(2,1)S(1)} %get-tuple-element.48), channel_id=1, source_target_pairs={{0,32},{16,240},{32,64},{48,16},{64,96},{80,48},{96,128},{112,80},... | collective-permute-start | bytes 589832 | tf_op jit(solution)/shard_map/ppermute | solution.py:197
  38.4 5.1 %collective-permute-start.8 = (bf16[768,128]{1,0:T(8,128)(2,1)S(1)}, bf16[768,128]{1,0:T(8,128)(2,1)S(1)}, u32[]{:S(2)}, u32[]{:S(2)}) collective-permute-start(bf16[768,128]{1,0:T(8,128)(2,1)S(1)} %get-tuple-element.49), channel_id=1, source_target_pairs={{0,224},{16,48},{32,0},{48,80},{64,32},{80,112},{96,64},{112,144},... | collective-permute-start | bytes 589832 | tf_op jit(solution)/shard_map/ppermute | solution.py:197
  43.6 0.0 collective-permute-done.4
  43.6 0.1 add_convert_fusion.1
  43.6 0.0 collective-permute-done.2
  43.7 3.9 %collective-permute-done.3 = bf16[768,128]{1,0:T(8,128)(2,1)S(1)} collective-permute-done((bf16[768,128]{1,0:T(8,128)(2,1)S(1)}, bf16[768,128]{1,0:T(8,128)(2,1)S(1)}, u32[]{:S(2)}, u32[]{:S(2)}) %collective-permute-start.3) | collective-permute-done | bytes 196640 | tf_op jit(solution)/shard_map/ppermute | solution.py:197
  47.6 0.1 add_convert_fusion.2
  47.7 1.9 %collective-permute-start.5 = (bf16[768,128]{1,0:T(8,128)(2,1)S(1)}, bf16[768,128]{1,0:T(8,128)(2,1)S(1)}, u32[]{:S(2)}, u32[]{:S(2)}) collective-permute-start(bf16[768,128]{1,0:T(8,128)(2,1)S(1)} %add_convert_fusion.2), channel_id=1, source_target_pairs={{0,64},{16,208},{32,96},{48,240},{64,128},{80,16},{96,160},{112,48... | collective-permute-start | bytes 589832 | tf_op jit(solution)/shard_map/ppermute | solution.py:197
  49.6 6.0 %collective-permute-start.6 = (bf16[768,128]{1,0:T(8,128)(2,1)S(1)}, bf16[768,128]{1,0:T(8,128)(2,1)S(1)}, u32[]{:S(2)}, u32[]{:S(2)}) collective-permute-start(bf16[768,128]{1,0:T(8,128)(2,1)S(1)} %add_convert_fusion.1), channel_id=1, source_target_pairs={{0,192},{16,80},{32,224},{48,112},{64,0},{80,144},{96,32},{112,176... | collective-permute-start | bytes 589832 | tf_op jit(solution)/shard_map/ppermute | solution.py:197
  55.7 4.8 %collective-permute-start.9 = (bf16[128,256]{1,0:T(8,128)(2,1)S(1)}, bf16[128,256]{1,0:T(8,128)(2,1)S(1)}, u32[]{:S(2)}, u32[]{:S(2)}) collective-permute-start(bf16[128,256]{1,0:T(8,128)(2,1)S(1)} %slice.67), channel_id=1, source_target_pairs={{16,0},{32,16},{48,32},{64,48},{80,64},{96,80},{112,96},{128,112},... | collective-permute-start | bytes 196616 | tf_op jit(solution)/shard_map/ppermute | solution.py:244
  60.4 0.0 collective-permute-done.7
  60.5 0.0 collective-permute-done.8
  60.5 1.3 %collective-permute-done.5 = bf16[768,128]{1,0:T(8,128)(2,1)S(1)} collective-permute-done((bf16[768,128]{1,0:T(8,128)(2,1)S(1)}, bf16[768,128]{1,0:T(8,128)(2,1)S(1)}, u32[]{:S(2)}, u32[]{:S(2)}) %collective-permute-start.5) | collective-permute-done | bytes 196640 | tf_op jit(solution)/shard_map/ppermute | solution.py:197
  61.8 0.0 collective-permute-done.6
  61.8 0.8 add_convert_fusion
  62.6 0.0 collective-permute-done.9.back_ref
  62.6 7.5 %all-to-all-start = ((bf16[3,256,128]{2,1,0:T(8,128)(2,1)}), bf16[3,256,128]{2,1,0:T(8,128)(2,1)S(1)}, u32[]{:S(2)}, u32[]{:S(2)}) async-start(bf16[3,256,128]{2,1,0:T(8,128)(2,1)} %bitcast), calls=%async_computation | async-start | bytes 393216 | tf_op jit(solution)/shard_map/all_to_all | solution.py:247
  70.1 0.0 copy-done.1
  70.1 0.0 copy-done.2
  70.1 0.0 copy-done.3
  70.1 3.8 %shard_map.107 = (bf16[384,256]{1,0:T(8,128)(2,1)}, bf16[384,256]{1,0:T(8,128)(2,1)}, bf16[384,256]{1,0:T(8,128)(2,1)}) custom-call(s32[8,384]{1,0:T(8,128)S(1)} %get-tuple-element.30.same_ref, s32[8,128]{1,0:T(8,128)S(1)} %get-tuple-element.31.stays_ref, bf16[384,256]{1,0:T(8,128)(2,1)S(1)} %copy-done.1, bf16[384,256]{1,0:T(8,128)(2,1)S(1)} %copy-done.2, ...), custom_call_target="tpu_custom_call" | custom-call | tf_op jit(solution)/shard_map/pallas_call | solution.py:180
  73.9 6.0 %all-to-all-done = bf16[3,256,128]{2,1,0:T(8,128)(2,1)S(1)} async-done(((bf16[3,256,128]{2,1,0:T(8,128)(2,1)}), bf16[3,256,128]{2,1,0:T(8,128)(2,1)S(1)}, u32[]{:S(2)}, u32[]{:S(2)}) %all-to-all-start) | async-done | bytes 196640 | tf_op jit(solution)/shard_map/all_to_all | solution.py:247
  79.8 0.7 add_bitcast_fusion
  (1 shorter events, 0.0 us)
Async XLA Ops:
  2.4 19.1 %collective-permute-start = (bf16[256,128]{1,0:T(8,128)(2,1)S(1)}, bf16[256,128]{1,0:T(8,128)(2,1)S(1)}, u32[]{:S(2)}, u32[]{:S(2)}) collective-permute-start(bf16[256,128]{1,0:T(8,128)(2,1)S(1)} %get-tuple-element.39), channel_id=1, source_target_pairs={{0,16},{16,32},{32,48},{48,64},{64,80},{80,96},{96,112},{112,128},... | collective-permute-start | bytes 196616 | tf_op jit(solution)/shard_map/ppermute | solution.py:224
  4.3 3.7 %copy-start = (bf16[256,6144]{1,0:T(8,128)(2,1)S(1)}, bf16[256,6144]{1,0:T(8,128)(2,1)}, u32[]{:S(2)}) copy-start(bf16[256,6144]{1,0:T(8,128)(2,1)} %w_ref.1) | copy-start | bytes 9437188
  22.8 5.3 %collective-permute-start.1 = (bf16[6144,128]{1,0:T(8,128)(2,1)S(1)}, bf16[6144,128]{1,0:T(8,128)(2,1)S(1)}, u32[]{:S(2)}, u32[]{:S(2)}) collective-permute-start(bf16[6144,128]{1,0:T(8,128)(2,1)S(1)} %shard_map.106), channel_id=1, source_target_pairs={{0,16},{16,0},{32,48},{48,32},{64,80},{80,64},{96,112},{112,96},{1... | collective-permute-start | bytes 4718600 | tf_op jit(solution)/shard_map/ppermute | solution.py:197
  28.5 41.6 %copy-start.1 = (bf16[384,256]{1,0:T(8,128)(2,1)S(1)}, bf16[384,256]{1,0:T(8,128)(2,1)}, u32[]{:S(2)}) copy-start(bf16[384,256]{1,0:T(8,128)(2,1)} %q_ref.1) | copy-start | bytes 589828
  28.5 41.6 %copy-start.2 = (bf16[384,256]{1,0:T(8,128)(2,1)S(1)}, bf16[384,256]{1,0:T(8,128)(2,1)}, u32[]{:S(2)}) copy-start(bf16[384,256]{1,0:T(8,128)(2,1)} %k_ref.1) | copy-start | bytes 589828
  28.6 41.5 %copy-start.3 = (bf16[384,256]{1,0:T(8,128)(2,1)S(1)}, bf16[384,256]{1,0:T(8,128)(2,1)}, u32[]{:S(2)}) copy-start(bf16[384,256]{1,0:T(8,128)(2,1)} %v_ref.1) | copy-start | bytes 589828
  28.6 15.0 %collective-permute-start.4 = (bf16[768,128]{1,0:T(8,128)(2,1)S(1)}, bf16[768,128]{1,0:T(8,128)(2,1)S(1)}, u32[]{:S(2)}, u32[]{:S(2)}) collective-permute-start(bf16[768,128]{1,0:T(8,128)(2,1)S(1)} %get-tuple-element.45), channel_id=1, source_target_pairs={{0,224},{16,48},{32,0},{48,80},{64,32},{80,112},{96,64},{112,144},... | collective-permute-start | bytes 589832 | tf_op jit(solution)/shard_map/ppermute | solution.py:197
  30.6 13.0 %collective-permute-start.2 = (bf16[768,128]{1,0:T(8,128)(2,1)S(1)}, bf16[768,128]{1,0:T(8,128)(2,1)S(1)}, u32[]{:S(2)}, u32[]{:S(2)}) collective-permute-start(bf16[768,128]{1,0:T(8,128)(2,1)S(1)} %get-tuple-element.42), channel_id=1, source_target_pairs={{0,32},{16,240},{32,64},{48,16},{64,96},{80,48},{96,128},{112,80},... | collective-permute-start | bytes 589832 | tf_op jit(solution)/shard_map/ppermute | solution.py:197
  34.6 13.0 %collective-permute-start.3 = (bf16[768,128]{1,0:T(8,128)(2,1)S(1)}, bf16[768,128]{1,0:T(8,128)(2,1)S(1)}, u32[]{:S(2)}, u32[]{:S(2)}) collective-permute-start(bf16[768,128]{1,0:T(8,128)(2,1)S(1)} %get-tuple-element.43), channel_id=1, source_target_pairs={{0,64},{16,208},{32,96},{48,240},{64,128},{80,16},{96,160},{112,48... | collective-permute-start | bytes 589832 | tf_op jit(solution)/shard_map/ppermute | solution.py:197
  36.5 23.9 %collective-permute-start.7 = (bf16[768,128]{1,0:T(8,128)(2,1)S(1)}, bf16[768,128]{1,0:T(8,128)(2,1)S(1)}, u32[]{:S(2)}, u32[]{:S(2)}) collective-permute-start(bf16[768,128]{1,0:T(8,128)(2,1)S(1)} %get-tuple-element.48), channel_id=1, source_target_pairs={{0,32},{16,240},{32,64},{48,16},{64,96},{80,48},{96,128},{112,80},... | collective-permute-start | bytes 589832 | tf_op jit(solution)/shard_map/ppermute | solution.py:197
  38.4 22.0 %collective-permute-start.8 = (bf16[768,128]{1,0:T(8,128)(2,1)S(1)}, bf16[768,128]{1,0:T(8,128)(2,1)S(1)}, u32[]{:S(2)}, u32[]{:S(2)}) collective-permute-start(bf16[768,128]{1,0:T(8,128)(2,1)S(1)} %get-tuple-element.49), channel_id=1, source_target_pairs={{0,224},{16,48},{32,0},{48,80},{64,32},{80,112},{96,64},{112,144},... | collective-permute-start | bytes 589832 | tf_op jit(solution)/shard_map/ppermute | solution.py:197
  47.7 14.1 %collective-permute-start.5 = (bf16[768,128]{1,0:T(8,128)(2,1)S(1)}, bf16[768,128]{1,0:T(8,128)(2,1)S(1)}, u32[]{:S(2)}, u32[]{:S(2)}) collective-permute-start(bf16[768,128]{1,0:T(8,128)(2,1)S(1)} %add_convert_fusion.2), channel_id=1, source_target_pairs={{0,64},{16,208},{32,96},{48,240},{64,128},{80,16},{96,160},{112,48... | collective-permute-start | bytes 589832 | tf_op jit(solution)/shard_map/ppermute | solution.py:197
  49.6 12.2 %collective-permute-start.6 = (bf16[768,128]{1,0:T(8,128)(2,1)S(1)}, bf16[768,128]{1,0:T(8,128)(2,1)S(1)}, u32[]{:S(2)}, u32[]{:S(2)}) collective-permute-start(bf16[768,128]{1,0:T(8,128)(2,1)S(1)} %add_convert_fusion.1), channel_id=1, source_target_pairs={{0,192},{16,80},{32,224},{48,112},{64,0},{80,144},{96,32},{112,176... | collective-permute-start | bytes 589832 | tf_op jit(solution)/shard_map/ppermute | solution.py:197
  55.7 7.0 %collective-permute-start.9 = (bf16[128,256]{1,0:T(8,128)(2,1)S(1)}, bf16[128,256]{1,0:T(8,128)(2,1)S(1)}, u32[]{:S(2)}, u32[]{:S(2)}) collective-permute-start(bf16[128,256]{1,0:T(8,128)(2,1)S(1)} %slice.67), channel_id=1, source_target_pairs={{16,0},{32,16},{48,32},{64,48},{80,64},{96,80},{112,96},{128,112},... | collective-permute-start | bytes 196616 | tf_op jit(solution)/shard_map/ppermute | solution.py:244
  62.6 17.2 %all-to-all-start = ((bf16[3,256,128]{2,1,0:T(8,128)(2,1)}), bf16[3,256,128]{2,1,0:T(8,128)(2,1)S(1)}, u32[]{:S(2)}, u32[]{:S(2)}) async-start(bf16[3,256,128]{2,1,0:T(8,128)(2,1)} %bitcast), calls=%async_computation | async-start | bytes 393216 | tf_op jit(solution)/shard_map/all_to_all | solution.py:247

commit v11 on v10

--- a/solution.py
+++ b/solution.py
@@ -234,18 +234,19 @@
     got = send(partial_grad(True, stay, came, g_near), sibling)
     own = partial_grad(False, stay, came, g_near)
     parts = [rounded_total(*pair) for pair in zip(cut(own), cut(got), strict=True)]
-    part = dict(zip(ORDER, lax.optimization_barrier(parts), strict=True))
+    *parts, tail = lax.optimization_barrier((*parts, grad_ctx[row_count:]))
+    part = dict(zip(ORDER, parts, strict=True))
     far, up, down = send(part[4], along_y(2)), send(part[3], along_y(1)), send(part[-3], along_y(-1))
     near = send(part[1], along_y(1)), send(part[-1], along_y(-1))
+    back = lax.ppermute(tail, "dp", [((i + 1) % ranks, i) for i in range(ranks)])
 
     up, down = rounded_total(part[2], up, far), rounded_total(part[-2], down)
-    up, down, tail = lax.optimization_barrier((up, down, grad_ctx[row_count:]))
+    down, back = lax.optimization_barrier((down, back))
     up, down = send(up, along_y(2)), send(down, along_y(-2))
-    back = lax.ppermute(tail, "dp", [((i + 1) % ranks, i) for i in range(ranks)])
     sums = rounded_total(part[0], up, down, *near).reshape(NZ, -1, UNIT)
-    sums, back = lax.optimization_barrier((sums, back))
+    grads = backward(same, stays, queries, key_rows, value_rows, grad_ctx, back)
+    sums, *grads = lax.optimization_barrier((sums, *grads))
     sums = lax.all_to_all(sums, "dp", 0, 0, axis_index_groups=same_place())
-    grads = backward(same, stays, queries, key_rows, value_rows, grad_ctx, back)
     grad_weight = total(*sums)
     return (*grads, grad_weight)
 

time: 81.3 us -> 84 us (1.033)
  blocking collectives: 0 us -> 13.5 us
  waiting for transfers between devices: 24.9 us -> 17.3 us
  starting transfers between devices: 39 us -> 35.7 us
    all_to_all x0 -> x1, blocking collectives: none -> 13.5 us  [local(): sums = lax.all_to_all(sums, 'dp', 0, 0, axis_index_groups=same_place())]
    all_to_all x1 -> x0, starting transfers between devices: 7.48 us -> none  [local(): sums = lax.all_to_all(sums, 'dp', 0, 0, axis_index_groups=same_place())]
    ppermute x1, starting transfers between devices: 4.78 us -> 11.1 us  [local(): lax.ppermute(tail, 'dp', [((i + 1) % ranks, i) for i in range(ranks)])]
    all_to_all x1 -> x0, waiting for transfers between devices: 5.97 us -> none  [local(): sums = lax.all_to_all(sums, 'dp', 0, 0, axis_index_groups=same_place())]
    ppermute x8, starting transfers between devices: 24.8 us -> 22.7 us  [send(): lax.ppermute(block, 'dp', [(index(*p), index(*to(*p))) for p in PLACES])]
    ppermute x8, waiting for transfers between devices: 7.27 us -> 5.69 us  [send(): lax.ppermute(block, 'dp', [(index(*p), index(*to(*p))) for p in PLACES])]
  transfers between devices with their start and end apart: 11 -> 10, of which waited for: 5 -> 4; matrix products, arithmetic and copies ran while one was open for 1% -> 0% of each run, Pallas kernels for 12% -> 12%
where the time goes in v11:
time: 84 us; the launch traced here: 82.5 us
  starting transfers between devices  35.7 us (43%)
  waiting for transfers between devices  17.3 us (21%)
  blocking collectives  13.5 us (16%)
  Pallas kernels  13 us (15%)
  other arithmetic  1.36 us (2%)
  between operations  0.85 us (1%)
    ppermute x8, starting transfers between devices, send(): lax.ppermute(block, 'dp', [(index(*p), index(*to(*p))) for p in PLACES])  22.7 us
    all_to_all x1, blocking collectives, local(): sums = lax.all_to_all(sums, 'dp', 0, 0, axis_index_groups=same_place())  13.5 us
    ppermute x1, waiting for transfers between devices, local(): lax.ppermute(leave, 'dp', [(i, (i + 1) % ranks) for i in range(ranks)])  11.6 us
    ppermute x1, starting transfers between devices, local(): lax.ppermute(tail, 'dp', [((i + 1) % ranks, i) for i in range(ranks)])  11.1 us
    ppermute x8, waiting for transfers between devices, send(): lax.ppermute(block, 'dp', [(index(*p), index(*to(*p))) for p in PLACES])  5.69 us
    pallas_call x1, Pallas kernels, backward(): pl.pallas_call(backward_kernel, in_specs=[VMEM] * 7, out_specs=[VMEM] * 3...  3.77 us
    pallas_call x1, Pallas kernels, staying_context(): pl.pallas_call(context_kernel, in_specs=[VMEM] * 5 + [pl.BlockSpec(memory...  2.95 us
    pallas_call x2, Pallas kernels, partial_grad(): pl.pallas_call(functools.partial(partial_kernel, other), in_specs=[VMEM,...  2.75 us
  transfers between devices with their start and end apart: 10, of which 4 were waited for; matrix products, arithmetic and copies ran while one was open for 0% of the time, Pallas kernels for 12%

profile of v11, /device:TPU:6, one launch (start us, length us, event | category | flops | bytes accessed | tf_op | source)
XLA Modules:
  0.0 82.5 jit_solution(12093499934523298045)
XLA Ops:
  0.6 1.7 %shard_map.102 = (bf16[256,128]{1,0:T(8,128)(2,1)S(1)}, s32[8,384]{1,0:T(8,128)S(1)}, s32[8,128]{1,0:T(8,128)S(1)}, bf16[384,256]{1,0:T(8,128)(2,1)S(1)}, bf16[3...) custom-call(s32[384]{0:T(512)} %ids_hbm.1, s32[384]{0:T(512)} %slot_hbm.1, bf16[384,256]{1,0:T(8,128)(2,1)} %q_ref.1, ...), custom_call_target="tpu_custom_call" | custom-call | tf_op jit(solution)/shard_map/pallas_call | solution.py:68
  2.4 1.9 %collective-permute-start = (bf16[256,128]{1,0:T(8,128)(2,1)S(1)}, bf16[256,128]{1,0:T(8,128)(2,1)S(1)}, u32[]{:S(2)}, u32[]{:S(2)}) collective-permute-start(bf16[256,128]{1,0:T(8,128)(2,1)S(1)} %get-tuple-element.40), channel_id=1, source_target_pairs={{0,16},{16,32},{32,48},{48,64},{64,80},{80,96},{96,112},{112,128},... | collective-permute-start | bytes 196616 | tf_op jit(solution)/shard_map/ppermute | solution.py:224
  4.3 0.0 copy-start
  4.3 2.9 %shard_map.103 = (bf16[256,384]{1,0:T(8,128)(2,1)S(1)}, bf16[512,6144]{1,0:T(8,128)(2,1)S(1)}) custom-call(s32[8,384]{1,0:T(8,128)S(1)} %get-tuple-element.32.same_ref, s32[8,128]{1,0:T(8,128)S(1)} %get-tuple-element.33.stays_ref, bf16[384,256]{1,0:T(8,128)(2,1)S(1)} %get-tuple-element.34.q_ref, bf16[384,256]{1,0:T(8,128)(2,1)S(1)} %get-tuple-element.35.k_ref, ...), custom_call_target="tpu_custom_call" | custom-call | tf_op jit(solution)/shard_map/pallas_call | solution.py:98
  7.3 0.7 copy-done
  8.0 1.8 %shard_map.104.g_ref = bf16[512,256]{1,0:T(8,128)(2,1)S(1)} custom-call(bf16[512,6144]{1,0:T(8,128)(2,1)S(1)} %get-tuple-element.38.g_ref, bf16[256,6144]{1,0:T(8,128)(2,1)S(1)} %copy-done), custom_call_target="tpu_custom_call" | custom-call | tf_op jit(solution)/shard_map/pallas_call | solution.py:148
  9.8 11.6 %collective-permute-done.came_ref = bf16[256,128]{1,0:T(8,128)(2,1)S(1)} collective-permute-done((bf16[256,128]{1,0:T(8,128)(2,1)S(1)}, bf16[256,128]{1,0:T(8,128)(2,1)S(1)}, u32[]{:S(2)}, u32[]{:S(2)}) %collective-permute-start) | collective-permute-done | bytes 65568 | tf_op jit(solution)/shard_map/ppermute | solution.py:224
  21.5 1.3 %shard_map.106 = bf16[6144,128]{1,0:T(8,128)(2,1)S(1)} custom-call(bf16[256,384]{1,0:T(8,128)(2,1)S(1)} %get-tuple-element.39.stay_ref, bf16[256,128]{1,0:T(8,128)(2,1)S(1)} %collective-permute-done.came_ref, bf16[512,6144]{1,0:T(8,128)(2,1)S(1)} %get-tuple-element.38.g_ref), custom_call_target="tpu_custom_call" | custom-call | tf_op jit(solution)/shard_map/pallas_call | solution.py:129
  22.8 1.9 %collective-permute-start.1 = (bf16[6144,128]{1,0:T(8,128)(2,1)S(1)}, bf16[6144,128]{1,0:T(8,128)(2,1)S(1)}, u32[]{:S(2)}, u32[]{:S(2)}) collective-permute-start(bf16[6144,128]{1,0:T(8,128)(2,1)S(1)} %shard_map.106), channel_id=1, source_target_pairs={{0,16},{16,0},{32,48},{48,32},{64,80},{80,64},{96,112},{112,96},{1... | collective-permute-start | bytes 4718600 | tf_op jit(solution)/shard_map/ppermute | solution.py:197
  24.8 1.4 %shard_map.105 = bf16[6144,128]{1,0:T(8,128)(2,1)S(1)} custom-call(bf16[256,384]{1,0:T(8,128)(2,1)S(1)} %get-tuple-element.39.stay_ref, bf16[256,128]{1,0:T(8,128)(2,1)S(1)} %collective-permute-done.came_ref, bf16[512,6144]{1,0:T(8,128)(2,1)S(1)} %get-tuple-element.38.g_ref), custom_call_target="tpu_custom_call" | custom-call | tf_op jit(solution)/shard_map/pallas_call | solution.py:129
  26.2 0.0 copy-start.1
  26.2 0.0 copy-start.2
  26.2 0.0 copy-start.3
  26.2 1.9 %collective-permute-done.1 = bf16[6144,128]{1,0:T(8,128)(2,1)S(1)} collective-permute-done((bf16[6144,128]{1,0:T(8,128)(2,1)S(1)}, bf16[6144,128]{1,0:T(8,128)(2,1)S(1)}, u32[]{:S(2)}, u32[]{:S(2)}) %collective-permute-start.1) | collective-permute-done | bytes 1572896 | tf_op jit(solution)/shard_map/ppermute | solution.py:197
  28.1 0.4 add_convert_fusion.3
  28.5 1.9 %collective-permute-start.5 = (bf16[768,128]{1,0:T(8,128)(2,1)S(1)}, bf16[768,128]{1,0:T(8,128)(2,1)S(1)}, u32[]{:S(2)}, u32[]{:S(2)}) collective-permute-start(bf16[768,128]{1,0:T(8,128)(2,1)S(1)} %get-tuple-element.47), channel_id=1, source_target_pairs={{0,224},{16,48},{32,0},{48,80},{64,32},{80,112},{96,64},{112,144},... | collective-permute-start | bytes 589832 | tf_op jit(solution)/shard_map/ppermute | solution.py:197
  30.5 11.1 %collective-permute-start.6 = (bf16[128,256]{1,0:T(8,128)(2,1)S(1)}, bf16[128,256]{1,0:T(8,128)(2,1)S(1)}, u32[]{:S(2)}, u32[]{:S(2)}) collective-permute-start(bf16[128,256]{1,0:T(8,128)(2,1)S(1)} %slice.67), channel_id=1, source_target_pairs={{16,0},{32,16},{48,32},{64,48},{80,64},{96,80},{112,96},{128,112},... | collective-permute-start | bytes 196616 | tf_op jit(solution)/shard_map/ppermute | solution.py:241
  41.5 1.9 %collective-permute-start.2 = (bf16[768,128]{1,0:T(8,128)(2,1)S(1)}, bf16[768,128]{1,0:T(8,128)(2,1)S(1)}, u32[]{:S(2)}, u32[]{:S(2)}) collective-permute-start(bf16[768,128]{1,0:T(8,128)(2,1)S(1)} %get-tuple-element.44), channel_id=1, source_target_pairs={{0,32},{16,240},{32,64},{48,16},{64,96},{80,48},{96,128},{112,80},... | collective-permute-start | bytes 589832 | tf_op jit(solution)/shard_map/ppermute | solution.py:197
  43.5 1.9 %collective-permute-start.3 = (bf16[768,128]{1,0:T(8,128)(2,1)S(1)}, bf16[768,128]{1,0:T(8,128)(2,1)S(1)}, u32[]{:S(2)}, u32[]{:S(2)}) collective-permute-start(bf16[768,128]{1,0:T(8,128)(2,1)S(1)} %get-tuple-element.45), channel_id=1, source_target_pairs={{0,64},{16,208},{32,96},{48,240},{64,128},{80,16},{96,160},{112,48... | collective-permute-start | bytes 589832 | tf_op jit(solution)/shard_map/ppermute | solution.py:197
  45.4 1.9 %collective-permute-start.8 = (bf16[768,128]{1,0:T(8,128)(2,1)S(1)}, bf16[768,128]{1,0:T(8,128)(2,1)S(1)}, u32[]{:S(2)}, u32[]{:S(2)}) collective-permute-start(bf16[768,128]{1,0:T(8,128)(2,1)S(1)} %get-tuple-element.50), channel_id=1, source_target_pairs={{0,32},{16,240},{32,64},{48,16},{64,96},{80,48},{96,128},{112,80},... | collective-permute-start | bytes 589832 | tf_op jit(solution)/shard_map/ppermute | solution.py:197
  47.3 0.0 collective-permute-done.5
  47.3 5.1 %collective-permute-start.9 = (bf16[768,128]{1,0:T(8,128)(2,1)S(1)}, bf16[768,128]{1,0:T(8,128)(2,1)S(1)}, u32[]{:S(2)}, u32[]{:S(2)}) collective-permute-start(bf16[768,128]{1,0:T(8,128)(2,1)S(1)} %get-tuple-element.51), channel_id=1, source_target_pairs={{0,224},{16,48},{32,0},{48,80},{64,32},{80,112},{96,64},{112,144},... | collective-permute-start | bytes 589832 | tf_op jit(solution)/shard_map/ppermute | solution.py:197
  52.5 0.1 add_convert_fusion.1
  52.5 0.0 collective-permute-done.6.back_ref
  52.5 0.0 collective-permute-done.2
  52.6 3.3 %collective-permute-done.3 = bf16[768,128]{1,0:T(8,128)(2,1)S(1)} collective-permute-done((bf16[768,128]{1,0:T(8,128)(2,1)S(1)}, bf16[768,128]{1,0:T(8,128)(2,1)S(1)}, u32[]{:S(2)}, u32[]{:S(2)}) %collective-permute-start.3) | collective-permute-done | bytes 196640 | tf_op jit(solution)/shard_map/ppermute | solution.py:197
  55.8 0.1 add_convert_fusion.2
  55.9 1.9 %collective-permute-start.4 = (bf16[768,128]{1,0:T(8,128)(2,1)S(1)}, bf16[768,128]{1,0:T(8,128)(2,1)S(1)}, u32[]{:S(2)}, u32[]{:S(2)}) collective-permute-start(bf16[768,128]{1,0:T(8,128)(2,1)S(1)} %add_convert_fusion.2), channel_id=1, source_target_pairs={{0,64},{16,208},{32,96},{48,240},{64,128},{80,16},{96,160},{112,48... | collective-permute-start | bytes 589832 | tf_op jit(solution)/shard_map/ppermute | solution.py:197
  57.8 6.0 %collective-permute-start.7 = (bf16[768,128]{1,0:T(8,128)(2,1)S(1)}, bf16[768,128]{1,0:T(8,128)(2,1)S(1)}, u32[]{:S(2)}, u32[]{:S(2)}) collective-permute-start(bf16[768,128]{1,0:T(8,128)(2,1)S(1)} %add_convert_fusion.1), channel_id=1, source_target_pairs={{0,192},{16,80},{32,224},{48,112},{64,0},{80,144},{96,32},{112,176... | collective-permute-start | bytes 589832 | tf_op jit(solution)/shard_map/ppermute | solution.py:197
  63.9 0.0 copy-done.1
  63.9 0.0 copy-done.2
  63.9 0.0 copy-done.3
  63.9 3.8 %shard_map.107 = (bf16[384,256]{1,0:T(8,128)(2,1)}, bf16[384,256]{1,0:T(8,128)(2,1)}, bf16[384,256]{1,0:T(8,128)(2,1)}) custom-call(s32[8,384]{1,0:T(8,128)S(1)} %get-tuple-element.32.same_ref, s32[8,128]{1,0:T(8,128)S(1)} %get-tuple-element.33.stays_ref, bf16[384,256]{1,0:T(8,128)(2,1)S(1)} %copy-done.1, bf16[384,256]{1,0:T(8,128)(2,1)S(1)} %copy-done.2, ...), custom_call_target="tpu_custom_call" | custom-call | tf_op jit(solution)/shard_map/pallas_call | solution.py:180
  67.7 0.0 collective-permute-done.8
  67.7 0.0 collective-permute-done.9
  67.7 0.0 collective-permute-done.4
  67.7 0.5 collective-permute-done.7
  68.2 0.1 add_convert_fusion
  68.3 13.5 %all_to_all.5 = bf16[3,256,128]{2,1,0:T(8,128)(2,1)S(1)} all-to-all(bf16[3,256,128]{2,1,0:T(8,128)(2,1)S(1)} %bitcast.3), channel_id=1, replica_groups={{0,256,512},{16,272,528},{32,288,544},{48,304,560},{64,320,576},{80,336..., dimensions={0} | all-to-all | bytes 393216 | tf_op jit(solution)/shard_map/all_to_all | solution.py:249
  81.8 0.7 add_bitcast_fusion
  (1 shorter events, 0.0 us)
Async XLA Ops:
  2.4 19.1 %collective-permute-start = (bf16[256,128]{1,0:T(8,128)(2,1)S(1)}, bf16[256,128]{1,0:T(8,128)(2,1)S(1)}, u32[]{:S(2)}, u32[]{:S(2)}) collective-permute-start(bf16[256,128]{1,0:T(8,128)(2,1)S(1)} %get-tuple-element.40), channel_id=1, source_target_pairs={{0,16},{16,32},{32,48},{48,64},{64,80},{80,96},{96,112},{112,128},... | collective-permute-start | bytes 196616 | tf_op jit(solution)/shard_map/ppermute | solution.py:224
  4.3 3.7 %copy-start = (bf16[256,6144]{1,0:T(8,128)(2,1)S(1)}, bf16[256,6144]{1,0:T(8,128)(2,1)}, u32[]{:S(2)}) copy-start(bf16[256,6144]{1,0:T(8,128)(2,1)} %w_ref.1) | copy-start | bytes 9437188
  22.8 5.3 %collective-permute-start.1 = (bf16[6144,128]{1,0:T(8,128)(2,1)S(1)}, bf16[6144,128]{1,0:T(8,128)(2,1)S(1)}, u32[]{:S(2)}, u32[]{:S(2)}) collective-permute-start(bf16[6144,128]{1,0:T(8,128)(2,1)S(1)} %shard_map.106), channel_id=1, source_target_pairs={{0,16},{16,0},{32,48},{48,32},{64,80},{80,64},{96,112},{112,96},{1... | collective-permute-start | bytes 4718600 | tf_op jit(solution)/shard_map/ppermute | solution.py:197
  26.2 37.7 %copy-start.1 = (bf16[384,256]{1,0:T(8,128)(2,1)S(1)}, bf16[384,256]{1,0:T(8,128)(2,1)}, u32[]{:S(2)}) copy-start(bf16[384,256]{1,0:T(8,128)(2,1)} %q_ref.1) | copy-start | bytes 589828
  26.2 37.7 %copy-start.2 = (bf16[384,256]{1,0:T(8,128)(2,1)S(1)}, bf16[384,256]{1,0:T(8,128)(2,1)}, u32[]{:S(2)}) copy-start(bf16[384,256]{1,0:T(8,128)(2,1)} %k_ref.1) | copy-start | bytes 589828
  26.2 37.7 %copy-start.3 = (bf16[384,256]{1,0:T(8,128)(2,1)S(1)}, bf16[384,256]{1,0:T(8,128)(2,1)}, u32[]{:S(2)}) copy-start(bf16[384,256]{1,0:T(8,128)(2,1)} %v_ref.1) | copy-start | bytes 589828
  28.5 18.8 %collective-permute-start.5 = (bf16[768,128]{1,0:T(8,128)(2,1)S(1)}, bf16[768,128]{1,0:T(8,128)(2,1)S(1)}, u32[]{:S(2)}, u32[]{:S(2)}) collective-permute-start(bf16[768,128]{1,0:T(8,128)(2,1)S(1)} %get-tuple-element.47), channel_id=1, source_target_pairs={{0,224},{16,48},{32,0},{48,80},{64,32},{80,112},{96,64},{112,144},... | collective-permute-start | bytes 589832 | tf_op jit(solution)/shard_map/ppermute | solution.py:197
  30.5 22.1 %collective-permute-start.6 = (bf16[128,256]{1,0:T(8,128)(2,1)S(1)}, bf16[128,256]{1,0:T(8,128)(2,1)S(1)}, u32[]{:S(2)}, u32[]{:S(2)}) collective-permute-start(bf16[128,256]{1,0:T(8,128)(2,1)S(1)} %slice.67), channel_id=1, source_target_pairs={{16,0},{32,16},{48,32},{64,48},{80,64},{96,80},{112,96},{128,112},... | collective-permute-start | bytes 196616 | tf_op jit(solution)/shard_map/ppermute | solution.py:241
  41.5 11.0 %collective-permute-start.2 = (bf16[768,128]{1,0:T(8,128)(2,1)S(1)}, bf16[768,128]{1,0:T(8,128)(2,1)S(1)}, u32[]{:S(2)}, u32[]{:S(2)}) collective-permute-start(bf16[768,128]{1,0:T(8,128)(2,1)S(1)} %get-tuple-element.44), channel_id=1, source_target_pairs={{0,32},{16,240},{32,64},{48,16},{64,96},{80,48},{96,128},{112,80},... | collective-permute-start | bytes 589832 | tf_op jit(solution)/shard_map/ppermute | solution.py:197
  43.5 12.4 %collective-permute-start.3 = (bf16[768,128]{1,0:T(8,128)(2,1)S(1)}, bf16[768,128]{1,0:T(8,128)(2,1)S(1)}, u32[]{:S(2)}, u32[]{:S(2)}) collective-permute-start(bf16[768,128]{1,0:T(8,128)(2,1)S(1)} %get-tuple-element.45), channel_id=1, source_target_pairs={{0,64},{16,208},{32,96},{48,240},{64,128},{80,16},{96,160},{112,48... | collective-permute-start | bytes 589832 | tf_op jit(solution)/shard_map/ppermute | solution.py:197
  45.4 22.3 %collective-permute-start.8 = (bf16[768,128]{1,0:T(8,128)(2,1)S(1)}, bf16[768,128]{1,0:T(8,128)(2,1)S(1)}, u32[]{:S(2)}, u32[]{:S(2)}) collective-permute-start(bf16[768,128]{1,0:T(8,128)(2,1)S(1)} %get-tuple-element.50), channel_id=1, source_target_pairs={{0,32},{16,240},{32,64},{48,16},{64,96},{80,48},{96,128},{112,80},... | collective-permute-start | bytes 589832 | tf_op jit(solution)/shard_map/ppermute | solution.py:197
  47.3 20.3 %collective-permute-start.9 = (bf16[768,128]{1,0:T(8,128)(2,1)S(1)}, bf16[768,128]{1,0:T(8,128)(2,1)S(1)}, u32[]{:S(2)}, u32[]{:S(2)}) collective-permute-start(bf16[768,128]{1,0:T(8,128)(2,1)S(1)} %get-tuple-element.51), channel_id=1, source_target_pairs={{0,224},{16,48},{32,0},{48,80},{64,32},{80,112},{96,64},{112,144},... | collective-permute-start | bytes 589832 | tf_op jit(solution)/shard_map/ppermute | solution.py:197
  55.9 11.8 %collective-permute-start.4 = (bf16[768,128]{1,0:T(8,128)(2,1)S(1)}, bf16[768,128]{1,0:T(8,128)(2,1)S(1)}, u32[]{:S(2)}, u32[]{:S(2)}) collective-permute-start(bf16[768,128]{1,0:T(8,128)(2,1)S(1)} %add_convert_fusion.2), channel_id=1, source_target_pairs={{0,64},{16,208},{32,96},{48,240},{64,128},{80,16},{96,160},{112,48... | collective-permute-start | bytes 589832 | tf_op jit(solution)/shard_map/ppermute | solution.py:197
  57.8 10.3 %collective-permute-start.7 = (bf16[768,128]{1,0:T(8,128)(2,1)S(1)}, bf16[768,128]{1,0:T(8,128)(2,1)S(1)}, u32[]{:S(2)}, u32[]{:S(2)}) collective-permute-start(bf16[768,128]{1,0:T(8,128)(2,1)S(1)} %add_convert_fusion.1), channel_id=1, source_target_pairs={{0,192},{16,80},{32,224},{48,112},{64,0},{80,144},{96,32},{112,176... | collective-permute-start | bytes 589832 | tf_op jit(solution)/shard_map/ppermute | solution.py:197

commit v12 on v10

--- a/solution.py
+++ b/solution.py
@@ -10,7 +10,7 @@
 HD = 128
 UNIT = 128
 NZ, NY, NC = 3, 8, 2
-ORDER = (4, 3, -3, 2, -2, 1, -1, 0)
+ORDER = (4, 3, 1, -3, -1, 2, -2, 0)
 VMEM = pl.BlockSpec(memory_space=pltpu.VMEM)
 PARAMS = pltpu.CompilerParams(vmem_limit_bytes=8 * 1024 * 1024)
 
@@ -228,21 +228,21 @@
 
     size = NZ * width
 
-    def cut(x):
-        return [x[i : i + size] for i in range(0, x.shape[0], size)]
-
     got = send(partial_grad(True, stay, came, g_near), sibling)
     own = partial_grad(False, stay, came, g_near)
-    parts = [rounded_total(*pair) for pair in zip(cut(own), cut(got), strict=True)]
-    part = dict(zip(ORDER, lax.optimization_barrier(parts), strict=True))
-    far, up, down = send(part[4], along_y(2)), send(part[3], along_y(1)), send(part[-3], along_y(-1))
-    near = send(part[1], along_y(1)), send(part[-1], along_y(-1))
-
-    up, down = rounded_total(part[2], up, far), rounded_total(part[-2], down)
+    parts = []
+    for first, last in ((4, 4), (3, 1), (-3, -1), (2, 2), (-2, -2), (0, 0)):
+        rows = slice(ORDER.index(first) * size, (ORDER.index(last) + 1) * size)
+        parts.append(rounded_total(own[rows], got[rows]))
+    far, up, down, up2, down2, here = lax.optimization_barrier(parts)
+    far, up, down = send(far, along_y(2)), send(up, along_y(1)), send(down, along_y(-1))
+    near = up[size:], down[size:]
+
+    up, down = rounded_total(up2, up[:size], far), rounded_total(down2, down[:size])
     up, down, tail = lax.optimization_barrier((up, down, grad_ctx[row_count:]))
     up, down = send(up, along_y(2)), send(down, along_y(-2))
     back = lax.ppermute(tail, "dp", [((i + 1) % ranks, i) for i in range(ranks)])
-    sums = rounded_total(part[0], up, down, *near).reshape(NZ, -1, UNIT)
+    sums = rounded_total(here, up, down, *near).reshape(NZ, -1, UNIT)
     sums, back = lax.optimization_barrier((sums, back))
     sums = lax.all_to_all(sums, "dp", 0, 0, axis_index_groups=same_place())
     grads = backward(same, stays, queries, key_rows, value_rows, grad_ctx, back)

time: 81.3 us -> 84.4 us (1.038)
  waiting for transfers between devices: 24.9 us -> 31.1 us
  starting transfers between devices: 39 us -> 35.2 us
    ppermute x8 -> x6, starting transfers between devices: 24.8 us -> 17.8 us  [send(): lax.ppermute(block, 'dp', [(index(*p), index(*to(*p))) for p in PLACES])]
    ppermute x1, starting transfers between devices: 4.78 us -> 10.8 us  [local(): lax.ppermute(tail, 'dp', [((i + 1) % ranks, i) for i in range(ranks)])]
    ppermute x8 -> x6, waiting for transfers between devices: 7.27 us -> 11.4 us  [send(): lax.ppermute(block, 'dp', [(index(*p), index(*to(*p))) for p in PLACES])]
    all_to_all x1, starting transfers between devices: 7.48 us -> 4.76 us  [local(): sums = lax.all_to_all(sums, 'dp', 0, 0, axis_index_groups=same_place())]
    all_to_all x1, waiting for transfers between devices: 5.97 us -> 7.1 us  [local(): sums = lax.all_to_all(sums, 'dp', 0, 0, axis_index_groups=same_place())]
    ppermute x1, waiting for transfers between devices: 0.01 us -> 1.02 us  [local(): lax.ppermute(tail, 'dp', [((i + 1) % ranks, i) for i in range(ranks)])]
  transfers between devices with their start and end apart: 11 -> 9, of which waited for: 5 -> 6; matrix products, arithmetic and copies ran while one was open for 1% -> 1% of each run, Pallas kernels for 12% -> 12%
where the time goes in v12:
time: 84.4 us; the launch traced here: 83 us
  starting transfers between devices  35.2 us (42%)
  waiting for transfers between devices  31.1 us (37%)
  Pallas kernels  13 us (15%)
  other arithmetic  2.07 us (2%)
    ppermute x6, starting transfers between devices, send(): lax.ppermute(block, 'dp', [(index(*p), index(*to(*p))) for p in PLACES])  17.8 us
    ppermute x1, waiting for transfers between devices, local(): lax.ppermute(leave, 'dp', [(i, (i + 1) % ranks) for i in range(ranks)])  11.6 us
    ppermute x6, waiting for transfers between devices, send(): lax.ppermute(block, 'dp', [(index(*p), index(*to(*p))) for p in PLACES])  11.4 us
    ppermute x1, starting transfers between devices, local(): lax.ppermute(tail, 'dp', [((i + 1) % ranks, i) for i in range(ranks)])  10.8 us
    all_to_all x1, waiting for transfers between devices, local(): sums = lax.all_to_all(sums, 'dp', 0, 0, axis_index_groups=same_place())  7.1 us
    all_to_all x1, starting transfers between devices, local(): sums = lax.all_to_all(sums, 'dp', 0, 0, axis_index_groups=same_place())  4.76 us
    pallas_call x1, Pallas kernels, backward(): pl.pallas_call(backward_kernel, in_specs=[VMEM] * 7, out_specs=[VMEM] * 3...  3.75 us
    pallas_call x1, Pallas kernels, staying_context(): pl.pallas_call(context_kernel, in_specs=[VMEM] * 5 + [pl.BlockSpec(memory...  2.95 us
  transfers between devices with their start and end apart: 9, of which 6 were waited for; matrix products, arithmetic and copies ran while one was open for 1% of the time, Pallas kernels for 12%

profile of v12, /device:TPU:6, one launch (start us, length us, event | category | flops | bytes accessed | tf_op | source)
XLA Modules:
  0.0 83.0 jit_solution(5334615652365093085)
XLA Ops:
  0.6 1.7 %shard_map.102 = (bf16[256,128]{1,0:T(8,128)(2,1)S(1)}, s32[8,384]{1,0:T(8,128)S(1)}, s32[8,128]{1,0:T(8,128)S(1)}, bf16[384,256]{1,0:T(8,128)(2,1)S(1)}, bf16[3...) custom-call(s32[384]{0:T(512)} %ids_hbm.1, s32[384]{0:T(512)} %slot_hbm.1, bf16[384,256]{1,0:T(8,128)(2,1)} %q_ref.1, ...), custom_call_target="tpu_custom_call" | custom-call | tf_op jit(solution)/shard_map/pallas_call | solution.py:68
  2.4 1.9 %collective-permute-start = (bf16[256,128]{1,0:T(8,128)(2,1)S(1)}, bf16[256,128]{1,0:T(8,128)(2,1)S(1)}, u32[]{:S(2)}, u32[]{:S(2)}) collective-permute-start(bf16[256,128]{1,0:T(8,128)(2,1)S(1)} %get-tuple-element.37), channel_id=1, source_target_pairs={{0,16},{16,32},{32,48},{48,64},{64,80},{80,96},{96,112},{112,128},... | collective-permute-start | bytes 196616 | tf_op jit(solution)/shard_map/ppermute | solution.py:224
  4.3 0.0 copy-start
  4.3 2.9 %shard_map.103 = (bf16[256,384]{1,0:T(8,128)(2,1)S(1)}, bf16[512,6144]{1,0:T(8,128)(2,1)S(1)}) custom-call(s32[8,384]{1,0:T(8,128)S(1)} %get-tuple-element.28.same_ref, s32[8,128]{1,0:T(8,128)S(1)} %get-tuple-element.29.stays_ref, bf16[384,256]{1,0:T(8,128)(2,1)S(1)} %get-tuple-element.30.q_ref, bf16[384,256]{1,0:T(8,128)(2,1)S(1)} %get-tuple-element.31.k_ref, ...), custom_call_target="tpu_custom_call" | custom-call | tf_op jit(solution)/shard_map/pallas_call | solution.py:98
  7.3 0.7 copy-done
  8.0 1.8 %shard_map.104.g_ref = bf16[512,256]{1,0:T(8,128)(2,1)S(1)} custom-call(bf16[512,6144]{1,0:T(8,128)(2,1)S(1)} %get-tuple-element.34.g_ref, bf16[256,6144]{1,0:T(8,128)(2,1)S(1)} %copy-done), custom_call_target="tpu_custom_call" | custom-call | tf_op jit(solution)/shard_map/pallas_call | solution.py:148
  9.8 11.6 %collective-permute-done.came_ref = bf16[256,128]{1,0:T(8,128)(2,1)S(1)} collective-permute-done((bf16[256,128]{1,0:T(8,128)(2,1)S(1)}, bf16[256,128]{1,0:T(8,128)(2,1)S(1)}, u32[]{:S(2)}, u32[]{:S(2)}) %collective-permute-start) | collective-permute-done | bytes 65568 | tf_op jit(solution)/shard_map/ppermute | solution.py:224
  21.5 1.3 %shard_map.106 = bf16[6144,128]{1,0:T(8,128)(2,1)S(1)} custom-call(bf16[256,384]{1,0:T(8,128)(2,1)S(1)} %get-tuple-element.36.stay_ref, bf16[256,128]{1,0:T(8,128)(2,1)S(1)} %collective-permute-done.came_ref, bf16[512,6144]{1,0:T(8,128)(2,1)S(1)} %get-tuple-element.34.g_ref), custom_call_target="tpu_custom_call" | custom-call | tf_op jit(solution)/shard_map/pallas_call | solution.py:129
  22.8 1.9 %collective-permute-start.1 = (bf16[6144,128]{1,0:T(8,128)(2,1)S(1)}, bf16[6144,128]{1,0:T(8,128)(2,1)S(1)}, u32[]{:S(2)}, u32[]{:S(2)}) collective-permute-start(bf16[6144,128]{1,0:T(8,128)(2,1)S(1)} %shard_map.106), channel_id=1, source_target_pairs={{0,16},{16,0},{32,48},{48,32},{64,80},{80,64},{96,112},{112,96},{1... | collective-permute-start | bytes 4718600 | tf_op jit(solution)/shard_map/ppermute | solution.py:197
  24.7 1.4 %shard_map.105 = bf16[6144,128]{1,0:T(8,128)(2,1)S(1)} custom-call(bf16[256,384]{1,0:T(8,128)(2,1)S(1)} %get-tuple-element.36.stay_ref, bf16[256,128]{1,0:T(8,128)(2,1)S(1)} %collective-permute-done.came_ref, bf16[512,6144]{1,0:T(8,128)(2,1)S(1)} %get-tuple-element.34.g_ref), custom_call_target="tpu_custom_call" | custom-call | tf_op jit(solution)/shard_map/pallas_call | solution.py:129
  26.1 2.0 %collective-permute-done.1 = bf16[6144,128]{1,0:T(8,128)(2,1)S(1)} collective-permute-done((bf16[6144,128]{1,0:T(8,128)(2,1)S(1)}, bf16[6144,128]{1,0:T(8,128)(2,1)S(1)}, u32[]{:S(2)}, u32[]{:S(2)}) %collective-permute-start.1) | collective-permute-done | bytes 1572896 | tf_op jit(solution)/shard_map/ppermute | solution.py:197
  28.1 0.2 add_convert_fusion
  28.3 0.2 add_convert_fusion.5
  28.5 0.0 copy-start.1
  28.6 0.0 copy-start.2
  28.6 0.0 copy-start.3
  28.6 2.1 %collective-permute-start.4 = (bf16[1536,128]{1,0:T(8,128)(2,1)S(1)}, bf16[1536,128]{1,0:T(8,128)(2,1)S(1)}, u32[]{:S(2)}, u32[]{:S(2)}) collective-permute-start(bf16[1536,128]{1,0:T(8,128)(2,1)S(1)} %get-tuple-element.43), channel_id=1, source_target_pairs={{0,224},{16,48},{32,0},{48,80},{64,32},{80,112},{96,64},{112,144},... | collective-permute-start | bytes 1179656 | tf_op jit(solution)/shard_map/ppermute | solution.py:197
  30.6 3.9 %collective-permute-start.2 = (bf16[1536,128]{1,0:T(8,128)(2,1)S(1)}, bf16[1536,128]{1,0:T(8,128)(2,1)S(1)}, u32[]{:S(2)}, u32[]{:S(2)}) collective-permute-start(bf16[1536,128]{1,0:T(8,128)(2,1)S(1)} %get-tuple-element.40), channel_id=1, source_target_pairs={{0,32},{16,240},{32,64},{48,16},{64,96},{80,48},{96,128},{112,80},... | collective-permute-start | bytes 1179656 | tf_op jit(solution)/shard_map/ppermute | solution.py:197
  34.6 1.9 %collective-permute-start.3 = (bf16[768,128]{1,0:T(8,128)(2,1)S(1)}, bf16[768,128]{1,0:T(8,128)(2,1)S(1)}, u32[]{:S(2)}, u32[]{:S(2)}) collective-permute-start(bf16[768,128]{1,0:T(8,128)(2,1)S(1)} %get-tuple-element.41), channel_id=1, source_target_pairs={{0,64},{16,208},{32,96},{48,240},{64,128},{80,16},{96,160},{112,48... | collective-permute-start | bytes 589832 | tf_op jit(solution)/shard_map/ppermute | solution.py:197
  36.5 6.4 %collective-permute-done.4 = bf16[1536,128]{1,0:T(8,128)(2,1)S(1)} collective-permute-done((bf16[1536,128]{1,0:T(8,128)(2,1)S(1)}, bf16[1536,128]{1,0:T(8,128)(2,1)S(1)}, u32[]{:S(2)}, u32[]{:S(2)}) %collective-permute-start.4) | collective-permute-done | bytes 393248 | tf_op jit(solution)/shard_map/ppermute | solution.py:197
  42.9 0.1 add_convert_fusion.3
  43.0 3.0 %collective-permute-done.3 = bf16[768,128]{1,0:T(8,128)(2,1)S(1)} collective-permute-done((bf16[768,128]{1,0:T(8,128)(2,1)S(1)}, bf16[768,128]{1,0:T(8,128)(2,1)S(1)}, u32[]{:S(2)}, u32[]{:S(2)}) %collective-permute-start.3) | collective-permute-done | bytes 196640 | tf_op jit(solution)/shard_map/ppermute | solution.py:197
  46.0 0.0 collective-permute-done.2
  46.0 0.1 add_convert_fusion.4
  46.0 1.9 %collective-permute-start.5 = (bf16[768,128]{1,0:T(8,128)(2,1)S(1)}, bf16[768,128]{1,0:T(8,128)(2,1)S(1)}, u32[]{:S(2)}, u32[]{:S(2)}) collective-permute-start(bf16[768,128]{1,0:T(8,128)(2,1)S(1)} %add_convert_fusion.4), channel_id=1, source_target_pairs={{0,64},{16,208},{32,96},{48,240},{64,128},{80,16},{96,160},{112,48... | collective-permute-start | bytes 589832 | tf_op jit(solution)/shard_map/ppermute | solution.py:197
  48.0 6.0 %collective-permute-start.6 = (bf16[768,128]{1,0:T(8,128)(2,1)S(1)}, bf16[768,128]{1,0:T(8,128)(2,1)S(1)}, u32[]{:S(2)}, u32[]{:S(2)}) collective-permute-start(bf16[768,128]{1,0:T(8,128)(2,1)S(1)} %add_convert_fusion.3), channel_id=1, source_target_pairs={{0,192},{16,80},{32,224},{48,112},{64,0},{80,144},{96,32},{112,176... | collective-permute-start | bytes 589832 | tf_op jit(solution)/shard_map/ppermute | solution.py:197
  54.0 10.8 %collective-permute-start.7 = (bf16[128,256]{1,0:T(8,128)(2,1)S(1)}, bf16[128,256]{1,0:T(8,128)(2,1)S(1)}, u32[]{:S(2)}, u32[]{:S(2)}) collective-permute-start(bf16[128,256]{1,0:T(8,128)(2,1)S(1)} %slice.65), channel_id=1, source_target_pairs={{16,0},{32,16},{48,32},{64,48},{80,64},{96,80},{112,96},{128,112},... | collective-permute-start | bytes 196616 | tf_op jit(solution)/shard_map/ppermute | solution.py:244
  64.8 0.0 collective-permute-done.5
  64.8 0.0 collective-permute-done.6
  64.8 0.8 %add_convert_fusion.2 = bf16[768,128]{1,0:T(8,128)(2,1)} fusion(bf16[768,128]{1,0:T(8,128)(2,1)S(1)} %collective-permute-done.6, bf16[768,128]{1,0:T(8,128)(2,1)S(1)} %collective-permute-done.5, bf16[768,128]{1,0:T(8,128)(2,1)S(1)} %get-tuple-element.38, bf16[1536,128]{1,0:T(8,128)(2,1)S(1)} %collective-permute-done.4, ...), kind=kLoop, calls=%fused_computation.2 | loop fusion | flops 983040 | bytes 1179648 | tf_op jit(solution)/shard_map/convert_element_type | solution.py:217
  65.7 1.0 %collective-permute-done.7.back_ref = bf16[128,256]{1,0:T(8,128)(2,1)S(1)} collective-permute-done((bf16[128,256]{1,0:T(8,128)(2,1)S(1)}, bf16[128,256]{1,0:T(8,128)(2,1)S(1)}, u32[]{:S(2)}, u32[]{:S(2)}) %collective-permute-start.7) | collective-permute-done | bytes 65568 | tf_op jit(solution)/shard_map/ppermute | solution.py:244
  66.7 4.8 %all-to-all-start = ((bf16[3,256,128]{2,1,0:T(8,128)(2,1)}), bf16[3,256,128]{2,1,0:T(8,128)(2,1)S(1)}, u32[]{:S(2)}, u32[]{:S(2)}) async-start(bf16[3,256,128]{2,1,0:T(8,128)(2,1)} %bitcast), calls=%async_computation | async-start | bytes 393216 | tf_op jit(solution)/shard_map/all_to_all | solution.py:247
  71.4 0.0 copy-done.1
  71.4 0.0 copy-done.2
  71.4 0.0 copy-done.3
  71.4 3.8 %shard_map.107 = (bf16[384,256]{1,0:T(8,128)(2,1)}, bf16[384,256]{1,0:T(8,128)(2,1)}, bf16[384,256]{1,0:T(8,128)(2,1)}) custom-call(s32[8,384]{1,0:T(8,128)S(1)} %get-tuple-element.28.same_ref, s32[8,128]{1,0:T(8,128)S(1)} %get-tuple-element.29.stays_ref, bf16[384,256]{1,0:T(8,128)(2,1)S(1)} %copy-done.1, bf16[384,256]{1,0:T(8,128)(2,1)S(1)} %copy-done.2, ...), custom_call_target="tpu_custom_call" | custom-call | tf_op jit(solution)/shard_map/pallas_call | solution.py:180
  75.2 7.1 %all-to-all-done = bf16[3,256,128]{2,1,0:T(8,128)(2,1)S(1)} async-done(((bf16[3,256,128]{2,1,0:T(8,128)(2,1)}), bf16[3,256,128]{2,1,0:T(8,128)(2,1)S(1)}, u32[]{:S(2)}, u32[]{:S(2)}) %all-to-all-start) | async-done | bytes 196640 | tf_op jit(solution)/shard_map/all_to_all | solution.py:247
  82.3 0.7 add_bitcast_fusion
  (1 shorter events, 0.0 us)
Async XLA Ops:
  2.4 19.1 %collective-permute-start = (bf16[256,128]{1,0:T(8,128)(2,1)S(1)}, bf16[256,128]{1,0:T(8,128)(2,1)S(1)}, u32[]{:S(2)}, u32[]{:S(2)}) collective-permute-start(bf16[256,128]{1,0:T(8,128)(2,1)S(1)} %get-tuple-element.37), channel_id=1, source_target_pairs={{0,16},{16,32},{32,48},{48,64},{64,80},{80,96},{96,112},{112,128},... | collective-permute-start | bytes 196616 | tf_op jit(solution)/shard_map/ppermute | solution.py:224
  4.3 3.7 %copy-start = (bf16[256,6144]{1,0:T(8,128)(2,1)S(1)}, bf16[256,6144]{1,0:T(8,128)(2,1)}, u32[]{:S(2)}) copy-start(bf16[256,6144]{1,0:T(8,128)(2,1)} %w_ref.1) | copy-start | bytes 9437188
  22.8 5.3 %collective-permute-start.1 = (bf16[6144,128]{1,0:T(8,128)(2,1)S(1)}, bf16[6144,128]{1,0:T(8,128)(2,1)S(1)}, u32[]{:S(2)}, u32[]{:S(2)}) collective-permute-start(bf16[6144,128]{1,0:T(8,128)(2,1)S(1)} %shard_map.106), channel_id=1, source_target_pairs={{0,16},{16,0},{32,48},{48,32},{64,80},{80,64},{96,112},{112,96},{1... | collective-permute-start | bytes 4718600 | tf_op jit(solution)/shard_map/ppermute | solution.py:197
  28.5 42.9 %copy-start.1 = (bf16[384,256]{1,0:T(8,128)(2,1)S(1)}, bf16[384,256]{1,0:T(8,128)(2,1)}, u32[]{:S(2)}) copy-start(bf16[384,256]{1,0:T(8,128)(2,1)} %q_ref.1) | copy-start | bytes 589828
  28.6 42.9 %copy-start.2 = (bf16[384,256]{1,0:T(8,128)(2,1)S(1)}, bf16[384,256]{1,0:T(8,128)(2,1)}, u32[]{:S(2)}) copy-start(bf16[384,256]{1,0:T(8,128)(2,1)} %k_ref.1) | copy-start | bytes 589828
  28.6 42.9 %copy-start.3 = (bf16[384,256]{1,0:T(8,128)(2,1)S(1)}, bf16[384,256]{1,0:T(8,128)(2,1)}, u32[]{:S(2)}) copy-start(bf16[384,256]{1,0:T(8,128)(2,1)} %v_ref.1) | copy-start | bytes 589828
  28.6 14.3 %collective-permute-start.4 = (bf16[1536,128]{1,0:T(8,128)(2,1)S(1)}, bf16[1536,128]{1,0:T(8,128)(2,1)S(1)}, u32[]{:S(2)}, u32[]{:S(2)}) collective-permute-start(bf16[1536,128]{1,0:T(8,128)(2,1)S(1)} %get-tuple-element.43), channel_id=1, source_target_pairs={{0,224},{16,48},{32,0},{48,80},{64,32},{80,112},{96,64},{112,144},... | collective-permute-start | bytes 1179656 | tf_op jit(solution)/shard_map/ppermute | solution.py:197
  30.6 15.3 %collective-permute-start.2 = (bf16[1536,128]{1,0:T(8,128)(2,1)S(1)}, bf16[1536,128]{1,0:T(8,128)(2,1)S(1)}, u32[]{:S(2)}, u32[]{:S(2)}) collective-permute-start(bf16[1536,128]{1,0:T(8,128)(2,1)S(1)} %get-tuple-element.40), channel_id=1, source_target_pairs={{0,32},{16,240},{32,64},{48,16},{64,96},{80,48},{96,128},{112,80},... | collective-permute-start | bytes 1179656 | tf_op jit(solution)/shard_map/ppermute | solution.py:197
  34.6 11.4 %collective-permute-start.3 = (bf16[768,128]{1,0:T(8,128)(2,1)S(1)}, bf16[768,128]{1,0:T(8,128)(2,1)S(1)}, u32[]{:S(2)}, u32[]{:S(2)}) collective-permute-start(bf16[768,128]{1,0:T(8,128)(2,1)S(1)} %get-tuple-element.41), channel_id=1, source_target_pairs={{0,64},{16,208},{32,96},{48,240},{64,128},{80,16},{96,160},{112,48... | collective-permute-start | bytes 589832 | tf_op jit(solution)/shard_map/ppermute | solution.py:197
  46.0 18.8 %collective-permute-start.5 = (bf16[768,128]{1,0:T(8,128)(2,1)S(1)}, bf16[768,128]{1,0:T(8,128)(2,1)S(1)}, u32[]{:S(2)}, u32[]{:S(2)}) collective-permute-start(bf16[768,128]{1,0:T(8,128)(2,1)S(1)} %add_convert_fusion.4), channel_id=1, source_target_pairs={{0,64},{16,208},{32,96},{48,240},{64,128},{80,16},{96,160},{112,48... | collective-permute-start | bytes 589832 | tf_op jit(solution)/shard_map/ppermute | solution.py:197
  48.0 16.8 %collective-permute-start.6 = (bf16[768,128]{1,0:T(8,128)(2,1)S(1)}, bf16[768,128]{1,0:T(8,128)(2,1)S(1)}, u32[]{:S(2)}, u32[]{:S(2)}) collective-permute-start(bf16[768,128]{1,0:T(8,128)(2,1)S(1)} %add_convert_fusion.3), channel_id=1, source_target_pairs={{0,192},{16,80},{32,224},{48,112},{64,0},{80,144},{96,32},{112,176... | collective-permute-start | bytes 589832 | tf_op jit(solution)/shard_map/ppermute | solution.py:197
  54.0 12.7 %collective-permute-start.7 = (bf16[128,256]{1,0:T(8,128)(2,1)S(1)}, bf16[128,256]{1,0:T(8,128)(2,1)S(1)}, u32[]{:S(2)}, u32[]{:S(2)}) collective-permute-start(bf16[128,256]{1,0:T(8,128)(2,1)S(1)} %slice.65), channel_id=1, source_target_pairs={{16,0},{32,16},{48,32},{64,48},{80,64},{96,80},{112,96},{128,112},... | collective-permute-start | bytes 196616 | tf_op jit(solution)/shard_map/ppermute | solution.py:244
  66.7 15.6 %all-to-all-start = ((bf16[3,256,128]{2,1,0:T(8,128)(2,1)}), bf16[3,256,128]{2,1,0:T(8,128)(2,1)S(1)}, u32[]{:S(2)}, u32[]{:S(2)}) async-start(bf16[3,256,128]{2,1,0:T(8,128)(2,1)} %bitcast), calls=%async_computation | async-start | bytes 393216 | tf_op jit(solution)/shard_map/all_to_all | solution.py:247

commit v13 on v10

--- a/solution.py
+++ b/solution.py
@@ -236,13 +236,13 @@
     parts = [rounded_total(*pair) for pair in zip(cut(own), cut(got), strict=True)]
     part = dict(zip(ORDER, lax.optimization_barrier(parts), strict=True))
     far, up, down = send(part[4], along_y(2)), send(part[3], along_y(1)), send(part[-3], along_y(-1))
-    near = send(part[1], along_y(1)), send(part[-1], along_y(-1))
+    near = send(part[1], along_y(1))
 
     up, down = rounded_total(part[2], up, far), rounded_total(part[-2], down)
-    up, down, tail = lax.optimization_barrier((up, down, grad_ctx[row_count:]))
-    up, down = send(up, along_y(2)), send(down, along_y(-2))
+    up, down, other, tail = lax.optimization_barrier((up, down, part[-1], grad_ctx[row_count:]))
+    up, down, other = send(up, along_y(2)), send(down, along_y(-2)), send(other, along_y(-1))
     back = lax.ppermute(tail, "dp", [((i + 1) % ranks, i) for i in range(ranks)])
-    sums = rounded_total(part[0], up, down, *near).reshape(NZ, -1, UNIT)
+    sums = rounded_total(part[0], up, down, near, other).reshape(NZ, -1, UNIT)
     sums, back = lax.optimization_barrier((sums, back))
     sums = lax.all_to_all(sums, "dp", 0, 0, axis_index_groups=same_place())
     grads = backward(same, stays, queries, key_rows, value_rows, grad_ctx, back)

time: 81.3 us -> 85.1 us (1.047)
  the two profiles are of different devices: /device:TPU:6 before, /device:TPU:63 now
where the time goes in v13:
time: 85.1 us; the launch traced here: 84.7 us
  starting transfers between devices  46.1 us (54%)
  waiting for transfers between devices  21.8 us (26%)
  Pallas kernels  13.1 us (15%)
  other arithmetic  2.03 us (2%)
    ppermute x8, starting transfers between devices, send(): lax.ppermute(block, 'dp', [(index(*p), index(*to(*p))) for p in PLACES])  21.9 us
    ppermute x8, waiting for transfers between devices, send(): lax.ppermute(block, 'dp', [(index(*p), index(*to(*p))) for p in PLACES])  12.8 us
    ppermute x1, starting transfers between devices, local(): lax.ppermute(leave, 'dp', [(i, (i + 1) % ranks) for i in range(ranks)])  10.4 us
    all_to_all x1, starting transfers between devices, local(): sums = lax.all_to_all(sums, 'dp', 0, 0, axis_index_groups=same_place())  10.3 us
    all_to_all x1, waiting for transfers between devices, local(): sums = lax.all_to_all(sums, 'dp', 0, 0, axis_index_groups=same_place())  5.74 us
    pallas_call x1, Pallas kernels, backward(): pl.pallas_call(backward_kernel, in_specs=[VMEM] * 7, out_specs=[VMEM] * 3...  3.76 us
    ppermute x1, starting transfers between devices, local(): lax.ppermute(tail, 'dp', [((i + 1) % ranks, i) for i in range(ranks)])  3.52 us
    ppermute x1, waiting for transfers between devices, local(): lax.ppermute(tail, 'dp', [((i + 1) % ranks, i) for i in range(ranks)])  3.23 us
  transfers between devices with their start and end apart: 11, of which 7 were waited for; matrix products, arithmetic and copies ran while one was open for 1% of the time, Pallas kernels for 12%

profile of v13, /device:TPU:63, one launch (start us, length us, event | category | flops | bytes accessed | tf_op | source)
XLA Modules:
  0.0 84.7 jit_solution(5324175948314011953)
XLA Ops:
  0.6 1.7 %shard_map.102 = (bf16[256,128]{1,0:T(8,128)(2,1)S(1)}, s32[8,384]{1,0:T(8,128)S(1)}, s32[8,128]{1,0:T(8,128)S(1)}, bf16[384,256]{1,0:T(8,128)(2,1)S(1)}, bf16[3...) custom-call(s32[384]{0:T(512)} %ids_hbm.1, s32[384]{0:T(512)} %slot_hbm.1, bf16[384,256]{1,0:T(8,128)(2,1)} %q_ref.1, ...), custom_call_target="tpu_custom_call" | custom-call | tf_op jit(solution)/shard_map/pallas_call | solution.py:68
  2.4 10.4 %collective-permute-start = (bf16[256,128]{1,0:T(8,128)(2,1)S(1)}, bf16[256,128]{1,0:T(8,128)(2,1)S(1)}, u32[]{:S(2)}, u32[]{:S(2)}) collective-permute-start(bf16[256,128]{1,0:T(8,128)(2,1)S(1)} %get-tuple-element.40), channel_id=1, source_target_pairs={{0,16},{16,32},{32,48},{48,64},{64,80},{80,96},{96,112},{112,128},... | collective-permute-start | bytes 196616 | tf_op jit(solution)/shard_map/ppermute | solution.py:224
  12.8 0.0 copy-start
  12.8 2.9 %shard_map.103 = (bf16[256,384]{1,0:T(8,128)(2,1)S(1)}, bf16[512,6144]{1,0:T(8,128)(2,1)S(1)}) custom-call(s32[8,384]{1,0:T(8,128)S(1)} %get-tuple-element.31.same_ref, s32[8,128]{1,0:T(8,128)S(1)} %get-tuple-element.32.stays_ref, bf16[384,256]{1,0:T(8,128)(2,1)S(1)} %get-tuple-element.33.q_ref, bf16[384,256]{1,0:T(8,128)(2,1)S(1)} %get-tuple-element.34.k_ref, ...), custom_call_target="tpu_custom_call" | custom-call | tf_op jit(solution)/shard_map/pallas_call | solution.py:98
  15.8 0.7 copy-done
  16.5 1.8 %shard_map.104.g_ref = bf16[512,256]{1,0:T(8,128)(2,1)S(1)} custom-call(bf16[512,6144]{1,0:T(8,128)(2,1)S(1)} %get-tuple-element.37.g_ref, bf16[256,6144]{1,0:T(8,128)(2,1)S(1)} %copy-done), custom_call_target="tpu_custom_call" | custom-call | tf_op jit(solution)/shard_map/pallas_call | solution.py:148
  18.3 0.0 collective-permute-done.came_ref
  18.3 1.4 %shard_map.106 = bf16[6144,128]{1,0:T(8,128)(2,1)S(1)} custom-call(bf16[256,384]{1,0:T(8,128)(2,1)S(1)} %get-tuple-element.39.stay_ref, bf16[256,128]{1,0:T(8,128)(2,1)S(1)} %collective-permute-done.came_ref, bf16[512,6144]{1,0:T(8,128)(2,1)S(1)} %get-tuple-element.37.g_ref), custom_call_target="tpu_custom_call" | custom-call | tf_op jit(solution)/shard_map/pallas_call | solution.py:129
  19.7 1.9 %collective-permute-start.1 = (bf16[6144,128]{1,0:T(8,128)(2,1)S(1)}, bf16[6144,128]{1,0:T(8,128)(2,1)S(1)}, u32[]{:S(2)}, u32[]{:S(2)}) collective-permute-start(bf16[6144,128]{1,0:T(8,128)(2,1)S(1)} %shard_map.106), channel_id=1, source_target_pairs={{0,16},{16,0},{32,48},{48,32},{64,80},{80,64},{96,112},{112,96},{1... | collective-permute-start | bytes 4718600 | tf_op jit(solution)/shard_map/ppermute | solution.py:197
  21.7 1.4 %shard_map.105 = bf16[6144,128]{1,0:T(8,128)(2,1)S(1)} custom-call(bf16[256,384]{1,0:T(8,128)(2,1)S(1)} %get-tuple-element.39.stay_ref, bf16[256,128]{1,0:T(8,128)(2,1)S(1)} %collective-permute-done.came_ref, bf16[512,6144]{1,0:T(8,128)(2,1)S(1)} %get-tuple-element.37.g_ref), custom_call_target="tpu_custom_call" | custom-call | tf_op jit(solution)/shard_map/pallas_call | solution.py:129
  23.1 2.0 %collective-permute-done.1 = bf16[6144,128]{1,0:T(8,128)(2,1)S(1)} collective-permute-done((bf16[6144,128]{1,0:T(8,128)(2,1)S(1)}, bf16[6144,128]{1,0:T(8,128)(2,1)S(1)}, u32[]{:S(2)}, u32[]{:S(2)}) %collective-permute-start.1) | collective-permute-done | bytes 1572896 | tf_op jit(solution)/shard_map/ppermute | solution.py:197
  25.0 0.4 add_convert_fusion.3
  25.4 0.0 copy-start.1
  25.5 0.0 copy-start.2
  25.5 0.0 copy-start.3
  25.5 4.9 %collective-permute-start.4 = (bf16[768,128]{1,0:T(8,128)(2,1)S(1)}, bf16[768,128]{1,0:T(8,128)(2,1)S(1)}, u32[]{:S(2)}, u32[]{:S(2)}) collective-permute-start(bf16[768,128]{1,0:T(8,128)(2,1)S(1)} %get-tuple-element.46), channel_id=1, source_target_pairs={{0,224},{16,48},{32,0},{48,80},{64,32},{80,112},{96,64},{112,144},... | collective-permute-start | bytes 589832 | tf_op jit(solution)/shard_map/ppermute | solution.py:197
  30.4 1.9 %collective-permute-start.2 = (bf16[768,128]{1,0:T(8,128)(2,1)S(1)}, bf16[768,128]{1,0:T(8,128)(2,1)S(1)}, u32[]{:S(2)}, u32[]{:S(2)}) collective-permute-start(bf16[768,128]{1,0:T(8,128)(2,1)S(1)} %get-tuple-element.43), channel_id=1, source_target_pairs={{0,32},{16,240},{32,64},{48,16},{64,96},{80,48},{96,128},{112,80},... | collective-permute-start | bytes 589832 | tf_op jit(solution)/shard_map/ppermute | solution.py:197
  32.4 1.9 %collective-permute-start.3 = (bf16[768,128]{1,0:T(8,128)(2,1)S(1)}, bf16[768,128]{1,0:T(8,128)(2,1)S(1)}, u32[]{:S(2)}, u32[]{:S(2)}) collective-permute-start(bf16[768,128]{1,0:T(8,128)(2,1)S(1)} %get-tuple-element.44), channel_id=1, source_target_pairs={{0,64},{16,208},{32,96},{48,240},{64,128},{80,16},{96,160},{112,48... | collective-permute-start | bytes 589832 | tf_op jit(solution)/shard_map/ppermute | solution.py:197
  34.3 1.9 %collective-permute-start.7 = (bf16[768,128]{1,0:T(8,128)(2,1)S(1)}, bf16[768,128]{1,0:T(8,128)(2,1)S(1)}, u32[]{:S(2)}, u32[]{:S(2)}) collective-permute-start(bf16[768,128]{1,0:T(8,128)(2,1)S(1)} %get-tuple-element.50), channel_id=1, source_target_pairs={{0,32},{16,240},{32,64},{48,16},{64,96},{80,48},{96,128},{112,80},... | collective-permute-start | bytes 589832 | tf_op jit(solution)/shard_map/ppermute | solution.py:197
  36.2 0.0 collective-permute-done.4
  36.2 0.1 add_convert_fusion.1
  36.3 1.8 %collective-permute-done.2 = bf16[768,128]{1,0:T(8,128)(2,1)S(1)} collective-permute-done((bf16[768,128]{1,0:T(8,128)(2,1)S(1)}, bf16[768,128]{1,0:T(8,128)(2,1)S(1)}, u32[]{:S(2)}, u32[]{:S(2)}) %collective-permute-start.2) | collective-permute-done | bytes 196640 | tf_op jit(solution)/shard_map/ppermute | solution.py:197
  38.0 5.1 %collective-permute-done.3 = bf16[768,128]{1,0:T(8,128)(2,1)S(1)} collective-permute-done((bf16[768,128]{1,0:T(8,128)(2,1)S(1)}, bf16[768,128]{1,0:T(8,128)(2,1)S(1)}, u32[]{:S(2)}, u32[]{:S(2)}) %collective-permute-start.3) | collective-permute-done | bytes 196640 | tf_op jit(solution)/shard_map/ppermute | solution.py:197
  43.1 0.1 add_convert_fusion.2
  43.2 1.9 %collective-permute-start.5 = (bf16[768,128]{1,0:T(8,128)(2,1)S(1)}, bf16[768,128]{1,0:T(8,128)(2,1)S(1)}, u32[]{:S(2)}, u32[]{:S(2)}) collective-permute-start(bf16[768,128]{1,0:T(8,128)(2,1)S(1)} %add_convert_fusion.2), channel_id=1, source_target_pairs={{0,64},{16,208},{32,96},{48,240},{64,128},{80,16},{96,160},{112,48... | collective-permute-start | bytes 589832 | tf_op jit(solution)/shard_map/ppermute | solution.py:197
  45.1 5.5 %collective-permute-start.6 = (bf16[768,128]{1,0:T(8,128)(2,1)S(1)}, bf16[768,128]{1,0:T(8,128)(2,1)S(1)}, u32[]{:S(2)}, u32[]{:S(2)}) collective-permute-start(bf16[768,128]{1,0:T(8,128)(2,1)S(1)} %add_convert_fusion.1), channel_id=1, source_target_pairs={{0,192},{16,80},{32,224},{48,112},{64,0},{80,144},{96,32},{112,176... | collective-permute-start | bytes 589832 | tf_op jit(solution)/shard_map/ppermute | solution.py:197
  50.6 1.9 %collective-permute-start.8 = (bf16[768,128]{1,0:T(8,128)(2,1)S(1)}, bf16[768,128]{1,0:T(8,128)(2,1)S(1)}, u32[]{:S(2)}, u32[]{:S(2)}) collective-permute-start(bf16[768,128]{1,0:T(8,128)(2,1)S(1)} %get-tuple-element.51), channel_id=1, source_target_pairs={{0,224},{16,48},{32,0},{48,80},{64,32},{80,112},{96,64},{112,144},... | collective-permute-start | bytes 589832 | tf_op jit(solution)/shard_map/ppermute | solution.py:197
  52.6 3.5 %collective-permute-start.9 = (bf16[128,256]{1,0:T(8,128)(2,1)S(1)}, bf16[128,256]{1,0:T(8,128)(2,1)S(1)}, u32[]{:S(2)}, u32[]{:S(2)}) collective-permute-start(bf16[128,256]{1,0:T(8,128)(2,1)S(1)} %slice.67), channel_id=1, source_target_pairs={{16,0},{32,16},{48,32},{64,48},{80,64},{96,80},{112,96},{128,112},... | collective-permute-start | bytes 196616 | tf_op jit(solution)/shard_map/ppermute | solution.py:244
  56.1 0.0 collective-permute-done.7
  56.1 0.0 collective-permute-done.5
  56.1 1.3 %collective-permute-done.6 = bf16[768,128]{1,0:T(8,128)(2,1)S(1)} collective-permute-done((bf16[768,128]{1,0:T(8,128)(2,1)S(1)}, bf16[768,128]{1,0:T(8,128)(2,1)S(1)}, u32[]{:S(2)}, u32[]{:S(2)}) %collective-permute-start.6) | collective-permute-done | bytes 196640 | tf_op jit(solution)/shard_map/ppermute | solution.py:197
  57.4 2.8 %collective-permute-done.8 = bf16[768,128]{1,0:T(8,128)(2,1)S(1)} collective-permute-done((bf16[768,128]{1,0:T(8,128)(2,1)S(1)}, bf16[768,128]{1,0:T(8,128)(2,1)S(1)}, u32[]{:S(2)}, u32[]{:S(2)}) %collective-permute-start.8) | collective-permute-done | bytes 196640 | tf_op jit(solution)/shard_map/ppermute | solution.py:197
  60.1 0.8 add_convert_fusion
  60.9 3.2 %collective-permute-done.9.back_ref = bf16[128,256]{1,0:T(8,128)(2,1)S(1)} collective-permute-done((bf16[128,256]{1,0:T(8,128)(2,1)S(1)}, bf16[128,256]{1,0:T(8,128)(2,1)S(1)}, u32[]{:S(2)}, u32[]{:S(2)}) %collective-permute-start.9) | collective-permute-done | bytes 65568 | tf_op jit(solution)/shard_map/ppermute | solution.py:244
  64.2 10.3 %all-to-all-start = ((bf16[3,256,128]{2,1,0:T(8,128)(2,1)}), bf16[3,256,128]{2,1,0:T(8,128)(2,1)S(1)}, u32[]{:S(2)}, u32[]{:S(2)}) async-start(bf16[3,256,128]{2,1,0:T(8,128)(2,1)} %bitcast), calls=%async_computation | async-start | bytes 393216 | tf_op jit(solution)/shard_map/all_to_all | solution.py:247
  74.5 0.0 copy-done.1
  74.5 0.0 copy-done.2
  74.5 0.0 copy-done.3
  74.5 3.8 %shard_map.107 = (bf16[384,256]{1,0:T(8,128)(2,1)}, bf16[384,256]{1,0:T(8,128)(2,1)}, bf16[384,256]{1,0:T(8,128)(2,1)}) custom-call(s32[8,384]{1,0:T(8,128)S(1)} %get-tuple-element.31.same_ref, s32[8,128]{1,0:T(8,128)S(1)} %get-tuple-element.32.stays_ref, bf16[384,256]{1,0:T(8,128)(2,1)S(1)} %copy-done.1, bf16[384,256]{1,0:T(8,128)(2,1)S(1)} %copy-done.2, ...), custom_call_target="tpu_custom_call" | custom-call | tf_op jit(solution)/shard_map/pallas_call | solution.py:180
  78.2 5.7 %all-to-all-done = bf16[3,256,128]{2,1,0:T(8,128)(2,1)S(1)} async-done(((bf16[3,256,128]{2,1,0:T(8,128)(2,1)}), bf16[3,256,128]{2,1,0:T(8,128)(2,1)S(1)}, u32[]{:S(2)}, u32[]{:S(2)}) %all-to-all-start) | async-done | bytes 196640 | tf_op jit(solution)/shard_map/all_to_all | solution.py:247
  84.0 0.7 add_bitcast_fusion
  (1 shorter events, 0.0 us)
Async XLA Ops:
  2.4 15.9 %collective-permute-start = (bf16[256,128]{1,0:T(8,128)(2,1)S(1)}, bf16[256,128]{1,0:T(8,128)(2,1)S(1)}, u32[]{:S(2)}, u32[]{:S(2)}) collective-permute-start(bf16[256,128]{1,0:T(8,128)(2,1)S(1)} %get-tuple-element.40), channel_id=1, source_target_pairs={{0,16},{16,32},{32,48},{48,64},{64,80},{80,96},{96,112},{112,128},... | collective-permute-start | bytes 196616 | tf_op jit(solution)/shard_map/ppermute | solution.py:224
  12.8 3.7 %copy-start = (bf16[256,6144]{1,0:T(8,128)(2,1)S(1)}, bf16[256,6144]{1,0:T(8,128)(2,1)}, u32[]{:S(2)}) copy-start(bf16[256,6144]{1,0:T(8,128)(2,1)} %w_ref.1) | copy-start | bytes 9437188
  19.7 5.3 %collective-permute-start.1 = (bf16[6144,128]{1,0:T(8,128)(2,1)S(1)}, bf16[6144,128]{1,0:T(8,128)(2,1)S(1)}, u32[]{:S(2)}, u32[]{:S(2)}) collective-permute-start(bf16[6144,128]{1,0:T(8,128)(2,1)S(1)} %shard_map.106), channel_id=1, source_target_pairs={{0,16},{16,0},{32,48},{48,32},{64,80},{80,64},{96,112},{112,96},{1... | collective-permute-start | bytes 4718600 | tf_op jit(solution)/shard_map/ppermute | solution.py:197
  25.4 49.0 %copy-start.1 = (bf16[384,256]{1,0:T(8,128)(2,1)S(1)}, bf16[384,256]{1,0:T(8,128)(2,1)}, u32[]{:S(2)}) copy-start(bf16[384,256]{1,0:T(8,128)(2,1)} %q_ref.1) | copy-start | bytes 589828
  25.5 49.0 %copy-start.2 = (bf16[384,256]{1,0:T(8,128)(2,1)S(1)}, bf16[384,256]{1,0:T(8,128)(2,1)}, u32[]{:S(2)}) copy-start(bf16[384,256]{1,0:T(8,128)(2,1)} %k_ref.1) | copy-start | bytes 589828
  25.5 49.0 %copy-start.3 = (bf16[384,256]{1,0:T(8,128)(2,1)S(1)}, bf16[384,256]{1,0:T(8,128)(2,1)}, u32[]{:S(2)}) copy-start(bf16[384,256]{1,0:T(8,128)(2,1)} %v_ref.1) | copy-start | bytes 589828
  25.5 10.7 %collective-permute-start.4 = (bf16[768,128]{1,0:T(8,128)(2,1)S(1)}, bf16[768,128]{1,0:T(8,128)(2,1)S(1)}, u32[]{:S(2)}, u32[]{:S(2)}) collective-permute-start(bf16[768,128]{1,0:T(8,128)(2,1)S(1)} %get-tuple-element.46), channel_id=1, source_target_pairs={{0,224},{16,48},{32,0},{48,80},{64,32},{80,112},{96,64},{112,144},... | collective-permute-start | bytes 589832 | tf_op jit(solution)/shard_map/ppermute | solution.py:197
  30.4 7.6 %collective-permute-start.2 = (bf16[768,128]{1,0:T(8,128)(2,1)S(1)}, bf16[768,128]{1,0:T(8,128)(2,1)S(1)}, u32[]{:S(2)}, u32[]{:S(2)}) collective-permute-start(bf16[768,128]{1,0:T(8,128)(2,1)S(1)} %get-tuple-element.43), channel_id=1, source_target_pairs={{0,32},{16,240},{32,64},{48,16},{64,96},{80,48},{96,128},{112,80},... | collective-permute-start | bytes 589832 | tf_op jit(solution)/shard_map/ppermute | solution.py:197
  32.4 10.8 %collective-permute-start.3 = (bf16[768,128]{1,0:T(8,128)(2,1)S(1)}, bf16[768,128]{1,0:T(8,128)(2,1)S(1)}, u32[]{:S(2)}, u32[]{:S(2)}) collective-permute-start(bf16[768,128]{1,0:T(8,128)(2,1)S(1)} %get-tuple-element.44), channel_id=1, source_target_pairs={{0,64},{16,208},{32,96},{48,240},{64,128},{80,16},{96,160},{112,48... | collective-permute-start | bytes 589832 | tf_op jit(solution)/shard_map/ppermute | solution.py:197
  34.3 21.8 %collective-permute-start.7 = (bf16[768,128]{1,0:T(8,128)(2,1)S(1)}, bf16[768,128]{1,0:T(8,128)(2,1)S(1)}, u32[]{:S(2)}, u32[]{:S(2)}) collective-permute-start(bf16[768,128]{1,0:T(8,128)(2,1)S(1)} %get-tuple-element.50), channel_id=1, source_target_pairs={{0,32},{16,240},{32,64},{48,16},{64,96},{80,48},{96,128},{112,80},... | collective-permute-start | bytes 589832 | tf_op jit(solution)/shard_map/ppermute | solution.py:197
  43.2 12.9 %collective-permute-start.5 = (bf16[768,128]{1,0:T(8,128)(2,1)S(1)}, bf16[768,128]{1,0:T(8,128)(2,1)S(1)}, u32[]{:S(2)}, u32[]{:S(2)}) collective-permute-start(bf16[768,128]{1,0:T(8,128)(2,1)S(1)} %add_convert_fusion.2), channel_id=1, source_target_pairs={{0,64},{16,208},{32,96},{48,240},{64,128},{80,16},{96,160},{112,48... | collective-permute-start | bytes 589832 | tf_op jit(solution)/shard_map/ppermute | solution.py:197
  45.1 12.2 %collective-permute-start.6 = (bf16[768,128]{1,0:T(8,128)(2,1)S(1)}, bf16[768,128]{1,0:T(8,128)(2,1)S(1)}, u32[]{:S(2)}, u32[]{:S(2)}) collective-permute-start(bf16[768,128]{1,0:T(8,128)(2,1)S(1)} %add_convert_fusion.1), channel_id=1, source_target_pairs={{0,192},{16,80},{32,224},{48,112},{64,0},{80,144},{96,32},{112,176... | collective-permute-start | bytes 589832 | tf_op jit(solution)/shard_map/ppermute | solution.py:197
  50.6 9.5 %collective-permute-start.8 = (bf16[768,128]{1,0:T(8,128)(2,1)S(1)}, bf16[768,128]{1,0:T(8,128)(2,1)S(1)}, u32[]{:S(2)}, u32[]{:S(2)}) collective-permute-start(bf16[768,128]{1,0:T(8,128)(2,1)S(1)} %get-tuple-element.51), channel_id=1, source_target_pairs={{0,224},{16,48},{32,0},{48,80},{64,32},{80,112},{96,64},{112,144},... | collective-permute-start | bytes 589832 | tf_op jit(solution)/shard_map/ppermute | solution.py:197
  52.6 11.6 %collective-permute-start.9 = (bf16[128,256]{1,0:T(8,128)(2,1)S(1)}, bf16[128,256]{1,0:T(8,128)(2,1)S(1)}, u32[]{:S(2)}, u32[]{:S(2)}) collective-permute-start(bf16[128,256]{1,0:T(8,128)(2,1)S(1)} %slice.67), channel_id=1, source_target_pairs={{16,0},{32,16},{48,32},{64,48},{80,64},{96,80},{112,96},{128,112},... | collective-permute-start | bytes 196616 | tf_op jit(solution)/shard_map/ppermute | solution.py:244
  64.2 19.8 %all-to-all-start = ((bf16[3,256,128]{2,1,0:T(8,128)(2,1)}), bf16[3,256,128]{2,1,0:T(8,128)(2,1)S(1)}, u32[]{:S(2)}, u32[]{:S(2)}) async-start(bf16[3,256,128]{2,1,0:T(8,128)(2,1)} %bitcast), calls=%async_computation | async-start | bytes 393216 | tf_op jit(solution)/shard_map/all_to_all | solution.py:247

commit v14 on v13

--- a/solution.py
+++ b/solution.py
@@ -10,7 +10,7 @@
 HD = 128
 UNIT = 128
 NZ, NY, NC = 3, 8, 2
-ORDER = (4, 3, -3, 2, -2, 1, -1, 0)
+ORDER = (4, -3, 3, -2, 2, -1, 1, 0)
 VMEM = pl.BlockSpec(memory_space=pltpu.VMEM)
 PARAMS = pltpu.CompilerParams(vmem_limit_bytes=8 * 1024 * 1024)
 
@@ -235,14 +235,13 @@
     own = partial_grad(False, stay, came, g_near)
     parts = [rounded_total(*pair) for pair in zip(cut(own), cut(got), strict=True)]
     part = dict(zip(ORDER, lax.optimization_barrier(parts), strict=True))
-    far, up, down = send(part[4], along_y(2)), send(part[3], along_y(1)), send(part[-3], along_y(-1))
-    near = send(part[1], along_y(1))
-
-    up, down = rounded_total(part[2], up, far), rounded_total(part[-2], down)
-    up, down, other, tail = lax.optimization_barrier((up, down, part[-1], grad_ctx[row_count:]))
-    up, down, other = send(up, along_y(2)), send(down, along_y(-2)), send(other, along_y(-1))
+    up, down = send(part[4], along_y(1)), send(part[-3], along_y(-1))
+    up, down = send(rounded_total(part[3], up), along_y(1)), send(rounded_total(part[-2], down), along_y(-1))
+    up, tail = lax.optimization_barrier((rounded_total(part[2], up), grad_ctx[row_count:]))
+    up, down = send(up, along_y(1)), send(rounded_total(part[-1], down), along_y(-1))
     back = lax.ppermute(tail, "dp", [((i + 1) % ranks, i) for i in range(ranks)])
-    sums = rounded_total(part[0], up, down, near, other).reshape(NZ, -1, UNIT)
+    up = send(rounded_total(part[1], up), along_y(1))
+    sums = rounded_total(part[0], up, down).reshape(NZ, -1, UNIT)
     sums, back = lax.optimization_barrier((sums, back))
     sums = lax.all_to_all(sums, "dp", 0, 0, axis_index_groups=same_place())
     grads = backward(same, stays, queries, key_rows, value_rows, grad_ctx, back)

time: 85.1 us -> 86.7 us (1.019)
  the two profiles are of different devices: /device:TPU:63 before, /device:TPU:6 now
where the time goes in v14:
time: 86.7 us; the launch traced here: 86.2 us
  starting transfers between devices  38.5 us (44%)
  waiting for transfers between devices  31 us (36%)
  Pallas kernels  13 us (15%)
  other arithmetic  2.11 us (2%)
    ppermute x8, starting transfers between devices, send(): lax.ppermute(block, 'dp', [(index(*p), index(*to(*p))) for p in PLACES])  25.2 us
    ppermute x8, waiting for transfers between devices, send(): lax.ppermute(block, 'dp', [(index(*p), index(*to(*p))) for p in PLACES])  14.7 us
    ppermute x1, waiting for transfers between devices, local(): lax.ppermute(leave, 'dp', [(i, (i + 1) % ranks) for i in range(ranks)])  11.6 us
    all_to_all x1, starting transfers between devices, local(): sums = lax.all_to_all(sums, 'dp', 0, 0, axis_index_groups=same_place())  8.31 us
    all_to_all x1, waiting for transfers between devices, local(): sums = lax.all_to_all(sums, 'dp', 0, 0, axis_index_groups=same_place())  4.67 us
    pallas_call x1, Pallas kernels, backward(): pl.pallas_call(backward_kernel, in_specs=[VMEM] * 7, out_specs=[VMEM] * 3...  3.76 us
    ppermute x1, starting transfers between devices, local(): lax.ppermute(tail, 'dp', [((i + 1) % ranks, i) for i in range(ranks)])  3.06 us
    pallas_call x1, Pallas kernels, staying_context(): pl.pallas_call(context_kernel, in_specs=[VMEM] * 5 + [pl.BlockSpec(memory...  2.95 us
  transfers between devices with their start and end apart: 11, of which 7 were waited for; matrix products, arithmetic and copies ran while one was open for 1% of the time, Pallas kernels for 12%

profile of v14, /device:TPU:6, one launch (start us, length us, event | category | flops | bytes accessed | tf_op | source)
XLA Modules:
  0.0 86.2 jit_solution(6669184436914615497)
XLA Ops:
  0.6 1.7 %shard_map.102 = (bf16[256,128]{1,0:T(8,128)(2,1)S(1)}, s32[8,384]{1,0:T(8,128)S(1)}, s32[8,128]{1,0:T(8,128)S(1)}, bf16[384,256]{1,0:T(8,128)(2,1)S(1)}, bf16[3...) custom-call(s32[384]{0:T(512)} %ids_hbm.1, s32[384]{0:T(512)} %slot_hbm.1, bf16[384,256]{1,0:T(8,128)(2,1)} %q_ref.1, ...), custom_call_target="tpu_custom_call" | custom-call | tf_op jit(solution)/shard_map/pallas_call | solution.py:68
  2.4 1.9 %collective-permute-start = (bf16[256,128]{1,0:T(8,128)(2,1)S(1)}, bf16[256,128]{1,0:T(8,128)(2,1)S(1)}, u32[]{:S(2)}, u32[]{:S(2)}) collective-permute-start(bf16[256,128]{1,0:T(8,128)(2,1)S(1)} %get-tuple-element.38), channel_id=1, source_target_pairs={{0,16},{16,32},{32,48},{48,64},{64,80},{80,96},{96,112},{112,128},... | collective-permute-start | bytes 196616 | tf_op jit(solution)/shard_map/ppermute | solution.py:224
  4.3 0.0 copy-start
  4.3 2.9 %shard_map.103 = (bf16[256,384]{1,0:T(8,128)(2,1)S(1)}, bf16[512,6144]{1,0:T(8,128)(2,1)S(1)}) custom-call(s32[8,384]{1,0:T(8,128)S(1)} %get-tuple-element.29.same_ref, s32[8,128]{1,0:T(8,128)S(1)} %get-tuple-element.30.stays_ref, bf16[384,256]{1,0:T(8,128)(2,1)S(1)} %get-tuple-element.31.q_ref, bf16[384,256]{1,0:T(8,128)(2,1)S(1)} %get-tuple-element.32.k_ref, ...), custom_call_target="tpu_custom_call" | custom-call | tf_op jit(solution)/shard_map/pallas_call | solution.py:98
  7.3 0.7 copy-done
  8.0 1.8 %shard_map.104.g_ref = bf16[512,256]{1,0:T(8,128)(2,1)S(1)} custom-call(bf16[512,6144]{1,0:T(8,128)(2,1)S(1)} %get-tuple-element.35.g_ref, bf16[256,6144]{1,0:T(8,128)(2,1)S(1)} %copy-done), custom_call_target="tpu_custom_call" | custom-call | tf_op jit(solution)/shard_map/pallas_call | solution.py:148
  9.8 11.6 %collective-permute-done.came_ref = bf16[256,128]{1,0:T(8,128)(2,1)S(1)} collective-permute-done((bf16[256,128]{1,0:T(8,128)(2,1)S(1)}, bf16[256,128]{1,0:T(8,128)(2,1)S(1)}, u32[]{:S(2)}, u32[]{:S(2)}) %collective-permute-start) | collective-permute-done | bytes 65568 | tf_op jit(solution)/shard_map/ppermute | solution.py:224
  21.5 1.3 %shard_map.106 = bf16[6144,128]{1,0:T(8,128)(2,1)S(1)} custom-call(bf16[256,384]{1,0:T(8,128)(2,1)S(1)} %get-tuple-element.37.stay_ref, bf16[256,128]{1,0:T(8,128)(2,1)S(1)} %collective-permute-done.came_ref, bf16[512,6144]{1,0:T(8,128)(2,1)S(1)} %get-tuple-element.35.g_ref), custom_call_target="tpu_custom_call" | custom-call | tf_op jit(solution)/shard_map/pallas_call | solution.py:129
  22.8 1.9 %collective-permute-start.1 = (bf16[6144,128]{1,0:T(8,128)(2,1)S(1)}, bf16[6144,128]{1,0:T(8,128)(2,1)S(1)}, u32[]{:S(2)}, u32[]{:S(2)}) collective-permute-start(bf16[6144,128]{1,0:T(8,128)(2,1)S(1)} %shard_map.106), channel_id=1, source_target_pairs={{0,16},{16,0},{32,48},{48,32},{64,80},{80,64},{96,112},{112,96},{1... | collective-permute-start | bytes 4718600 | tf_op jit(solution)/shard_map/ppermute | solution.py:197
  24.7 1.4 %shard_map.105 = bf16[6144,128]{1,0:T(8,128)(2,1)S(1)} custom-call(bf16[256,384]{1,0:T(8,128)(2,1)S(1)} %get-tuple-element.37.stay_ref, bf16[256,128]{1,0:T(8,128)(2,1)S(1)} %collective-permute-done.came_ref, bf16[512,6144]{1,0:T(8,128)(2,1)S(1)} %get-tuple-element.35.g_ref), custom_call_target="tpu_custom_call" | custom-call | tf_op jit(solution)/shard_map/pallas_call | solution.py:129
  26.2 2.0 %collective-permute-done.1 = bf16[6144,128]{1,0:T(8,128)(2,1)S(1)} collective-permute-done((bf16[6144,128]{1,0:T(8,128)(2,1)S(1)}, bf16[6144,128]{1,0:T(8,128)(2,1)S(1)}, u32[]{:S(2)}, u32[]{:S(2)}) %collective-permute-start.1) | collective-permute-done | bytes 1572896 | tf_op jit(solution)/shard_map/ppermute | solution.py:197
  28.1 0.4 add_convert_fusion.6
  28.5 1.9 %collective-permute-start.2 = (bf16[768,128]{1,0:T(8,128)(2,1)S(1)}, bf16[768,128]{1,0:T(8,128)(2,1)S(1)}, u32[]{:S(2)}, u32[]{:S(2)}) collective-permute-start(bf16[768,128]{1,0:T(8,128)(2,1)S(1)} %get-tuple-element.43), channel_id=1, source_target_pairs={{0,32},{16,240},{32,64},{48,16},{64,96},{80,48},{96,128},{112,80},... | collective-permute-start | bytes 589832 | tf_op jit(solution)/shard_map/ppermute | solution.py:197
  30.5 5.1 %collective-permute-start.6 = (bf16[768,128]{1,0:T(8,128)(2,1)S(1)}, bf16[768,128]{1,0:T(8,128)(2,1)S(1)}, u32[]{:S(2)}, u32[]{:S(2)}) collective-permute-start(bf16[768,128]{1,0:T(8,128)(2,1)S(1)} %get-tuple-element.47), channel_id=1, source_target_pairs={{0,224},{16,48},{32,0},{48,80},{64,32},{80,112},{96,64},{112,144},... | collective-permute-start | bytes 589832 | tf_op jit(solution)/shard_map/ppermute | solution.py:197
  35.6 2.7 %collective-permute-done.2 = bf16[768,128]{1,0:T(8,128)(2,1)S(1)} collective-permute-done((bf16[768,128]{1,0:T(8,128)(2,1)S(1)}, bf16[768,128]{1,0:T(8,128)(2,1)S(1)}, u32[]{:S(2)}, u32[]{:S(2)}) %collective-permute-start.2) | collective-permute-done | bytes 196640 | tf_op jit(solution)/shard_map/ppermute | solution.py:197
  38.3 0.1 add_convert_fusion.5
  38.4 1.9 %collective-permute-start.3 = (bf16[768,128]{1,0:T(8,128)(2,1)S(1)}, bf16[768,128]{1,0:T(8,128)(2,1)S(1)}, u32[]{:S(2)}, u32[]{:S(2)}) collective-permute-start(bf16[768,128]{1,0:T(8,128)(2,1)S(1)} %add_convert_fusion.5), channel_id=1, source_target_pairs={{0,32},{16,240},{32,64},{48,16},{64,96},{80,48},{96,128},{112,80},... | collective-permute-start | bytes 589832 | tf_op jit(solution)/shard_map/ppermute | solution.py:197
  40.3 0.0 collective-permute-done.6
  40.3 0.1 add_convert_fusion.2
  40.4 0.0 copy-start.1
  40.4 0.0 copy-start.2
  40.4 0.0 copy-start.3
  40.4 5.3 %collective-permute-start.7 = (bf16[768,128]{1,0:T(8,128)(2,1)S(1)}, bf16[768,128]{1,0:T(8,128)(2,1)S(1)}, u32[]{:S(2)}, u32[]{:S(2)}) collective-permute-start(bf16[768,128]{1,0:T(8,128)(2,1)S(1)} %add_convert_fusion.2), channel_id=1, source_target_pairs={{0,224},{16,48},{32,0},{48,80},{64,32},{80,112},{96,64},{112,144},... | collective-permute-start | bytes 589832 | tf_op jit(solution)/shard_map/ppermute | solution.py:197
  45.7 3.4 %collective-permute-done.3 = bf16[768,128]{1,0:T(8,128)(2,1)S(1)} collective-permute-done((bf16[768,128]{1,0:T(8,128)(2,1)S(1)}, bf16[768,128]{1,0:T(8,128)(2,1)S(1)}, u32[]{:S(2)}, u32[]{:S(2)}) %collective-permute-start.3) | collective-permute-done | bytes 196640 | tf_op jit(solution)/shard_map/ppermute | solution.py:197
  49.1 0.1 add_convert_fusion.4
  49.1 1.9 %collective-permute-start.4 = (bf16[768,128]{1,0:T(8,128)(2,1)S(1)}, bf16[768,128]{1,0:T(8,128)(2,1)S(1)}, u32[]{:S(2)}, u32[]{:S(2)}) collective-permute-start(bf16[768,128]{1,0:T(8,128)(2,1)S(1)} %add_convert_fusion.4), channel_id=1, source_target_pairs={{0,32},{16,240},{32,64},{48,16},{64,96},{80,48},{96,128},{112,80},... | collective-permute-start | bytes 589832 | tf_op jit(solution)/shard_map/ppermute | solution.py:197
  51.1 0.0 collective-permute-done.7
  51.1 0.1 add_convert_fusion.1
  51.1 5.2 %collective-permute-start.8 = (bf16[768,128]{1,0:T(8,128)(2,1)S(1)}, bf16[768,128]{1,0:T(8,128)(2,1)S(1)}, u32[]{:S(2)}, u32[]{:S(2)}) collective-permute-start(bf16[768,128]{1,0:T(8,128)(2,1)S(1)} %add_convert_fusion.1), channel_id=1, source_target_pairs={{0,224},{16,48},{32,0},{48,80},{64,32},{80,112},{96,64},{112,144},... | collective-permute-start | bytes 589832 | tf_op jit(solution)/shard_map/ppermute | solution.py:197
  56.3 2.8 %collective-permute-done.4 = bf16[768,128]{1,0:T(8,128)(2,1)S(1)} collective-permute-done((bf16[768,128]{1,0:T(8,128)(2,1)S(1)}, bf16[768,128]{1,0:T(8,128)(2,1)S(1)}, u32[]{:S(2)}, u32[]{:S(2)}) %collective-permute-start.4) | collective-permute-done | bytes 196640 | tf_op jit(solution)/shard_map/ppermute | solution.py:197
  59.2 0.1 add_convert_fusion.3
  59.2 1.9 %collective-permute-start.5 = (bf16[768,128]{1,0:T(8,128)(2,1)S(1)}, bf16[768,128]{1,0:T(8,128)(2,1)S(1)}, u32[]{:S(2)}, u32[]{:S(2)}) collective-permute-start(bf16[768,128]{1,0:T(8,128)(2,1)S(1)} %add_convert_fusion.3), channel_id=1, source_target_pairs={{0,32},{16,240},{32,64},{48,16},{64,96},{80,48},{96,128},{112,80},... | collective-permute-start | bytes 589832 | tf_op jit(solution)/shard_map/ppermute | solution.py:197
  61.2 3.1 %collective-permute-start.9 = (bf16[128,256]{1,0:T(8,128)(2,1)S(1)}, bf16[128,256]{1,0:T(8,128)(2,1)S(1)}, u32[]{:S(2)}, u32[]{:S(2)}) collective-permute-start(bf16[128,256]{1,0:T(8,128)(2,1)S(1)} %slice.67), channel_id=1, source_target_pairs={{16,0},{32,16},{48,32},{64,48},{80,64},{96,80},{112,96},{128,112},... | collective-permute-start | bytes 196616 | tf_op jit(solution)/shard_map/ppermute | solution.py:242
  64.2 0.0 collective-permute-done.8
  64.2 3.8 %collective-permute-done.5 = bf16[768,128]{1,0:T(8,128)(2,1)S(1)} collective-permute-done((bf16[768,128]{1,0:T(8,128)(2,1)S(1)}, bf16[768,128]{1,0:T(8,128)(2,1)S(1)}, u32[]{:S(2)}, u32[]{:S(2)}) %collective-permute-start.5) | collective-permute-done | bytes 196640 | tf_op jit(solution)/shard_map/ppermute | solution.py:197
  68.0 0.8 add_convert_fusion
  68.8 0.0 collective-permute-done.9.back_ref
  68.8 8.3 %all-to-all-start = ((bf16[3,256,128]{2,1,0:T(8,128)(2,1)}), bf16[3,256,128]{2,1,0:T(8,128)(2,1)S(1)}, u32[]{:S(2)}, u32[]{:S(2)}) async-start(bf16[3,256,128]{2,1,0:T(8,128)(2,1)} %bitcast), calls=%async_computation | async-start | bytes 393216 | tf_op jit(solution)/shard_map/all_to_all | solution.py:246
  77.1 0.0 copy-done.1
  77.1 0.0 copy-done.2
  77.1 0.0 copy-done.3
  77.1 3.8 %shard_map.107 = (bf16[384,256]{1,0:T(8,128)(2,1)}, bf16[384,256]{1,0:T(8,128)(2,1)}, bf16[384,256]{1,0:T(8,128)(2,1)}) custom-call(s32[8,384]{1,0:T(8,128)S(1)} %get-tuple-element.29.same_ref, s32[8,128]{1,0:T(8,128)S(1)} %get-tuple-element.30.stays_ref, bf16[384,256]{1,0:T(8,128)(2,1)S(1)} %copy-done.1, bf16[384,256]{1,0:T(8,128)(2,1)S(1)} %copy-done.2, ...), custom_call_target="tpu_custom_call" | custom-call | tf_op jit(solution)/shard_map/pallas_call | solution.py:180
  80.8 4.7 %all-to-all-done = bf16[3,256,128]{2,1,0:T(8,128)(2,1)S(1)} async-done(((bf16[3,256,128]{2,1,0:T(8,128)(2,1)}), bf16[3,256,128]{2,1,0:T(8,128)(2,1)S(1)}, u32[]{:S(2)}, u32[]{:S(2)}) %all-to-all-start) | async-done | bytes 196640 | tf_op jit(solution)/shard_map/all_to_all | solution.py:246
  85.5 0.7 add_bitcast_fusion
  (1 shorter events, 0.0 us)
Async XLA Ops:
  2.4 19.1 %collective-permute-start = (bf16[256,128]{1,0:T(8,128)(2,1)S(1)}, bf16[256,128]{1,0:T(8,128)(2,1)S(1)}, u32[]{:S(2)}, u32[]{:S(2)}) collective-permute-start(bf16[256,128]{1,0:T(8,128)(2,1)S(1)} %get-tuple-element.38), channel_id=1, source_target_pairs={{0,16},{16,32},{32,48},{48,64},{64,80},{80,96},{96,112},{112,128},... | collective-permute-start | bytes 196616 | tf_op jit(solution)/shard_map/ppermute | solution.py:224
  4.3 3.7 %copy-start = (bf16[256,6144]{1,0:T(8,128)(2,1)S(1)}, bf16[256,6144]{1,0:T(8,128)(2,1)}, u32[]{:S(2)}) copy-start(bf16[256,6144]{1,0:T(8,128)(2,1)} %w_ref.1) | copy-start | bytes 9437188
  22.8 5.3 %collective-permute-start.1 = (bf16[6144,128]{1,0:T(8,128)(2,1)S(1)}, bf16[6144,128]{1,0:T(8,128)(2,1)S(1)}, u32[]{:S(2)}, u32[]{:S(2)}) collective-permute-start(bf16[6144,128]{1,0:T(8,128)(2,1)S(1)} %shard_map.106), channel_id=1, source_target_pairs={{0,16},{16,0},{32,48},{48,32},{64,80},{80,64},{96,112},{112,96},{1... | collective-permute-start | bytes 4718600 | tf_op jit(solution)/shard_map/ppermute | solution.py:197
  28.5 9.8 %collective-permute-start.2 = (bf16[768,128]{1,0:T(8,128)(2,1)S(1)}, bf16[768,128]{1,0:T(8,128)(2,1)S(1)}, u32[]{:S(2)}, u32[]{:S(2)}) collective-permute-start(bf16[768,128]{1,0:T(8,128)(2,1)S(1)} %get-tuple-element.43), channel_id=1, source_target_pairs={{0,32},{16,240},{32,64},{48,16},{64,96},{80,48},{96,128},{112,80},... | collective-permute-start | bytes 589832 | tf_op jit(solution)/shard_map/ppermute | solution.py:197
  30.5 9.8 %collective-permute-start.6 = (bf16[768,128]{1,0:T(8,128)(2,1)S(1)}, bf16[768,128]{1,0:T(8,128)(2,1)S(1)}, u32[]{:S(2)}, u32[]{:S(2)}) collective-permute-start(bf16[768,128]{1,0:T(8,128)(2,1)S(1)} %get-tuple-element.47), channel_id=1, source_target_pairs={{0,224},{16,48},{32,0},{48,80},{64,32},{80,112},{96,64},{112,144},... | collective-permute-start | bytes 589832 | tf_op jit(solution)/shard_map/ppermute | solution.py:197
  38.4 10.7 %collective-permute-start.3 = (bf16[768,128]{1,0:T(8,128)(2,1)S(1)}, bf16[768,128]{1,0:T(8,128)(2,1)S(1)}, u32[]{:S(2)}, u32[]{:S(2)}) collective-permute-start(bf16[768,128]{1,0:T(8,128)(2,1)S(1)} %add_convert_fusion.5), channel_id=1, source_target_pairs={{0,32},{16,240},{32,64},{48,16},{64,96},{80,48},{96,128},{112,80},... | collective-permute-start | bytes 589832 | tf_op jit(solution)/shard_map/ppermute | solution.py:197
  40.4 36.7 %copy-start.1 = (bf16[384,256]{1,0:T(8,128)(2,1)S(1)}, bf16[384,256]{1,0:T(8,128)(2,1)}, u32[]{:S(2)}) copy-start(bf16[384,256]{1,0:T(8,128)(2,1)} %q_ref.1) | copy-start | bytes 589828
  40.4 36.7 %copy-start.2 = (bf16[384,256]{1,0:T(8,128)(2,1)S(1)}, bf16[384,256]{1,0:T(8,128)(2,1)}, u32[]{:S(2)}) copy-start(bf16[384,256]{1,0:T(8,128)(2,1)} %k_ref.1) | copy-start | bytes 589828
  40.4 36.7 %copy-start.3 = (bf16[384,256]{1,0:T(8,128)(2,1)S(1)}, bf16[384,256]{1,0:T(8,128)(2,1)}, u32[]{:S(2)}) copy-start(bf16[384,256]{1,0:T(8,128)(2,1)} %v_ref.1) | copy-start | bytes 589828
  40.4 10.7 %collective-permute-start.7 = (bf16[768,128]{1,0:T(8,128)(2,1)S(1)}, bf16[768,128]{1,0:T(8,128)(2,1)S(1)}, u32[]{:S(2)}, u32[]{:S(2)}) collective-permute-start(bf16[768,128]{1,0:T(8,128)(2,1)S(1)} %add_convert_fusion.2), channel_id=1, source_target_pairs={{0,224},{16,48},{32,0},{48,80},{64,32},{80,112},{96,64},{112,144},... | collective-permute-start | bytes 589832 | tf_op jit(solution)/shard_map/ppermute | solution.py:197
  49.1 10.0 %collective-permute-start.4 = (bf16[768,128]{1,0:T(8,128)(2,1)S(1)}, bf16[768,128]{1,0:T(8,128)(2,1)S(1)}, u32[]{:S(2)}, u32[]{:S(2)}) collective-permute-start(bf16[768,128]{1,0:T(8,128)(2,1)S(1)} %add_convert_fusion.4), channel_id=1, source_target_pairs={{0,32},{16,240},{32,64},{48,16},{64,96},{80,48},{96,128},{112,80},... | collective-permute-start | bytes 589832 | tf_op jit(solution)/shard_map/ppermute | solution.py:197
  51.1 13.1 %collective-permute-start.8 = (bf16[768,128]{1,0:T(8,128)(2,1)S(1)}, bf16[768,128]{1,0:T(8,128)(2,1)S(1)}, u32[]{:S(2)}, u32[]{:S(2)}) collective-permute-start(bf16[768,128]{1,0:T(8,128)(2,1)S(1)} %add_convert_fusion.1), channel_id=1, source_target_pairs={{0,224},{16,48},{32,0},{48,80},{64,32},{80,112},{96,64},{112,144},... | collective-permute-start | bytes 589832 | tf_op jit(solution)/shard_map/ppermute | solution.py:197
  59.2 8.8 %collective-permute-start.5 = (bf16[768,128]{1,0:T(8,128)(2,1)S(1)}, bf16[768,128]{1,0:T(8,128)(2,1)S(1)}, u32[]{:S(2)}, u32[]{:S(2)}) collective-permute-start(bf16[768,128]{1,0:T(8,128)(2,1)S(1)} %add_convert_fusion.3), channel_id=1, source_target_pairs={{0,32},{16,240},{32,64},{48,16},{64,96},{80,48},{96,128},{112,80},... | collective-permute-start | bytes 589832 | tf_op jit(solution)/shard_map/ppermute | solution.py:197
  61.2 7.6 %collective-permute-start.9 = (bf16[128,256]{1,0:T(8,128)(2,1)S(1)}, bf16[128,256]{1,0:T(8,128)(2,1)S(1)}, u32[]{:S(2)}, u32[]{:S(2)}) collective-permute-start(bf16[128,256]{1,0:T(8,128)(2,1)S(1)} %slice.67), channel_id=1, source_target_pairs={{16,0},{32,16},{48,32},{64,48},{80,64},{96,80},{112,96},{128,112},... | collective-permute-start | bytes 196616 | tf_op jit(solution)/shard_map/ppermute | solution.py:242
  68.8 16.7 %all-to-all-start = ((bf16[3,256,128]{2,1,0:T(8,128)(2,1)}), bf16[3,256,128]{2,1,0:T(8,128)(2,1)S(1)}, u32[]{:S(2)}, u32[]{:S(2)}) async-start(bf16[3,256,128]{2,1,0:T(8,128)(2,1)} %bitcast), calls=%async_computation | async-start | bytes 393216 | tf_op jit(solution)/shard_map/all_to_all | solution.py:246

commit v15 on v10

--- a/solution.py
+++ b/solution.py
@@ -237,6 +237,7 @@
     part = dict(zip(ORDER, lax.optimization_barrier(parts), strict=True))
     far, up, down = send(part[4], along_y(2)), send(part[3], along_y(1)), send(part[-3], along_y(-1))
     near = send(part[1], along_y(1)), send(part[-1], along_y(-1))
+    far, up, down = lax.optimization_barrier((far, up, down))
 
     up, down = rounded_total(part[2], up, far), rounded_total(part[-2], down)
     up, down, tail = lax.optimization_barrier((up, down, grad_ctx[row_count:]))

time: 81.3 us -> 81.8 us (level)
  the two profiles are of different devices: /device:TPU:6 before, /device:TPU:1 now
where the time goes in v15:
time: 81.8 us; the launch traced here: 81.3 us
  starting transfers between devices  48.4 us (59%)
  waiting for transfers between devices  16.2 us (20%)
  Pallas kernels  13 us (16%)
  other arithmetic  2.02 us (2%)
  between operations  0.84 us (1%)
    ppermute x8, starting transfers between devices, send(): lax.ppermute(block, 'dp', [(index(*p), index(*to(*p))) for p in PLACES])  29.6 us
    all_to_all x1, starting transfers between devices, local(): sums = lax.all_to_all(sums, 'dp', 0, 0, axis_index_groups=same_place())  8.3 us
    all_to_all x1, waiting for transfers between devices, local(): sums = lax.all_to_all(sums, 'dp', 0, 0, axis_index_groups=same_place())  6.63 us
    ppermute x8, waiting for transfers between devices, send(): lax.ppermute(block, 'dp', [(index(*p), index(*to(*p))) for p in PLACES])  6.54 us
    ppermute x1, starting transfers between devices, local(): lax.ppermute(tail, 'dp', [((i + 1) % ranks, i) for i in range(ranks)])  5.89 us
    ppermute x1, starting transfers between devices, local(): lax.ppermute(leave, 'dp', [(i, (i + 1) % ranks) for i in range(ranks)])  4.6 us
    pallas_call x1, Pallas kernels, backward(): pl.pallas_call(backward_kernel, in_specs=[VMEM] * 7, out_specs=[VMEM] * 3...  3.76 us
    ppermute x1, waiting for transfers between devices, local(): lax.ppermute(leave, 'dp', [(i, (i + 1) % ranks) for i in range(ranks)])  3.04 us
  transfers between devices with their start and end apart: 11, of which 5 were waited for; matrix products, arithmetic and copies ran while one was open for 1% of the time, Pallas kernels for 12%

profile of v15, /device:TPU:1, one launch (start us, length us, event | category | flops | bytes accessed | tf_op | source)
XLA Modules:
  0.0 81.3 jit_solution(7010043508384739528)
XLA Ops:
  0.6 1.7 %shard_map.102 = (bf16[256,128]{1,0:T(8,128)(2,1)S(1)}, s32[8,384]{1,0:T(8,128)S(1)}, s32[8,128]{1,0:T(8,128)S(1)}, bf16[384,256]{1,0:T(8,128)(2,1)S(1)}, bf16[3...) custom-call(s32[384]{0:T(512)} %ids_hbm.1, s32[384]{0:T(512)} %slot_hbm.1, bf16[384,256]{1,0:T(8,128)(2,1)} %q_ref.1, ...), custom_call_target="tpu_custom_call" | custom-call | tf_op jit(solution)/shard_map/pallas_call | solution.py:68
  2.4 4.6 %collective-permute-start = (bf16[256,128]{1,0:T(8,128)(2,1)S(1)}, bf16[256,128]{1,0:T(8,128)(2,1)S(1)}, u32[]{:S(2)}, u32[]{:S(2)}) collective-permute-start(bf16[256,128]{1,0:T(8,128)(2,1)S(1)} %get-tuple-element.42), channel_id=1, source_target_pairs={{0,16},{16,32},{32,48},{48,64},{64,80},{80,96},{96,112},{112,128},... | collective-permute-start | bytes 196616 | tf_op jit(solution)/shard_map/ppermute | solution.py:224
  7.0 0.0 copy-start
  7.0 2.9 %shard_map.103 = (bf16[256,384]{1,0:T(8,128)(2,1)S(1)}, bf16[512,6144]{1,0:T(8,128)(2,1)S(1)}) custom-call(s32[8,384]{1,0:T(8,128)S(1)} %get-tuple-element.33.same_ref, s32[8,128]{1,0:T(8,128)S(1)} %get-tuple-element.34.stays_ref, bf16[384,256]{1,0:T(8,128)(2,1)S(1)} %get-tuple-element.35.q_ref, bf16[384,256]{1,0:T(8,128)(2,1)S(1)} %get-tuple-element.36.k_ref, ...), custom_call_target="tpu_custom_call" | custom-call | tf_op jit(solution)/shard_map/pallas_call | solution.py:98
  10.0 0.7 copy-done
  10.7 1.8 %shard_map.104.g_ref = bf16[512,256]{1,0:T(8,128)(2,1)S(1)} custom-call(bf16[512,6144]{1,0:T(8,128)(2,1)S(1)} %get-tuple-element.39.g_ref, bf16[256,6144]{1,0:T(8,128)(2,1)S(1)} %copy-done), custom_call_target="tpu_custom_call" | custom-call | tf_op jit(solution)/shard_map/pallas_call | solution.py:148
  12.5 3.0 %collective-permute-done.came_ref = bf16[256,128]{1,0:T(8,128)(2,1)S(1)} collective-permute-done((bf16[256,128]{1,0:T(8,128)(2,1)S(1)}, bf16[256,128]{1,0:T(8,128)(2,1)S(1)}, u32[]{:S(2)}, u32[]{:S(2)}) %collective-permute-start) | collective-permute-done | bytes 65568 | tf_op jit(solution)/shard_map/ppermute | solution.py:224
  15.6 1.4 %shard_map.106 = bf16[6144,128]{1,0:T(8,128)(2,1)S(1)} custom-call(bf16[256,384]{1,0:T(8,128)(2,1)S(1)} %get-tuple-element.41.stay_ref, bf16[256,128]{1,0:T(8,128)(2,1)S(1)} %collective-permute-done.came_ref, bf16[512,6144]{1,0:T(8,128)(2,1)S(1)} %get-tuple-element.39.g_ref), custom_call_target="tpu_custom_call" | custom-call | tf_op jit(solution)/shard_map/pallas_call | solution.py:129
  16.9 10.8 %collective-permute-start.1 = (bf16[6144,128]{1,0:T(8,128)(2,1)S(1)}, bf16[6144,128]{1,0:T(8,128)(2,1)S(1)}, u32[]{:S(2)}, u32[]{:S(2)}) collective-permute-start(bf16[6144,128]{1,0:T(8,128)(2,1)S(1)} %shard_map.106), channel_id=1, source_target_pairs={{0,16},{16,0},{32,48},{48,32},{64,80},{80,64},{96,112},{112,96},{1... | collective-permute-start | bytes 4718600 | tf_op jit(solution)/shard_map/ppermute | solution.py:197
  27.8 1.4 %shard_map.105 = bf16[6144,128]{1,0:T(8,128)(2,1)S(1)} custom-call(bf16[256,384]{1,0:T(8,128)(2,1)S(1)} %get-tuple-element.41.stay_ref, bf16[256,128]{1,0:T(8,128)(2,1)S(1)} %collective-permute-done.came_ref, bf16[512,6144]{1,0:T(8,128)(2,1)S(1)} %get-tuple-element.39.g_ref), custom_call_target="tpu_custom_call" | custom-call | tf_op jit(solution)/shard_map/pallas_call | solution.py:129
  29.2 1.6 %collective-permute-done.1 = bf16[6144,128]{1,0:T(8,128)(2,1)S(1)} collective-permute-done((bf16[6144,128]{1,0:T(8,128)(2,1)S(1)}, bf16[6144,128]{1,0:T(8,128)(2,1)S(1)}, u32[]{:S(2)}, u32[]{:S(2)}) %collective-permute-start.1) | collective-permute-done | bytes 1572896 | tf_op jit(solution)/shard_map/ppermute | solution.py:197
  30.8 0.4 add_convert_fusion.3
  31.2 0.0 copy-start.1
  31.2 0.0 copy-start.2
  31.2 0.0 copy-start.3
  31.2 2.1 %collective-permute-start.2 = (bf16[768,128]{1,0:T(8,128)(2,1)S(1)}, bf16[768,128]{1,0:T(8,128)(2,1)S(1)}, u32[]{:S(2)}, u32[]{:S(2)}) collective-permute-start(bf16[768,128]{1,0:T(8,128)(2,1)S(1)} %get-tuple-element.45), channel_id=1, source_target_pairs={{0,64},{16,208},{32,96},{48,240},{64,128},{80,16},{96,160},{112,48... | collective-permute-start | bytes 589832 | tf_op jit(solution)/shard_map/ppermute | solution.py:197
  33.3 1.9 %collective-permute-start.3 = (bf16[768,128]{1,0:T(8,128)(2,1)S(1)}, bf16[768,128]{1,0:T(8,128)(2,1)S(1)}, u32[]{:S(2)}, u32[]{:S(2)}) collective-permute-start(bf16[768,128]{1,0:T(8,128)(2,1)S(1)} %get-tuple-element.46), channel_id=1, source_target_pairs={{0,32},{16,240},{32,64},{48,16},{64,96},{80,48},{96,128},{112,80},... | collective-permute-start | bytes 589832 | tf_op jit(solution)/shard_map/ppermute | solution.py:197
  35.2 3.4 %collective-permute-start.4 = (bf16[768,128]{1,0:T(8,128)(2,1)S(1)}, bf16[768,128]{1,0:T(8,128)(2,1)S(1)}, u32[]{:S(2)}, u32[]{:S(2)}) collective-permute-start(bf16[768,128]{1,0:T(8,128)(2,1)S(1)} %get-tuple-element.47), channel_id=1, source_target_pairs={{0,224},{16,48},{32,0},{48,80},{64,32},{80,112},{96,64},{112,144},... | collective-permute-start | bytes 589832 | tf_op jit(solution)/shard_map/ppermute | solution.py:197
  38.6 3.1 %collective-permute-start.7 = (bf16[768,128]{1,0:T(8,128)(2,1)S(1)}, bf16[768,128]{1,0:T(8,128)(2,1)S(1)}, u32[]{:S(2)}, u32[]{:S(2)}) collective-permute-start(bf16[768,128]{1,0:T(8,128)(2,1)S(1)} %get-tuple-element.54), channel_id=1, source_target_pairs={{0,32},{16,240},{32,64},{48,16},{64,96},{80,48},{96,128},{112,80},... | collective-permute-start | bytes 589832 | tf_op jit(solution)/shard_map/ppermute | solution.py:197
  41.7 2.2 %collective-permute-start.8 = (bf16[768,128]{1,0:T(8,128)(2,1)S(1)}, bf16[768,128]{1,0:T(8,128)(2,1)S(1)}, u32[]{:S(2)}, u32[]{:S(2)}) collective-permute-start(bf16[768,128]{1,0:T(8,128)(2,1)S(1)} %get-tuple-element.55), channel_id=1, source_target_pairs={{0,224},{16,48},{32,0},{48,80},{64,32},{80,112},{96,64},{112,144},... | collective-permute-start | bytes 589832 | tf_op jit(solution)/shard_map/ppermute | solution.py:197
  43.9 0.0 collective-permute-done.2
  43.9 0.0 collective-permute-done.3
  43.9 1.7 %collective-permute-done.4 = bf16[768,128]{1,0:T(8,128)(2,1)S(1)} collective-permute-done((bf16[768,128]{1,0:T(8,128)(2,1)S(1)}, bf16[768,128]{1,0:T(8,128)(2,1)S(1)}, u32[]{:S(2)}, u32[]{:S(2)}) %collective-permute-start.4) | collective-permute-done | bytes 196640 | tf_op jit(solution)/shard_map/ppermute | solution.py:197
  45.6 0.1 add_convert_fusion.1
  45.8 1.9 %collective-permute-start.5 = (bf16[768,128]{1,0:T(8,128)(2,1)S(1)}, bf16[768,128]{1,0:T(8,128)(2,1)S(1)}, u32[]{:S(2)}, u32[]{:S(2)}) collective-permute-start(bf16[768,128]{1,0:T(8,128)(2,1)S(1)} %get-tuple-element.52), channel_id=1, source_target_pairs={{0,64},{16,208},{32,96},{48,240},{64,128},{80,16},{96,160},{112,48... | collective-permute-start | bytes 589832 | tf_op jit(solution)/shard_map/ppermute | solution.py:197
  47.7 4.3 %collective-permute-start.6 = (bf16[768,128]{1,0:T(8,128)(2,1)S(1)}, bf16[768,128]{1,0:T(8,128)(2,1)S(1)}, u32[]{:S(2)}, u32[]{:S(2)}) collective-permute-start(bf16[768,128]{1,0:T(8,128)(2,1)S(1)} %get-tuple-element.53), channel_id=1, source_target_pairs={{0,192},{16,80},{32,224},{48,112},{64,0},{80,144},{96,32},{112,176... | collective-permute-start | bytes 589832 | tf_op jit(solution)/shard_map/ppermute | solution.py:197
  52.0 5.9 %collective-permute-start.9 = (bf16[128,256]{1,0:T(8,128)(2,1)S(1)}, bf16[128,256]{1,0:T(8,128)(2,1)S(1)}, u32[]{:S(2)}, u32[]{:S(2)}) collective-permute-start(bf16[128,256]{1,0:T(8,128)(2,1)S(1)} %slice.67), channel_id=1, source_target_pairs={{16,0},{32,16},{48,32},{64,48},{80,64},{96,80},{112,96},{128,112},... | collective-permute-start | bytes 196616 | tf_op jit(solution)/shard_map/ppermute | solution.py:245
  57.9 0.0 collective-permute-done.7
  57.9 0.0 collective-permute-done.8
  57.9 0.0 collective-permute-done.5
  57.9 3.2 %collective-permute-done.6 = bf16[768,128]{1,0:T(8,128)(2,1)S(1)} collective-permute-done((bf16[768,128]{1,0:T(8,128)(2,1)S(1)}, bf16[768,128]{1,0:T(8,128)(2,1)S(1)}, u32[]{:S(2)}, u32[]{:S(2)}) %collective-permute-start.6) | collective-permute-done | bytes 196640 | tf_op jit(solution)/shard_map/ppermute | solution.py:197
  61.1 0.8 add_convert_fusion
  61.9 0.0 collective-permute-done.9.back_ref
  61.9 8.3 %all-to-all-start = ((bf16[3,256,128]{2,1,0:T(8,128)(2,1)}), bf16[3,256,128]{2,1,0:T(8,128)(2,1)S(1)}, u32[]{:S(2)}, u32[]{:S(2)}) async-start(bf16[3,256,128]{2,1,0:T(8,128)(2,1)} %bitcast), calls=%async_computation | async-start | bytes 393216 | tf_op jit(solution)/shard_map/all_to_all | solution.py:248
  70.2 0.0 copy-done.1
  70.2 0.0 copy-done.2
  70.2 0.0 copy-done.3
  70.2 3.8 %shard_map.107 = (bf16[384,256]{1,0:T(8,128)(2,1)}, bf16[384,256]{1,0:T(8,128)(2,1)}, bf16[384,256]{1,0:T(8,128)(2,1)}) custom-call(s32[8,384]{1,0:T(8,128)S(1)} %get-tuple-element.33.same_ref, s32[8,128]{1,0:T(8,128)S(1)} %get-tuple-element.34.stays_ref, bf16[384,256]{1,0:T(8,128)(2,1)S(1)} %copy-done.1, bf16[384,256]{1,0:T(8,128)(2,1)S(1)} %copy-done.2, ...), custom_call_target="tpu_custom_call" | custom-call | tf_op jit(solution)/shard_map/pallas_call | solution.py:180
  74.0 6.6 %all-to-all-done = bf16[3,256,128]{2,1,0:T(8,128)(2,1)S(1)} async-done(((bf16[3,256,128]{2,1,0:T(8,128)(2,1)}), bf16[3,256,128]{2,1,0:T(8,128)(2,1)S(1)}, u32[]{:S(2)}, u32[]{:S(2)}) %all-to-all-start) | async-done | bytes 196640 | tf_op jit(solution)/shard_map/all_to_all | solution.py:248
  80.6 0.7 add_bitcast_fusion
  (1 shorter events, 0.0 us)
Async XLA Ops:
  2.4 13.2 %collective-permute-start = (bf16[256,128]{1,0:T(8,128)(2,1)S(1)}, bf16[256,128]{1,0:T(8,128)(2,1)S(1)}, u32[]{:S(2)}, u32[]{:S(2)}) collective-permute-start(bf16[256,128]{1,0:T(8,128)(2,1)S(1)} %get-tuple-element.42), channel_id=1, source_target_pairs={{0,16},{16,32},{32,48},{48,64},{64,80},{80,96},{96,112},{112,128},... | collective-permute-start | bytes 196616 | tf_op jit(solution)/shard_map/ppermute | solution.py:224
  7.0 3.7 %copy-start = (bf16[256,6144]{1,0:T(8,128)(2,1)S(1)}, bf16[256,6144]{1,0:T(8,128)(2,1)}, u32[]{:S(2)}) copy-start(bf16[256,6144]{1,0:T(8,128)(2,1)} %w_ref.1) | copy-start | bytes 9437188
  16.9 13.9 %collective-permute-start.1 = (bf16[6144,128]{1,0:T(8,128)(2,1)S(1)}, bf16[6144,128]{1,0:T(8,128)(2,1)S(1)}, u32[]{:S(2)}, u32[]{:S(2)}) collective-permute-start(bf16[6144,128]{1,0:T(8,128)(2,1)S(1)} %shard_map.106), channel_id=1, source_target_pairs={{0,16},{16,0},{32,48},{48,32},{64,80},{80,64},{96,112},{112,96},{1... | collective-permute-start | bytes 4718600 | tf_op jit(solution)/shard_map/ppermute | solution.py:197
  31.2 39.0 %copy-start.1 = (bf16[384,256]{1,0:T(8,128)(2,1)S(1)}, bf16[384,256]{1,0:T(8,128)(2,1)}, u32[]{:S(2)}) copy-start(bf16[384,256]{1,0:T(8,128)(2,1)} %q_ref.1) | copy-start | bytes 589828
  31.2 39.0 %copy-start.2 = (bf16[384,256]{1,0:T(8,128)(2,1)S(1)}, bf16[384,256]{1,0:T(8,128)(2,1)}, u32[]{:S(2)}) copy-start(bf16[384,256]{1,0:T(8,128)(2,1)} %k_ref.1) | copy-start | bytes 589828
  31.2 39.0 %copy-start.3 = (bf16[384,256]{1,0:T(8,128)(2,1)S(1)}, bf16[384,256]{1,0:T(8,128)(2,1)}, u32[]{:S(2)}) copy-start(bf16[384,256]{1,0:T(8,128)(2,1)} %v_ref.1) | copy-start | bytes 589828
  31.2 12.7 %collective-permute-start.2 = (bf16[768,128]{1,0:T(8,128)(2,1)S(1)}, bf16[768,128]{1,0:T(8,128)(2,1)S(1)}, u32[]{:S(2)}, u32[]{:S(2)}) collective-permute-start(bf16[768,128]{1,0:T(8,128)(2,1)S(1)} %get-tuple-element.45), channel_id=1, source_target_pairs={{0,64},{16,208},{32,96},{48,240},{64,128},{80,16},{96,160},{112,48... | collective-permute-start | bytes 589832 | tf_op jit(solution)/shard_map/ppermute | solution.py:197
  33.3 10.6 %collective-permute-start.3 = (bf16[768,128]{1,0:T(8,128)(2,1)S(1)}, bf16[768,128]{1,0:T(8,128)(2,1)S(1)}, u32[]{:S(2)}, u32[]{:S(2)}) collective-permute-start(bf16[768,128]{1,0:T(8,128)(2,1)S(1)} %get-tuple-element.46), channel_id=1, source_target_pairs={{0,32},{16,240},{32,64},{48,16},{64,96},{80,48},{96,128},{112,80},... | collective-permute-start | bytes 589832 | tf_op jit(solution)/shard_map/ppermute | solution.py:197
  35.2 10.4 %collective-permute-start.4 = (bf16[768,128]{1,0:T(8,128)(2,1)S(1)}, bf16[768,128]{1,0:T(8,128)(2,1)S(1)}, u32[]{:S(2)}, u32[]{:S(2)}) collective-permute-start(bf16[768,128]{1,0:T(8,128)(2,1)S(1)} %get-tuple-element.47), channel_id=1, source_target_pairs={{0,224},{16,48},{32,0},{48,80},{64,32},{80,112},{96,64},{112,144},... | collective-permute-start | bytes 589832 | tf_op jit(solution)/shard_map/ppermute | solution.py:197
  38.6 19.3 %collective-permute-start.7 = (bf16[768,128]{1,0:T(8,128)(2,1)S(1)}, bf16[768,128]{1,0:T(8,128)(2,1)S(1)}, u32[]{:S(2)}, u32[]{:S(2)}) collective-permute-start(bf16[768,128]{1,0:T(8,128)(2,1)S(1)} %get-tuple-element.54), channel_id=1, source_target_pairs={{0,32},{16,240},{32,64},{48,16},{64,96},{80,48},{96,128},{112,80},... | collective-permute-start | bytes 589832 | tf_op jit(solution)/shard_map/ppermute | solution.py:197
  41.7 16.1 %collective-permute-start.8 = (bf16[768,128]{1,0:T(8,128)(2,1)S(1)}, bf16[768,128]{1,0:T(8,128)(2,1)S(1)}, u32[]{:S(2)}, u32[]{:S(2)}) collective-permute-start(bf16[768,128]{1,0:T(8,128)(2,1)S(1)} %get-tuple-element.55), channel_id=1, source_target_pairs={{0,224},{16,48},{32,0},{48,80},{64,32},{80,112},{96,64},{112,144},... | collective-permute-start | bytes 589832 | tf_op jit(solution)/shard_map/ppermute | solution.py:197
  45.8 12.1 %collective-permute-start.5 = (bf16[768,128]{1,0:T(8,128)(2,1)S(1)}, bf16[768,128]{1,0:T(8,128)(2,1)S(1)}, u32[]{:S(2)}, u32[]{:S(2)}) collective-permute-start(bf16[768,128]{1,0:T(8,128)(2,1)S(1)} %get-tuple-element.52), channel_id=1, source_target_pairs={{0,64},{16,208},{32,96},{48,240},{64,128},{80,16},{96,160},{112,48... | collective-permute-start | bytes 589832 | tf_op jit(solution)/shard_map/ppermute | solution.py:197
  47.7 13.4 %collective-permute-start.6 = (bf16[768,128]{1,0:T(8,128)(2,1)S(1)}, bf16[768,128]{1,0:T(8,128)(2,1)S(1)}, u32[]{:S(2)}, u32[]{:S(2)}) collective-permute-start(bf16[768,128]{1,0:T(8,128)(2,1)S(1)} %get-tuple-element.53), channel_id=1, source_target_pairs={{0,192},{16,80},{32,224},{48,112},{64,0},{80,144},{96,32},{112,176... | collective-permute-start | bytes 589832 | tf_op jit(solution)/shard_map/ppermute | solution.py:197
  52.0 9.9 %collective-permute-start.9 = (bf16[128,256]{1,0:T(8,128)(2,1)S(1)}, bf16[128,256]{1,0:T(8,128)(2,1)S(1)}, u32[]{:S(2)}, u32[]{:S(2)}) collective-permute-start(bf16[128,256]{1,0:T(8,128)(2,1)S(1)} %slice.67), channel_id=1, source_target_pairs={{16,0},{32,16},{48,32},{64,48},{80,64},{96,80},{112,96},{128,112},... | collective-permute-start | bytes 196616 | tf_op jit(solution)/shard_map/ppermute | solution.py:245
  61.9 18.7 %all-to-all-start = ((bf16[3,256,128]{2,1,0:T(8,128)(2,1)}), bf16[3,256,128]{2,1,0:T(8,128)(2,1)S(1)}, u32[]{:S(2)}, u32[]{:S(2)}) async-start(bf16[3,256,128]{2,1,0:T(8,128)(2,1)} %bitcast), calls=%async_computation | async-start | bytes 393216 | tf_op jit(solution)/shard_map/all_to_all | solution.py:248

commit v16 on v11

--- a/solution.py
+++ b/solution.py
@@ -241,7 +241,6 @@
     back = lax.ppermute(tail, "dp", [((i + 1) % ranks, i) for i in range(ranks)])
 
     up, down = rounded_total(part[2], up, far), rounded_total(part[-2], down)
-    down, back = lax.optimization_barrier((down, back))
     up, down = send(up, along_y(2)), send(down, along_y(-2))
     sums = rounded_total(part[0], up, down, *near).reshape(NZ, -1, UNIT)
     grads = backward(same, stays, queries, key_rows, value_rows, grad_ctx, back)

time: 84 us -> 82.8 us (0.986)
  the two profiles are of different devices: /device:TPU:6 before, /device:TPU:65 now
where the time goes in v16:
time: 82.8 us; the launch traced here: 82.4 us
  starting transfers between devices  41.3 us (50%)
  blocking collectives  20.5 us (25%)
  Pallas kernels  13.1 us (16%)
  waiting for transfers between devices  4.52 us (5%)
  other arithmetic  1.36 us (2%)
  between operations  0.86 us (1%)
    ppermute x8, starting transfers between devices, send(): lax.ppermute(block, 'dp', [(index(*p), index(*to(*p))) for p in PLACES])  30.5 us
    all_to_all x1, blocking collectives, local(): sums = lax.all_to_all(sums, 'dp', 0, 0, axis_index_groups=same_place())  20.5 us
    ppermute x1, starting transfers between devices, local(): lax.ppermute(tail, 'dp', [((i + 1) % ranks, i) for i in range(ranks)])  7.04 us
    pallas_call x1, Pallas kernels, backward(): pl.pallas_call(backward_kernel, in_specs=[VMEM] * 7, out_specs=[VMEM] * 3...  3.77 us
    ppermute x1, starting transfers between devices, local(): lax.ppermute(leave, 'dp', [(i, (i + 1) % ranks) for i in range(ranks)])  3.76 us
    pallas_call x1, Pallas kernels, staying_context(): pl.pallas_call(context_kernel, in_specs=[VMEM] * 5 + [pl.BlockSpec(memory...  2.95 us
    ppermute x1, waiting for transfers between devices, local(): lax.ppermute(tail, 'dp', [((i + 1) % ranks, i) for i in range(ranks)])  2.92 us
    pallas_call x2, Pallas kernels, partial_grad(): pl.pallas_call(functools.partial(partial_kernel, other), in_specs=[VMEM,...  2.78 us
  transfers between devices with their start and end apart: 10, of which 2 were waited for; matrix products, arithmetic and copies ran while one was open for 0% of the time, Pallas kernels for 12%

profile of v16, /device:TPU:65, one launch (start us, length us, event | category | flops | bytes accessed | tf_op | source)
XLA Modules:
  0.0 82.4 jit_solution(6378945376269410136)
XLA Ops:
  0.6 1.7 %shard_map.102 = (bf16[256,128]{1,0:T(8,128)(2,1)S(1)}, s32[8,384]{1,0:T(8,128)S(1)}, s32[8,128]{1,0:T(8,128)S(1)}, bf16[384,256]{1,0:T(8,128)(2,1)S(1)}, bf16[3...) custom-call(s32[384]{0:T(512)} %ids_hbm.1, s32[384]{0:T(512)} %slot_hbm.1, bf16[384,256]{1,0:T(8,128)(2,1)} %q_ref.1, ...), custom_call_target="tpu_custom_call" | custom-call | tf_op jit(solution)/shard_map/pallas_call | solution.py:68
  2.4 3.8 %collective-permute-start = (bf16[256,128]{1,0:T(8,128)(2,1)S(1)}, bf16[256,128]{1,0:T(8,128)(2,1)S(1)}, u32[]{:S(2)}, u32[]{:S(2)}) collective-permute-start(bf16[256,128]{1,0:T(8,128)(2,1)S(1)} %get-tuple-element.38), channel_id=1, source_target_pairs={{0,16},{16,32},{32,48},{48,64},{64,80},{80,96},{96,112},{112,128},... | collective-permute-start | bytes 196616 | tf_op jit(solution)/shard_map/ppermute | solution.py:224
  6.2 0.0 copy-start
  6.2 2.9 %shard_map.103 = (bf16[256,384]{1,0:T(8,128)(2,1)S(1)}, bf16[512,6144]{1,0:T(8,128)(2,1)S(1)}) custom-call(s32[8,384]{1,0:T(8,128)S(1)} %get-tuple-element.30.same_ref, s32[8,128]{1,0:T(8,128)S(1)} %get-tuple-element.31.stays_ref, bf16[384,256]{1,0:T(8,128)(2,1)S(1)} %get-tuple-element.32.q_ref, bf16[384,256]{1,0:T(8,128)(2,1)S(1)} %get-tuple-element.33.k_ref, ...), custom_call_target="tpu_custom_call" | custom-call | tf_op jit(solution)/shard_map/pallas_call | solution.py:98
  9.1 0.7 copy-done
  9.9 1.8 %shard_map.104.g_ref = bf16[512,256]{1,0:T(8,128)(2,1)S(1)} custom-call(bf16[512,6144]{1,0:T(8,128)(2,1)S(1)} %get-tuple-element.36.g_ref, bf16[256,6144]{1,0:T(8,128)(2,1)S(1)} %copy-done), custom_call_target="tpu_custom_call" | custom-call | tf_op jit(solution)/shard_map/pallas_call | solution.py:148
  11.7 0.0 collective-permute-done.came_ref
  11.7 1.4 %shard_map.106 = bf16[6144,128]{1,0:T(8,128)(2,1)S(1)} custom-call(bf16[256,384]{1,0:T(8,128)(2,1)S(1)} %get-tuple-element.37.stay_ref, bf16[256,128]{1,0:T(8,128)(2,1)S(1)} %collective-permute-done.came_ref, bf16[512,6144]{1,0:T(8,128)(2,1)S(1)} %get-tuple-element.36.g_ref), custom_call_target="tpu_custom_call" | custom-call | tf_op jit(solution)/shard_map/pallas_call | solution.py:129
  13.1 11.3 %collective-permute-start.1 = (bf16[6144,128]{1,0:T(8,128)(2,1)S(1)}, bf16[6144,128]{1,0:T(8,128)(2,1)S(1)}, u32[]{:S(2)}, u32[]{:S(2)}) collective-permute-start(bf16[6144,128]{1,0:T(8,128)(2,1)S(1)} %shard_map.106), channel_id=1, source_target_pairs={{0,16},{16,0},{32,48},{48,32},{64,80},{80,64},{96,112},{112,96},{1... | collective-permute-start | bytes 4718600 | tf_op jit(solution)/shard_map/ppermute | solution.py:197
  24.4 1.4 %shard_map.105 = bf16[6144,128]{1,0:T(8,128)(2,1)S(1)} custom-call(bf16[256,384]{1,0:T(8,128)(2,1)S(1)} %get-tuple-element.37.stay_ref, bf16[256,128]{1,0:T(8,128)(2,1)S(1)} %collective-permute-done.came_ref, bf16[512,6144]{1,0:T(8,128)(2,1)S(1)} %get-tuple-element.36.g_ref), custom_call_target="tpu_custom_call" | custom-call | tf_op jit(solution)/shard_map/pallas_call | solution.py:129
  25.8 0.0 copy-start.1
  25.8 0.0 copy-start.2
  25.8 0.0 copy-start.3
  25.8 1.6 %collective-permute-done.1 = bf16[6144,128]{1,0:T(8,128)(2,1)S(1)} collective-permute-done((bf16[6144,128]{1,0:T(8,128)(2,1)S(1)}, bf16[6144,128]{1,0:T(8,128)(2,1)S(1)}, u32[]{:S(2)}, u32[]{:S(2)}) %collective-permute-start.1) | collective-permute-done | bytes 1572896 | tf_op jit(solution)/shard_map/ppermute | solution.py:197
  27.4 0.4 add_convert_fusion.3
  27.8 2.7 %collective-permute-start.2 = (bf16[768,128]{1,0:T(8,128)(2,1)S(1)}, bf16[768,128]{1,0:T(8,128)(2,1)S(1)}, u32[]{:S(2)}, u32[]{:S(2)}) collective-permute-start(bf16[768,128]{1,0:T(8,128)(2,1)S(1)} %get-tuple-element.42), channel_id=1, source_target_pairs={{0,32},{16,240},{32,64},{48,16},{64,96},{80,48},{96,128},{112,80},... | collective-permute-start | bytes 589832 | tf_op jit(solution)/shard_map/ppermute | solution.py:197
  30.5 1.9 %collective-permute-start.3 = (bf16[768,128]{1,0:T(8,128)(2,1)S(1)}, bf16[768,128]{1,0:T(8,128)(2,1)S(1)}, u32[]{:S(2)}, u32[]{:S(2)}) collective-permute-start(bf16[768,128]{1,0:T(8,128)(2,1)S(1)} %get-tuple-element.43), channel_id=1, source_target_pairs={{0,64},{16,208},{32,96},{48,240},{64,128},{80,16},{96,160},{112,48... | collective-permute-start | bytes 589832 | tf_op jit(solution)/shard_map/ppermute | solution.py:197
  32.5 3.1 %collective-permute-start.5 = (bf16[768,128]{1,0:T(8,128)(2,1)S(1)}, bf16[768,128]{1,0:T(8,128)(2,1)S(1)}, u32[]{:S(2)}, u32[]{:S(2)}) collective-permute-start(bf16[768,128]{1,0:T(8,128)(2,1)S(1)} %get-tuple-element.45), channel_id=1, source_target_pairs={{0,224},{16,48},{32,0},{48,80},{64,32},{80,112},{96,64},{112,144},... | collective-permute-start | bytes 589832 | tf_op jit(solution)/shard_map/ppermute | solution.py:197
  35.6 3.4 %collective-permute-start.7 = (bf16[768,128]{1,0:T(8,128)(2,1)S(1)}, bf16[768,128]{1,0:T(8,128)(2,1)S(1)}, u32[]{:S(2)}, u32[]{:S(2)}) collective-permute-start(bf16[768,128]{1,0:T(8,128)(2,1)S(1)} %get-tuple-element.46), channel_id=1, source_target_pairs={{0,32},{16,240},{32,64},{48,16},{64,96},{80,48},{96,128},{112,80},... | collective-permute-start | bytes 589832 | tf_op jit(solution)/shard_map/ppermute | solution.py:197
  39.0 1.9 %collective-permute-start.8 = (bf16[768,128]{1,0:T(8,128)(2,1)S(1)}, bf16[768,128]{1,0:T(8,128)(2,1)S(1)}, u32[]{:S(2)}, u32[]{:S(2)}) collective-permute-start(bf16[768,128]{1,0:T(8,128)(2,1)S(1)} %get-tuple-element.47), channel_id=1, source_target_pairs={{0,224},{16,48},{32,0},{48,80},{64,32},{80,112},{96,64},{112,144},... | collective-permute-start | bytes 589832 | tf_op jit(solution)/shard_map/ppermute | solution.py:197
  40.9 0.0 collective-permute-done.2
  40.9 0.0 collective-permute-done.3
  40.9 0.1 add_convert_fusion.2
  41.0 3.1 %collective-permute-start.4 = (bf16[768,128]{1,0:T(8,128)(2,1)S(1)}, bf16[768,128]{1,0:T(8,128)(2,1)S(1)}, u32[]{:S(2)}, u32[]{:S(2)}) collective-permute-start(bf16[768,128]{1,0:T(8,128)(2,1)S(1)} %add_convert_fusion.2), channel_id=1, source_target_pairs={{0,64},{16,208},{32,96},{48,240},{64,128},{80,16},{96,160},{112,48... | collective-permute-start | bytes 589832 | tf_op jit(solution)/shard_map/ppermute | solution.py:197
  44.1 0.0 collective-permute-done.5
  44.1 0.1 add_convert_fusion.1
  44.2 3.1 %collective-permute-start.6 = (bf16[768,128]{1,0:T(8,128)(2,1)S(1)}, bf16[768,128]{1,0:T(8,128)(2,1)S(1)}, u32[]{:S(2)}, u32[]{:S(2)}) collective-permute-start(bf16[768,128]{1,0:T(8,128)(2,1)S(1)} %add_convert_fusion.1), channel_id=1, source_target_pairs={{0,192},{16,80},{32,224},{48,112},{64,0},{80,144},{96,32},{112,176... | collective-permute-start | bytes 589832 | tf_op jit(solution)/shard_map/ppermute | solution.py:197
  47.3 7.0 %collective-permute-start.9 = (bf16[128,256]{1,0:T(8,128)(2,1)S(1)}, bf16[128,256]{1,0:T(8,128)(2,1)S(1)}, u32[]{:S(2)}, u32[]{:S(2)}) collective-permute-start(bf16[128,256]{1,0:T(8,128)(2,1)S(1)} %slice.67), channel_id=1, source_target_pairs={{16,0},{32,16},{48,32},{64,48},{80,64},{96,80},{112,96},{128,112},... | collective-permute-start | bytes 196616 | tf_op jit(solution)/shard_map/ppermute | solution.py:241
  54.3 2.9 %collective-permute-done.9.back_ref = bf16[128,256]{1,0:T(8,128)(2,1)S(1)} collective-permute-done((bf16[128,256]{1,0:T(8,128)(2,1)S(1)}, bf16[128,256]{1,0:T(8,128)(2,1)S(1)}, u32[]{:S(2)}, u32[]{:S(2)}) %collective-permute-start.9) | collective-permute-done | bytes 65568 | tf_op jit(solution)/shard_map/ppermute | solution.py:241
  57.3 0.0 copy-done.1
  57.3 0.0 copy-done.2
  57.3 0.0 copy-done.3
  57.3 3.8 %shard_map.107 = (bf16[384,256]{1,0:T(8,128)(2,1)}, bf16[384,256]{1,0:T(8,128)(2,1)}, bf16[384,256]{1,0:T(8,128)(2,1)}) custom-call(s32[8,384]{1,0:T(8,128)S(1)} %get-tuple-element.30.same_ref, s32[8,128]{1,0:T(8,128)S(1)} %get-tuple-element.31.stays_ref, bf16[384,256]{1,0:T(8,128)(2,1)S(1)} %copy-done.1, bf16[384,256]{1,0:T(8,128)(2,1)S(1)} %copy-done.2, ...), custom_call_target="tpu_custom_call" | custom-call | tf_op jit(solution)/shard_map/pallas_call | solution.py:180
  61.0 0.0 collective-permute-done.7
  61.0 0.0 collective-permute-done.8
  61.0 0.0 collective-permute-done.4
  61.1 0.0 collective-permute-done.6
  61.1 0.1 add_convert_fusion
  61.2 20.5 %all_to_all.5 = bf16[3,256,128]{2,1,0:T(8,128)(2,1)S(1)} all-to-all(bf16[3,256,128]{2,1,0:T(8,128)(2,1)S(1)} %bitcast.3), channel_id=1, replica_groups={{0,256,512},{16,272,528},{32,288,544},{48,304,560},{64,320,576},{80,336..., dimensions={0} | all-to-all | bytes 393216 | tf_op jit(solution)/shard_map/all_to_all | solution.py:248
  81.7 0.7 add_bitcast_fusion
  (1 shorter events, 0.0 us)
Async XLA Ops:
  2.4 9.3 %collective-permute-start = (bf16[256,128]{1,0:T(8,128)(2,1)S(1)}, bf16[256,128]{1,0:T(8,128)(2,1)S(1)}, u32[]{:S(2)}, u32[]{:S(2)}) collective-permute-start(bf16[256,128]{1,0:T(8,128)(2,1)S(1)} %get-tuple-element.38), channel_id=1, source_target_pairs={{0,16},{16,32},{32,48},{48,64},{64,80},{80,96},{96,112},{112,128},... | collective-permute-start | bytes 196616 | tf_op jit(solution)/shard_map/ppermute | solution.py:224
  6.2 3.7 %copy-start = (bf16[256,6144]{1,0:T(8,128)(2,1)S(1)}, bf16[256,6144]{1,0:T(8,128)(2,1)}, u32[]{:S(2)}) copy-start(bf16[256,6144]{1,0:T(8,128)(2,1)} %w_ref.1) | copy-start | bytes 9437188
  13.1 14.3 %collective-permute-start.1 = (bf16[6144,128]{1,0:T(8,128)(2,1)S(1)}, bf16[6144,128]{1,0:T(8,128)(2,1)S(1)}, u32[]{:S(2)}, u32[]{:S(2)}) collective-permute-start(bf16[6144,128]{1,0:T(8,128)(2,1)S(1)} %shard_map.106), channel_id=1, source_target_pairs={{0,16},{16,0},{32,48},{48,32},{64,80},{80,64},{96,112},{112,96},{1... | collective-permute-start | bytes 4718600 | tf_op jit(solution)/shard_map/ppermute | solution.py:197
  25.8 31.5 %copy-start.1 = (bf16[384,256]{1,0:T(8,128)(2,1)S(1)}, bf16[384,256]{1,0:T(8,128)(2,1)}, u32[]{:S(2)}) copy-start(bf16[384,256]{1,0:T(8,128)(2,1)} %q_ref.1) | copy-start | bytes 589828
  25.8 31.4 %copy-start.2 = (bf16[384,256]{1,0:T(8,128)(2,1)S(1)}, bf16[384,256]{1,0:T(8,128)(2,1)}, u32[]{:S(2)}) copy-start(bf16[384,256]{1,0:T(8,128)(2,1)} %k_ref.1) | copy-start | bytes 589828
  25.8 31.4 %copy-start.3 = (bf16[384,256]{1,0:T(8,128)(2,1)S(1)}, bf16[384,256]{1,0:T(8,128)(2,1)}, u32[]{:S(2)}) copy-start(bf16[384,256]{1,0:T(8,128)(2,1)} %v_ref.1) | copy-start | bytes 589828
  27.8 13.1 %collective-permute-start.2 = (bf16[768,128]{1,0:T(8,128)(2,1)S(1)}, bf16[768,128]{1,0:T(8,128)(2,1)S(1)}, u32[]{:S(2)}, u32[]{:S(2)}) collective-permute-start(bf16[768,128]{1,0:T(8,128)(2,1)S(1)} %get-tuple-element.42), channel_id=1, source_target_pairs={{0,32},{16,240},{32,64},{48,16},{64,96},{80,48},{96,128},{112,80},... | collective-permute-start | bytes 589832 | tf_op jit(solution)/shard_map/ppermute | solution.py:197
  30.5 10.4 %collective-permute-start.3 = (bf16[768,128]{1,0:T(8,128)(2,1)S(1)}, bf16[768,128]{1,0:T(8,128)(2,1)S(1)}, u32[]{:S(2)}, u32[]{:S(2)}) collective-permute-start(bf16[768,128]{1,0:T(8,128)(2,1)S(1)} %get-tuple-element.43), channel_id=1, source_target_pairs={{0,64},{16,208},{32,96},{48,240},{64,128},{80,16},{96,160},{112,48... | collective-permute-start | bytes 589832 | tf_op jit(solution)/shard_map/ppermute | solution.py:197
  32.5 11.6 %collective-permute-start.5 = (bf16[768,128]{1,0:T(8,128)(2,1)S(1)}, bf16[768,128]{1,0:T(8,128)(2,1)S(1)}, u32[]{:S(2)}, u32[]{:S(2)}) collective-permute-start(bf16[768,128]{1,0:T(8,128)(2,1)S(1)} %get-tuple-element.45), channel_id=1, source_target_pairs={{0,224},{16,48},{32,0},{48,80},{64,32},{80,112},{96,64},{112,144},... | collective-permute-start | bytes 589832 | tf_op jit(solution)/shard_map/ppermute | solution.py:197
  35.6 25.5 %collective-permute-start.7 = (bf16[768,128]{1,0:T(8,128)(2,1)S(1)}, bf16[768,128]{1,0:T(8,128)(2,1)S(1)}, u32[]{:S(2)}, u32[]{:S(2)}) collective-permute-start(bf16[768,128]{1,0:T(8,128)(2,1)S(1)} %get-tuple-element.46), channel_id=1, source_target_pairs={{0,32},{16,240},{32,64},{48,16},{64,96},{80,48},{96,128},{112,80},... | collective-permute-start | bytes 589832 | tf_op jit(solution)/shard_map/ppermute | solution.py:197
  39.0 22.1 %collective-permute-start.8 = (bf16[768,128]{1,0:T(8,128)(2,1)S(1)}, bf16[768,128]{1,0:T(8,128)(2,1)S(1)}, u32[]{:S(2)}, u32[]{:S(2)}) collective-permute-start(bf16[768,128]{1,0:T(8,128)(2,1)S(1)} %get-tuple-element.47), channel_id=1, source_target_pairs={{0,224},{16,48},{32,0},{48,80},{64,32},{80,112},{96,64},{112,144},... | collective-permute-start | bytes 589832 | tf_op jit(solution)/shard_map/ppermute | solution.py:197
  41.0 20.0 %collective-permute-start.4 = (bf16[768,128]{1,0:T(8,128)(2,1)S(1)}, bf16[768,128]{1,0:T(8,128)(2,1)S(1)}, u32[]{:S(2)}, u32[]{:S(2)}) collective-permute-start(bf16[768,128]{1,0:T(8,128)(2,1)S(1)} %add_convert_fusion.2), channel_id=1, source_target_pairs={{0,64},{16,208},{32,96},{48,240},{64,128},{80,16},{96,160},{112,48... | collective-permute-start | bytes 589832 | tf_op jit(solution)/shard_map/ppermute | solution.py:197
  44.2 16.9 %collective-permute-start.6 = (bf16[768,128]{1,0:T(8,128)(2,1)S(1)}, bf16[768,128]{1,0:T(8,128)(2,1)S(1)}, u32[]{:S(2)}, u32[]{:S(2)}) collective-permute-start(bf16[768,128]{1,0:T(8,128)(2,1)S(1)} %add_convert_fusion.1), channel_id=1, source_target_pairs={{0,192},{16,80},{32,224},{48,112},{64,0},{80,144},{96,32},{112,176... | collective-permute-start | bytes 589832 | tf_op jit(solution)/shard_map/ppermute | solution.py:197
  47.3 10.0 %collective-permute-start.9 = (bf16[128,256]{1,0:T(8,128)(2,1)S(1)}, bf16[128,256]{1,0:T(8,128)(2,1)S(1)}, u32[]{:S(2)}, u32[]{:S(2)}) collective-permute-start(bf16[128,256]{1,0:T(8,128)(2,1)S(1)} %slice.67), channel_id=1, source_target_pairs={{16,0},{32,16},{48,32},{64,48},{80,64},{96,80},{112,96},{128,112},... | collective-permute-start | bytes 196616 | tf_op jit(solution)/shard_map/ppermute | solution.py:241
